TPU v7x, 32 devices: a whole 2x2x4 slice. The times are simulated.
32 devices in a mesh: groups: 2 (over x), dp: 16 (over z, y, core).
Axes of the slice: x: 2, y: 2, z: 4, core: 2. Of those that a mesh axis runs over, the one named last changes fastest.
Arguments:
- logits: bfloat16 [64, 32000], P(('groups', 'dp')), parts along dimension 0, may hold values from -4 to 152
- embed: bfloat16 [32000, 4096], P('dp'), may hold values from -512 to 512
- norm_gain: bfloat16 [4096], replicated, may hold values from 0.25 to 1.75
- w_gate: bfloat16 [4096, 14336], P(None, 'dp'), may hold values from -0.09375 to 0.09375
- w_up: bfloat16 [4096, 14336], P(None, 'dp'), may hold values from -0.09375 to 0.09375
- w_down: bfloat16 [14336, 4096], P('dp'), may hold values from -0.046875 to 0.046875
- head: bfloat16 [4096], replicated, may hold values from -0.09375 to 0.09375
- counts: int32 [8], P('groups'), parts along dimension 0, may hold values from 2 to 8, as said below
Outputs:
- guidance: bfloat16 [64, 32000], P(('groups', 'dp')), parts along dimension 0
- rewards: float32 [8], P('groups'), parts along dimension 0
There are 2 independent parts, one for each index of `groups`. A program takes and returns all parts, laid end to end along the dimension named above; an argument that names none is the same for every part. Nothing has to cross between parts.
Inputs may be any that keep to these rules, and one draw needn't show every extreme that they name: `counts`: some request is full in every draw.
All inputs are finite; a program needn't handle non-finite values.
Results may differ from a plain program's by a relative error of at most 0.0095.
Values may be sent and summed in bfloat16 or wider, within the bound.
No kernel may reach another device: no remote copies, remote signals or barrier semaphores. Data moves between devices by JAX's collectives and lax.ppermute only.
A program may use at most 128 MiB of HBM per device.

v0:
```python
import math

import jax
import jax.numpy as jnp
from jax import lax
from jax.sharding import PartitionSpec as P

VOC = 32000


def norm_rows(x_rows, gain32):
    inv = lax.rsqrt(jnp.mean(x_rows * x_rows, axis=-1, keepdims=True) + 1e-05)
    return (inv, (x_rows * inv * gain32).astype(jnp.bfloat16))


def input_grad(x_rows, inv, d_normed, gain32, valid_rows, head32):
    scaled = d_normed * gain32
    result = inv * scaled - x_rows * inv * inv * inv * jnp.mean(
        scaled * x_rows, axis=-1, keepdims=True
    )
    return (result + valid_rows[:, None] * head32[None, :]).astype(jnp.bfloat16)


def valid_mask(position, request_len, counts):
    request = position // request_len
    member = request[:, None] == jnp.arange(counts.shape[0], dtype=jnp.int32)[None, :]
    limit = jnp.sum(jnp.where(member, counts[None, :], 0), axis=-1)
    return ((position % request_len < limit).astype(jnp.float32), member.astype(jnp.float32))


def hidden_grads(a_gate, b_up, d_hidden, w_down, head32):
    f32 = jnp.float32
    sigma = jax.nn.sigmoid(a_gate)
    active = a_gate * sigma
    hidden = (active * b_up).astype(jnp.bfloat16)
    branch_rows = jnp.dot(hidden, w_down, preferred_element_type=f32)
    branch = jnp.dot(branch_rows, head32, precision=lax.Precision.HIGHEST)
    d_gate = (d_hidden * b_up * sigma * (1.0 + a_gate * (1.0 - sigma))).astype(jnp.bfloat16)
    d_up = (d_hidden * active).astype(jnp.bfloat16)
    return (branch, d_gate, d_up)


def body(logits, embed, norm_gain, w_gate, w_up, w_down, head, counts):
    f32 = jnp.float32
    devices = lax.axis_size("dp")
    rank = lax.axis_index("dp")
    rows = logits.shape[0]
    total = rows * devices
    request_len = total // counts.shape[0]
    gain32 = norm_gain.astype(f32)
    head32 = head.astype(f32)
    probs32 = jax.nn.softmax(logits.astype(f32), axis=-1)
    probs = probs32.astype(jnp.bfloat16)
    slices = lax.all_to_all(probs, "dp", split_axis=1, concat_axis=0, tiled=True)
    position_all = jnp.arange(total, dtype=jnp.int32)
    valid_all, member_all = valid_mask(position_all, request_len, counts)
    upstream = (valid_all[:, None] * head32[None, :]).astype(jnp.bfloat16)
    d_hidden = jnp.einsum("td,fd->tf", upstream, w_down, preferred_element_type=f32)
    position_own = rank * rows + jnp.arange(rows, dtype=jnp.int32)
    valid_own, member_own = valid_mask(position_own, request_len, counts)
    partial_value = jnp.dot(slices, embed, preferred_element_type=f32)
    x_rows = lax.psum_scatter(partial_value, "dp", scatter_dimension=0, tiled=True)
    inv, normed_rows = norm_rows(x_rows, gain32)
    normed = lax.all_gather(normed_rows, "dp", axis=0, tiled=True)
    a_gate = jnp.dot(normed, w_gate, preferred_element_type=f32)
    b_up = jnp.dot(normed, w_up, preferred_element_type=f32)
    branch, d_gate, d_up = hidden_grads(a_gate, b_up, d_hidden, w_down, head32)
    d_part = jnp.einsum("tf,df->td", d_gate, w_gate, preferred_element_type=f32)
    d_part = d_part + jnp.einsum("tf,df->td", d_up, w_up, preferred_element_type=f32)
    d_rows, branch_rows = (
        lax.psum_scatter(d_part, "dp", scatter_dimension=0, tiled=True),
        lax.psum_scatter(branch, "dp", scatter_dimension=0, tiled=True),
    )
    score_own = jnp.dot(x_rows, head32, precision=lax.Precision.HIGHEST) + branch_rows
    own_sums = jnp.dot(valid_own * score_own, member_own, precision=lax.Precision.HIGHEST)
    sums = lax.psum(own_sums, "dp")
    d_own = input_grad(x_rows, inv, d_rows, gain32, valid_own, head32)
    d_input = lax.all_gather(d_own, "dp", axis=0, tiled=True)
    rewards = sums / counts.astype(f32)
    d_slices = jnp.einsum("td,vd->tv", d_input, embed, preferred_element_type=f32)
    d_probs = lax.all_to_all(
        d_slices.astype(jnp.bfloat16), "dp", split_axis=0, concat_axis=1, tiled=True
    ).astype(d_slices.dtype)
    d_logits = probs32 * (d_probs - jnp.sum(probs32 * d_probs, axis=-1, keepdims=True))
    guidance = (math.sqrt(VOC) * d_logits).astype(jnp.bfloat16)
    return (guidance, rewards)


def solution(mesh):
    placed = (
        P(("groups", "dp"), None),
        P("dp", None),
        P(),
        P(None, "dp"),
        P(None, "dp"),
        P("dp", None),
        P(),
        P("groups"),
    )
    return jax.shard_map(
        body,
        mesh=mesh,
        in_specs=placed,
        out_specs=(P(("groups", "dp"), None), P("groups")),
        check_vma=False,
    )
```

profile of v0, /device:TPU:0, one launch (start us, length us, event | category | flops | bytes accessed | tf_op | source)
XLA Modules:
  0.0 335.2 jit_solution(812883220374164035)
XLA Ops:
  7.2 1.3 reduce_max.14
  8.5 1.4 fusion.7
  9.8 1.2 fusion.22
  11.3 0.8 copy.15
  12.1 7.4 %all-to-all-start = ((bf16[2,16,2000]{2,0,1:T(2,128)(2,1)}), bf16[2,16,2000]{2,0,1:T(2,128)(2,1)S(1)}, u32[]{:S(2)}, u32[]{:S(2)}) async-start(bf16[2,16,2000]{2,0,1:T(2,128)(2,1)} %copy.15), calls=%async_computation | async-start | bytes 262144 | tf_op jit(solution)/shard_map/all_to_all | solution.py:54
  19.5 0.7 select_reduce_fusion
  20.3 0.7 convert_element_type.66
  21.0 5.4 %fusion.3 = f32[32,896]{1,0:T(8,128)S(1)} fusion(bf16[896,4096]{1,0:T(8,128)(2,1)} %param.13, f32[4096]{0:T(1024)S(1)} %convert_element_type.66, f32[32]{0:T(128)S(1)} %compare_convert_fusion), kind=kOutput, calls=%fused_computation.9 | convolution fusion | flops 235143168 | bytes 7471232 | tf_op jit(solution)/shard_map/td,fd->tf/dot_general | solution.py:58
  26.4 1.0 all-to-all-done
  27.5 9.4 %fusion.24 = f32[32,4096]{1,0:T(8,128)} fusion(bf16[32,2000]{1,0:T(8,128)(2,1)S(1)} %all_to_all.27, bf16[2000,4096]{1,0:T(8,128)(2,1)} %param.9), kind=kOutput, calls=%fused_computation.60 | convolution fusion | flops 524288000 | bytes 17036288 | tf_op jit(solution)/shard_map/dot_general | solution.py:61
  37.3 0.6 dynamic-slice
  38.5 89.0 %all-reduce.6.cloned.1.call-done = f32[32,4096]{1,0:T(8,128)} async-done(((f32[32,4096]{1,0:T(8,128)}), f32[32,4096]{1,0:T(8,128)}) %all-reduce.6.cloned.1.call-update) | async-done | bytes 524304
  127.5 1.1 multiply_reduce_fusion.2
  128.6 1.0 fusion.14
  129.6 21.6 %all-gather = bf16[16,2,4096]{2,1,0:T(2,128)(2,1)S(1)} all-gather(bf16[1,2,4096]{2,1,0:T(2,128)(2,1)S(1)} %fusion.14), channel_id=1, replica_groups=mesh['groups'=2,'dp'=16] {'dp'}, dimensions={0}, use_global_device_ids=true | all-gather | bytes 278528 | tf_op jit(solution)/shard_map/all_gather | solution.py:64
  151.3 4.4 %fusion.26 = f32[32,896]{1,0:T(8,128)S(1)} fusion(bf16[32,4096]{1,0:T(8,128)(2,1)S(1)} %reshape.96, bf16[4096,896]{1,0:T(8,128)(2,1)} %param.11), kind=kOutput, calls=%fused_computation.62 | convolution fusion | flops 234881024 | bytes 7716864 | tf_op jit(solution)/shard_map/dot_general | solution.py:65
  155.7 4.4 %fusion.25 = f32[32,896]{1,0:T(8,128)S(1)} fusion(bf16[32,4096]{1,0:T(8,128)(2,1)S(1)} %reshape.96, bf16[4096,896]{1,0:T(8,128)(2,1)} %param.12), kind=kOutput, calls=%fused_computation.61 | convolution fusion | flops 234881024 | bytes 7716864 | tf_op jit(solution)/shard_map/dot_general | solution.py:66
  160.2 2.2 fusion.9
  162.5 3.1 convolution_add_fusion
  165.6 4.5 %fusion.10 = f32[32,4096]{1,0:T(8,128)S(1)} fusion(bf16[896,4096]{1,0:T(8,128)(2,1)} %param.13, f32[32,896]{1,0:T(8,128)S(1)} %fusion.25, f32[32,896]{1,0:T(8,128)S(1)} %fusion.26), kind=kOutput, calls=%fused_computation.24 | convolution fusion | flops 235053056 | bytes 8093696 | tf_op jit(solution)/shard_map/dot_general | solution.py:36
  170.4 29.9 %all-reduce.2 = f32[32]{0:T(128)S(1)} all-reduce(f32[32]{0:T(128)S(1)} %convolution_bitcast_fusion.1), channel_id=4, replica_groups=mesh['groups'=2,'dp'=16] {'dp'}, use_global_device_ids=true, to_apply=%region_9.10.clone | all-reduce | flops 32 | bytes 256
  200.3 1.2 fusion.2
  201.5 51.6 %all-reduce.8.cloned.1.call-done = f32[32,4096]{1,0:T(8,128)} async-done(((f32[32,4096]{1,0:T(8,128)}), f32[32,4096]{1,0:T(8,128)}) %all-reduce.8.cloned.1.call-update) | async-done | bytes 524304
  253.1 1.1 multiply_reduce_fusion.1
  254.2 1.1 fusion.15
  255.3 21.7 %all-gather.1 = bf16[16,2,4096]{2,1,0:T(2,128)(2,1)S(1)} all-gather(bf16[1,2,4096]{2,1,0:T(2,128)(2,1)S(1)} %fusion.15), channel_id=1, replica_groups=mesh['groups'=2,'dp'=16] {'dp'}, dimensions={0}, use_global_device_ids=true | all-gather | bytes 278528 | tf_op jit(solution)/shard_map/all_gather | solution.py:78
  277.1 10.4 %convolution_convert_fusion = bf16[32,2000]{1,0:T(8,128)(2,1)S(1)} fusion(bf16[32,4096]{1,0:T(8,128)(2,1)S(1)} %reshape.98, bf16[2000,4096]{1,0:T(8,128)(2,1)} %param.9), kind=kOutput, calls=%fused_computation.1 | convolution fusion | flops 524352000 | bytes 16774144 | tf_op jit(solution)/shard_map/td,vd->tv/dot_general | solution.py:80
  287.6 0.8 all_to_all.28
  288.4 3.5 %all-to-all-start.1 = ((bf16[16,2,2000]{2,1,0:T(2,128)(2,1)}), bf16[16,2,2000]{2,1,0:T(2,128)(2,1)S(1)}, u32[]{:S(2)}, u32[]{:S(2)}) async-start(bf16[16,2,2000]{2,1,0:T(2,128)(2,1)} %all_to_all.28), calls=%async_computation.1 | async-start | bytes 262144 | tf_op jit(solution)/shard_map/all_to_all | solution.py:81
  292.1 33.8 %psum.7 = f32[4]{0:T(128)S(1)} all-reduce(f32[4]{0:T(128)S(1)} %convolution_bitcast_fusion), channel_id=1, replica_groups=mesh['groups'=2,'dp'=16] {'dp'}, use_global_device_ids=true, to_apply=%region_10.11 | all-reduce | flops 4 | bytes 32 | tf_op jit(solution)/shard_map/psum | solution.py:76
  325.9 0.5 convert_divide_fusion
  327.4 0.9 multiply_convert_fusion.2
  (43 shorter events, 2.6 us)
Async XLA Ops:
  12.1 15.3 %all-to-all-start = ((bf16[2,16,2000]{2,0,1:T(2,128)(2,1)}), bf16[2,16,2000]{2,0,1:T(2,128)(2,1)S(1)}, u32[]{:S(2)}, u32[]{:S(2)}) async-start(bf16[2,16,2000]{2,0,1:T(2,128)(2,1)} %copy.15), calls=%async_computation | async-start | bytes 262144 | tf_op jit(solution)/shard_map/all_to_all | solution.py:54
  19.5 108.1 %all-reduce.6.cloned.1.call-start = ((), (), s32[]{:S(2)}) async-start(), calls=%async_computation.2 | async-start | bytes 1048576
  27.5 9.5 %copy-start.2 = (s32[4]{0:T(128)S(1)}, s32[4]{0:T(128)}, u32[]{:S(2)}) copy-start(s32[4]{0:T(128)} %param.15) | copy-start | bytes 52
  27.5 9.7 %copy-start = (bf16[4096]{0:T(1024)(128)(2,1)S(1)}, bf16[4096]{0:T(1024)(128)(2,1)}, u32[]{:S(2)}) copy-start(bf16[4096]{0:T(1024)(128)(2,1)} %param.14) | copy-start | bytes 24580
  27.5 9.7 %copy-start.1 = (bf16[4096]{0:T(1024)(128)(2,1)S(1)}, bf16[4096]{0:T(1024)(128)(2,1)}, u32[]{:S(2)}) copy-start(bf16[4096]{0:T(1024)(128)(2,1)} %param.10) | copy-start | bytes 24580
  27.5 9.8 %copy-start.3 = (u32[32]{0:T(128)S(1)}, u32[32]{0:T(128)}, u32[]{:S(2)}) copy-start(u32[32]{0:T(128)} %constant.77) | copy-start | bytes 388
  37.0 216.1 %all-reduce.8.cloned.1.call-start = ((), (), s32[]{:S(2)}) async-start(), calls=%async_computation.3 | async-start | bytes 1048576
  151.3 8.9 %slice-start = ((s8[7340032]{0:T(1024)(128)(4,1)}), s8[4194304]{0:T(1024)(128)(4,1)S(1)}, s32[]{:S(2)}) async-start(s8[7340032]{0:T(1024)(128)(4,1)} %bitcast.38), calls=%async_computation.4 | async-start | bytes 8388608
  151.3 11.2 %slice-start.2 = ((s8[7340032]{0:T(1024)(128)(4,1)}), s8[4194304]{0:T(1024)(128)(4,1)S(1)}, s32[]{:S(2)}) async-start(s8[7340032]{0:T(1024)(128)(4,1)} %bitcast.40), calls=%async_computation.6 | async-start | bytes 8388608
  155.7 4.5 %slice-start.1 = ((s8[7340032]{0:T(1024)(128)(4,1)}), s8[3145728]{0:T(1024)(128)(4,1)S(1)}, s32[]{:S(2)}) async-start(s8[7340032]{0:T(1024)(128)(4,1)} %bitcast.38), calls=%async_computation.5 | async-start | bytes 6291456
  155.7 6.7 %slice-start.3 = ((s8[7340032]{0:T(1024)(128)(4,1)}), s8[3145728]{0:T(1024)(128)(4,1)S(1)}, s32[]{:S(2)}) async-start(s8[7340032]{0:T(1024)(128)(4,1)} %bitcast.40), calls=%async_computation.7 | async-start | bytes 6291456
  288.4 38.0 %all-to-all-start.1 = ((bf16[16,2,2000]{2,1,0:T(2,128)(2,1)}), bf16[16,2,2000]{2,1,0:T(2,128)(2,1)S(1)}, u32[]{:S(2)}, u32[]{:S(2)}) async-start(bf16[16,2,2000]{2,1,0:T(2,128)(2,1)} %all_to_all.28), calls=%async_computation.1 | async-start | bytes 262144 | tf_op jit(solution)/shard_map/all_to_all | solution.py:81
Sparse Core Ops, SparseCore 0:
  37.1 90.3 all-reduce.5
  165.7 87.3 all-reduce.7
where the time goes:
time: 336 us; the launch traced here: 335 us
  waiting for transfers between devices  142 us (42%)
  blocking collectives  107 us (32%)
  matrix products  45.6 us (14%)
  between operations  15 us (4%)
  other arithmetic  11.7 us (3%)
  starting transfers between devices  11 us (3%)
    unnamed x4, waiting for transfers between devices  141 us
    psum x1, blocking collectives, body(): sums = lax.psum(own_sums, 'dp')  33.8 us
    unnamed x1, blocking collectives  29.9 us
    all_gather x1, blocking collectives, body(): d_input = lax.all_gather(d_own, 'dp', axis=0, tiled=True)  21.7 us
    all_gather x1, blocking collectives, body(): normed = lax.all_gather(normed_rows, 'dp', axis=0, tiled=True)  21.6 us
    dot_general x1, matrix products, body(): jnp.einsum('td,vd->tv', d_input, embed, preferred_element_type=f32)  10.4 us
    dot_general x1, matrix products, body(): partial_value = jnp.dot(slices, embed, preferred_element_type=f32)  9.42 us
    all_to_all x1, starting transfers between devices, body(): lax.all_to_all(probs, 'dp', split_axis=1, concat_axis=0, tiled=True)  7.39 us
  transfers between devices with their start and end apart: 4, of which 3 were waited for; matrix products, arithmetic and copies ran while one was open for 4% of the time, Pallas kernels for 0%

commit v1 on v0

v1 whole, which is shorter than its diff:
```python
import math

import jax
import jax.numpy as jnp
from jax import lax
from jax.sharding import PartitionSpec as P

VOC = 32000


def exchange(blocks):
    return lax.all_to_all(blocks, "dp", split_axis=0, concat_axis=0, tiled=True)


def split3(value):
    hi = lax.reduce_precision(value, 8, 7)
    rest = value - hi
    mid = lax.reduce_precision(rest, 8, 7)
    low = rest - mid
    return jnp.stack([hi, mid, low], axis=-1).astype(jnp.bfloat16)


def all_sum(part, devices):
    tokens, width = part.shape
    own = width // devices
    blocks = part.reshape(tokens, devices, own).transpose(1, 0, 2)
    mine = jnp.sum(exchange(blocks).astype(jnp.float32), axis=0).astype(jnp.bfloat16)
    whole = exchange(jnp.broadcast_to(mine[None], (devices, tokens, own)))
    return whole.transpose(1, 0, 2).reshape(tokens, width).astype(jnp.float32)


def body(logits, embed, norm_gain, w_gate, w_up, w_down, head, counts):
    f32, bf16 = jnp.float32, jnp.bfloat16
    devices = lax.axis_size("dp")
    rows, voc = logits.shape
    part = voc // devices
    requests = counts.shape[0]
    total = rows * devices
    request_len = total // requests
    gain32 = norm_gain.astype(f32)
    head32 = head.astype(f32)
    probs32 = jax.nn.softmax(logits.astype(f32), axis=-1)
    probs = probs32.astype(bf16)
    slices = exchange(probs.reshape(rows, devices, part).transpose(1, 0, 2)).reshape(total, part)
    down_head = jnp.sum(w_down.astype(f32) * head32[None, :], axis=-1)
    position = jnp.arange(total, dtype=jnp.int32)
    member = (position // request_len)[:, None] == jnp.arange(requests, dtype=jnp.int32)[None, :]
    limit = jnp.sum(jnp.where(member, counts[None, :], 0), axis=-1)
    valid = (position % request_len < limit).astype(f32)
    partial_value = jnp.dot(slices, embed, preferred_element_type=f32)
    score_x = jnp.sum(partial_value * head32[None, :], axis=-1)
    x0 = all_sum(partial_value.astype(bf16), devices)
    inv = lax.rsqrt(jnp.mean(x0 * x0, axis=-1, keepdims=True) + 1e-05)
    normed = (x0 * inv * gain32).astype(bf16)
    a_gate = jnp.dot(normed, w_gate, preferred_element_type=f32)
    b_up = jnp.dot(normed, w_up, preferred_element_type=f32)
    sigma = jax.nn.sigmoid(a_gate)
    active = a_gate * sigma
    hidden = (active * b_up).astype(bf16).astype(f32)
    d_hidden = valid[:, None] * down_head[None, :]
    d_gate = (d_hidden * b_up * sigma * (1.0 + a_gate * (1.0 - sigma))).astype(bf16)
    d_up = (d_hidden * active).astype(bf16)
    score = score_x + jnp.sum(hidden * down_head[None, :], axis=-1)
    own_rewards = jnp.sum(jnp.where(member, (valid * score)[:, None], 0.0), axis=0)
    d_part = jnp.einsum("tf,df->td", d_gate, w_gate, preferred_element_type=f32)
    d_part = d_part + jnp.einsum("tf,df->td", d_up, w_up, preferred_element_type=f32)
    d_normed = all_sum(d_part.astype(bf16), devices)
    scaled = d_normed * gain32
    d_input = inv * scaled - x0 * inv * inv * inv * jnp.mean(scaled * x0, axis=-1, keepdims=True)
    d_input = (d_input + valid[:, None] * head32[None, :]).astype(bf16)
    d_slices = jnp.einsum("td,vd->tv", d_input, embed, preferred_element_type=f32).astype(bf16)
    extra = split3(own_rewards).reshape(1, 1, requests * 3)
    extra = jnp.broadcast_to(extra, (devices, rows, requests * 3))
    back = exchange(jnp.concatenate([d_slices.reshape(devices, rows, part), extra], axis=-1))
    sums = jnp.sum(back[:, 0, part:].astype(f32).reshape(devices, requests, 3), axis=(0, 2))
    rewards = sums / counts.astype(f32)
    d_probs = back[:, :, :part].transpose(1, 0, 2).reshape(rows, voc).astype(f32)
    d_logits = probs32 * (d_probs - jnp.sum(probs32 * d_probs, axis=-1, keepdims=True))
    guidance = (math.sqrt(VOC) * d_logits).astype(bf16)
    return (guidance, rewards)


def solution(mesh):
    placed = (
        P(("groups", "dp"), None),
        P("dp", None),
        P(),
        P(None, "dp"),
        P(None, "dp"),
        P("dp", None),
        P(),
        P("groups"),
    )
    return jax.shard_map(
        body,
        mesh=mesh,
        in_specs=placed,
        out_specs=(P(("groups", "dp"), None), P("groups")),
        check_vma=False,
    )
```

time: 336 us -> 125 us (0.37)
  waiting for transfers between devices: 142 us -> 41.8 us
  blocking collectives: 107 us -> 10.7 us
  matrix products: 45.6 us -> 30.1 us
  between operations: 15 us -> 0.93 us
  starting transfers between devices: 11 us -> 21.7 us
    unnamed x4 -> x0, waiting for transfers between devices: 141 us -> none
    all_gather x2 -> x0, blocking collectives: 43.3 us -> none  [the longest x1 21.7 us: body(): d_input = lax.all_gather(d_own, 'dp', axis=0, tiled=True)]
    all_to_all x2 -> x5, waiting for transfers between devices: 1.04 us -> 41.8 us  [exchange(): return lax.all_to_all(blocks, 'dp', split_axis=0, concat_axis=0, tiled=True)]
    psum x1 -> x0, blocking collectives: 33.8 us -> none  [body(): sums = lax.psum(own_sums, 'dp')]
    unnamed x1 -> x0, blocking collectives: 29.9 us -> none
    dot_general x5 -> x0, matrix products: 11.5 us -> none  [the longest x1 5.35 us: body(): jnp.einsum('td,fd->tf', upstream, w_down, preferred_element_type=f32)]
    all_to_all x2 -> x5, starting transfers between devices: 10.9 us -> 21.7 us  [exchange(): return lax.all_to_all(blocks, 'dp', split_axis=0, concat_axis=0, tiled=True)]
    all_to_all x0 -> x1, blocking collectives: none -> 10.7 us  [exchange(): return lax.all_to_all(blocks, 'dp', split_axis=0, concat_axis=0, tiled=True)]
  transfers between devices with their start and end apart: 4 -> 5, of which waited for: 3 -> 5; matrix products, arithmetic and copies ran while one was open for 4% -> 5% of each run, Pallas kernels for 0% -> 0%
where the time goes in v1:
time: 125 us; the launch traced here: 124 us
  waiting for transfers between devices  41.8 us (33%)
  matrix products  30.1 us (24%)
  starting transfers between devices  21.7 us (17%)
  other arithmetic  13.1 us (10%)
  blocking collectives  10.7 us (9%)
  local copies, waits for them, and re-layouts  5.82 us (5%)
    all_to_all x5, waiting for transfers between devices, exchange(): return lax.all_to_all(blocks, 'dp', split_axis=0, concat_axis=0, tiled=True)  41.8 us
    all_to_all x5, starting transfers between devices, exchange(): return lax.all_to_all(blocks, 'dp', split_axis=0, concat_axis=0, tiled=True)  21.7 us
    all_to_all x1, blocking collectives, exchange(): return lax.all_to_all(blocks, 'dp', split_axis=0, concat_axis=0, tiled=True)  10.7 us
    dot_general x1, matrix products, body(): jnp.einsum('td,vd->tv', d_input, embed, preferred_element_type=f32)  10.7 us
    dot_general x1, matrix products, body(): partial_value = jnp.dot(slices, embed, preferred_element_type=f32)  8.71 us
    dot_general x1, matrix products, body(): a_gate = jnp.dot(normed, w_gate, preferred_element_type=f32)  4.74 us
    reduce_sum x1, other arithmetic, body(): down_head = jnp.sum(w_down.astype(f32) * head32[None, :], axis=-1)  4.73 us
  transfers between devices with their start and end apart: 5, of which 5 were waited for; matrix products, arithmetic and copies ran while one was open for 5% of the time, Pallas kernels for 0%

profile of v1, /device:TPU:0, one launch (start us, length us, event | category | flops | bytes accessed | tf_op | source)
XLA Modules:
  0.0 124.1 jit_solution(6803401456506069758)
XLA Ops:
  0.6 1.3 %reduce_max.14 = bf16[2]{0:T(256)(128)(2,1)S(1)} reduce(bf16[2,32000]{1,0:T(2,128)(2,1)} %param.8, bf16[]{:T(256)} %constant.39.clone.1), dimensions={1}, to_apply=%region_0.0 | reduce | flops 63998 | bytes 128006 | tf_op jit(solution)/shard_map/reduce_max | solution.py:42
  1.9 1.4 %fusion.9 = f32[2]{0:T(128)S(1)} fusion(bf16[2,32000]{1,0:T(2,128)(2,1)} %param.8, f32[2]{0:T(128)S(1)} %reduce_max.15), kind=kLoop, calls=%fused_computation.26 | loop fusion | flops 191998 | bytes 128016 | tf_op jit(solution)/shard_map/reduce_sum | solution.py:42
  3.3 1.9 %fusion.32 = (bf16[2,32000]{1,0:T(2,128)(2,1)S(1)}, f32[2,32000]{1,0:T(2,128)}) fusion(f32[2]{0:T(128)S(1)} %fusion.9, f32[2]{0:T(128)S(1)} %reduce_max.15, bf16[2,32000]{1,0:T(2,128)(2,1)} %param.8), kind=kLoop, calls=%fused_computation.71 | loop fusion | flops 256000 | bytes 512016 | tf_op jit(solution)/shard_map/convert_element_type | solution.py:43
  5.5 0.8 copy.38
  6.3 7.4 %all-to-all-start = ((bf16[16,2,2000]{2,1,0:T(2,128)(2,1)}), bf16[16,2,2000]{2,1,0:T(2,128)(2,1)S(1)}, u32[]{:S(2)}, u32[]{:S(2)}) async-start(bf16[16,2,2000]{2,1,0:T(2,128)(2,1)} %bitcast.40), calls=%async_computation | async-start | bytes 262144 | tf_op jit(solution)/shard_map/all_to_all | solution.py:12
  13.7 0.7 convert_element_type.114
  14.4 7.2 %all-to-all-done = bf16[16,2,2000]{2,1,0:T(2,128)(2,1)S(1)} async-done(((bf16[16,2,2000]{2,1,0:T(2,128)(2,1)}), bf16[16,2,2000]{2,1,0:T(2,128)(2,1)S(1)}, u32[]{:S(2)}, u32[]{:S(2)}) %all-to-all-start) | async-done | bytes 128032 | tf_op jit(solution)/shard_map/all_to_all | solution.py:12
  21.7 8.7 %multiply_reduce_fusion.1 = (f32[32]{0:T(128)S(1)}, bf16[32,4096]{1,0:T(8,128)(2,1)S(1)}) fusion(f32[4096]{0:T(1024)S(1)} %convert_element_type.114, bf16[32,2000]{1,0:T(8,128)(2,1)S(1)} %reshape.126, bf16[2000,4096]{1,0:T(8,128)(2,1)} %param.9), kind=kOutput, calls=%fused_computation.11 | convolution fusion | flops 524681184 | bytes 16790656 | tf_op jit(solution)/shard_map/dot_general | solution.py:50
  30.4 0.7 copy.37
  31.1 3.5 %all-to-all-start.1 = ((bf16[16,32,256]{2,1,0:T(8,128)(2,1)}), bf16[16,32,256]{2,1,0:T(8,128)(2,1)S(1)}, u32[]{:S(2)}, u32[]{:S(2)}) async-start(bf16[16,32,256]{2,1,0:T(8,128)(2,1)} %bitcast.39), calls=%async_computation.1 | async-start | bytes 524288 | tf_op jit(solution)/shard_map/all_to_all | solution.py:12
  34.8 9.9 %all-to-all-done.1 = bf16[16,32,256]{2,1,0:T(8,128)(2,1)S(1)} async-done(((bf16[16,32,256]{2,1,0:T(8,128)(2,1)}), bf16[16,32,256]{2,1,0:T(8,128)(2,1)S(1)}, u32[]{:S(2)}, u32[]{:S(2)}) %all-to-all-start.1) | async-done | bytes 262176 | tf_op jit(solution)/shard_map/all_to_all | solution.py:12
  44.7 0.7 broadcast_in_dim.26
  45.4 3.5 %all-to-all-start.2 = ((bf16[16,32,256]{2,1,0:T(8,128)(2,1)}), bf16[16,32,256]{2,1,0:T(8,128)(2,1)S(1)}, u32[]{:S(2)}, u32[]{:S(2)}) async-start(bf16[16,32,256]{2,1,0:T(8,128)(2,1)} %broadcast_in_dim.26), calls=%async_computation.2 | async-start | bytes 524288 | tf_op jit(solution)/shard_map/all_to_all | solution.py:12
  49.0 4.7 %multiply_reduce_fusion = f32[896]{0:T(1024)S(1)} fusion(bf16[896,4096]{1,0:T(8,128)(2,1)} %param.13, f32[4096]{0:T(1024)S(1)} %convert_element_type.114), kind=kLoop, calls=%fused_computation | loop fusion | flops 11009152 | bytes 7360000 | tf_op jit(solution)/shard_map/reduce_sum | solution.py:45
  53.7 5.3 %all-to-all-done.2 = bf16[16,32,256]{2,1,0:T(8,128)(2,1)S(1)} async-done(((bf16[16,32,256]{2,1,0:T(8,128)(2,1)}), bf16[16,32,256]{2,1,0:T(8,128)(2,1)S(1)}, u32[]{:S(2)}, u32[]{:S(2)}) %all-to-all-start.2) | async-done | bytes 262176 | tf_op jit(solution)/shard_map/all_to_all | solution.py:12
  59.3 4.7 %fusion.30 = f32[32,896]{1,0:T(8,128)S(1)} fusion(bf16[4096,896]{1,0:T(8,128)(2,1)} %param.11, f32[32,4096]{1,0:T(8,128)S(1)} %bitcast.45, f32[4096]{0:T(1024)S(1)} %convert_element_type.118, f32[32]{0:T(128)S(1)} %add_rsqrt_fusion), kind=kOutput, calls=%fused_computation.69 | convolution fusion | flops 235274240 | bytes 7995520 | tf_op jit(solution)/shard_map/dot_general | solution.py:55
  64.1 1.5 %multiply_reduce_fusion.3 = (f32[32]{0:T(128)S(1)}, f32[32,896]{1,0:T(8,128)S(1)}) fusion(f32[896]{0:T(1024)S(1)} %multiply_reduce_fusion, f32[32,896]{1,0:T(8,128)S(1)} %fusion.30, bf16[4096,896]{1,0:T(8,128)(2,1)S(1)} %bitcast.44, f32[32,4096]{1,0:T(8,128)S(1)} %bitcast.46, f32[4096]{0:T(1024)S(1)} %convert_element_type.118, f32[32]{0:T(128)S(1)} %add_rsqrt_fusion), kind=kOutput, calls=%fused_computation.35 | convolution fusion | flops 235532256 | bytes 8113920 | tf_op jit(solution)/shard_map/dot_general | solution.py:56
  65.6 0.6 slice-done.1
  66.1 2.3 %fusion.16 = f32[32,4096]{1,0:T(8,128)S(1)} fusion(bf16[4096,896]{1,0:T(8,128)(2,1)S(1)} %bitcast.42, f32[32,896]{1,0:T(8,128)S(1)} %get-tuple-element.11, f32[32,896]{1,0:T(8,128)S(1)} %fusion.30, f32[896]{0:T(1024)S(1)} %multiply_reduce_fusion, f32[32]{0:T(128)S(1)} %fusion.29), kind=kOutput, calls=%fused_computation.39 | convolution fusion | flops 235196416 | bytes 8097408 | tf_op jit(solution)/shard_map/tf,df->td/dot_general | solution.py:65
  68.4 2.3 %fusion = bf16[32,4096]{1,0:T(8,128)(2,1)S(1)} fusion(f32[32,4096]{1,0:T(8,128)S(1)} %fusion.16, bf16[4096,896]{1,0:T(8,128)(2,1)S(1)} %bitcast.44, f32[896]{0:T(1024)S(1)} %multiply_reduce_fusion, f32[32]{0:T(128)S(1)} %fusion.29, f32[32,896]{1,0:T(8,128)S(1)} %fusion.30), kind=kOutput, calls=%fused_computation.2 | convolution fusion | flops 235343872 | bytes 8244864 | tf_op jit(solution)/shard_map/tf,df->td/dot_general | solution.py:66
  70.7 0.7 copy.36
  71.4 3.5 %all-to-all-start.3 = ((bf16[16,32,256]{2,1,0:T(8,128)(2,1)}), bf16[16,32,256]{2,1,0:T(8,128)(2,1)S(1)}, u32[]{:S(2)}, u32[]{:S(2)}) async-start(bf16[16,32,256]{2,1,0:T(8,128)(2,1)} %bitcast.37), calls=%async_computation.3 | async-start | bytes 524288 | tf_op jit(solution)/shard_map/all_to_all | solution.py:12
  75.0 10.0 %all-to-all-done.3 = bf16[16,32,256]{2,1,0:T(8,128)(2,1)S(1)} async-done(((bf16[16,32,256]{2,1,0:T(8,128)(2,1)}), bf16[16,32,256]{2,1,0:T(8,128)(2,1)S(1)}, u32[]{:S(2)}, u32[]{:S(2)}) %all-to-all-start.3) | async-done | bytes 262176 | tf_op jit(solution)/shard_map/all_to_all | solution.py:12
  85.0 0.7 broadcast_in_dim.33
  85.7 3.7 %all-to-all-start.4 = ((bf16[16,32,256]{2,1,0:T(8,128)(2,1)}), bf16[16,32,256]{2,1,0:T(8,128)(2,1)S(1)}, u32[]{:S(2)}, u32[]{:S(2)}) async-start(bf16[16,32,256]{2,1,0:T(8,128)(2,1)} %broadcast_in_dim.33), calls=%async_computation.4 | async-start | bytes 524288 | tf_op jit(solution)/shard_map/all_to_all | solution.py:12
  89.9 9.4 %all-to-all-done.4 = bf16[16,32,256]{2,1,0:T(8,128)(2,1)S(1)} async-done(((bf16[16,32,256]{2,1,0:T(8,128)(2,1)}), bf16[16,32,256]{2,1,0:T(8,128)(2,1)S(1)}, u32[]{:S(2)}, u32[]{:S(2)}) %all-to-all-start.4) | async-done | bytes 262176 | tf_op jit(solution)/shard_map/all_to_all | solution.py:12
  99.6 10.7 %convolution_convert_fusion = bf16[32,2000]{1,0:T(8,128)(2,1)S(1)} fusion(bf16[2000,4096]{1,0:T(8,128)(2,1)} %param.9, f32[32,4096]{1,0:T(8,128)S(1)} %bitcast.48, f32[32,4096]{1,0:T(8,128)} %bitcast.47, f32[4096]{0:T(1024)S(1)} %convert_element_type.114, f32[32]{0:T(128)S(1)} %fusion.29, f32[32]{0:T(128)S(1)} %broadcast_multiply_fusion, ...), kind=kOutput, calls=%fused_computation.3 | convolution fusion | flops 525662720 | bytes 17593728 | tf_op jit(solution)/shard_map/td,vd->tv/dot_general | solution.py:71
  110.6 10.7 %all_to_all.30 = bf16[16,2,2012]{2,1,0:T(2,128)(2,1)S(1)} all-to-all(bf16[16,2,2012]{2,1,0:T(2,128)(2,1)S(1)} %pad_maximum_fusion), channel_id=1, replica_groups=mesh['groups'=2,'dp'=16] {'dp'}, dimensions={0} | all-to-all | bytes 257536 | tf_op jit(solution)/shard_map/all_to_all | solution.py:12
  121.6 0.4 reshape.132
  122.0 0.4 multiply_reduce_fusion.2
  122.3 0.9 multiply_convert_fusion.1
  123.5 0.5 convert_divide_fusion
  (49 shorter events, 2.5 us)
Async XLA Ops:
  6.3 15.3 %all-to-all-start = ((bf16[16,2,2000]{2,1,0:T(2,128)(2,1)}), bf16[16,2,2000]{2,1,0:T(2,128)(2,1)S(1)}, u32[]{:S(2)}, u32[]{:S(2)}) async-start(bf16[16,2,2000]{2,1,0:T(2,128)(2,1)} %bitcast.40), calls=%async_computation | async-start | bytes 262144 | tf_op jit(solution)/shard_map/all_to_all | solution.py:12
  21.7 13.0 %copy-start.2 = (bf16[4096]{0:T(1024)(128)(2,1)S(1)}, bf16[4096]{0:T(1024)(128)(2,1)}, u32[]{:S(2)}) copy-start(bf16[4096]{0:T(1024)(128)(2,1)} %param.10) | copy-start | bytes 24580
  21.7 13.0 %copy-start.3 = (s32[4]{0:T(128)S(1)}, s32[4]{0:T(128)}, u32[]{:S(2)}) copy-start(s32[4]{0:T(128)} %param.15) | copy-start | bytes 52
  31.1 13.5 %all-to-all-start.1 = ((bf16[16,32,256]{2,1,0:T(8,128)(2,1)}), bf16[16,32,256]{2,1,0:T(8,128)(2,1)S(1)}, u32[]{:S(2)}, u32[]{:S(2)}) async-start(bf16[16,32,256]{2,1,0:T(8,128)(2,1)} %bitcast.39), calls=%async_computation.1 | async-start | bytes 524288 | tf_op jit(solution)/shard_map/all_to_all | solution.py:12
  45.4 13.5 %all-to-all-start.2 = ((bf16[16,32,256]{2,1,0:T(8,128)(2,1)}), bf16[16,32,256]{2,1,0:T(8,128)(2,1)S(1)}, u32[]{:S(2)}, u32[]{:S(2)}) async-start(bf16[16,32,256]{2,1,0:T(8,128)(2,1)} %broadcast_in_dim.26), calls=%async_computation.2 | async-start | bytes 524288 | tf_op jit(solution)/shard_map/all_to_all | solution.py:12
  49.0 15.1 %slice-start.2 = ((s8[7340032]{0:T(1024)(128)(4,1)}), s8[3145728]{0:T(1024)(128)(4,1)S(1)}, s32[]{:S(2)}) async-start(s8[7340032]{0:T(1024)(128)(4,1)} %bitcast.43), calls=%async_computation.8 | async-start | bytes 6291456
  59.0 5.0 %slice-start.3 = ((s8[7340032]{0:T(1024)(128)(4,1)}), s8[4194304]{0:T(1024)(128)(4,1)S(1)}, s32[]{:S(2)}) async-start(s8[7340032]{0:T(1024)(128)(4,1)} %bitcast.43), calls=%async_computation.9 | async-start | bytes 8388608
  59.1 6.5 %copy-start = (f32[16,4,8,256]{3,2,0,1:T(8,128)}, f32[16,4,8,256]{3,2,0,1:T(8,128)S(1)}, u32[]{:S(2)}) copy-start(f32[16,4,8,256]{3,2,0,1:T(8,128)S(1)} %copy.31) | copy-start | bytes 1572868
  59.3 6.3 %slice-start = ((s8[7340032]{0:T(1024)(128)(4,1)}), s8[4194304]{0:T(1024)(128)(4,1)S(1)}, s32[]{:S(2)}) async-start(s8[7340032]{0:T(1024)(128)(4,1)} %bitcast.41), calls=%async_computation.6 | async-start | bytes 8388608
  64.1 2.1 %slice-start.1 = ((s8[7340032]{0:T(1024)(128)(4,1)}), s8[3145728]{0:T(1024)(128)(4,1)S(1)}, s32[]{:S(2)}) async-start(s8[7340032]{0:T(1024)(128)(4,1)} %bitcast.41), calls=%async_computation.7 | async-start | bytes 6291456
  71.4 13.5 %all-to-all-start.3 = ((bf16[16,32,256]{2,1,0:T(8,128)(2,1)}), bf16[16,32,256]{2,1,0:T(8,128)(2,1)S(1)}, u32[]{:S(2)}, u32[]{:S(2)}) async-start(bf16[16,32,256]{2,1,0:T(8,128)(2,1)} %bitcast.37), calls=%async_computation.3 | async-start | bytes 524288 | tf_op jit(solution)/shard_map/all_to_all | solution.py:12
  85.7 13.5 %all-to-all-start.4 = ((bf16[16,32,256]{2,1,0:T(8,128)(2,1)}), bf16[16,32,256]{2,1,0:T(8,128)(2,1)S(1)}, u32[]{:S(2)}, u32[]{:S(2)}) async-start(bf16[16,32,256]{2,1,0:T(8,128)(2,1)} %broadcast_in_dim.33), calls=%async_computation.4 | async-start | bytes 524288 | tf_op jit(solution)/shard_map/all_to_all | solution.py:12
  99.6 22.3 %copy-start.1 = (f32[2,32000]{1,0:T(2,128)S(1)}, f32[2,32000]{1,0:T(2,128)}, u32[]{:S(2)}) copy-start(f32[2,32000]{1,0:T(2,128)} %get-tuple-element.3) | copy-start | bytes 768004

commit v2 on v1

--- a/solution.py
+++ b/solution.py
@@ -20,13 +20,60 @@
     return jnp.stack([hi, mid, low], axis=-1).astype(jnp.bfloat16)
 
 
+def swap(value, mask, devices):
+    return lax.ppermute(value, "dp", [(i, i ^ mask) for i in range(devices)])
+
+
+def pick(blocks, index):
+    return lax.dynamic_index_in_dim(blocks, index, 0, keepdims=False)
+
+
+def gather_doubling(mine, devices):
+    rank = lax.axis_index("dp")
+    held = mine[None]
+    mask = devices // 2
+    while mask:
+        got = swap(held, mask, devices)
+        upper = (rank & mask) != 0
+        held = jnp.where(upper, jnp.concatenate([got, held]), jnp.concatenate([held, got]))
+        mask //= 2
+    return held
+
+
+def reverse_bits(value, devices):
+    bits = devices.bit_length() - 1
+    return sum(((value >> i) & 1) << (bits - 1 - i) for i in range(bits))
+
+
 def all_sum(part, devices):
     tokens, width = part.shape
     own = width // devices
     blocks = part.reshape(tokens, devices, own).transpose(1, 0, 2)
+    blocks = jnp.stack([blocks[reverse_bits(r, devices)] for r in range(devices)])
     mine = jnp.sum(exchange(blocks).astype(jnp.float32), axis=0).astype(jnp.bfloat16)
-    whole = exchange(jnp.broadcast_to(mine[None], (devices, tokens, own)))
+    whole = gather_doubling(mine, devices)
     return whole.transpose(1, 0, 2).reshape(tokens, width).astype(jnp.float32)
+
+
+def all_sum_chips(part, devices):
+    tokens, width = part.shape
+    own = width // devices
+    chips = devices // 2
+    rank = lax.axis_index("dp")
+    core, chip = rank % 2, rank // 2
+    blocks = part.reshape(tokens, 2, chips, own).transpose(1, 2, 0, 3)
+    got = swap(pick(blocks, 1 - core), 1, devices)
+    half = (pick(blocks, core).astype(jnp.float32) + got.astype(jnp.float32)).astype(jnp.bfloat16)
+    total = pick(half, chip).astype(jnp.float32)
+    arrived = [swap(pick(half, chip ^ s), 2 * s, devices) for s in range(1, chips)]
+    for block in arrived:
+        total = total + block.astype(jnp.float32)
+    mine = total.astype(jnp.bfloat16)
+    held = jnp.stack([mine] + [swap(mine, 2 * s, devices) for s in range(1, chips)])
+    held = jnp.stack([pick(held, chip ^ s) for s in range(chips)])
+    got = swap(held, 1, devices)
+    whole = jnp.where(core == 1, jnp.stack([got, held]), jnp.stack([held, got]))
+    return whole.reshape(devices, tokens, own).transpose(1, 0, 2).reshape(tokens, width).astype(jnp.float32)
 
 
 def body(logits, embed, norm_gain, w_gate, w_up, w_down, head, counts):
@@ -64,7 +111,7 @@
     own_rewards = jnp.sum(jnp.where(member, (valid * score)[:, None], 0.0), axis=0)
     d_part = jnp.einsum("tf,df->td", d_gate, w_gate, preferred_element_type=f32)
     d_part = d_part + jnp.einsum("tf,df->td", d_up, w_up, preferred_element_type=f32)
-    d_normed = all_sum(d_part.astype(bf16), devices)
+    d_normed = all_sum_chips(d_part.astype(bf16), devices)
     scaled = d_normed * gain32
     d_input = inv * scaled - x0 * inv * inv * inv * jnp.mean(scaled * x0, axis=-1, keepdims=True)
     d_input = (d_input + valid[:, None] * head32[None, :]).astype(bf16)

time: 125 us -> 131 us (1.048)
  waiting for transfers between devices: 41.8 us -> 23.7 us
  blocking collectives: 10.7 us -> 23.7 us
  starting transfers between devices: 21.7 us -> 32 us
  other arithmetic: 13.1 us -> 15.3 us
  local copies, waits for them, and re-layouts: 5.82 us -> 3.69 us
    all_to_all x5 -> x1, waiting for transfers between devices: 41.8 us -> 7.23 us  [exchange(): return lax.all_to_all(blocks, 'dp', split_axis=0, concat_axis=0, tiled=True)]
    ppermute x0 -> x20, starting transfers between devices: none -> 24.6 us  [swap(): return lax.ppermute(value, 'dp', [(i, i ^ mask) for i in range(devices)])]
    ppermute x0 -> x20, waiting for transfers between devices: none -> 16.4 us  [swap(): return lax.ppermute(value, 'dp', [(i, i ^ mask) for i in range(devices)])]
    all_to_all x5 -> x1, starting transfers between devices: 21.7 us -> 7.39 us  [exchange(): return lax.all_to_all(blocks, 'dp', split_axis=0, concat_axis=0, tiled=True)]
    all_to_all x1 -> x2, blocking collectives: 10.7 us -> 23.7 us  [exchange(): return lax.all_to_all(blocks, 'dp', split_axis=0, concat_axis=0, tiled=True)]
    reshape x2 -> x1, local copies, waits for them, and re-layouts: 1.48 us -> 0.02 us  [all_sum(): blocks = part.reshape(tokens, devices, own).transpose(1, 0, 2)]
    broadcast_in_dim x2 -> x0, local copies, waits for them, and re-layouts: 1.45 us -> none  [all_sum(): whole = exchange(jnp.broadcast_to(mine[None], (devices, tokens, own)))]
  transfers between devices with their start and end apart: 5 -> 21, of which waited for: 5 -> 9; matrix products, arithmetic and copies ran while one was open for 5% -> 6% of each run, Pallas kernels for 0% -> 0%
where the time goes in v2:
time: 131 us
  starting transfers between devices  32 us (24%)
  matrix products  31.3 us (24%)
  waiting for transfers between devices  23.7 us (18%)
  blocking collectives  23.7 us (18%)
  other arithmetic  15.3 us (12%)
  local copies, waits for them, and re-layouts  3.69 us (3%)
    ppermute x20, starting transfers between devices, swap(): return lax.ppermute(value, 'dp', [(i, i ^ mask) for i in range(devices)])  24.6 us
    all_to_all x2, blocking collectives, exchange(): return lax.all_to_all(blocks, 'dp', split_axis=0, concat_axis=0, tiled=True)  23.7 us
    ppermute x20, waiting for transfers between devices, swap(): return lax.ppermute(value, 'dp', [(i, i ^ mask) for i in range(devices)])  16.4 us
    dot_general x1, matrix products, body(): jnp.einsum('td,vd->tv', d_input, embed, preferred_element_type=f32)  10.7 us
    dot_general x1, matrix products, body(): partial_value = jnp.dot(slices, embed, preferred_element_type=f32)  9.22 us
    all_to_all x1, starting transfers between devices, exchange(): return lax.all_to_all(blocks, 'dp', split_axis=0, concat_axis=0, tiled=True)  7.39 us
    all_to_all x1, waiting for transfers between devices, exchange(): return lax.all_to_all(blocks, 'dp', split_axis=0, concat_axis=0, tiled=True)  7.23 us
    dot_general x1, matrix products, body(): a_gate = jnp.dot(normed, w_gate, preferred_element_type=f32)  4.82 us
  transfers between devices with their start and end apart: 21, of which 9 were waited for; matrix products, arithmetic and copies ran while one was open for 6% of the time, Pallas kernels for 0%

profile of v2, /device:TPU:0, one launch (start us, length us, event | category | flops | bytes accessed | tf_op | source)
XLA Modules:
  0.0 130.8 jit_solution(5253786479136121733)
XLA Ops:
  0.6 1.3 reduce_max.14
  1.9 1.4 %fusion.10 = f32[2]{0:T(128)S(1)} fusion(bf16[2,32000]{1,0:T(2,128)(2,1)} %param.8, f32[2]{0:T(128)S(1)} %reduce_max.15), kind=kLoop, calls=%fused_computation.29 | loop fusion | flops 191998 | bytes 128016 | tf_op jit(solution)/shard_map/reduce_sum | solution.py:89
  5.6 7.4 %all-to-all-start = ((bf16[16,2,2000]{2,1,0:T(2,128)(2,1)}), bf16[16,2,2000]{2,1,0:T(2,128)(2,1)S(1)}, u32[]{:S(2)}, u32[]{:S(2)}) async-start(bf16[16,2,2000]{2,1,0:T(2,128)(2,1)} %bitcast.88), calls=%async_computation | async-start | bytes 262144 | tf_op jit(solution)/shard_map/all_to_all | solution.py:12
  13.7 7.2 %all-to-all-done = bf16[16,2,2000]{2,1,0:T(2,128)(2,1)S(1)} async-done(((bf16[16,2,2000]{2,1,0:T(2,128)(2,1)}), bf16[16,2,2000]{2,1,0:T(2,128)(2,1)S(1)}, u32[]{:S(2)}, u32[]{:S(2)}) %all-to-all-start) | async-done | bytes 128032 | tf_op jit(solution)/shard_map/all_to_all | solution.py:12
  21.0 9.2 %multiply_reduce_fusion.1 = (f32[32]{0:T(128)}, bf16[32,4096]{1,0:T(8,128)(2,1)S(1)}) fusion(f32[4096]{0:T(1024)S(1)} %convert_element_type.161, bf16[32,2000]{1,0:T(8,128)(2,1)S(1)} %reshape.137, bf16[2000,4096]{1,0:T(8,128)(2,1)} %param.9), kind=kOutput, calls=%fused_computation.11 | convolution fusion | flops 524681184 | bytes 16790656 | tf_op jit(solution)/shard_map/dot_general | solution.py:97
  30.4 12.6 %all_to_all.15 = bf16[16,32,256]{2,1,0:T(8,128)(2,1)S(1)} all-to-all(bf16[16,32,256]{2,1,0:T(8,128)(2,1)S(1)} %constant_dynamic-update-slice_fusion), channel_id=1, replica_groups=mesh['groups'=2,'dp'=16] {'dp'}, dimensions={0} | all-to-all | bytes 524288 | tf_op jit(solution)/shard_map/all_to_all | solution.py:12
  44.2 4.6 %multiply_reduce_fusion = f32[896]{0:T(1024)S(1)} fusion(bf16[896,4096]{1,0:T(8,128)(2,1)} %param.13, f32[4096]{0:T(1024)S(1)} %convert_element_type.161), kind=kLoop, calls=%fused_computation | loop fusion | flops 11009152 | bytes 7360000 | tf_op jit(solution)/shard_map/reduce_sum | solution.py:92
  50.0 2.8 %collective-permute-done.1 = bf16[2,32,256]{2,1,0:T(8,128)(2,1)S(1)} collective-permute-done((bf16[2,32,256]{2,1,0:T(8,128)(2,1)S(1)}, bf16[2,32,256]{2,1,0:T(8,128)(2,1)S(1)}, u32[]{:S(2)}, u32[]{:S(2)}) %collective-permute-start.1) | collective-permute-done | bytes 32800 | tf_op jit(solution)/shard_map/ppermute | solution.py:24
  53.0 4.1 %collective-permute-done.2 = bf16[4,32,256]{2,1,0:T(8,128)(2,1)S(1)} collective-permute-done((bf16[4,32,256]{2,1,0:T(8,128)(2,1)S(1)}, bf16[4,32,256]{2,1,0:T(8,128)(2,1)S(1)}, u32[]{:S(2)}, u32[]{:S(2)}) %collective-permute-start.2) | collective-permute-done | bytes 65568 | tf_op jit(solution)/shard_map/ppermute | solution.py:24
  57.3 1.3 %collective-permute-done.3 = bf16[8,32,256]{2,1,0:T(8,128)(2,1)S(1)} collective-permute-done((bf16[8,32,256]{2,1,0:T(8,128)(2,1)S(1)}, bf16[8,32,256]{2,1,0:T(8,128)(2,1)S(1)}, u32[]{:S(2)}, u32[]{:S(2)}) %collective-permute-start.3) | collective-permute-done | bytes 131104 | tf_op jit(solution)/shard_map/ppermute | solution.py:24
  59.3 4.8 %fusion.38 = f32[32,896]{1,0:T(8,128)S(1)} fusion(bf16[4096,896]{1,0:T(8,128)(2,1)} %param.11, f32[32,4096]{1,0:T(8,128)S(1)} %bitcast.93, f32[4096]{0:T(1024)} %convert_element_type.165, f32[32]{0:T(128)S(1)} %add_rsqrt_fusion), kind=kOutput, calls=%fused_computation.125 | convolution fusion | flops 235274240 | bytes 7995520 | tf_op jit(solution)/shard_map/dot_general | solution.py:102
  64.1 2.0 %multiply_reduce_fusion.3 = (f32[32]{0:T(128)}, f32[32,896]{1,0:T(8,128)S(1)}) fusion(f32[896]{0:T(1024)S(1)} %multiply_reduce_fusion, f32[32,896]{1,0:T(8,128)S(1)} %fusion.38, bf16[4096,896]{1,0:T(8,128)(2,1)S(1)} %bitcast.92, f32[32,4096]{1,0:T(8,128)S(1)} %bitcast.94, f32[4096]{0:T(1024)S(1)} %copy-done.2, f32[32]{0:T(128)S(1)} %add_rsqrt_fusion), kind=kOutput, calls=%fused_computation.40 | convolution fusion | flops 235532256 | bytes 8113920 | tf_op jit(solution)/shard_map/dot_general | solution.py:103
  66.2 2.3 %fusion.17 = f32[32,4096]{1,0:T(8,128)S(1)} fusion(bf16[4096,896]{1,0:T(8,128)(2,1)S(1)} %bitcast.90, f32[32,896]{1,0:T(8,128)S(1)} %get-tuple-element.22, f32[32,896]{1,0:T(8,128)S(1)} %fusion.38, f32[896]{0:T(1024)S(1)} %multiply_reduce_fusion, f32[32]{0:T(128)S(1)} %fusion.37), kind=kOutput, calls=%fused_computation.77 | convolution fusion | flops 235196416 | bytes 8097408 | tf_op jit(solution)/shard_map/tf,df->td/dot_general | solution.py:112
  68.5 2.3 %fusion = bf16[32,4096]{1,0:T(8,128)(2,1)S(1)} fusion(f32[32,4096]{1,0:T(8,128)S(1)} %fusion.17, bf16[4096,896]{1,0:T(8,128)(2,1)S(1)} %bitcast.92, f32[896]{0:T(1024)S(1)} %multiply_reduce_fusion, f32[32]{0:T(128)S(1)} %fusion.37, f32[32,896]{1,0:T(8,128)S(1)} %fusion.38), kind=kOutput, calls=%fused_computation.2 | convolution fusion | flops 235343872 | bytes 8244864 | tf_op jit(solution)/shard_map/tf,df->td/dot_general | solution.py:113
  71.1 1.2 collective-permute-done.4
  72.4 1.4 %collective-permute-start.10 = (bf16[32,256]{1,0:T(8,128)(2,1)S(1)}, bf16[32,256]{1,0:T(8,128)(2,1)S(1)}, u32[]{:S(2)}, u32[]{:S(2)}) collective-permute-start(bf16[32,256]{1,0:T(8,128)(2,1)S(1)} %get-tuple-element.12), channel_id=1, source_target_pairs={{0,12},{1,13},{2,14},{3,15},{4,8},{5,9},{6,10},{7,11},{8,4},{9,5},... | collective-permute-start | bytes 49160 | tf_op jit(solution)/shard_map/ppermute | solution.py:24
  73.8 1.9 %collective-permute-start.11 = (bf16[32,256]{1,0:T(8,128)(2,1)S(1)}, bf16[32,256]{1,0:T(8,128)(2,1)S(1)}, u32[]{:S(2)}, u32[]{:S(2)}) collective-permute-start(bf16[32,256]{1,0:T(8,128)(2,1)S(1)} %get-tuple-element.11), channel_id=1, source_target_pairs={{0,14},{1,15},{2,12},{3,13},{4,10},{5,11},{6,8},{7,9},{8,6},{9,7},... | collective-permute-start | bytes 49160 | tf_op jit(solution)/shard_map/ppermute | solution.py:24
  76.4 2.0 %collective-permute-start.5 = (bf16[32,256]{1,0:T(8,128)(2,1)S(1)}, bf16[32,256]{1,0:T(8,128)(2,1)S(1)}, u32[]{:S(2)}, u32[]{:S(2)}) collective-permute-start(bf16[32,256]{1,0:T(8,128)(2,1)S(1)} %get-tuple-element.10), channel_id=1, source_target_pairs={{0,2},{1,3},{2,0},{3,1},{4,6},{5,7},{6,4},{7,5},{8,10},{9,11},{10,... | collective-permute-start | bytes 49160 | tf_op jit(solution)/shard_map/ppermute | solution.py:24
  78.5 1.5 %collective-permute-start.7 = (bf16[32,256]{1,0:T(8,128)(2,1)S(1)}, bf16[32,256]{1,0:T(8,128)(2,1)S(1)}, u32[]{:S(2)}, u32[]{:S(2)}) collective-permute-start(bf16[32,256]{1,0:T(8,128)(2,1)S(1)} %get-tuple-element.15), channel_id=1, source_target_pairs={{0,6},{1,7},{2,4},{3,5},{4,2},{5,3},{6,0},{7,1},{8,14},{9,15},{10,... | collective-permute-start | bytes 49160 | tf_op jit(solution)/shard_map/ppermute | solution.py:24
  80.9 3.4 %collective-permute-start.9 = (bf16[32,256]{1,0:T(8,128)(2,1)S(1)}, bf16[32,256]{1,0:T(8,128)(2,1)S(1)}, u32[]{:S(2)}, u32[]{:S(2)}) collective-permute-start(bf16[32,256]{1,0:T(8,128)(2,1)S(1)} %get-tuple-element.13), channel_id=1, source_target_pairs={{0,10},{1,11},{2,8},{3,9},{4,14},{5,15},{6,12},{7,13},{8,2},{9,3},... | collective-permute-start | bytes 49160 | tf_op jit(solution)/shard_map/ppermute | solution.py:24
  85.0 1.5 %collective-permute-done.9 = bf16[32,256]{1,0:T(8,128)(2,1)S(1)} collective-permute-done((bf16[32,256]{1,0:T(8,128)(2,1)S(1)}, bf16[32,256]{1,0:T(8,128)(2,1)S(1)}, u32[]{:S(2)}, u32[]{:S(2)}) %collective-permute-start.9) | collective-permute-done | bytes 16416 | tf_op jit(solution)/shard_map/ppermute | solution.py:24
  86.5 1.2 collective-permute-start.12
  88.4 1.9 %collective-permute-start.13 = (bf16[32,256]{1,0:T(8,128)(2,1)S(1)}, bf16[32,256]{1,0:T(8,128)(2,1)S(1)}, u32[]{:S(2)}, u32[]{:S(2)}) collective-permute-start(bf16[32,256]{1,0:T(8,128)(2,1)S(1)} %get-tuple-element.3), channel_id=1, source_target_pairs={{0,4},{1,5},{2,6},{3,7},{4,0},{5,1},{6,2},{7,3},{8,12},{9,13},{10,... | collective-permute-start | bytes 49160 | tf_op jit(solution)/shard_map/ppermute | solution.py:24
  90.9 1.9 %collective-permute-start.15 = (bf16[32,256]{1,0:T(8,128)(2,1)S(1)}, bf16[32,256]{1,0:T(8,128)(2,1)S(1)}, u32[]{:S(2)}, u32[]{:S(2)}) collective-permute-start(bf16[32,256]{1,0:T(8,128)(2,1)S(1)} %get-tuple-element.3), channel_id=1, source_target_pairs={{0,8},{1,9},{2,10},{3,11},{4,12},{5,13},{6,14},{7,15},{8,0},{9,1},... | collective-permute-start | bytes 49160 | tf_op jit(solution)/shard_map/ppermute | solution.py:24
  92.8 1.5 %collective-permute-start.16 = (bf16[32,256]{1,0:T(8,128)(2,1)S(1)}, bf16[32,256]{1,0:T(8,128)(2,1)S(1)}, u32[]{:S(2)}, u32[]{:S(2)}) collective-permute-start(bf16[32,256]{1,0:T(8,128)(2,1)S(1)} %get-tuple-element.3), channel_id=1, source_target_pairs={{0,10},{1,11},{2,8},{3,9},{4,14},{5,15},{6,12},{7,13},{8,2},{9,3},... | collective-permute-start | bytes 49160 | tf_op jit(solution)/shard_map/ppermute | solution.py:24
  94.3 2.3 %collective-permute-start.17 = (bf16[32,256]{1,0:T(8,128)(2,1)S(1)}, bf16[32,256]{1,0:T(8,128)(2,1)S(1)}, u32[]{:S(2)}, u32[]{:S(2)}) collective-permute-start(bf16[32,256]{1,0:T(8,128)(2,1)S(1)} %get-tuple-element.3), channel_id=1, source_target_pairs={{0,12},{1,13},{2,14},{3,15},{4,8},{5,9},{6,10},{7,11},{8,4},{9,5},... | collective-permute-start | bytes 49160 | tf_op jit(solution)/shard_map/ppermute | solution.py:24
  96.7 1.9 %collective-permute-start.18 = (bf16[32,256]{1,0:T(8,128)(2,1)S(1)}, bf16[32,256]{1,0:T(8,128)(2,1)S(1)}, u32[]{:S(2)}, u32[]{:S(2)}) collective-permute-start(bf16[32,256]{1,0:T(8,128)(2,1)S(1)} %get-tuple-element.3), channel_id=1, source_target_pairs={{0,14},{1,15},{2,12},{3,13},{4,10},{5,11},{6,8},{7,9},{8,6},{9,7},... | collective-permute-start | bytes 49160 | tf_op jit(solution)/shard_map/ppermute | solution.py:24
  98.6 1.2 collective-permute-done.17
  99.9 3.2 %collective-permute-done.18 = bf16[32,256]{1,0:T(8,128)(2,1)S(1)} collective-permute-done((bf16[32,256]{1,0:T(8,128)(2,1)S(1)}, bf16[32,256]{1,0:T(8,128)(2,1)S(1)}, u32[]{:S(2)}, u32[]{:S(2)}) %collective-permute-start.18) | collective-permute-done | bytes 16416 | tf_op jit(solution)/shard_map/ppermute | solution.py:24
  104.7 1.2 fusion.2
  106.0 10.7 %convolution_convert_fusion = bf16[32,2000]{1,0:T(8,128)(2,1)S(1)} fusion(bf16[2000,4096]{1,0:T(8,128)(2,1)} %param.9, f32[32,4096]{1,0:T(8,128)S(1)} %bitcast.96, f32[32,4096]{1,0:T(8,128)} %bitcast.95, f32[4096]{0:T(1024)S(1)} %convert_element_type.161, f32[32]{0:T(128)} %copy-done.5, f32[32]{0:T(128)S(1)} %broadcast_multiply_fusion, ...), kind=kOutput, calls=%fused_computation.3 | convolution fusion | flops 525662720 | bytes 17593728 | tf_op jit(solution)/shard_map/td,vd->tv/dot_general | solution.py:118
  117.0 11.0 %all_to_all.16 = bf16[16,2,2012]{2,1,0:T(2,128)(2,1)S(1)} all-to-all(bf16[16,2,2012]{2,1,0:T(2,128)(2,1)S(1)} %pad_maximum_fusion), channel_id=1, replica_groups=mesh['groups'=2,'dp'=16] {'dp'}, dimensions={0} | all-to-all | bytes 257536 | tf_op jit(solution)/shard_map/all_to_all | solution.py:12
  (131 shorter events, 15.1 us)
Async XLA Ops:
  5.6 15.3 %all-to-all-start = ((bf16[16,2,2000]{2,1,0:T(2,128)(2,1)}), bf16[16,2,2000]{2,1,0:T(2,128)(2,1)S(1)}, u32[]{:S(2)}, u32[]{:S(2)}) async-start(bf16[16,2,2000]{2,1,0:T(2,128)(2,1)} %bitcast.88), calls=%async_computation | async-start | bytes 262144 | tf_op jit(solution)/shard_map/all_to_all | solution.py:12
  30.2 19.2 %copy-start.3 = (bf16[4096]{0:T(1024)(128)(2,1)S(1)}, bf16[4096]{0:T(1024)(128)(2,1)}, u32[]{:S(2)}) copy-start(bf16[4096]{0:T(1024)(128)(2,1)} %param.10) | copy-start | bytes 24580
  30.2 22.7 %copy-start.7 = (s32[4]{0:T(128)S(1)}, s32[4]{0:T(128)}, u32[]{:S(2)}) copy-start(s32[4]{0:T(128)} %param.15) | copy-start | bytes 52
  43.1 21.0 %slice-start.2 = ((s8[7340032]{0:T(1024)(128)(4,1)}), s8[3145728]{0:T(1024)(128)(4,1)S(1)}, s32[]{:S(2)}) async-start(s8[7340032]{0:T(1024)(128)(4,1)} %bitcast.91), calls=%async_computation.5 | async-start | bytes 6291456
  43.1 5.7 %collective-permute-start = (bf16[1,32,256]{2,1,0:T(8,128)(2,1)S(1)}, bf16[1,32,256]{2,1,0:T(8,128)(2,1)S(1)}, u32[]{:S(2)}, u32[]{:S(2)}) collective-permute-start(bf16[1,32,256]{2,1,0:T(8,128)(2,1)S(1)} %bitcast.119), channel_id=1, source_target_pairs={{0,8},{1,9},{2,10},{3,11},{4,12},{5,13},{6,14},{7,15},{8,0},{9,1},... | collective-permute-start | bytes 49160 | tf_op jit(solution)/shard_map/ppermute | solution.py:24
  48.8 4.0 %collective-permute-start.1 = (bf16[2,32,256]{2,1,0:T(8,128)(2,1)S(1)}, bf16[2,32,256]{2,1,0:T(8,128)(2,1)S(1)}, u32[]{:S(2)}, u32[]{:S(2)}) collective-permute-start(bf16[2,32,256]{2,1,0:T(8,128)(2,1)S(1)} %maximum_select_fusion.4), channel_id=1, source_target_pairs={{0,4},{1,5},{2,6},{3,7},{4,0},{5,1},{6,2},{7,3},{8,12},{9,13},{10,... | collective-permute-start | bytes 98312 | tf_op jit(solution)/shard_map/ppermute | solution.py:24
  50.0 14.1 %copy-start.2 = (f32[4096]{0:T(1024)S(1)}, f32[4096]{0:T(1024)}, u32[]{:S(2)}) copy-start(f32[4096]{0:T(1024)} %convert_element_type.165) | copy-start | bytes 49156
  52.8 4.3 %collective-permute-start.2 = (bf16[4,32,256]{2,1,0:T(8,128)(2,1)S(1)}, bf16[4,32,256]{2,1,0:T(8,128)(2,1)S(1)}, u32[]{:S(2)}, u32[]{:S(2)}) collective-permute-start(bf16[4,32,256]{2,1,0:T(8,128)(2,1)S(1)} %maximum_select_fusion.3), channel_id=1, source_target_pairs={{0,2},{1,3},{2,0},{3,1},{4,6},{5,7},{6,4},{7,5},{8,10},{9,11},{10,... | collective-permute-start | bytes 196616 | tf_op jit(solution)/shard_map/ppermute | solution.py:24
  53.0 13.2 %copy-start.6 = (s32[32]{0:T(128)}, s32[32]{0:T(128)S(1)}, u32[]{:S(2)}) copy-start(s32[32]{0:T(128)S(1)} %select_reduce_fusion.1) | copy-start | bytes 388
  57.2 1.4 %collective-permute-start.3 = (bf16[8,32,256]{2,1,0:T(8,128)(2,1)S(1)}, bf16[8,32,256]{2,1,0:T(8,128)(2,1)S(1)}, u32[]{:S(2)}, u32[]{:S(2)}) collective-permute-start(bf16[8,32,256]{2,1,0:T(8,128)(2,1)S(1)} %maximum_select_fusion.2), channel_id=1, source_target_pairs={{0,1},{1,0},{2,3},{3,2},{4,5},{5,4},{6,7},{7,6},{8,9},{9,8},{10,11... | collective-permute-start | bytes 393224 | tf_op jit(solution)/shard_map/ppermute | solution.py:24
  57.3 11.2 %copy-start.5 = (f32[32]{0:T(128)}, f32[32]{0:T(128)S(1)}, u32[]{:S(2)}) copy-start(f32[32]{0:T(128)S(1)} %fusion.37) | copy-start | bytes 388
  58.8 7.4 %copy-start.4 = (f32[32]{0:T(128)}, f32[32]{0:T(128)S(1)}, u32[]{:S(2)}) copy-start(f32[32]{0:T(128)S(1)} %add_rsqrt_fusion) | copy-start | bytes 388
  58.9 5.3 %slice-start.3 = ((s8[7340032]{0:T(1024)(128)(4,1)}), s8[4194304]{0:T(1024)(128)(4,1)S(1)}, s32[]{:S(2)}) async-start(s8[7340032]{0:T(1024)(128)(4,1)} %bitcast.91), calls=%async_computation.6 | async-start | bytes 8388608
  59.3 6.9 %copy-start = (f32[16,4,8,256]{3,2,0,1:T(8,128)}, f32[16,4,8,256]{3,2,0,1:T(8,128)S(1)}, u32[]{:S(2)}) copy-start(f32[16,4,8,256]{3,2,0,1:T(8,128)S(1)} %copy.40) | copy-start | bytes 1572868
  59.3 6.9 %slice-start = ((s8[7340032]{0:T(1024)(128)(4,1)}), s8[4194304]{0:T(1024)(128)(4,1)S(1)}, s32[]{:S(2)}) async-start(s8[7340032]{0:T(1024)(128)(4,1)} %bitcast.89), calls=%async_computation.3 | async-start | bytes 8388608
  70.9 1.4 %collective-permute-start.4 = (bf16[8,32,256]{2,1,0:T(8,128)(2,1)S(1)}, bf16[8,32,256]{2,1,0:T(8,128)(2,1)S(1)}, u32[]{:S(2)}, u32[]{:S(2)}) collective-permute-start(bf16[8,32,256]{2,1,0:T(8,128)(2,1)S(1)} %bitcast.118), channel_id=1, source_target_pairs={{0,1},{1,0},{2,3},{3,2},{4,5},{5,4},{6,7},{7,6},{8,9},{9,8},{10,11... | collective-permute-start | bytes 393224 | tf_op jit(solution)/shard_map/ppermute | solution.py:24
  72.4 7.6 %collective-permute-start.10 = (bf16[32,256]{1,0:T(8,128)(2,1)S(1)}, bf16[32,256]{1,0:T(8,128)(2,1)S(1)}, u32[]{:S(2)}, u32[]{:S(2)}) collective-permute-start(bf16[32,256]{1,0:T(8,128)(2,1)S(1)} %get-tuple-element.12), channel_id=1, source_target_pairs={{0,12},{1,13},{2,14},{3,15},{4,8},{5,9},{6,10},{7,11},{8,4},{9,5},... | collective-permute-start | bytes 49160 | tf_op jit(solution)/shard_map/ppermute | solution.py:24
  73.8 7.1 %collective-permute-start.11 = (bf16[32,256]{1,0:T(8,128)(2,1)S(1)}, bf16[32,256]{1,0:T(8,128)(2,1)S(1)}, u32[]{:S(2)}, u32[]{:S(2)}) collective-permute-start(bf16[32,256]{1,0:T(8,128)(2,1)S(1)} %get-tuple-element.11), channel_id=1, source_target_pairs={{0,14},{1,15},{2,12},{3,13},{4,10},{5,11},{6,8},{7,9},{8,6},{9,7},... | collective-permute-start | bytes 49160 | tf_op jit(solution)/shard_map/ppermute | solution.py:24
  76.4 8.6 %collective-permute-start.5 = (bf16[32,256]{1,0:T(8,128)(2,1)S(1)}, bf16[32,256]{1,0:T(8,128)(2,1)S(1)}, u32[]{:S(2)}, u32[]{:S(2)}) collective-permute-start(bf16[32,256]{1,0:T(8,128)(2,1)S(1)} %get-tuple-element.10), channel_id=1, source_target_pairs={{0,2},{1,3},{2,0},{3,1},{4,6},{5,7},{6,4},{7,5},{8,10},{9,11},{10,... | collective-permute-start | bytes 49160 | tf_op jit(solution)/shard_map/ppermute | solution.py:24
  78.4 6.5 %collective-permute-start.6 = (bf16[32,256]{1,0:T(8,128)(2,1)S(1)}, bf16[32,256]{1,0:T(8,128)(2,1)S(1)}, u32[]{:S(2)}, u32[]{:S(2)}) collective-permute-start(bf16[32,256]{1,0:T(8,128)(2,1)S(1)} %get-tuple-element.16), channel_id=1, source_target_pairs={{0,4},{1,5},{2,6},{3,7},{4,0},{5,1},{6,2},{7,3},{8,12},{9,13},{10,... | collective-permute-start | bytes 49160 | tf_op jit(solution)/shard_map/ppermute | solution.py:24
  78.5 6.5 %collective-permute-start.7 = (bf16[32,256]{1,0:T(8,128)(2,1)S(1)}, bf16[32,256]{1,0:T(8,128)(2,1)S(1)}, u32[]{:S(2)}, u32[]{:S(2)}) collective-permute-start(bf16[32,256]{1,0:T(8,128)(2,1)S(1)} %get-tuple-element.15), channel_id=1, source_target_pairs={{0,6},{1,7},{2,4},{3,5},{4,2},{5,3},{6,0},{7,1},{8,14},{9,15},{10,... | collective-permute-start | bytes 49160 | tf_op jit(solution)/shard_map/ppermute | solution.py:24
  80.0 5.0 %collective-permute-start.8 = (bf16[32,256]{1,0:T(8,128)(2,1)S(1)}, bf16[32,256]{1,0:T(8,128)(2,1)S(1)}, u32[]{:S(2)}, u32[]{:S(2)}) collective-permute-start(bf16[32,256]{1,0:T(8,128)(2,1)S(1)} %get-tuple-element.14), channel_id=1, source_target_pairs={{0,8},{1,9},{2,10},{3,11},{4,12},{5,13},{6,14},{7,15},{8,0},{9,1},... | collective-permute-start | bytes 49160 | tf_op jit(solution)/shard_map/ppermute | solution.py:24
  80.9 5.5 %collective-permute-start.9 = (bf16[32,256]{1,0:T(8,128)(2,1)S(1)}, bf16[32,256]{1,0:T(8,128)(2,1)S(1)}, u32[]{:S(2)}, u32[]{:S(2)}) collective-permute-start(bf16[32,256]{1,0:T(8,128)(2,1)S(1)} %get-tuple-element.13), channel_id=1, source_target_pairs={{0,10},{1,11},{2,8},{3,9},{4,14},{5,15},{6,12},{7,13},{8,2},{9,3},... | collective-permute-start | bytes 49160 | tf_op jit(solution)/shard_map/ppermute | solution.py:24
  86.5 7.8 %collective-permute-start.12 = (bf16[32,256]{1,0:T(8,128)(2,1)S(1)}, bf16[32,256]{1,0:T(8,128)(2,1)S(1)}, u32[]{:S(2)}, u32[]{:S(2)}) collective-permute-start(bf16[32,256]{1,0:T(8,128)(2,1)S(1)} %get-tuple-element.3), channel_id=1, source_target_pairs={{0,2},{1,3},{2,0},{3,1},{4,6},{5,7},{6,4},{7,5},{8,10},{9,11},{10,... | collective-permute-start | bytes 49160 | tf_op jit(solution)/shard_map/ppermute | solution.py:24
  88.4 8.2 %collective-permute-start.13 = (bf16[32,256]{1,0:T(8,128)(2,1)S(1)}, bf16[32,256]{1,0:T(8,128)(2,1)S(1)}, u32[]{:S(2)}, u32[]{:S(2)}) collective-permute-start(bf16[32,256]{1,0:T(8,128)(2,1)S(1)} %get-tuple-element.3), channel_id=1, source_target_pairs={{0,4},{1,5},{2,6},{3,7},{4,0},{5,1},{6,2},{7,3},{8,12},{9,13},{10,... | collective-permute-start | bytes 49160 | tf_op jit(solution)/shard_map/ppermute | solution.py:24
  90.3 8.3 %collective-permute-start.14 = (bf16[32,256]{1,0:T(8,128)(2,1)S(1)}, bf16[32,256]{1,0:T(8,128)(2,1)S(1)}, u32[]{:S(2)}, u32[]{:S(2)}) collective-permute-start(bf16[32,256]{1,0:T(8,128)(2,1)S(1)} %get-tuple-element.3), channel_id=1, source_target_pairs={{0,6},{1,7},{2,4},{3,5},{4,2},{5,3},{6,0},{7,1},{8,14},{9,15},{10,... | collective-permute-start | bytes 49160 | tf_op jit(solution)/shard_map/ppermute | solution.py:24
  90.9 7.7 %collective-permute-start.15 = (bf16[32,256]{1,0:T(8,128)(2,1)S(1)}, bf16[32,256]{1,0:T(8,128)(2,1)S(1)}, u32[]{:S(2)}, u32[]{:S(2)}) collective-permute-start(bf16[32,256]{1,0:T(8,128)(2,1)S(1)} %get-tuple-element.3), channel_id=1, source_target_pairs={{0,8},{1,9},{2,10},{3,11},{4,12},{5,13},{6,14},{7,15},{8,0},{9,1},... | collective-permute-start | bytes 49160 | tf_op jit(solution)/shard_map/ppermute | solution.py:24
  92.8 5.8 %collective-permute-start.16 = (bf16[32,256]{1,0:T(8,128)(2,1)S(1)}, bf16[32,256]{1,0:T(8,128)(2,1)S(1)}, u32[]{:S(2)}, u32[]{:S(2)}) collective-permute-start(bf16[32,256]{1,0:T(8,128)(2,1)S(1)} %get-tuple-element.3), channel_id=1, source_target_pairs={{0,10},{1,11},{2,8},{3,9},{4,14},{5,15},{6,12},{7,13},{8,2},{9,3},... | collective-permute-start | bytes 49160 | tf_op jit(solution)/shard_map/ppermute | solution.py:24
  94.3 5.5 %collective-permute-start.17 = (bf16[32,256]{1,0:T(8,128)(2,1)S(1)}, bf16[32,256]{1,0:T(8,128)(2,1)S(1)}, u32[]{:S(2)}, u32[]{:S(2)}) collective-permute-start(bf16[32,256]{1,0:T(8,128)(2,1)S(1)} %get-tuple-element.3), channel_id=1, source_target_pairs={{0,12},{1,13},{2,14},{3,15},{4,8},{5,9},{6,10},{7,11},{8,4},{9,5},... | collective-permute-start | bytes 49160 | tf_op jit(solution)/shard_map/ppermute | solution.py:24
  96.7 6.4 %collective-permute-start.18 = (bf16[32,256]{1,0:T(8,128)(2,1)S(1)}, bf16[32,256]{1,0:T(8,128)(2,1)S(1)}, u32[]{:S(2)}, u32[]{:S(2)}) collective-permute-start(bf16[32,256]{1,0:T(8,128)(2,1)S(1)} %get-tuple-element.3), channel_id=1, source_target_pairs={{0,14},{1,15},{2,12},{3,13},{4,10},{5,11},{6,8},{7,9},{8,6},{9,7},... | collective-permute-start | bytes 49160 | tf_op jit(solution)/shard_map/ppermute | solution.py:24
  103.2 1.4 %collective-permute-start.19 = (bf16[8,32,256]{2,1,0:T(8,128)(2,1)S(1)}, bf16[8,32,256]{2,1,0:T(8,128)(2,1)S(1)}, u32[]{:S(2)}, u32[]{:S(2)}) collective-permute-start(bf16[8,32,256]{2,1,0:T(8,128)(2,1)S(1)} %constant_dynamic-update-slice_fusion.24), channel_id=1, source_target_pairs={{0,1},{1,0},{2,3},{3,2},{4,5},{5,4},{6,7},{7,6},{8,9},{9,8},{10,11... | collective-permute-start | bytes 393224 | tf_op jit(solution)/shard_map/ppermute | solution.py:24
  106.0 24.2 %copy-start.8 = (s32[4]{0:T(128)S(1)}, s32[4]{0:T(128)}, u32[]{:S(2)}) copy-start(s32[4]{0:T(128)} %param.15) | copy-start | bytes 52
  (3 other events, 6.3 us)

commit v3 on v1

--- a/solution.py
+++ b/solution.py
@@ -20,13 +20,35 @@
     return jnp.stack([hi, mid, low], axis=-1).astype(jnp.bfloat16)
 
 
+def swap_cores(value, devices):
+    return lax.ppermute(value, "dp", [(i, i ^ 1) for i in range(devices)])
+
+
+def exchange_chips(blocks, devices):
+    groups = [list(range(core, devices, 2)) for core in range(2)]
+    return lax.all_to_all(
+        blocks, "dp", split_axis=0, concat_axis=0, axis_index_groups=groups, tiled=True
+    )
+
+
+def pick(blocks, index):
+    return lax.dynamic_index_in_dim(blocks, index, 0, keepdims=False)
+
+
 def all_sum(part, devices):
     tokens, width = part.shape
     own = width // devices
-    blocks = part.reshape(tokens, devices, own).transpose(1, 0, 2)
-    mine = jnp.sum(exchange(blocks).astype(jnp.float32), axis=0).astype(jnp.bfloat16)
-    whole = exchange(jnp.broadcast_to(mine[None], (devices, tokens, own)))
-    return whole.transpose(1, 0, 2).reshape(tokens, width).astype(jnp.float32)
+    chips = devices // 2
+    core = lax.axis_index("dp") % 2
+    blocks = part.reshape(tokens, 2, chips, own).transpose(1, 2, 0, 3)
+    got = swap_cores(pick(blocks, 1 - core), devices)
+    half = (pick(blocks, core).astype(jnp.float32) + got.astype(jnp.float32)).astype(jnp.bfloat16)
+    arrived = exchange_chips(half, devices)
+    mine = jnp.sum(arrived.astype(jnp.float32), axis=0).astype(jnp.bfloat16)
+    held = exchange_chips(jnp.broadcast_to(mine[None], (chips, tokens, own)), devices)
+    got = swap_cores(held, devices)
+    whole = jnp.where(core == 1, jnp.stack([got, held]), jnp.stack([held, got]))
+    return whole.reshape(devices, tokens, own).transpose(1, 0, 2).reshape(tokens, width).astype(jnp.float32)
 
 
 def body(logits, embed, norm_gain, w_gate, w_up, w_down, head, counts):

time: 125 us -> 119 us (0.952)
  waiting for transfers between devices: 41.8 us -> 27.6 us
  blocking collectives: 10.7 us -> 20.5 us
  starting transfers between devices: 21.7 us -> 19.4 us
  other arithmetic: 13.1 us -> 15 us
  local copies, waits for them, and re-layouts: 5.82 us -> 4.52 us
    all_to_all x5 -> x1, waiting for transfers between devices: 41.8 us -> 7.22 us  [exchange(): return lax.all_to_all(blocks, 'dp', split_axis=0, concat_axis=0, tiled=True)]
    all_to_all x0 -> x3, waiting for transfers between devices: none -> 15.5 us  [exchange_chips(): lax.all_to_all(blocks, 'dp', split_axis=0, concat_axis=0, axis_index_grou...]
    all_to_all x5 -> x1, starting transfers between devices: 21.7 us -> 7.39 us  [exchange(): return lax.all_to_all(blocks, 'dp', split_axis=0, concat_axis=0, tiled=True)]
    all_to_all x0 -> x3, starting transfers between devices: none -> 11.7 us  [exchange_chips(): lax.all_to_all(blocks, 'dp', split_axis=0, concat_axis=0, axis_index_grou...]
    all_to_all x0 -> x1, blocking collectives: none -> 9.97 us  [exchange_chips(): lax.all_to_all(blocks, 'dp', split_axis=0, concat_axis=0, axis_index_grou...]
    ppermute x0 -> x4, waiting for transfers between devices: none -> 4.91 us  [swap_cores(): return lax.ppermute(value, 'dp', [(i, i ^ 1) for i in range(devices)])]
    reshape x2 -> x0, local copies, waits for them, and re-layouts: 1.48 us -> none  [all_sum(): blocks = part.reshape(tokens, devices, own).transpose(1, 0, 2)]
  transfers between devices with their start and end apart: 5 -> 8, of which waited for: 5 -> 8; matrix products, arithmetic and copies ran while one was open for 5% -> 6% of each run, Pallas kernels for 0% -> 0%
where the time goes in v3:
time: 119 us
  matrix products  30.6 us (26%)
  waiting for transfers between devices  27.6 us (23%)
  blocking collectives  20.5 us (17%)
  starting transfers between devices  19.4 us (16%)
  other arithmetic  15 us (13%)
  local copies, waits for them, and re-layouts  4.52 us (4%)
    all_to_all x3, waiting for transfers between devices, exchange_chips(): lax.all_to_all(blocks, 'dp', split_axis=0, concat_axis=0, axis_index_grou...  15.5 us
    all_to_all x3, starting transfers between devices, exchange_chips(): lax.all_to_all(blocks, 'dp', split_axis=0, concat_axis=0, axis_index_grou...  11.7 us
    dot_general x1, matrix products, body(): jnp.einsum('td,vd->tv', d_input, embed, preferred_element_type=f32)  10.7 us
    all_to_all x1, blocking collectives, exchange(): return lax.all_to_all(blocks, 'dp', split_axis=0, concat_axis=0, tiled=True)  10.5 us
    all_to_all x1, blocking collectives, exchange_chips(): lax.all_to_all(blocks, 'dp', split_axis=0, concat_axis=0, axis_index_grou...  9.97 us
    dot_general x1, matrix products, body(): partial_value = jnp.dot(slices, embed, preferred_element_type=f32)  9.22 us
    all_to_all x1, starting transfers between devices, exchange(): return lax.all_to_all(blocks, 'dp', split_axis=0, concat_axis=0, tiled=True)  7.39 us
    all_to_all x1, waiting for transfers between devices, exchange(): return lax.all_to_all(blocks, 'dp', split_axis=0, concat_axis=0, tiled=True)  7.22 us
  transfers between devices with their start and end apart: 8, of which 8 were waited for; matrix products, arithmetic and copies ran while one was open for 6% of the time, Pallas kernels for 0%

profile of v3, /device:TPU:0, one launch (start us, length us, event | category | flops | bytes accessed | tf_op | source)
XLA Modules:
  0.0 118.7 jit_solution(11577339122098422038)
XLA Ops:
  0.6 1.3 %reduce_max.14 = bf16[2]{0:T(256)(128)(2,1)S(1)} reduce(bf16[2,32000]{1,0:T(2,128)(2,1)} %param.8, bf16[]{:T(256)} %constant.66.clone.1), dimensions={1}, to_apply=%region_0.0 | reduce | flops 63998 | bytes 128006 | tf_op jit(solution)/shard_map/reduce_max | solution.py:64
  1.9 1.4 %fusion.9 = f32[2]{0:T(128)S(1)} fusion(bf16[2,32000]{1,0:T(2,128)(2,1)} %param.8, f32[2]{0:T(128)S(1)} %reduce_max.15), kind=kLoop, calls=%fused_computation.27 | loop fusion | flops 191998 | bytes 128016 | tf_op jit(solution)/shard_map/reduce_sum | solution.py:64
  3.3 1.9 %fusion.32 = (bf16[2,32000]{1,0:T(2,128)(2,1)S(1)}, f32[2,32000]{1,0:T(2,128)}) fusion(f32[2]{0:T(128)S(1)} %fusion.9, f32[2]{0:T(128)S(1)} %reduce_max.15, bf16[2,32000]{1,0:T(2,128)(2,1)} %param.8), kind=kLoop, calls=%fused_computation.78 | loop fusion | flops 256000 | bytes 512016 | tf_op jit(solution)/shard_map/convert_element_type | solution.py:65
  5.5 0.8 copy.54
  6.3 7.4 %all-to-all-start = ((bf16[16,2,2000]{2,1,0:T(2,128)(2,1)}), bf16[16,2,2000]{2,1,0:T(2,128)(2,1)S(1)}, u32[]{:S(2)}, u32[]{:S(2)}) async-start(bf16[16,2,2000]{2,1,0:T(2,128)(2,1)} %bitcast.68), calls=%async_computation | async-start | bytes 262144 | tf_op jit(solution)/shard_map/all_to_all | solution.py:12
  13.7 0.7 convert_element_type.158
  14.4 7.2 %all-to-all-done = bf16[16,2,2000]{2,1,0:T(2,128)(2,1)S(1)} async-done(((bf16[16,2,2000]{2,1,0:T(2,128)(2,1)}), bf16[16,2,2000]{2,1,0:T(2,128)(2,1)S(1)}, u32[]{:S(2)}, u32[]{:S(2)}) %all-to-all-start) | async-done | bytes 128032 | tf_op jit(solution)/shard_map/all_to_all | solution.py:12
  21.6 9.2 %multiply_reduce_fusion.1 = (f32[32]{0:T(128)}, bf16[32,4096]{1,0:T(8,128)(2,1)S(1)}) fusion(f32[4096]{0:T(1024)S(1)} %convert_element_type.158, bf16[32,2000]{1,0:T(8,128)(2,1)S(1)} %reshape.148, bf16[2000,4096]{1,0:T(8,128)(2,1)} %param.9), kind=kOutput, calls=%fused_computation.4 | convolution fusion | flops 524681184 | bytes 16790656 | tf_op jit(solution)/shard_map/dot_general | solution.py:72
  31.1 1.3 %collective-permute-done = bf16[8,32,256]{2,1,0:T(8,128)(2,1)S(1)} collective-permute-done((bf16[8,32,256]{2,1,0:T(8,128)(2,1)S(1)}, bf16[8,32,256]{2,1,0:T(8,128)(2,1)S(1)}, u32[]{:S(2)}, u32[]{:S(2)}) %collective-permute-start) | collective-permute-done | bytes 131104 | tf_op jit(solution)/shard_map/ppermute | solution.py:24
  32.5 10.0 %all_to_all.30 = bf16[8,32,256]{2,1,0:T(8,128)(2,1)S(1)} all-to-all(bf16[8,32,256]{2,1,0:T(8,128)(2,1)S(1)} %fusion.2), channel_id=1, replica_groups={{0,2,4,6,8,10,12,14},{1,3,5,7,9,11,13,15},{16,18,20,22,24,26,28,30},{17..., dimensions={0} | all-to-all | bytes 262144 | tf_op jit(solution)/shard_map/all_to_all | solution.py:29
  42.4 0.6 broadcast_in_dim.26
  43.1 3.4 %all-to-all-start.2 = ((bf16[8,32,256]{2,1,0:T(8,128)(2,1)}), bf16[8,32,256]{2,1,0:T(8,128)(2,1)S(1)}, u32[]{:S(2)}, u32[]{:S(2)}) async-start(bf16[8,32,256]{2,1,0:T(8,128)(2,1)} %broadcast_in_dim.26), calls=%async_computation.2 | async-start | bytes 262144 | tf_op jit(solution)/shard_map/all_to_all | solution.py:29
  46.5 5.3 %multiply_reduce_fusion = f32[896]{0:T(1024)} fusion(bf16[896,4096]{1,0:T(8,128)(2,1)} %param.13, f32[4096]{0:T(1024)S(1)} %convert_element_type.158), kind=kLoop, calls=%fused_computation | loop fusion | flops 11009152 | bytes 7360000 | tf_op jit(solution)/shard_map/reduce_sum | solution.py:67
  51.8 0.6 convert_element_type.162
  52.5 1.2 %all-to-all-done.2 = bf16[8,32,256]{2,1,0:T(8,128)(2,1)S(1)} async-done(((bf16[8,32,256]{2,1,0:T(8,128)(2,1)}), bf16[8,32,256]{2,1,0:T(8,128)(2,1)S(1)}, u32[]{:S(2)}, u32[]{:S(2)}) %all-to-all-start.2) | async-done | bytes 131104 | tf_op jit(solution)/shard_map/all_to_all | solution.py:29
  53.8 1.3 %collective-permute-done.1 = bf16[8,32,256]{2,1,0:T(8,128)(2,1)S(1)} collective-permute-done((bf16[8,32,256]{2,1,0:T(8,128)(2,1)S(1)}, bf16[8,32,256]{2,1,0:T(8,128)(2,1)S(1)}, u32[]{:S(2)}, u32[]{:S(2)}) %collective-permute-start.1) | collective-permute-done | bytes 131104 | tf_op jit(solution)/shard_map/ppermute | solution.py:24
  55.5 4.7 %fusion.30 = f32[32,896]{1,0:T(8,128)S(1)} fusion(bf16[4096,896]{1,0:T(8,128)(2,1)} %param.11, f32[32,4096]{1,0:T(8,128)S(1)} %bitcast.73, f32[4096]{0:T(1024)} %convert_element_type.162, f32[32]{0:T(128)S(1)} %add_rsqrt_fusion), kind=kOutput, calls=%fused_computation.76 | convolution fusion | flops 235274240 | bytes 7995520 | tf_op jit(solution)/shard_map/dot_general | solution.py:77
  60.2 1.5 %multiply_reduce_fusion.5 = (f32[32]{0:T(128)S(1)}, f32[32,896]{1,0:T(8,128)S(1)}) fusion(f32[896]{0:T(1024)S(1)} %copy-done.4, f32[32,896]{1,0:T(8,128)S(1)} %fusion.30, bf16[4096,896]{1,0:T(8,128)(2,1)S(1)} %bitcast.72, f32[32,4096]{1,0:T(8,128)S(1)} %bitcast.74, f32[4096]{0:T(1024)S(1)} %copy-done.2, f32[32]{0:T(128)S(1)} %add_rsqrt_fusion), kind=kOutput, calls=%fused_computation.38 | convolution fusion | flops 235532256 | bytes 8113920 | tf_op jit(solution)/shard_map/dot_general | solution.py:78
  61.7 0.6 slice-done.1
  62.3 2.3 %fusion.16 = f32[32,4096]{1,0:T(8,128)S(1)} fusion(bf16[4096,896]{1,0:T(8,128)(2,1)S(1)} %bitcast.70, f32[32,896]{1,0:T(8,128)S(1)} %get-tuple-element.15, f32[32,896]{1,0:T(8,128)S(1)} %fusion.30, f32[896]{0:T(1024)S(1)} %copy-done.4, f32[32]{0:T(128)S(1)} %fusion.29), kind=kOutput, calls=%fused_computation.42 | convolution fusion | flops 235196416 | bytes 8097408 | tf_op jit(solution)/shard_map/tf,df->td/dot_general | solution.py:87
  64.7 2.3 %fusion = bf16[32,4096]{1,0:T(8,128)(2,1)S(1)} fusion(f32[32,4096]{1,0:T(8,128)S(1)} %fusion.16, bf16[4096,896]{1,0:T(8,128)(2,1)S(1)} %bitcast.72, f32[896]{0:T(1024)S(1)} %copy-done.4, f32[32]{0:T(128)S(1)} %fusion.29, f32[32,896]{1,0:T(8,128)S(1)} %fusion.30), kind=kOutput, calls=%fused_computation.2 | convolution fusion | flops 235343872 | bytes 8244864 | tf_op jit(solution)/shard_map/tf,df->td/dot_general | solution.py:88
  67.3 1.2 %collective-permute-done.2 = bf16[8,32,256]{2,1,0:T(8,128)(2,1)S(1)} collective-permute-done((bf16[8,32,256]{2,1,0:T(8,128)(2,1)S(1)}, bf16[8,32,256]{2,1,0:T(8,128)(2,1)S(1)}, u32[]{:S(2)}, u32[]{:S(2)}) %collective-permute-start.2) | collective-permute-done | bytes 131104 | tf_op jit(solution)/shard_map/ppermute | solution.py:24
  68.5 0.7 fusion.1
  69.2 4.8 %all-to-all-start.3 = ((bf16[8,32,256]{2,1,0:T(8,128)(2,1)}), bf16[8,32,256]{2,1,0:T(8,128)(2,1)S(1)}, u32[]{:S(2)}, u32[]{:S(2)}) async-start(bf16[8,32,256]{2,1,0:T(8,128)(2,1)} %fusion.1), calls=%async_computation.3 | async-start | bytes 262144 | tf_op jit(solution)/shard_map/all_to_all | solution.py:29
  73.9 7.3 %all-to-all-done.3 = bf16[8,32,256]{2,1,0:T(8,128)(2,1)S(1)} async-done(((bf16[8,32,256]{2,1,0:T(8,128)(2,1)}), bf16[8,32,256]{2,1,0:T(8,128)(2,1)S(1)}, u32[]{:S(2)}, u32[]{:S(2)}) %all-to-all-start.3) | async-done | bytes 131104 | tf_op jit(solution)/shard_map/all_to_all | solution.py:29
  81.3 0.7 broadcast_in_dim.33
  82.0 3.5 %all-to-all-start.4 = ((bf16[8,32,256]{2,1,0:T(8,128)(2,1)}), bf16[8,32,256]{2,1,0:T(8,128)(2,1)S(1)}, u32[]{:S(2)}, u32[]{:S(2)}) async-start(bf16[8,32,256]{2,1,0:T(8,128)(2,1)} %broadcast_in_dim.33), calls=%async_computation.4 | async-start | bytes 262144 | tf_op jit(solution)/shard_map/all_to_all | solution.py:29
  85.7 6.9 %all-to-all-done.4 = bf16[8,32,256]{2,1,0:T(8,128)(2,1)S(1)} async-done(((bf16[8,32,256]{2,1,0:T(8,128)(2,1)}), bf16[8,32,256]{2,1,0:T(8,128)(2,1)S(1)}, u32[]{:S(2)}, u32[]{:S(2)}) %all-to-all-start.4) | async-done | bytes 131104 | tf_op jit(solution)/shard_map/all_to_all | solution.py:29
  92.9 1.0 collective-permute-done.3
  94.4 10.7 %convolution_convert_fusion = bf16[32,2000]{1,0:T(8,128)(2,1)S(1)} fusion(bf16[2000,4096]{1,0:T(8,128)(2,1)} %param.9, f32[32,4096]{1,0:T(8,128)S(1)} %bitcast.78, f32[32,4096]{1,0:T(8,128)} %bitcast.75, f32[4096]{0:T(1024)S(1)} %convert_element_type.158, f32[32]{0:T(128)} %copy-done.7, f32[32]{0:T(128)S(1)} %broadcast_multiply_fusion, ...), kind=kOutput, calls=%fused_computation.3 | convolution fusion | flops 525662720 | bytes 17593728 | tf_op jit(solution)/shard_map/td,vd->tv/dot_general | solution.py:93
  105.3 10.5 %all_to_all.31 = bf16[16,2,2012]{2,1,0:T(2,128)(2,1)S(1)} all-to-all(bf16[16,2,2012]{2,1,0:T(2,128)(2,1)S(1)} %pad_maximum_fusion), channel_id=1, replica_groups=mesh['groups'=2,'dp'=16] {'dp'}, dimensions={0} | all-to-all | bytes 257536 | tf_op jit(solution)/shard_map/all_to_all | solution.py:12
  116.9 0.9 multiply_convert_fusion.1
  (86 shorter events, 4.4 us)
Async XLA Ops:
  6.3 15.3 %all-to-all-start = ((bf16[16,2,2000]{2,1,0:T(2,128)(2,1)}), bf16[16,2,2000]{2,1,0:T(2,128)(2,1)S(1)}, u32[]{:S(2)}, u32[]{:S(2)}) async-start(bf16[16,2,2000]{2,1,0:T(2,128)(2,1)} %bitcast.68), calls=%async_computation | async-start | bytes 262144 | tf_op jit(solution)/shard_map/all_to_all | solution.py:12
  30.9 20.9 %copy-start.5 = (bf16[4096]{0:T(1024)(128)(2,1)S(1)}, bf16[4096]{0:T(1024)(128)(2,1)}, u32[]{:S(2)}) copy-start(bf16[4096]{0:T(1024)(128)(2,1)} %param.10) | copy-start | bytes 24580
  30.9 21.5 %copy-start.11 = (s32[4]{0:T(128)S(1)}, s32[4]{0:T(128)}, u32[]{:S(2)}) copy-start(s32[4]{0:T(128)} %param.15) | copy-start | bytes 52
  31.0 1.4 %collective-permute-start = (bf16[8,32,256]{2,1,0:T(8,128)(2,1)S(1)}, bf16[8,32,256]{2,1,0:T(8,128)(2,1)S(1)}, u32[]{:S(2)}, u32[]{:S(2)}) collective-permute-start(bf16[8,32,256]{2,1,0:T(8,128)(2,1)S(1)} %bitcast.87), channel_id=1, source_target_pairs={{0,1},{1,0},{2,3},{3,2},{4,5},{5,4},{6,7},{7,6},{8,9},{9,8},{10,11... | collective-permute-start | bytes 393224 | tf_op jit(solution)/shard_map/ppermute | solution.py:24
  43.1 10.7 %all-to-all-start.2 = ((bf16[8,32,256]{2,1,0:T(8,128)(2,1)}), bf16[8,32,256]{2,1,0:T(8,128)(2,1)S(1)}, u32[]{:S(2)}, u32[]{:S(2)}) async-start(bf16[8,32,256]{2,1,0:T(8,128)(2,1)} %broadcast_in_dim.26), calls=%async_computation.2 | async-start | bytes 262144 | tf_op jit(solution)/shard_map/all_to_all | solution.py:29
  46.5 13.7 %slice-start.2 = ((s8[7340032]{0:T(1024)(128)(4,1)}), s8[3145728]{0:T(1024)(128)(4,1)S(1)}, s32[]{:S(2)}) async-start(s8[7340032]{0:T(1024)(128)(4,1)} %bitcast.71), calls=%async_computation.8 | async-start | bytes 6291456
  52.4 2.7 %copy-start.13 = (s32[32]{0:T(128)}, s32[32]{0:T(128)S(1)}, u32[]{:S(2)}) copy-start(s32[32]{0:T(128)S(1)} %and_select_fusion) | copy-start | bytes 388
  52.5 2.6 %copy-start.9 = (s32[32]{0:T(128)}, s32[32]{0:T(128)S(1)}, u32[]{:S(2)}) copy-start(s32[32]{0:T(128)S(1)} %select_reduce_fusion.1) | copy-start | bytes 388
  53.8 6.4 %copy-start.2 = (f32[4096]{0:T(1024)S(1)}, f32[4096]{0:T(1024)}, u32[]{:S(2)}) copy-start(f32[4096]{0:T(1024)} %convert_element_type.162) | copy-start | bytes 49156
  53.8 6.4 %copy-start.4 = (f32[896]{0:T(1024)S(1)}, f32[896]{0:T(1024)}, u32[]{:S(2)}) copy-start(f32[896]{0:T(1024)} %multiply_reduce_fusion) | copy-start | bytes 10756
  53.8 1.3 %collective-permute-start.1 = (bf16[8,32,256]{2,1,0:T(8,128)(2,1)S(1)}, bf16[8,32,256]{2,1,0:T(8,128)(2,1)S(1)}, u32[]{:S(2)}, u32[]{:S(2)}) collective-permute-start(bf16[8,32,256]{2,1,0:T(8,128)(2,1)S(1)} %all-to-all-done.2), channel_id=1, source_target_pairs={{0,1},{1,0},{2,3},{3,2},{4,5},{5,4},{6,7},{7,6},{8,9},{9,8},{10,11... | collective-permute-start | bytes 393224 | tf_op jit(solution)/shard_map/ppermute | solution.py:24
  53.8 10.8 %copy-start.7 = (f32[32]{0:T(128)}, f32[32]{0:T(128)S(1)}, u32[]{:S(2)}) copy-start(f32[32]{0:T(128)S(1)} %fusion.29) | copy-start | bytes 388
  55.4 4.8 %slice-start.3 = ((s8[7340032]{0:T(1024)(128)(4,1)}), s8[4194304]{0:T(1024)(128)(4,1)S(1)}, s32[]{:S(2)}) async-start(s8[7340032]{0:T(1024)(128)(4,1)} %bitcast.71), calls=%async_computation.9 | async-start | bytes 8388608
  55.4 6.2 %copy-start = (f32[4,8,16,256]{3,1,2,0:T(8,128)}, f32[4,8,16,256]{3,1,2,0:T(8,128)S(1)}, u32[]{:S(2)}) copy-start(f32[4,8,16,256]{3,1,2,0:T(8,128)S(1)} %copy.42) | copy-start | bytes 1572868
  55.5 6.2 %slice-start = ((s8[7340032]{0:T(1024)(128)(4,1)}), s8[4194304]{0:T(1024)(128)(4,1)S(1)}, s32[]{:S(2)}) async-start(s8[7340032]{0:T(1024)(128)(4,1)} %bitcast.69), calls=%async_computation.6 | async-start | bytes 8388608
  60.2 2.1 %slice-start.1 = ((s8[7340032]{0:T(1024)(128)(4,1)}), s8[3145728]{0:T(1024)(128)(4,1)S(1)}, s32[]{:S(2)}) async-start(s8[7340032]{0:T(1024)(128)(4,1)} %bitcast.69), calls=%async_computation.7 | async-start | bytes 6291456
  62.3 11.6 %copy-start.6 = (bf16[4096]{0:T(1024)(128)(2,1)S(1)}, bf16[4096]{0:T(1024)(128)(2,1)}, u32[]{:S(2)}) copy-start(bf16[4096]{0:T(1024)(128)(2,1)} %param.10) | copy-start | bytes 24580
  64.6 20.9 %copy-start.8 = (f32[32]{0:T(128)S(1)}, f32[32]{0:T(128)}, u32[]{:S(2)}) copy-start(f32[32]{0:T(128)} %get-tuple-element.4) | copy-start | bytes 388
  64.6 20.9 %copy-start.10 = (s32[32]{0:T(128)S(1)}, s32[32]{0:T(128)}, u32[]{:S(2)}) copy-start(s32[32]{0:T(128)} %copy-done.9) | copy-start | bytes 388
  64.6 20.9 %copy-start.14 = (s32[32]{0:T(128)S(1)}, s32[32]{0:T(128)}, u32[]{:S(2)}) copy-start(s32[32]{0:T(128)} %copy-done.13) | copy-start | bytes 388
  64.7 29.7 %copy-start.3 = (f32[4096]{0:T(1024)S(1)}, f32[4096]{0:T(1024)}, u32[]{:S(2)}) copy-start(f32[4096]{0:T(1024)} %convert_element_type.162) | copy-start | bytes 49156
  67.1 1.4 %collective-permute-start.2 = (bf16[8,32,256]{2,1,0:T(8,128)(2,1)S(1)}, bf16[8,32,256]{2,1,0:T(8,128)(2,1)S(1)}, u32[]{:S(2)}, u32[]{:S(2)}) collective-permute-start(bf16[8,32,256]{2,1,0:T(8,128)(2,1)S(1)} %bitcast.88), channel_id=1, source_target_pairs={{0,1},{1,0},{2,3},{3,2},{4,5},{5,4},{6,7},{7,6},{8,9},{9,8},{10,11... | collective-permute-start | bytes 393224 | tf_op jit(solution)/shard_map/ppermute | solution.py:24
  69.2 12.1 %all-to-all-start.3 = ((bf16[8,32,256]{2,1,0:T(8,128)(2,1)}), bf16[8,32,256]{2,1,0:T(8,128)(2,1)S(1)}, u32[]{:S(2)}, u32[]{:S(2)}) async-start(bf16[8,32,256]{2,1,0:T(8,128)(2,1)} %fusion.1), calls=%async_computation.3 | async-start | bytes 262144 | tf_op jit(solution)/shard_map/all_to_all | solution.py:29
  82.0 10.7 %all-to-all-start.4 = ((bf16[8,32,256]{2,1,0:T(8,128)(2,1)}), bf16[8,32,256]{2,1,0:T(8,128)(2,1)S(1)}, u32[]{:S(2)}, u32[]{:S(2)}) async-start(bf16[8,32,256]{2,1,0:T(8,128)(2,1)} %broadcast_in_dim.33), calls=%async_computation.4 | async-start | bytes 262144 | tf_op jit(solution)/shard_map/all_to_all | solution.py:29
  92.6 1.3 %collective-permute-start.3 = (bf16[8,32,256]{2,1,0:T(8,128)(2,1)S(1)}, bf16[8,32,256]{2,1,0:T(8,128)(2,1)S(1)}, u32[]{:S(2)}, u32[]{:S(2)}) collective-permute-start(bf16[8,32,256]{2,1,0:T(8,128)(2,1)S(1)} %all-to-all-done.4), channel_id=1, source_target_pairs={{0,1},{1,0},{2,3},{3,2},{4,5},{5,4},{6,7},{7,6},{8,9},{9,8},{10,11... | collective-permute-start | bytes 393224 | tf_op jit(solution)/shard_map/ppermute | solution.py:24
  94.4 22.2 %copy-start.1 = (f32[2,32000]{1,0:T(2,128)S(1)}, f32[2,32000]{1,0:T(2,128)}, u32[]{:S(2)}) copy-start(f32[2,32000]{1,0:T(2,128)} %get-tuple-element.3) | copy-start | bytes 768004
  94.4 23.8 %copy-start.12 = (s32[4]{0:T(128)S(1)}, s32[4]{0:T(128)}, u32[]{:S(2)}) copy-start(s32[4]{0:T(128)} %param.15) | copy-start | bytes 52

commit v4 on v1

v4 whole, which is shorter than its diff:
```python
import functools
import math

import jax
import jax.numpy as jnp
from jax import lax
from jax.experimental import pallas as pl
from jax.experimental.pallas import tpu as pltpu
from jax.sharding import PartitionSpec as P

VOC = 32000
F32, BF16 = jnp.float32, jnp.bfloat16
VMEM_BYTES = 12 * 1024 * 1024


def swap_cores(value, devices):
    return lax.ppermute(value, "dp", [(i, i ^ 1) for i in range(devices)])


def exchange(blocks):
    return lax.all_to_all(blocks, "dp", split_axis=0, concat_axis=0, tiled=True)


def exchange_chips(blocks, devices):
    groups = [list(range(core, devices, 2)) for core in range(2)]
    return lax.all_to_all(
        blocks, "dp", split_axis=0, concat_axis=0, axis_index_groups=groups, tiled=True
    )


def split3(value):
    hi = lax.reduce_precision(value, 8, 7)
    rest = value - hi
    mid = lax.reduce_precision(rest, 8, 7)
    low = rest - mid
    return jnp.stack([hi, mid, low], axis=-1).astype(BF16)


def call(kernel, outs, *args, resident=(), flops=0, scratch=()):
    size = sum(math.prod(a.shape) * a.dtype.itemsize for a in args)
    args = [
        pltpu.with_memory_space_constraint(a, pltpu.VMEM) if i in resident else a
        for i, a in enumerate(args)
    ]
    return pl.pallas_call(
        kernel,
        out_shape=outs,
        in_specs=[pl.BlockSpec(memory_space=pltpu.VMEM)] * len(args),
        out_specs=[pl.BlockSpec(memory_space=pltpu.VMEM)] * len(outs),
        scratch_shapes=list(scratch),
        compiler_params=pltpu.CompilerParams(vmem_limit_bytes=VMEM_BYTES),
        cost_estimate=pl.CostEstimate(flops=flops, bytes_accessed=size, transcendentals=0),
    )(*args)


def resident_kernel(source_ref, after_ref, out_ref, sems):
    del after_ref
    count = sems.shape[0]
    rows = source_ref.shape[0] // count
    copies = [
        pltpu.make_async_copy(
            source_ref.at[pl.ds(i * rows, rows)], out_ref.at[pl.ds(i * rows, rows)], sems.at[i]
        )
        for i in range(count)
    ]
    for copy in copies:
        copy.start()
    for copy in copies:
        copy.wait()


def make_resident(source, after):
    count = next(c for c in (5, 1) if source.shape[0] % (16 * c) == 0 or c == 1)
    return pl.pallas_call(
        resident_kernel,
        out_shape=pltpu.VMEM(source.shape, source.dtype),
        in_specs=[pl.BlockSpec(memory_space=pltpu.HBM), pl.BlockSpec(memory_space=pl.ANY)],
        out_specs=pl.BlockSpec(memory_space=pltpu.VMEM),
        scratch_shapes=[pltpu.SemaphoreType.DMA((count,))],
        compiler_params=pltpu.CompilerParams(vmem_limit_bytes=VMEM_BYTES),
        cost_estimate=pl.CostEstimate(
            flops=0, bytes_accessed=math.prod(source.shape) * 2, transcendentals=0
        ),
    )(pltpu.with_memory_space_constraint(source, pltpu.HBM), after)


def half_kernel(other, slices_ref, embed_ref, head_ref, out_ref, score_ref):
    chips, _, own = out_ref.shape
    core = lax.axis_index("dp") % 2
    half = (1 - core) if other else core
    score_ref[...] = jnp.zeros_like(score_ref)

    def step(j, _):
        columns = pl.ds(pl.multiple_of((half * chips + j) * own, own), own)
        part = jnp.dot(slices_ref[...], embed_ref[:, columns], preferred_element_type=F32)
        score_ref[...] += jnp.sum(
            part * head_ref[:, columns].astype(F32), axis=-1, keepdims=True
        )
        out_ref[j] = part.astype(out_ref.dtype)
        return 0

    lax.fori_loop(0, chips, step, 0)


def hidden_kernel(
    mine_ref, got_ref, gain_ref, gate_ref, up_ref, down_ref, valid_ref,
    send_ref, keep_ref, score_ref, a_ref, b_ref,
):
    chips, total, own = mine_ref.shape
    width = 2 * chips * own
    core = lax.axis_index("dp") % 2

    def square(j, acc):
        x, y = mine_ref[j].astype(F32), got_ref[j].astype(F32)
        return acc + jnp.sum(x * x + y * y, axis=-1, keepdims=True)

    squares = lax.fori_loop(0, chips, square, jnp.zeros((total, 1), F32))
    inv = lax.rsqrt(squares / width + 1e-05)
    a_ref[...] = jnp.zeros_like(a_ref)
    b_ref[...] = jnp.zeros_like(b_ref)

    def forward(ref, half):
        def step(j, _):
            rows = pl.ds(pl.multiple_of((half * chips + j) * own, own), own)
            gain = gain_ref[:, rows].astype(F32)
            normed = (ref[j].astype(F32) * inv * gain).astype(BF16)
            a_ref[...] += jnp.dot(normed, gate_ref[rows, :], preferred_element_type=F32)
            b_ref[...] += jnp.dot(normed, up_ref[rows, :], preferred_element_type=F32)
            return 0

        lax.fori_loop(0, chips, step, 0)

    forward(mine_ref, core)
    forward(got_ref, 1 - core)
    a, b = a_ref[...], b_ref[...]
    sigma = jax.nn.sigmoid(a)
    active = a * sigma
    down = down_ref[...]
    hidden = (active * b).astype(BF16).astype(F32)
    score_ref[...] = jnp.sum(hidden * down, axis=-1, keepdims=True)
    d_hidden = valid_ref[...] * down
    d_gate = (d_hidden * b * sigma * (1.0 + a * (1.0 - sigma))).astype(BF16)
    d_up = (d_hidden * active).astype(BF16)
    contract = (((1,), (1,)), ((), ()))

    def backward(ref, half):
        def step(j, _):
            rows = pl.ds(pl.multiple_of((half * chips + j) * own, own), own)
            part = lax.dot_general(
                d_gate, gate_ref[rows, :], contract, preferred_element_type=F32
            ) + lax.dot_general(d_up, up_ref[rows, :], contract, preferred_element_type=F32)
            ref[j] = part.astype(ref.dtype)
            return 0

        lax.fori_loop(0, chips, step, 0)

    backward(send_ref, 1 - core)
    backward(keep_ref, core)


def input_kernel(
    mine_ref, got_ref, d_mine_ref, d_got_ref, gain_ref, head_ref, valid_ref, embed_ref,
    out_ref, dx_ref,
):
    chips, total, own = mine_ref.shape
    width = 2 * chips * own
    core = lax.axis_index("dp") % 2
    sources = ((mine_ref, d_mine_ref, core), (got_ref, d_got_ref, 1 - core))
    squares = jnp.zeros((total, 1), F32)
    dots = jnp.zeros((total, 1), F32)
    for x_ref, d_ref, half in sources:
        for j in range(chips):
            columns = pl.ds(pl.multiple_of((half * chips + j) * own, own), own)
            x = x_ref[j].astype(F32)
            g = d_ref[j].astype(F32) * gain_ref[:, columns].astype(F32)
            squares += jnp.sum(x * x, axis=-1, keepdims=True)
            dots += jnp.sum(g * x, axis=-1, keepdims=True)
    inv = lax.rsqrt(squares / width + 1e-05)
    mean = dots / width
    valid = valid_ref[...]
    for x_ref, d_ref, half in sources:
        for j in range(chips):
            columns = pl.ds(pl.multiple_of((half * chips + j) * own, own), own)
            x = x_ref[j].astype(F32)
            g = d_ref[j].astype(F32) * gain_ref[:, columns].astype(F32)
            dx = inv * g - x * inv * inv * inv * mean
            dx_ref[:, columns] = (dx + valid * head_ref[:, columns].astype(F32)).astype(BF16)
    voc = embed_ref.shape[0]
    contract = (((1,), (1,)), ((), ()))
    tile = 256

    def step(j, _):
        rows = pl.ds(pl.multiple_of(j * tile, tile), tile)
        out_ref[:, rows] = lax.dot_general(
            dx_ref[...], embed_ref[rows, :], contract, preferred_element_type=F32
        ).astype(out_ref.dtype)
        return 0

    whole = voc // tile
    if whole:
        lax.fori_loop(0, whole, step, 0)
    if voc % tile:
        out_ref[:, whole * tile :] = lax.dot_general(
            dx_ref[...], embed_ref[whole * tile :, :], contract, preferred_element_type=F32
        ).astype(out_ref.dtype)


def swap_sum(send, keep, devices):
    return (keep.astype(F32) + swap_cores(send, devices).astype(F32)).astype(BF16)


def sum_and_gather(half, devices):
    total = jnp.sum(exchange_chips(half, devices).astype(F32), axis=0).astype(BF16)
    held = exchange_chips(jnp.broadcast_to(total[None], half.shape), devices)
    return held, swap_cores(held, devices)


def pick(blocks, index):
    return lax.dynamic_index_in_dim(blocks, index, 0, keepdims=False)


def split_halves(part, devices):
    total, width = part.shape
    core = lax.axis_index("dp") % 2
    blocks = part.reshape(total, 2, devices // 2, width // devices).transpose(1, 2, 0, 3)
    return pick(blocks, 1 - core).astype(BF16), pick(blocks, core)


def join_halves(mine, got):
    core = lax.axis_index("dp") % 2
    blocks = jnp.where(core == 1, jnp.stack([got, mine]), jnp.stack([mine, got]))
    _, chips, total, own = blocks.shape
    return blocks.transpose(2, 0, 1, 3).reshape(total, 2 * chips * own).astype(F32)


def norm_scale(x0):
    return lax.rsqrt(jnp.mean(x0 * x0, axis=-1, keepdims=True) + 1e-05)


def plain_half(slices, embed, head_row, devices):
    part = jnp.dot(slices, embed, preferred_element_type=F32)
    score = jnp.sum(part * head_row.astype(F32), axis=-1, keepdims=True)
    return *split_halves(part, devices), score


def plain_hidden(mine, got, gain_row, w_gate, w_up, down, valid, devices):
    x0 = join_halves(mine, got)
    normed = (x0 * norm_scale(x0) * gain_row.astype(F32)).astype(BF16)
    a = jnp.dot(normed, w_gate, preferred_element_type=F32)
    b = jnp.dot(normed, w_up, preferred_element_type=F32)
    sigma = jax.nn.sigmoid(a)
    active = a * sigma
    hidden = (active * b).astype(BF16).astype(F32)
    d_hidden = valid * down
    d_gate = (d_hidden * b * sigma * (1.0 + a * (1.0 - sigma))).astype(BF16)
    d_up = (d_hidden * active).astype(BF16)
    part = jnp.einsum("tf,df->td", d_gate, w_gate, preferred_element_type=F32)
    part = part + jnp.einsum("tf,df->td", d_up, w_up, preferred_element_type=F32)
    return *split_halves(part, devices), jnp.sum(hidden * down, axis=-1, keepdims=True)


def plain_input(mine, got, d_mine, d_got, gain_row, head_row, valid, embed):
    x0 = join_halves(mine, got)
    inv = norm_scale(x0)
    scaled = join_halves(d_mine, d_got) * gain_row.astype(F32)
    dx = inv * scaled - x0 * inv * inv * inv * jnp.mean(scaled * x0, axis=-1, keepdims=True)
    dx = (dx + valid * head_row.astype(F32)).astype(BF16)
    return jnp.einsum("td,vd->tv", dx, embed, preferred_element_type=F32).astype(BF16)


def body(logits, embed, norm_gain, w_gate, w_up, w_down, head, counts):
    devices = lax.axis_size("dp")
    rows, voc = logits.shape
    part = voc // devices
    width = embed.shape[1]
    hidden = w_gate.shape[1]
    own, chips = width // devices, devices // 2
    requests = counts.shape[0]
    total = rows * devices
    request_len = total // requests
    head32 = head.astype(F32)
    head_row, gain_row = head.reshape(1, width), norm_gain.reshape(1, width)
    probs32 = jax.nn.softmax(logits.astype(F32), axis=-1)
    probs = probs32.astype(BF16)
    blocked = probs.reshape(rows, devices, part).transpose(1, 0, 2)
    slices = exchange(blocked).reshape(total, part)
    down_head = jnp.sum(w_down.astype(F32) * head32[None, :], axis=-1)
    position = jnp.arange(total, dtype=jnp.int32)
    member = (position // request_len)[:, None] == jnp.arange(requests, dtype=jnp.int32)[None, :]
    limit = jnp.sum(jnp.where(member, counts[None, :], 0), axis=-1)
    valid = (position % request_len < limit).astype(F32)

    def blocks(dtype):
        return jax.ShapeDtypeStruct((chips, total, own), dtype)

    column = jax.ShapeDtypeStruct((total, 1), F32)
    flops = total * part * width
    down_row, valid_column = down_head.reshape(1, hidden), valid[:, None]
    tiled = own % 128 == 0 and hidden % 128 == 0 and total % 16 == 0
    if tiled:
        table = make_resident(embed, blocked)
        send, score_a = call(
            functools.partial(half_kernel, True), [blocks(BF16), column],
            slices, table, head_row, resident=(1,), flops=flops,
        )
        keep, score_b = call(
            functools.partial(half_kernel, False), [blocks(F32), column],
            slices, table, head_row, resident=(1,), flops=flops,
        )
        score_x = score_a + score_b
    else:
        send, keep, score_x = plain_half(slices, embed, head_row, devices)
    x_mine, x_got = sum_and_gather(swap_sum(send, keep, devices), devices)
    if tiled:
        wide = pltpu.VMEM((total, hidden), F32)
        send, keep, score_u = call(
            hidden_kernel, [blocks(BF16), blocks(F32), column],
            x_mine, x_got, gain_row, w_gate, w_up, down_row, valid_column,
            resident=(3, 4), flops=8 * total * hidden * width, scratch=(wide, wide),
        )
    else:
        send, keep, score_u = plain_hidden(
            x_mine, x_got, gain_row, w_gate, w_up, down_row, valid_column, devices
        )
    d_mine, d_got = sum_and_gather(swap_sum(send, keep, devices), devices)
    score = (score_x + score_u)[:, 0]
    own_rewards = jnp.sum(jnp.where(member, (valid * score)[:, None], 0.0), axis=0)
    sources = (x_mine, x_got, d_mine, d_got, gain_row, head_row, valid_column)
    if tiled:
        (d_slices,) = call(
            input_kernel, [jax.ShapeDtypeStruct((total, part), BF16)], *sources, table,
            resident=(7,), flops=2 * flops, scratch=(pltpu.VMEM((total, width), BF16),),
        )
    else:
        d_slices = plain_input(*sources, embed)
    extra = split3(own_rewards).reshape(1, 1, requests * 3)
    extra = jnp.broadcast_to(extra, (devices, rows, requests * 3))
    back = exchange(jnp.concatenate([d_slices.reshape(devices, rows, part), extra], axis=-1))
    sums = jnp.sum(back[:, 0, part:].astype(F32).reshape(devices, requests, 3), axis=(0, 2))
    rewards = sums / counts.astype(F32)
    d_probs = back[:, :, :part].transpose(1, 0, 2).reshape(rows, voc).astype(F32)
    d_logits = probs32 * (d_probs - jnp.sum(probs32 * d_probs, axis=-1, keepdims=True))
    guidance = (math.sqrt(VOC) * d_logits).astype(BF16)
    return (guidance, rewards)


def solution(mesh):
    placed = (
        P(("groups", "dp"), None),
        P("dp", None),
        P(),
        P(None, "dp"),
        P(None, "dp"),
        P("dp", None),
        P(),
        P("groups"),
    )
    return jax.shard_map(
        body,
        mesh=mesh,
        in_specs=placed,
        out_specs=(P(("groups", "dp"), None), P("groups")),
        check_vma=False,
    )
```

time: 125 us -> 132 us (1.056)
  matrix products: 30.1 us -> 0 us
  Pallas kernels: 0 us -> 28.9 us
  local copies, waits for them, and re-layouts: 5.82 us -> 27.4 us
  waiting for transfers between devices: 41.8 us -> 20.6 us
  blocking collectives: 10.7 us -> 21.2 us
    all_to_all x5 -> x1, waiting for transfers between devices: 41.8 us -> 0.01 us  [exchange(): return lax.all_to_all(blocks, 'dp', split_axis=0, concat_axis=0, tiled=True)]
    dot_general x6 -> x0, matrix products: 30.1 us -> none  [the longest x1 10.7 us: body(): jnp.einsum('td,vd->tv', d_input, embed, preferred_element_type=f32)]
    pallas_call x0 -> x5, Pallas kernels: none -> 28.9 us  [the longest x4 23.2 us: call(): pl.pallas_call(kernel, out_shape=outs, in_specs=[pl.BlockSpec(memory_spac...]
    unnamed x16, local copies, waits for them, and re-layouts: 0.63 us -> 23.1 us
    all_to_all x0 -> x3, waiting for transfers between devices: none -> 17 us  [exchange_chips(): lax.all_to_all(blocks, 'dp', split_axis=0, concat_axis=0, axis_index_grou...]
    all_to_all x5 -> x1, starting transfers between devices: 21.7 us -> 7.39 us  [exchange(): return lax.all_to_all(blocks, 'dp', split_axis=0, concat_axis=0, tiled=True)]
    all_to_all x0 -> x3, starting transfers between devices: none -> 12.4 us  [exchange_chips(): lax.all_to_all(blocks, 'dp', split_axis=0, concat_axis=0, axis_index_grou...]
    all_to_all x0 -> x1, blocking collectives: none -> 10.7 us  [exchange_chips(): lax.all_to_all(blocks, 'dp', split_axis=0, concat_axis=0, axis_index_grou...]
  transfers between devices with their start and end apart: 5 -> 8, of which waited for: 5 -> 6; matrix products, arithmetic and copies ran while one was open for 5% -> 5% of each run, Pallas kernels for 0% -> 7%
where the time goes in v4:
time: 132 us; the launch traced here: 131 us
  Pallas kernels  28.9 us (22%)
  local copies, waits for them, and re-layouts  27.4 us (21%)
  blocking collectives  21.2 us (16%)
  waiting for transfers between devices  20.6 us (16%)
  starting transfers between devices  20.5 us (16%)
  other arithmetic  11.8 us (9%)
    pallas_call x4, Pallas kernels, call(): pl.pallas_call(kernel, out_shape=outs, in_specs=[pl.BlockSpec(memory_spac...  23.2 us
    unnamed x16, local copies, waits for them, and re-layouts  23.1 us
    all_to_all x3, waiting for transfers between devices, exchange_chips(): lax.all_to_all(blocks, 'dp', split_axis=0, concat_axis=0, axis_index_grou...  17 us
    all_to_all x3, starting transfers between devices, exchange_chips(): lax.all_to_all(blocks, 'dp', split_axis=0, concat_axis=0, axis_index_grou...  12.4 us
    all_to_all x1, blocking collectives, exchange_chips(): lax.all_to_all(blocks, 'dp', split_axis=0, concat_axis=0, axis_index_grou...  10.7 us
    all_to_all x1, blocking collectives, exchange(): return lax.all_to_all(blocks, 'dp', split_axis=0, concat_axis=0, tiled=True)  10.5 us
    all_to_all x1, starting transfers between devices, exchange(): return lax.all_to_all(blocks, 'dp', split_axis=0, concat_axis=0, tiled=True)  7.39 us
    pallas_call x1, Pallas kernels, make_resident(): pl.pallas_call(resident_kernel, out_shape=pltpu.VMEM(source.shape, source...  5.78 us
  transfers between devices with their start and end apart: 8, of which 6 were waited for; matrix products, arithmetic and copies ran while one was open for 5% of the time, Pallas kernels for 7%

profile of v4, /device:TPU:0, one launch (start us, length us, event | category | flops | bytes accessed | tf_op | source)
XLA Modules:
  0.0 131.2 jit_solution(704062556681485887)
XLA Ops:
  0.6 1.3 reduce_max.14
  1.9 1.4 %fusion.1 = f32[2]{0:T(128)S(1)} fusion(bf16[2,32000]{1,0:T(2,128)(2,1)} %param.8, f32[2]{0:T(128)S(1)} %reduce_max.15), kind=kLoop, calls=%fused_computation.8 | loop fusion | flops 191998 | bytes 128016 | tf_op jit(solution)/shard_map/reduce_sum | solution.py:283
  3.3 1.2 fusion.10
  4.8 0.8 copy.22
  5.6 7.4 %all-to-all-start = ((bf16[16,2,2000]{2,1,0:T(2,128)(2,1)}), bf16[16,2,2000]{2,1,0:T(2,128)(2,1)S(1)}, u32[]{:S(2)}, u32[]{:S(2)}) async-start(bf16[16,2,2000]{2,1,0:T(2,128)(2,1)} %bitcast.12.after_ref), calls=%async_computation | async-start | bytes 262144 | tf_op jit(solution)/shard_map/all_to_all | solution.py:21
  13.0 0.7 reshape.120.head_ref
  13.7 5.8 %shard_map.95.embed_ref = bf16[2000,4096]{1,0:T(8,128)(2,1)S(1)} custom-call(bf16[2000,4096]{1,0:T(8,128)(2,1)} %source_ref.1, bf16[16,2,2000]{2,1,0:T(2,128)(2,1)} %bitcast.12.after_ref), custom_call_target="tpu_custom_call" | custom-call | bytes 16384000 | tf_op jit(solution)/shard_map/pallas_call | solution.py:74
  19.5 5.6 %copy-done = bf16[2000,4096]{1,0:T(8,128)(2,1)} copy-done((bf16[2000,4096]{1,0:T(8,128)(2,1)}, bf16[2000,4096]{1,0:T(8,128)(2,1)S(1)}, u32[]{:S(2)}) %copy-start) | copy-done | bytes 16384024
  25.2 5.6 %copy-done.1 = bf16[2000,4096]{1,0:T(8,128)(2,1)S(1)} copy-done((bf16[2000,4096]{1,0:T(8,128)(2,1)S(1)}, bf16[2000,4096]{1,0:T(8,128)(2,1)}, u32[]{:S(2)}) %copy-start.1) | copy-done | bytes 16384024
  30.8 3.0 %shard_map.97 = (bf16[8,32,256]{2,1,0:T(8,128)(2,1)S(1)}, f32[32,1]{1,0:T(8,128)S(1)}) custom-call(bf16[32,2000]{1,0:T(8,128)(2,1)S(1)} %reshape.119.slices_ref, bf16[2000,4096]{1,0:T(8,128)(2,1)S(1)} %copy-done.1, bf16[1,4096]{1,0:T(2,128)(2,1)S(1)} %reshape.120.head_ref), custom_call_target="tpu_custom_call" | custom-call | flops 262144000 | bytes 16520192 | tf_op jit(solution)/shard_map/pallas_call | solution.py:45
  34.3 3.0 %shard_map.96 = (f32[8,32,256]{2,1,0:T(8,128)S(1)}, f32[32,1]{1,0:T(8,128)S(1)}) custom-call(bf16[32,2000]{1,0:T(8,128)(2,1)S(1)} %reshape.119.slices_ref, bf16[2000,4096]{1,0:T(8,128)(2,1)S(1)} %copy-done.1, bf16[1,4096]{1,0:T(2,128)(2,1)S(1)} %reshape.120.head_ref), custom_call_target="tpu_custom_call" | custom-call | flops 262144000 | bytes 16520192 | tf_op jit(solution)/shard_map/pallas_call | solution.py:45
  37.3 0.7 add_convert_fusion.1
  38.0 5.7 %all-to-all-start.1 = ((bf16[8,32,256]{2,1,0:T(8,128)(2,1)}), bf16[8,32,256]{2,1,0:T(8,128)(2,1)S(1)}, u32[]{:S(2)}, u32[]{:S(2)}) async-start(bf16[8,32,256]{2,1,0:T(8,128)(2,1)} %add_convert_fusion.1), calls=%async_computation.1 | async-start | bytes 262144 | tf_op jit(solution)/shard_map/all_to_all | solution.py:26
  43.7 7.5 %all-to-all-done.1 = bf16[8,32,256]{2,1,0:T(8,128)(2,1)S(1)} async-done(((bf16[8,32,256]{2,1,0:T(8,128)(2,1)}), bf16[8,32,256]{2,1,0:T(8,128)(2,1)S(1)}, u32[]{:S(2)}, u32[]{:S(2)}) %all-to-all-start.1) | async-done | bytes 131104 | tf_op jit(solution)/shard_map/all_to_all | solution.py:26
  51.2 0.7 broadcast_in_dim.32
  51.9 3.4 %all-to-all-start.2 = ((bf16[8,32,256]{2,1,0:T(8,128)(2,1)}), bf16[8,32,256]{2,1,0:T(8,128)(2,1)S(1)}, u32[]{:S(2)}, u32[]{:S(2)}) async-start(bf16[8,32,256]{2,1,0:T(8,128)(2,1)} %broadcast_in_dim.32), calls=%async_computation.2 | async-start | bytes 262144 | tf_op jit(solution)/shard_map/all_to_all | solution.py:26
  55.2 4.6 %multiply_reduce_fusion = f32[896]{0:T(1024)S(1)} fusion(bf16[896,4096]{1,0:T(8,128)(2,1)} %param.13, f32[4096]{0:T(1024)S(1)} %convert_element_type.71), kind=kLoop, calls=%fused_computation | loop fusion | flops 11009152 | bytes 7360000 | tf_op jit(solution)/shard_map/reduce_sum | solution.py:287
  60.0 2.5 %all-to-all-done.2.mine_ref = bf16[8,32,256]{2,1,0:T(8,128)(2,1)S(1)} async-done(((bf16[8,32,256]{2,1,0:T(8,128)(2,1)}), bf16[8,32,256]{2,1,0:T(8,128)(2,1)S(1)}, u32[]{:S(2)}, u32[]{:S(2)}) %all-to-all-start.2) | async-done | bytes 131104 | tf_op jit(solution)/shard_map/all_to_all | solution.py:26
  62.5 1.3 %collective-permute-done.1.got_ref = bf16[8,32,256]{2,1,0:T(8,128)(2,1)S(1)} collective-permute-done((bf16[8,32,256]{2,1,0:T(8,128)(2,1)S(1)}, bf16[8,32,256]{2,1,0:T(8,128)(2,1)S(1)}, u32[]{:S(2)}, u32[]{:S(2)}) %collective-permute-start.1) | collective-permute-done | bytes 131104 | tf_op jit(solution)/shard_map/ppermute | solution.py:17
  63.9 3.1 %copy-done.3 = bf16[4096,896]{1,0:T(8,128)(2,1)S(1)} copy-done((bf16[4096,896]{1,0:T(8,128)(2,1)S(1)}, bf16[4096,896]{1,0:T(8,128)(2,1)}, u32[]{:S(2)}) %copy-start.3) | copy-done | bytes 7340056
  67.0 3.1 %copy-done.4 = bf16[4096,896]{1,0:T(8,128)(2,1)S(1)} copy-done((bf16[4096,896]{1,0:T(8,128)(2,1)S(1)}, bf16[4096,896]{1,0:T(8,128)(2,1)}, u32[]{:S(2)}) %copy-start.4) | copy-done | bytes 7340056
  70.0 11.0 %shard_map.98 = (bf16[8,32,256]{2,1,0:T(8,128)(2,1)S(1)}, f32[8,32,256]{2,1,0:T(8,128)S(1)}, f32[32,1]{1,0:T(8,128)S(1)}) custom-call(bf16[8,32,256]{2,1,0:T(8,128)(2,1)S(1)} %all-to-all-done.2.mine_ref, bf16[8,32,256]{2,1,0:T(8,128)(2,1)S(1)} %collective-permute-done.1.got_ref, bf16[1,4096]{1,0:T(2,128)(2,1)S(1)} %reshape.121.gain_ref, ...), custom_call_target="tpu_custom_call" | custom-call | flops 939524096 | bytes 14954112 | tf_op jit(solution)/shard_map/pallas_call | solution.py:45
  81.2 1.2 collective-permute-done.2
  82.4 10.7 %all_to_all.30 = bf16[8,32,256]{2,1,0:T(8,128)(2,1)S(1)} all-to-all(bf16[8,32,256]{2,1,0:T(8,128)(2,1)S(1)} %add_convert_fusion), channel_id=1, replica_groups={{0,2,4,6,8,10,12,14},{1,3,5,7,9,11,13,15},{16,18,20,22,24,26,28,30},{17..., dimensions={0} | all-to-all | bytes 262144 | tf_op jit(solution)/shard_map/all_to_all | solution.py:26
  93.1 0.7 broadcast_in_dim.35
  93.8 3.4 %all-to-all-start.4 = ((bf16[8,32,256]{2,1,0:T(8,128)(2,1)}), bf16[8,32,256]{2,1,0:T(8,128)(2,1)S(1)}, u32[]{:S(2)}, u32[]{:S(2)}) async-start(bf16[8,32,256]{2,1,0:T(8,128)(2,1)} %broadcast_in_dim.35), calls=%async_computation.4 | async-start | bytes 262144 | tf_op jit(solution)/shard_map/all_to_all | solution.py:26
  97.4 7.0 %all-to-all-done.4.d_mine_ref = bf16[8,32,256]{2,1,0:T(8,128)(2,1)S(1)} async-done(((bf16[8,32,256]{2,1,0:T(8,128)(2,1)}), bf16[8,32,256]{2,1,0:T(8,128)(2,1)S(1)}, u32[]{:S(2)}, u32[]{:S(2)}) %all-to-all-start.4) | async-done | bytes 131104 | tf_op jit(solution)/shard_map/all_to_all | solution.py:26
  104.8 1.0 collective-permute-done.3.d_got_ref
  105.8 5.7 %copy-done.2 = bf16[2000,4096]{1,0:T(8,128)(2,1)S(1)} copy-done((bf16[2000,4096]{1,0:T(8,128)(2,1)S(1)}, bf16[2000,4096]{1,0:T(8,128)(2,1)}, u32[]{:S(2)}) %copy-start.2) | copy-done | bytes 16384024
  111.5 6.2 %shard_map.99 = bf16[32,2000]{1,0:T(8,128)(2,1)S(1)} custom-call(bf16[8,32,256]{2,1,0:T(8,128)(2,1)S(1)} %all-to-all-done.2.mine_ref, bf16[8,32,256]{2,1,0:T(8,128)(2,1)S(1)} %collective-permute-done.1.got_ref, bf16[8,32,256]{2,1,0:T(8,128)(2,1)S(1)} %all-to-all-done.4.d_mine_ref, bf16[8,32,256]{2,1,0:T(8,128)(2,1)S(1)} %collective-permute-done.3.d_got_ref, ...), custom_call_target="tpu_custom_call" | custom-call | flops 524288000 | bytes 16924800 | tf_op jit(solution)/shard_map/pallas_call | solution.py:45
  117.9 10.5 %all_to_all.31 = bf16[16,2,2012]{2,1,0:T(2,128)(2,1)S(1)} all-to-all(bf16[16,2,2012]{2,1,0:T(2,128)(2,1)S(1)} %pad_maximum_fusion), channel_id=1, replica_groups=mesh['groups'=2,'dp'=16] {'dp'}, dimensions={0} | all-to-all | bytes 257536 | tf_op jit(solution)/shard_map/all_to_all | solution.py:21
  130.3 0.9 multiply_convert_fusion
  (47 shorter events, 4.0 us)
Async XLA Ops:
  5.6 19.5 %all-to-all-start = ((bf16[16,2,2000]{2,1,0:T(2,128)(2,1)}), bf16[16,2,2000]{2,1,0:T(2,128)(2,1)S(1)}, u32[]{:S(2)}, u32[]{:S(2)}) async-start(bf16[16,2,2000]{2,1,0:T(2,128)(2,1)} %bitcast.12.after_ref), calls=%async_computation | async-start | bytes 262144 | tf_op jit(solution)/shard_map/all_to_all | solution.py:21
  19.5 5.6 %copy-start = (bf16[2000,4096]{1,0:T(8,128)(2,1)}, bf16[2000,4096]{1,0:T(8,128)(2,1)S(1)}, u32[]{:S(2)}) copy-start(bf16[2000,4096]{1,0:T(8,128)(2,1)S(1)} %shard_map.95.embed_ref) | copy-start | bytes 49152004
  25.2 5.7 %copy-start.1 = (bf16[2000,4096]{1,0:T(8,128)(2,1)S(1)}, bf16[2000,4096]{1,0:T(8,128)(2,1)}, u32[]{:S(2)}) copy-start(bf16[2000,4096]{1,0:T(8,128)(2,1)} %copy-done) | copy-start | bytes 49152004
  30.8 12.9 %copy-start.5 = (bf16[4096]{0:T(1024)(128)(2,1)S(1)}, bf16[4096]{0:T(1024)(128)(2,1)}, u32[]{:S(2)}) copy-start(bf16[4096]{0:T(1024)(128)(2,1)} %param.14) | copy-start | bytes 24580
  33.8 26.0 %copy-start.7 = (s32[4]{0:T(128)S(1)}, s32[4]{0:T(128)}, u32[]{:S(2)}) copy-start(s32[4]{0:T(128)} %param.15) | copy-start | bytes 52
  33.8 26.2 %copy-start.6 = (bf16[4096]{0:T(1024)(128)(2,1)S(1)}, bf16[4096]{0:T(1024)(128)(2,1)}, u32[]{:S(2)}) copy-start(bf16[4096]{0:T(1024)(128)(2,1)} %param.10) | copy-start | bytes 24580
  33.8 3.5 %collective-permute-start = (bf16[8,32,256]{2,1,0:T(8,128)(2,1)S(1)}, bf16[8,32,256]{2,1,0:T(8,128)(2,1)S(1)}, u32[]{:S(2)}, u32[]{:S(2)}) collective-permute-start(bf16[8,32,256]{2,1,0:T(8,128)(2,1)S(1)} %get-tuple-element.10), channel_id=1, source_target_pairs={{0,1},{1,0},{2,3},{3,2},{4,5},{5,4},{6,7},{7,6},{8,9},{9,8},{10,11... | collective-permute-start | bytes 393224 | tf_op jit(solution)/shard_map/ppermute | solution.py:17
  38.0 13.2 %all-to-all-start.1 = ((bf16[8,32,256]{2,1,0:T(8,128)(2,1)}), bf16[8,32,256]{2,1,0:T(8,128)(2,1)S(1)}, u32[]{:S(2)}, u32[]{:S(2)}) async-start(bf16[8,32,256]{2,1,0:T(8,128)(2,1)} %add_convert_fusion.1), calls=%async_computation.1 | async-start | bytes 262144 | tf_op jit(solution)/shard_map/all_to_all | solution.py:26
  51.9 10.7 %all-to-all-start.2 = ((bf16[8,32,256]{2,1,0:T(8,128)(2,1)}), bf16[8,32,256]{2,1,0:T(8,128)(2,1)S(1)}, u32[]{:S(2)}, u32[]{:S(2)}) async-start(bf16[8,32,256]{2,1,0:T(8,128)(2,1)} %broadcast_in_dim.32), calls=%async_computation.2 | async-start | bytes 262144 | tf_op jit(solution)/shard_map/all_to_all | solution.py:26
  62.5 1.3 %collective-permute-start.1 = (bf16[8,32,256]{2,1,0:T(8,128)(2,1)S(1)}, bf16[8,32,256]{2,1,0:T(8,128)(2,1)S(1)}, u32[]{:S(2)}, u32[]{:S(2)}) collective-permute-start(bf16[8,32,256]{2,1,0:T(8,128)(2,1)S(1)} %all-to-all-done.2.mine_ref), channel_id=1, source_target_pairs={{0,1},{1,0},{2,3},{3,2},{4,5},{5,4},{6,7},{7,6},{8,9},{9,8},{10,11... | collective-permute-start | bytes 393224 | tf_op jit(solution)/shard_map/ppermute | solution.py:17
  63.9 3.1 %copy-start.3 = (bf16[4096,896]{1,0:T(8,128)(2,1)S(1)}, bf16[4096,896]{1,0:T(8,128)(2,1)}, u32[]{:S(2)}) copy-start(bf16[4096,896]{1,0:T(8,128)(2,1)} %gate_ref.1) | copy-start | bytes 22020100
  67.0 3.1 %copy-start.4 = (bf16[4096,896]{1,0:T(8,128)(2,1)S(1)}, bf16[4096,896]{1,0:T(8,128)(2,1)}, u32[]{:S(2)}) copy-start(bf16[4096,896]{1,0:T(8,128)(2,1)} %up_ref.1) | copy-start | bytes 22020100
  81.0 1.4 %collective-permute-start.2 = (bf16[8,32,256]{2,1,0:T(8,128)(2,1)S(1)}, bf16[8,32,256]{2,1,0:T(8,128)(2,1)S(1)}, u32[]{:S(2)}, u32[]{:S(2)}) collective-permute-start(bf16[8,32,256]{2,1,0:T(8,128)(2,1)S(1)} %get-tuple-element.12), channel_id=1, source_target_pairs={{0,1},{1,0},{2,3},{3,2},{4,5},{5,4},{6,7},{7,6},{8,9},{9,8},{10,11... | collective-permute-start | bytes 393224 | tf_op jit(solution)/shard_map/ppermute | solution.py:17
  93.8 10.7 %all-to-all-start.4 = ((bf16[8,32,256]{2,1,0:T(8,128)(2,1)}), bf16[8,32,256]{2,1,0:T(8,128)(2,1)S(1)}, u32[]{:S(2)}, u32[]{:S(2)}) async-start(bf16[8,32,256]{2,1,0:T(8,128)(2,1)} %broadcast_in_dim.35), calls=%async_computation.4 | async-start | bytes 262144 | tf_op jit(solution)/shard_map/all_to_all | solution.py:26
  104.5 1.3 %collective-permute-start.3 = (bf16[8,32,256]{2,1,0:T(8,128)(2,1)S(1)}, bf16[8,32,256]{2,1,0:T(8,128)(2,1)S(1)}, u32[]{:S(2)}, u32[]{:S(2)}) collective-permute-start(bf16[8,32,256]{2,1,0:T(8,128)(2,1)S(1)} %all-to-all-done.4.d_mine_ref), channel_id=1, source_target_pairs={{0,1},{1,0},{2,3},{3,2},{4,5},{5,4},{6,7},{7,6},{8,9},{9,8},{10,11... | collective-permute-start | bytes 393224 | tf_op jit(solution)/shard_map/ppermute | solution.py:17
  105.8 5.7 %copy-start.2 = (bf16[2000,4096]{1,0:T(8,128)(2,1)S(1)}, bf16[2000,4096]{1,0:T(8,128)(2,1)}, u32[]{:S(2)}) copy-start(bf16[2000,4096]{1,0:T(8,128)(2,1)} %copy-done) | copy-start | bytes 49152004

commit v5 on v4

v5 whole, which is shorter than its diff:
```python
import functools
import math

import jax
import jax.numpy as jnp
from jax import lax
from jax.experimental import pallas as pl
from jax.experimental.pallas import tpu as pltpu
from jax.sharding import PartitionSpec as P

VOC = 32000
F32, BF16 = jnp.float32, jnp.bfloat16
VMEM_BYTES = 12 * 1024 * 1024


def swap_cores(value, devices):
    return lax.ppermute(value, "dp", [(i, i ^ 1) for i in range(devices)])


def exchange(blocks):
    return lax.all_to_all(blocks, "dp", split_axis=0, concat_axis=0, tiled=True)


def exchange_chips(blocks, devices):
    groups = [list(range(core, devices, 2)) for core in range(2)]
    return lax.all_to_all(
        blocks, "dp", split_axis=0, concat_axis=0, axis_index_groups=groups, tiled=True
    )


def split3(value):
    hi = lax.reduce_precision(value, 8, 7)
    rest = value - hi
    mid = lax.reduce_precision(rest, 8, 7)
    low = rest - mid
    return jnp.stack([hi, mid, low], axis=-1).astype(BF16)


HBM_SPEC = pl.BlockSpec(memory_space=pltpu.HBM)
VMEM_SPEC = pl.BlockSpec(memory_space=pltpu.VMEM)


def call(kernel, outs, *args, streamed=(), flops=0, scratch=(), room=0):
    size = sum(math.prod(a.shape) * a.dtype.itemsize for a in args)
    args = [
        pltpu.with_memory_space_constraint(a, pltpu.HBM) if i in streamed else a
        for i, a in enumerate(args)
    ]
    return pl.pallas_call(
        kernel,
        out_shape=outs,
        in_specs=[HBM_SPEC if i in streamed else VMEM_SPEC for i in range(len(args))],
        out_specs=[VMEM_SPEC] * len(outs),
        scratch_shapes=list(scratch),
        compiler_params=pltpu.CompilerParams(vmem_limit_bytes=VMEM_BYTES + room),
        cost_estimate=pl.CostEstimate(flops=flops, bytes_accessed=size, transcendentals=0),
    )(*args)


def struct(shape, dtype):
    return jax.ShapeDtypeStruct(shape, dtype)


def this_core():
    return lax.axis_index("dp") % 2


def span(start, size):
    return pl.ds(pl.multiple_of(start, size), size)


def softmax_kernel(logits_ref, out_ref, top_ref, scale_ref):
    devices, _, part = out_ref.shape
    x = logits_ref[...].astype(F32)
    top = jnp.max(x, axis=-1, keepdims=True)
    e = jnp.exp(x - top)
    scale = 1.0 / jnp.sum(e, axis=-1, keepdims=True)
    probs = e * scale
    for d in range(devices):
        out_ref[d] = probs[:, d * part : (d + 1) * part].astype(BF16)
    top_ref[...] = top
    scale_ref[...] = scale


def final_kernel(
    logits_ref, top_ref, scale_ref, back_ref, counts_ref, out_ref, rewards_ref, d_ref
):
    devices, _, padded = back_ref.shape
    part = out_ref.shape[1] // devices
    requests = counts_ref.shape[1]
    sums = jnp.zeros((1, requests), F32)
    for d in range(devices):
        block = back_ref[d].astype(F32)
        d_ref[:, d * part : (d + 1) * part] = block[:, :part]
        for i in range(3):
            start = part + i * requests
            sums += block[:1, start : start + requests]
    rewards_ref[...] = sums / counts_ref[...]
    probs = jnp.exp(logits_ref[...].astype(F32) - top_ref[...]) * scale_ref[...]
    d_probs = d_ref[...]
    mean = jnp.sum(probs * d_probs, axis=-1, keepdims=True)
    out_ref[...] = (math.sqrt(VOC) * (probs * (d_probs - mean))).astype(BF16)


def half_kernel(other, slices_ref, embed_ref, head_ref, out_ref, score_ref, table, sems):
    chips, _, own = out_ref.shape
    core = this_core()
    half = (1 - core) if other else core

    def columns(j):
        return span((half * chips + j) * own, own)

    def copy(j):
        return pltpu.make_async_copy(embed_ref.at[:, columns(j)], table.at[j], sems.at[j])

    for j in range(chips):
        copy(j).start()
    slices = slices_ref[...]
    score = jnp.zeros(score_ref.shape, F32)
    for j in range(chips):
        copy(j).wait()
        part = jnp.dot(slices, table[j], preferred_element_type=F32)
        score += jnp.sum(part * head_ref[:, columns(j)].astype(F32), axis=-1, keepdims=True)
        out_ref[j] = part.astype(out_ref.dtype)
    score_ref[...] = score


def hidden_kernel(
    mine_ref, got_ref, gain_ref, gate_ref, up_ref, down_ref, valid_ref,
    send_ref, keep_ref, score_ref, gate, up, a_ref, b_ref, sems,
):
    chips, total, own = mine_ref.shape
    width = 2 * chips * own
    core = this_core()
    order = [(mine_ref, core, j) for j in range(chips)] + [
        (got_ref, 1 - core, j) for j in range(chips)
    ]

    def rows(half, j):
        return span((half * chips + j) * own, own)

    def copies(i):
        _, half, j = order[i]
        r = rows(half, j)
        return (
            pltpu.make_async_copy(gate_ref.at[r], gate.at[r], sems.at[0, i]),
            pltpu.make_async_copy(up_ref.at[r], up.at[r], sems.at[1, i]),
        )

    for i in range(2 * chips):
        for copy in copies(i):
            copy.start()
    squares = jnp.zeros((total, 1), F32)
    for j in range(chips):
        x, y = mine_ref[j].astype(F32), got_ref[j].astype(F32)
        squares += jnp.sum(x * x + y * y, axis=-1, keepdims=True)
    inv = lax.rsqrt(squares / width + 1e-05)
    for i, (ref, half, j) in enumerate(order):
        r = rows(half, j)
        normed = (ref[j].astype(F32) * inv * gain_ref[:, r].astype(F32)).astype(BF16)
        for copy in copies(i):
            copy.wait()
        a = jnp.dot(normed, gate[r], preferred_element_type=F32)
        b = jnp.dot(normed, up[r], preferred_element_type=F32)
        a_ref[...] = a_ref[...] + a if i else a
        b_ref[...] = b_ref[...] + b if i else b
    a, b = a_ref[...], b_ref[...]
    sigma = jax.nn.sigmoid(a)
    active = a * sigma
    down = down_ref[...]
    hidden = (active * b).astype(BF16).astype(F32)
    score_ref[...] = jnp.sum(hidden * down, axis=-1, keepdims=True)
    d_hidden = valid_ref[...] * down
    d_gate = (d_hidden * b * sigma * (1.0 + a * (1.0 - sigma))).astype(BF16)
    d_up = (d_hidden * active).astype(BF16)
    contract = (((1,), (1,)), ((), ()))
    for ref, half in ((send_ref, 1 - core), (keep_ref, core)):
        for j in range(chips):
            r = rows(half, j)
            part = lax.dot_general(d_gate, gate[r], contract, preferred_element_type=F32)
            part += lax.dot_general(d_up, up[r], contract, preferred_element_type=F32)
            ref[j] = part.astype(ref.dtype)


def input_kernel(
    mine_ref, got_ref, d_mine_ref, d_got_ref, gain_ref, head_ref, valid_ref,
    score_a_ref, score_b_ref, score_c_ref, member_ref, embed_ref,
    out_ref, dx_ref, table, sems,
):
    chips, total, own = mine_ref.shape
    devices, per, _ = out_ref.shape
    voc = embed_ref.shape[0]
    requests = member_ref.shape[1]
    width = 2 * chips * own
    core = this_core()
    tile = 256
    starts = [(i, min(tile, voc - i)) for i in range(0, voc, tile)]

    def copy(i):
        start, size = starts[i]
        return pltpu.make_async_copy(
            embed_ref.at[pl.ds(start, size)], table.at[pl.ds(start, size)], sems.at[i]
        )

    for i in range(len(starts)):
        copy(i).start()
    sources = ((mine_ref, d_mine_ref, core), (got_ref, d_got_ref, 1 - core))
    squares = jnp.zeros((total, 1), F32)
    dots = jnp.zeros((total, 1), F32)
    for x_ref, d_ref, half in sources:
        for j in range(chips):
            x = x_ref[j].astype(F32)
            g = d_ref[j].astype(F32) * gain_ref[:, span((half * chips + j) * own, own)].astype(F32)
            squares += jnp.sum(x * x, axis=-1, keepdims=True)
            dots += jnp.sum(g * x, axis=-1, keepdims=True)
    inv = lax.rsqrt(squares / width + 1e-05)
    mean = dots / width
    valid = valid_ref[...]
    for x_ref, d_ref, half in sources:
        for j in range(chips):
            columns = span((half * chips + j) * own, own)
            x = x_ref[j].astype(F32)
            g = d_ref[j].astype(F32) * gain_ref[:, columns].astype(F32)
            dx = inv * g - x * inv * inv * inv * mean
            dx_ref[:, columns] = (dx + valid * head_ref[:, columns].astype(F32)).astype(BF16)
    score = score_a_ref[...] + score_b_ref[...] + score_c_ref[...]
    value = jnp.sum(member_ref[...] * (valid * score), axis=0, keepdims=True)
    pieces = []
    for _ in range(3):
        piece = value.astype(BF16)
        pieces.append(piece)
        value = value - piece.astype(F32)
    for i, piece in enumerate(pieces):
        start = voc + i * requests
        spread = jnp.broadcast_to(piece.astype(F32), (per, requests)).astype(BF16)
        for d in range(devices):
            out_ref[d, :, start : start + requests] = spread
    contract = (((1,), (1,)), ((), ()))
    dx = dx_ref[...]
    for i, (start, size) in enumerate(starts):
        copy(i).wait()
        part = lax.dot_general(
            dx, table[start : start + size, :], contract, preferred_element_type=F32
        )
        for d in range(devices):
            out_ref[d, :, start : start + size] = part[d * per : (d + 1) * per].astype(BF16)


def swap_sum(send, keep, devices):
    return (keep.astype(F32) + swap_cores(send, devices).astype(F32)).astype(BF16)


def sum_and_gather(half, devices):
    total = jnp.sum(exchange_chips(half, devices).astype(F32), axis=0).astype(BF16)
    held = exchange_chips(jnp.broadcast_to(total[None], half.shape), devices)
    return held, swap_cores(held, devices)


def pick(blocks, index):
    return lax.dynamic_index_in_dim(blocks, index, 0, keepdims=False)


def split_halves(part, devices):
    total, width = part.shape
    core = lax.axis_index("dp") % 2
    blocks = part.reshape(total, 2, devices // 2, width // devices).transpose(1, 2, 0, 3)
    return pick(blocks, 1 - core).astype(BF16), pick(blocks, core)


def join_halves(mine, got):
    core = lax.axis_index("dp") % 2
    blocks = jnp.where(core == 1, jnp.stack([got, mine]), jnp.stack([mine, got]))
    _, chips, total, own = blocks.shape
    return blocks.transpose(2, 0, 1, 3).reshape(total, 2 * chips * own).astype(F32)


def norm_scale(x0):
    return lax.rsqrt(jnp.mean(x0 * x0, axis=-1, keepdims=True) + 1e-05)


def plain_half(slices, embed, head_row, devices):
    part = jnp.dot(slices, embed, preferred_element_type=F32)
    score = jnp.sum(part * head_row.astype(F32), axis=-1, keepdims=True)
    return *split_halves(part, devices), score


def plain_hidden(mine, got, gain_row, w_gate, w_up, down, valid, devices):
    x0 = join_halves(mine, got)
    normed = (x0 * norm_scale(x0) * gain_row.astype(F32)).astype(BF16)
    a = jnp.dot(normed, w_gate, preferred_element_type=F32)
    b = jnp.dot(normed, w_up, preferred_element_type=F32)
    sigma = jax.nn.sigmoid(a)
    active = a * sigma
    hidden = (active * b).astype(BF16).astype(F32)
    d_hidden = valid * down
    d_gate = (d_hidden * b * sigma * (1.0 + a * (1.0 - sigma))).astype(BF16)
    d_up = (d_hidden * active).astype(BF16)
    part = jnp.einsum("tf,df->td", d_gate, w_gate, preferred_element_type=F32)
    part = part + jnp.einsum("tf,df->td", d_up, w_up, preferred_element_type=F32)
    return *split_halves(part, devices), jnp.sum(hidden * down, axis=-1, keepdims=True)


def plain_input(mine, got, d_mine, d_got, gain_row, head_row, valid, embed):
    x0 = join_halves(mine, got)
    inv = norm_scale(x0)
    scaled = join_halves(d_mine, d_got) * gain_row.astype(F32)
    dx = inv * scaled - x0 * inv * inv * inv * jnp.mean(scaled * x0, axis=-1, keepdims=True)
    dx = (dx + valid * head_row.astype(F32)).astype(BF16)
    return jnp.einsum("td,vd->tv", dx, embed, preferred_element_type=F32).astype(BF16)


def body(logits, embed, norm_gain, w_gate, w_up, w_down, head, counts):
    devices = lax.axis_size("dp")
    rows, voc = logits.shape
    part = voc // devices
    width = embed.shape[1]
    hidden = w_gate.shape[1]
    own, chips = width // devices, devices // 2
    requests = counts.shape[0]
    total = rows * devices
    request_len = total // requests
    tiled = own % 128 == 0 and hidden % 128 == 0 and total % 16 == 0 and part % 16 == 0
    head32 = head.astype(F32)
    head_row, gain_row = head.reshape(1, width), norm_gain.reshape(1, width)
    if tiled:
        column = struct((rows, 1), F32)
        blocked, top, scale = call(
            softmax_kernel, [struct((devices, rows, part), BF16), column, column], logits
        )
    else:
        probs32 = jax.nn.softmax(logits.astype(F32), axis=-1)
        blocked = probs32.astype(BF16).reshape(rows, devices, part).transpose(1, 0, 2)
    slices = exchange(blocked).reshape(total, part)
    down_head = jnp.sum(w_down.astype(F32) * head32[None, :], axis=-1)
    position = jnp.arange(total, dtype=jnp.int32)
    member = (position // request_len)[:, None] == jnp.arange(requests, dtype=jnp.int32)[None, :]
    limit = jnp.sum(jnp.where(member, counts[None, :], 0), axis=-1, keepdims=True)
    valid = (position[:, None] % request_len < limit).astype(F32)
    member = member.astype(F32)
    down_row = down_head.reshape(1, hidden)
    column = struct((total, 1), F32)
    half = (chips, total, own)
    flops = total * part * width
    if tiled:
        table = [pltpu.VMEM((chips, part, own), BF16), pltpu.SemaphoreType.DMA((chips,))]
        args = dict(streamed=(1,), flops=flops, scratch=table, room=part * width)
        send, score_a = call(
            functools.partial(half_kernel, True), [struct(half, BF16), column],
            slices, embed, head_row, **args,
        )
        keep, score_b = call(
            functools.partial(half_kernel, False), [struct(half, F32), column],
            slices, embed, head_row, **args,
        )
    else:
        send, keep, score_a = plain_half(slices, embed, head_row, devices)
        score_b = jnp.zeros_like(score_a)
    x_mine, x_got = sum_and_gather(swap_sum(send, keep, devices), devices)
    if tiled:
        wide, weight = pltpu.VMEM((total, hidden), F32), pltpu.VMEM((width, hidden), BF16)
        send, keep, score_c = call(
            hidden_kernel, [struct(half, BF16), struct(half, F32), column],
            x_mine, x_got, gain_row, w_gate, w_up, down_row, valid,
            streamed=(3, 4), flops=8 * total * hidden * width, room=4 * width * hidden,
            scratch=(weight, weight, wide, wide, pltpu.SemaphoreType.DMA((2, devices))),
        )
    else:
        send, keep, score_c = plain_hidden(
            x_mine, x_got, gain_row, w_gate, w_up, down_row, valid, devices
        )
    d_mine, d_got = sum_and_gather(swap_sum(send, keep, devices), devices)
    sources = (x_mine, x_got, d_mine, d_got, gain_row, head_row, valid)
    padded = part + 3 * requests
    if tiled:
        (d_slices,) = call(
            input_kernel, [struct((devices, rows, padded), BF16)],
            *sources, score_a, score_b, score_c, member, embed,
            streamed=(11,), flops=2 * flops, room=2 * part * width,
            scratch=(
                pltpu.VMEM((total, width), BF16), pltpu.VMEM((part, width), BF16),
                pltpu.SemaphoreType.DMA((-(-part // 256),)),
            ),
        )
    else:
        d_slices = plain_input(*sources, embed).reshape(devices, rows, part)
        score = valid * (score_a + score_b + score_c)
        extra = split3(jnp.sum(member * score, axis=0)).reshape(1, 1, requests * 3)
        extra = jnp.broadcast_to(extra, (devices, rows, requests * 3))
        d_slices = jnp.concatenate([d_slices, extra], axis=-1)
    back = exchange(d_slices)
    counts32 = counts.astype(F32)
    if tiled:
        guidance, rewards = call(
            final_kernel, [struct((rows, voc), BF16), struct((1, requests), F32)],
            logits, top, scale, back, counts32.reshape(1, requests),
            scratch=(pltpu.VMEM((rows, voc), F32),),
        )
        return (guidance, rewards.reshape(requests))
    sums = jnp.sum(back[:, 0, part:].astype(F32).reshape(devices, requests, 3), axis=(0, 2))
    rewards = sums / counts32
    d_probs = back[:, :, :part].transpose(1, 0, 2).reshape(rows, voc).astype(F32)
    d_logits = probs32 * (d_probs - jnp.sum(probs32 * d_probs, axis=-1, keepdims=True))
    guidance = (math.sqrt(VOC) * d_logits).astype(BF16)
    return (guidance, rewards)


def solution(mesh):
    placed = (
        P(("groups", "dp"), None),
        P("dp", None),
        P(),
        P(None, "dp"),
        P(None, "dp"),
        P("dp", None),
        P(),
        P("groups"),
    )
    return jax.shard_map(
        body,
        mesh=mesh,
        in_specs=placed,
        out_specs=(P(("groups", "dp"), None), P("groups")),
        check_vma=False,
    )
```

time: 132 us -> 112 us (0.85)
  local copies, waits for them, and re-layouts: 27.4 us -> 2.47 us
  waiting for transfers between devices: 20.6 us -> 29.2 us
  other arithmetic: 11.8 us -> 5.65 us
  Pallas kernels: 28.9 us -> 34.9 us
  starting transfers between devices: 20.5 us -> 17.8 us
    unnamed x16 -> x10, local copies, waits for them, and re-layouts: 23.1 us -> 0.92 us
    all_to_all x1 -> x2, waiting for transfers between devices: 0.01 us -> 15.1 us  [exchange(): return lax.all_to_all(blocks, 'dp', split_axis=0, concat_axis=0, tiled=True)]
    all_to_all x1 -> x0, blocking collectives: 10.5 us -> none  [exchange(): return lax.all_to_all(blocks, 'dp', split_axis=0, concat_axis=0, tiled=True)]
    all_to_all x1 -> x2, blocking collectives: 10.7 us -> 20.6 us  [exchange_chips(): lax.all_to_all(blocks, 'dp', split_axis=0, concat_axis=0, axis_index_grou...]
    all_to_all x3 -> x2, waiting for transfers between devices: 17 us -> 10.2 us  [exchange_chips(): lax.all_to_all(blocks, 'dp', split_axis=0, concat_axis=0, axis_index_grou...]
    pallas_call x5 -> x6, Pallas kernels: 28.9 us -> 34.9 us  [call(): pl.pallas_call(kernel, out_shape=outs, in_specs=[HBM_SPEC if i in streame...]
    all_to_all x3 -> x2, starting transfers between devices: 12.4 us -> 6.74 us  [exchange_chips(): lax.all_to_all(blocks, 'dp', split_axis=0, concat_axis=0, axis_index_grou...]
    all_to_all x1 -> x2, starting transfers between devices: 7.39 us -> 10.9 us  [exchange(): return lax.all_to_all(blocks, 'dp', split_axis=0, concat_axis=0, tiled=True)]
  transfers between devices with their start and end apart: 8 -> 8, of which waited for: 6 -> 7; matrix products, arithmetic and copies ran while one was open for 5% -> 5% of each run, Pallas kernels for 7% -> 4%
where the time goes in v5:
time: 112 us; the launch traced here: 111 us
  Pallas kernels  34.9 us (31%)
  waiting for transfers between devices  29.2 us (26%)
  blocking collectives  20.6 us (18%)
  starting transfers between devices  17.8 us (16%)
  other arithmetic  5.65 us (5%)
  local copies, waits for them, and re-layouts  2.47 us (2%)
    pallas_call x6, Pallas kernels, call(): pl.pallas_call(kernel, out_shape=outs, in_specs=[HBM_SPEC if i in streame...  34.9 us
    all_to_all x2, blocking collectives, exchange_chips(): lax.all_to_all(blocks, 'dp', split_axis=0, concat_axis=0, axis_index_grou...  20.6 us
    all_to_all x2, waiting for transfers between devices, exchange(): return lax.all_to_all(blocks, 'dp', split_axis=0, concat_axis=0, tiled=True)  15.1 us
    all_to_all x2, starting transfers between devices, exchange(): return lax.all_to_all(blocks, 'dp', split_axis=0, concat_axis=0, tiled=True)  10.9 us
    all_to_all x2, waiting for transfers between devices, exchange_chips(): lax.all_to_all(blocks, 'dp', split_axis=0, concat_axis=0, axis_index_grou...  10.2 us
    all_to_all x2, starting transfers between devices, exchange_chips(): lax.all_to_all(blocks, 'dp', split_axis=0, concat_axis=0, axis_index_grou...  6.74 us
    reduce_sum x1, other arithmetic, body(): down_head = jnp.sum(w_down.astype(F32) * head32[None, :], axis=-1)  4.62 us
    ppermute x4, waiting for transfers between devices, swap_cores(): return lax.ppermute(value, 'dp', [(i, i ^ 1) for i in range(devices)])  3.9 us
  transfers between devices with their start and end apart: 8, of which 7 were waited for; matrix products, arithmetic and copies ran while one was open for 5% of the time, Pallas kernels for 4%

profile of v5, /device:TPU:0, one launch (start us, length us, event | category | flops | bytes accessed | tf_op | source)
XLA Modules:
  0.0 111.4 jit_solution(16352203681697450432)
XLA Ops:
  0.6 0.9 copy-done
  1.5 1.4 %shard_map.95 = (bf16[16,2,2000]{2,1,0:T(2,128)(2,1)}, f32[2,1]{1,0:T(2,128)S(1)}, f32[2,1]{1,0:T(2,128)S(1)}) custom-call(bf16[2,32000]{1,0:T(2,128)(2,1)S(1)} %copy-done), custom_call_target="tpu_custom_call" | custom-call | bytes 128000 | tf_op jit(solution)/shard_map/pallas_call | solution.py:49
  3.0 7.4 %all-to-all-start = ((bf16[16,2,2000]{2,1,0:T(2,128)(2,1)}), bf16[16,2,2000]{2,1,0:T(2,128)(2,1)S(1)}, u32[]{:S(2)}, u32[]{:S(2)}) async-start(bf16[16,2,2000]{2,1,0:T(2,128)(2,1)} %get-tuple-element.16), calls=%async_computation | async-start | bytes 262144 | tf_op jit(solution)/shard_map/all_to_all | solution.py:21
  10.3 0.7 reshape.80.head_ref
  11.1 7.2 %all-to-all-done = bf16[16,2,2000]{2,1,0:T(2,128)(2,1)S(1)} async-done(((bf16[16,2,2000]{2,1,0:T(2,128)(2,1)}), bf16[16,2,2000]{2,1,0:T(2,128)(2,1)S(1)}, u32[]{:S(2)}, u32[]{:S(2)}) %all-to-all-start) | async-done | bytes 128032 | tf_op jit(solution)/shard_map/all_to_all | solution.py:21
  18.3 0.1 reshape.79.slices_ref
  18.3 0.0 copy-start.2
  18.4 5.0 %shard_map.97 = (bf16[8,32,256]{2,1,0:T(8,128)(2,1)S(1)}, f32[32,1]{1,0:T(8,128)S(1)}) custom-call(bf16[32,2000]{1,0:T(8,128)(2,1)S(1)} %reshape.79.slices_ref, bf16[2000,4096]{1,0:T(8,128)(2,1)} %embed_ref.5, bf16[1,4096]{1,0:T(2,128)(2,1)S(1)} %reshape.80.head_ref), custom_call_target="tpu_custom_call" | custom-call | flops 262144000 | bytes 16520192 | tf_op jit(solution)/shard_map/pallas_call | solution.py:49
  23.4 0.0 copy-start.3
  23.4 0.1 collective-permute-start
  23.5 5.0 %shard_map.96 = (f32[8,32,256]{2,1,0:T(8,128)S(1)}, f32[32,1]{1,0:T(8,128)S(1)}) custom-call(bf16[32,2000]{1,0:T(8,128)(2,1)S(1)} %reshape.79.slices_ref, bf16[2000,4096]{1,0:T(8,128)(2,1)} %embed_ref.5, bf16[1,4096]{1,0:T(2,128)(2,1)S(1)} %reshape.80.head_ref), custom_call_target="tpu_custom_call" | custom-call | flops 262144000 | bytes 16520192 | tf_op jit(solution)/shard_map/pallas_call | solution.py:49
  28.5 0.7 add_convert_fusion.1
  29.2 3.4 %all-to-all-start.1 = ((bf16[8,32,256]{2,1,0:T(8,128)(2,1)}), bf16[8,32,256]{2,1,0:T(8,128)(2,1)S(1)}, u32[]{:S(2)}, u32[]{:S(2)}) async-start(bf16[8,32,256]{2,1,0:T(8,128)(2,1)} %add_convert_fusion.1), calls=%async_computation.1 | async-start | bytes 262144 | tf_op jit(solution)/shard_map/all_to_all | solution.py:26
  32.6 7.8 %all-to-all-done.1 = bf16[8,32,256]{2,1,0:T(8,128)(2,1)S(1)} async-done(((bf16[8,32,256]{2,1,0:T(8,128)(2,1)}), bf16[8,32,256]{2,1,0:T(8,128)(2,1)S(1)}, u32[]{:S(2)}, u32[]{:S(2)}) %all-to-all-start.1) | async-done | bytes 131104 | tf_op jit(solution)/shard_map/all_to_all | solution.py:26
  40.4 0.7 broadcast_in_dim.16
  41.1 3.4 %all-to-all-start.2 = ((bf16[8,32,256]{2,1,0:T(8,128)(2,1)}), bf16[8,32,256]{2,1,0:T(8,128)(2,1)S(1)}, u32[]{:S(2)}, u32[]{:S(2)}) async-start(bf16[8,32,256]{2,1,0:T(8,128)(2,1)} %broadcast_in_dim.16), calls=%async_computation.2 | async-start | bytes 262144 | tf_op jit(solution)/shard_map/all_to_all | solution.py:26
  44.4 4.6 %multiply_reduce_fusion = f32[896]{0:T(1024)S(1)} fusion(bf16[896,4096]{1,0:T(8,128)(2,1)} %param.13, f32[4096]{0:T(1024)S(1)} %convert_element_type.34), kind=kLoop, calls=%fused_computation | loop fusion | flops 11009152 | bytes 7360000 | tf_op jit(solution)/shard_map/reduce_sum | solution.py:334
  49.1 0.2 select_reduce_fusion
  49.3 0.1 copy.10
  49.4 2.3 %all-to-all-done.2.mine_ref = bf16[8,32,256]{2,1,0:T(8,128)(2,1)S(1)} async-done(((bf16[8,32,256]{2,1,0:T(8,128)(2,1)}), bf16[8,32,256]{2,1,0:T(8,128)(2,1)S(1)}, u32[]{:S(2)}, u32[]{:S(2)}) %all-to-all-start.2) | async-done | bytes 131104 | tf_op jit(solution)/shard_map/all_to_all | solution.py:26
  51.8 1.3 %collective-permute-done.1.got_ref = bf16[8,32,256]{2,1,0:T(8,128)(2,1)S(1)} collective-permute-done((bf16[8,32,256]{2,1,0:T(8,128)(2,1)S(1)}, bf16[8,32,256]{2,1,0:T(8,128)(2,1)S(1)}, u32[]{:S(2)}, u32[]{:S(2)}) %collective-permute-start.1) | collective-permute-done | bytes 131104 | tf_op jit(solution)/shard_map/ppermute | solution.py:17
  53.1 10.2 %shard_map.98 = (bf16[8,32,256]{2,1,0:T(8,128)(2,1)S(1)}, f32[8,32,256]{2,1,0:T(8,128)S(1)}, f32[32,1]{1,0:T(8,128)S(1)}) custom-call(bf16[8,32,256]{2,1,0:T(8,128)(2,1)S(1)} %all-to-all-done.2.mine_ref, bf16[8,32,256]{2,1,0:T(8,128)(2,1)S(1)} %collective-permute-done.1.got_ref, bf16[1,4096]{1,0:T(2,128)(2,1)S(1)} %reshape.81.gain_ref, ...), custom_call_target="tpu_custom_call" | custom-call | flops 939524096 | bytes 14954112 | tf_op jit(solution)/shard_map/pallas_call | solution.py:49
  63.2 0.1 collective-permute-start.2
  63.3 1.3 %collective-permute-done.2 = bf16[8,32,256]{2,1,0:T(8,128)(2,1)S(1)} collective-permute-done((bf16[8,32,256]{2,1,0:T(8,128)(2,1)S(1)}, bf16[8,32,256]{2,1,0:T(8,128)(2,1)S(1)}, u32[]{:S(2)}, u32[]{:S(2)}) %collective-permute-start.2) | collective-permute-done | bytes 131104 | tf_op jit(solution)/shard_map/ppermute | solution.py:17
  64.7 10.8 %all_to_all.30 = bf16[8,32,256]{2,1,0:T(8,128)(2,1)S(1)} all-to-all(bf16[8,32,256]{2,1,0:T(8,128)(2,1)S(1)} %add_convert_fusion), channel_id=1, replica_groups={{0,2,4,6,8,10,12,14},{1,3,5,7,9,11,13,15},{16,18,20,22,24,26,28,30},{17..., dimensions={0} | all-to-all | bytes 262144 | tf_op jit(solution)/shard_map/all_to_all | solution.py:26
  75.5 9.8 %all_to_all.31.d_mine_ref = bf16[8,32,256]{2,1,0:T(8,128)(2,1)S(1)} all-to-all(bf16[8,32,256]{2,1,0:T(8,128)(2,1)S(1)} %broadcast_in_dim.19), channel_id=1, replica_groups={{0,2,4,6,8,10,12,14},{1,3,5,7,9,11,13,15},{16,18,20,22,24,26,28,30},{17..., dimensions={0} | all-to-all | bytes 262144 | tf_op jit(solution)/shard_map/all_to_all | solution.py:26
  85.3 0.1 fusion.1.member_ref
  85.4 1.3 %collective-permute-done.3.d_got_ref = bf16[8,32,256]{2,1,0:T(8,128)(2,1)S(1)} collective-permute-done((bf16[8,32,256]{2,1,0:T(8,128)(2,1)S(1)}, bf16[8,32,256]{2,1,0:T(8,128)(2,1)S(1)}, u32[]{:S(2)}, u32[]{:S(2)}) %collective-permute-start.3) | collective-permute-done | bytes 131104 | tf_op jit(solution)/shard_map/ppermute | solution.py:17
  86.6 12.1 %shard_map.99 = bf16[16,2,2012]{2,1,0:T(2,128)(2,1)} custom-call(bf16[8,32,256]{2,1,0:T(8,128)(2,1)S(1)} %all-to-all-done.2.mine_ref, bf16[8,32,256]{2,1,0:T(8,128)(2,1)S(1)} %collective-permute-done.1.got_ref, bf16[8,32,256]{2,1,0:T(8,128)(2,1)S(1)} %all_to_all.31.d_mine_ref, bf16[8,32,256]{2,1,0:T(8,128)(2,1)S(1)} %collective-permute-done.3.d_got_ref, ...), custom_call_target="tpu_custom_call" | custom-call | flops 524288000 | bytes 16925696 | tf_op jit(solution)/shard_map/pallas_call | solution.py:49
  98.7 3.5 %all-to-all-start.5 = ((bf16[16,2,2012]{2,1,0:T(2,128)(2,1)}), bf16[16,2,2012]{2,1,0:T(2,128)(2,1)S(1)}, u32[]{:S(2)}, u32[]{:S(2)}) async-start(bf16[16,2,2012]{2,1,0:T(2,128)(2,1)} %shard_map.99), calls=%async_computation.5 | async-start | bytes 262144 | tf_op jit(solution)/shard_map/all_to_all | solution.py:21
  102.3 7.9 %all-to-all-done.5.back_ref = bf16[16,2,2012]{2,1,0:T(2,128)(2,1)S(1)} async-done(((bf16[16,2,2012]{2,1,0:T(2,128)(2,1)}), bf16[16,2,2012]{2,1,0:T(2,128)(2,1)S(1)}, u32[]{:S(2)}, u32[]{:S(2)}) %all-to-all-start.5) | async-done | bytes 128800 | tf_op jit(solution)/shard_map/all_to_all | solution.py:21
  110.1 1.2 %shard_map.100 = (bf16[2,32000]{1,0:T(2,128)(2,1)}, f32[1,4]{1,0:T(1,128)}) custom-call(bf16[2,32000]{1,0:T(2,128)(2,1)S(1)} %copy-done.1, f32[2,1]{1,0:T(2,128)S(1)} %get-tuple-element.14.top_ref, f32[2,1]{1,0:T(2,128)S(1)} %get-tuple-element.15.scale_ref, bf16[16,2,2012]{2,1,0:T(2,128)(2,1)S(1)} %all-to-all-done.5.back_ref, ...), custom_call_target="tpu_custom_call" | custom-call | bytes 256800 | tf_op jit(solution)/shard_map/pallas_call | solution.py:49
  (20 shorter events, 0.2 us)
Async XLA Ops:
  0.6 0.9 copy-start
  3.0 15.3 %all-to-all-start = ((bf16[16,2,2000]{2,1,0:T(2,128)(2,1)}), bf16[16,2,2000]{2,1,0:T(2,128)(2,1)S(1)}, u32[]{:S(2)}, u32[]{:S(2)}) async-start(bf16[16,2,2000]{2,1,0:T(2,128)(2,1)} %get-tuple-element.16), calls=%async_computation | async-start | bytes 262144 | tf_op jit(solution)/shard_map/all_to_all | solution.py:21
  18.3 14.2 %copy-start.2 = (bf16[4096]{0:T(1024)(128)(2,1)S(1)}, bf16[4096]{0:T(1024)(128)(2,1)}, u32[]{:S(2)}) copy-start(bf16[4096]{0:T(1024)(128)(2,1)} %param.14) | copy-start | bytes 24580
  23.4 25.7 %copy-start.3 = (bf16[4096]{0:T(1024)(128)(2,1)S(1)}, bf16[4096]{0:T(1024)(128)(2,1)}, u32[]{:S(2)}) copy-start(bf16[4096]{0:T(1024)(128)(2,1)} %param.10) | copy-start | bytes 24580
  23.4 25.7 %copy-start.4 = (s32[4]{0:T(128)S(1)}, s32[4]{0:T(128)}, u32[]{:S(2)}) copy-start(s32[4]{0:T(128)} %param.15) | copy-start | bytes 52
  23.4 5.1 %collective-permute-start = (bf16[8,32,256]{2,1,0:T(8,128)(2,1)S(1)}, bf16[8,32,256]{2,1,0:T(8,128)(2,1)S(1)}, u32[]{:S(2)}, u32[]{:S(2)}) collective-permute-start(bf16[8,32,256]{2,1,0:T(8,128)(2,1)S(1)} %get-tuple-element.18), channel_id=1, source_target_pairs={{0,1},{1,0},{2,3},{3,2},{4,5},{5,4},{6,7},{7,6},{8,9},{9,8},{10,11... | collective-permute-start | bytes 393224 | tf_op jit(solution)/shard_map/ppermute | solution.py:17
  29.2 11.2 %all-to-all-start.1 = ((bf16[8,32,256]{2,1,0:T(8,128)(2,1)}), bf16[8,32,256]{2,1,0:T(8,128)(2,1)S(1)}, u32[]{:S(2)}, u32[]{:S(2)}) async-start(bf16[8,32,256]{2,1,0:T(8,128)(2,1)} %add_convert_fusion.1), calls=%async_computation.1 | async-start | bytes 262144 | tf_op jit(solution)/shard_map/all_to_all | solution.py:26
  41.1 10.7 %all-to-all-start.2 = ((bf16[8,32,256]{2,1,0:T(8,128)(2,1)}), bf16[8,32,256]{2,1,0:T(8,128)(2,1)S(1)}, u32[]{:S(2)}, u32[]{:S(2)}) async-start(bf16[8,32,256]{2,1,0:T(8,128)(2,1)} %broadcast_in_dim.16), calls=%async_computation.2 | async-start | bytes 262144 | tf_op jit(solution)/shard_map/all_to_all | solution.py:26
  51.7 1.3 %collective-permute-start.1 = (bf16[8,32,256]{2,1,0:T(8,128)(2,1)S(1)}, bf16[8,32,256]{2,1,0:T(8,128)(2,1)S(1)}, u32[]{:S(2)}, u32[]{:S(2)}) collective-permute-start(bf16[8,32,256]{2,1,0:T(8,128)(2,1)S(1)} %all-to-all-done.2.mine_ref), channel_id=1, source_target_pairs={{0,1},{1,0},{2,3},{3,2},{4,5},{5,4},{6,7},{7,6},{8,9},{9,8},{10,11... | collective-permute-start | bytes 393224 | tf_op jit(solution)/shard_map/ppermute | solution.py:17
  51.7 58.4 %copy-start.1 = (bf16[2,32000]{1,0:T(2,128)(2,1)S(1)}, bf16[2,32000]{1,0:T(2,128)(2,1)}, u32[]{:S(2)}) copy-start(bf16[2,32000]{1,0:T(2,128)(2,1)} %logits_ref.3) | copy-start | bytes 384004
  63.2 1.4 %collective-permute-start.2 = (bf16[8,32,256]{2,1,0:T(8,128)(2,1)S(1)}, bf16[8,32,256]{2,1,0:T(8,128)(2,1)S(1)}, u32[]{:S(2)}, u32[]{:S(2)}) collective-permute-start(bf16[8,32,256]{2,1,0:T(8,128)(2,1)S(1)} %get-tuple-element.20), channel_id=1, source_target_pairs={{0,1},{1,0},{2,3},{3,2},{4,5},{5,4},{6,7},{7,6},{8,9},{9,8},{10,11... | collective-permute-start | bytes 393224 | tf_op jit(solution)/shard_map/ppermute | solution.py:17
  85.3 1.3 %collective-permute-start.3 = (bf16[8,32,256]{2,1,0:T(8,128)(2,1)S(1)}, bf16[8,32,256]{2,1,0:T(8,128)(2,1)S(1)}, u32[]{:S(2)}, u32[]{:S(2)}) collective-permute-start(bf16[8,32,256]{2,1,0:T(8,128)(2,1)S(1)} %all_to_all.31.d_mine_ref), channel_id=1, source_target_pairs={{0,1},{1,0},{2,3},{3,2},{4,5},{5,4},{6,7},{7,6},{8,9},{9,8},{10,11... | collective-permute-start | bytes 393224 | tf_op jit(solution)/shard_map/ppermute | solution.py:17
  98.7 11.4 %all-to-all-start.5 = ((bf16[16,2,2012]{2,1,0:T(2,128)(2,1)}), bf16[16,2,2012]{2,1,0:T(2,128)(2,1)S(1)}, u32[]{:S(2)}, u32[]{:S(2)}) async-start(bf16[16,2,2012]{2,1,0:T(2,128)(2,1)} %shard_map.99), calls=%async_computation.5 | async-start | bytes 262144 | tf_op jit(solution)/shard_map/all_to_all | solution.py:21

commit v6 on v5

--- a/solution.py
+++ b/solution.py
@@ -38,23 +38,46 @@
 
 HBM_SPEC = pl.BlockSpec(memory_space=pltpu.HBM)
 VMEM_SPEC = pl.BlockSpec(memory_space=pltpu.VMEM)
-
-
-def call(kernel, outs, *args, streamed=(), flops=0, scratch=(), room=0):
+SMEM_SPEC = pl.BlockSpec(memory_space=pltpu.SMEM)
+
+
+WINDOW = 6
+
+
+def call(kernel, outs, *args, streamed=(), kept=(), scalars=(), flops=0, scratch=(), room=0):
     size = sum(math.prod(a.shape) * a.dtype.itemsize for a in args)
-    args = [
-        pltpu.with_memory_space_constraint(a, pltpu.HBM) if i in streamed else a
-        for i, a in enumerate(args)
+    places = {i: pltpu.HBM for i in streamed} | {i: pltpu.VMEM for i in kept}
+    specs = [
+        HBM_SPEC if i in streamed else SMEM_SPEC if i in scalars else VMEM_SPEC
+        for i in range(len(args))
     ]
     return pl.pallas_call(
         kernel,
         out_shape=outs,
-        in_specs=[HBM_SPEC if i in streamed else VMEM_SPEC for i in range(len(args))],
+        in_specs=specs,
         out_specs=[VMEM_SPEC] * len(outs),
         scratch_shapes=list(scratch),
         compiler_params=pltpu.CompilerParams(vmem_limit_bytes=VMEM_BYTES + room),
         cost_estimate=pl.CostEstimate(flops=flops, bytes_accessed=size, transcendentals=0),
-    )(*args)
+    )(*[
+        pltpu.with_memory_space_constraint(a, places[i]) if i in places else a
+        for i, a in enumerate(args)
+    ])
+
+
+class Stream:
+    def __init__(self, copies):
+        self.copies = copies
+        self.done = 0
+        for copy in copies[:WINDOW]:
+            copy.start()
+
+    def wait(self, count):
+        while self.done < count:
+            self.copies[self.done].wait()
+            self.done += 1
+            if self.done + WINDOW <= len(self.copies):
+                self.copies[self.done + WINDOW - 1].start()
 
 
 def struct(shape, dtype):
@@ -102,108 +125,160 @@
     out_ref[...] = (math.sqrt(VOC) * (probs * (d_probs - mean))).astype(BF16)
 
 
+def valid_column(counts_ref, total):
+    requests = counts_ref.shape[0]
+    length = total // requests
+    position = lax.broadcasted_iota(jnp.int32, (total, 1), 0)
+    valid = jnp.zeros((total, 1), F32)
+    for r in range(requests):
+        inside = (position >= r * length) & (position < r * length + counts_ref[r])
+        valid = jnp.where(inside, 1.0, valid)
+    return valid, position // length
+
+
 def half_kernel(other, slices_ref, embed_ref, head_ref, out_ref, score_ref, table, sems):
     chips, _, own = out_ref.shape
+    part = embed_ref.shape[0]
+    cuts = sems.shape[0] // chips
     core = this_core()
     half = (1 - core) if other else core
+    rows = part // cuts
 
     def columns(j):
         return span((half * chips + j) * own, own)
 
-    def copy(j):
-        return pltpu.make_async_copy(embed_ref.at[:, columns(j)], table.at[j], sems.at[j])
-
-    for j in range(chips):
-        copy(j).start()
+    stream = Stream([
+        pltpu.make_async_copy(
+            embed_ref.at[pl.ds(i * rows, rows), columns(j)],
+            table.at[j, pl.ds(i * rows, rows)],
+            sems.at[j * cuts + i],
+        )
+        for j in range(chips)
+        for i in range(cuts)
+    ])
     slices = slices_ref[...]
     score = jnp.zeros(score_ref.shape, F32)
     for j in range(chips):
-        copy(j).wait()
+        stream.wait((j + 1) * cuts)
         part = jnp.dot(slices, table[j], preferred_element_type=F32)
         score += jnp.sum(part * head_ref[:, columns(j)].astype(F32), axis=-1, keepdims=True)
         out_ref[j] = part.astype(out_ref.dtype)
     score_ref[...] = score
 
 
-def hidden_kernel(
-    mine_ref, got_ref, gain_ref, gate_ref, up_ref, down_ref, valid_ref,
-    send_ref, keep_ref, score_ref, gate, up, a_ref, b_ref, sems,
+def down_kernel(head_ref, down_ref, out_ref, table, sems):
+    steps = sems.shape[0]
+    rows = down_ref.shape[0] // steps
+    stream = Stream([
+        pltpu.make_async_copy(
+            down_ref.at[pl.ds(i * rows, rows)], table.at[pl.ds(i * rows, rows)], sems.at[i]
+        )
+        for i in range(steps)
+    ])
+    head = jnp.broadcast_to(head_ref[...].astype(F32), (16, head_ref.shape[1])).astype(BF16)
+    contract = (((1,), (1,)), ((), ()))
+    for i in range(steps):
+        stream.wait(i + 1)
+        part = lax.dot_general(
+            head, table[i * rows : (i + 1) * rows], contract, preferred_element_type=F32
+        )
+        out_ref[:, i * rows : (i + 1) * rows] = part[:1]
+
+
+def forward_half(x_ref, gain_ref, gate_ref, up_ref, gate, up, sems, half, sums):
+    chips, _, own = x_ref.shape
+
+    def rows(j):
+        return span((half * chips + j) * own, own)
+
+    stream = Stream([
+        pltpu.make_async_copy(source.at[rows(j)], target.at[pl.ds(j * own, own)], sems.at[k, j])
+        for j in range(chips)
+        for k, (source, target) in enumerate(((gate_ref, gate), (up_ref, up)))
+    ])
+    a, b, squares = sums
+    scaled = []
+    for j in range(chips):
+        x = x_ref[j].astype(F32)
+        squares = squares + jnp.sum(x * x, axis=-1, keepdims=True)
+        scaled.append((x * gain_ref[:, rows(j)].astype(F32)).astype(BF16))
+    for j in range(chips):
+        r = slice(j * own, (j + 1) * own)
+        stream.wait(2 * (j + 1))
+        a = a + jnp.dot(scaled[j], gate[r], preferred_element_type=F32)
+        b = b + jnp.dot(scaled[j], up[r], preferred_element_type=F32)
+    return a, b, squares
+
+
+def backward_half(d_gate, d_up, gate, up, out_ref):
+    chips, _, own = out_ref.shape
+    contract = (((1,), (1,)), ((), ()))
+    for j in range(chips):
+        r = slice(j * own, (j + 1) * own)
+        part = lax.dot_general(d_gate, gate[r], contract, preferred_element_type=F32)
+        part += lax.dot_general(d_up, up[r], contract, preferred_element_type=F32)
+        out_ref[j] = part.astype(out_ref.dtype)
+
+
+def first_kernel(
+    x_ref, gain_ref, gate_ref, up_ref, a_ref, b_ref, squares_ref, gate, up, sems
 ):
-    chips, total, own = mine_ref.shape
-    width = 2 * chips * own
-    core = this_core()
-    order = [(mine_ref, core, j) for j in range(chips)] + [
-        (got_ref, 1 - core, j) for j in range(chips)
-    ]
-
-    def rows(half, j):
-        return span((half * chips + j) * own, own)
-
-    def copies(i):
-        _, half, j = order[i]
-        r = rows(half, j)
-        return (
-            pltpu.make_async_copy(gate_ref.at[r], gate.at[r], sems.at[0, i]),
-            pltpu.make_async_copy(up_ref.at[r], up.at[r], sems.at[1, i]),
-        )
-
-    for i in range(2 * chips):
-        for copy in copies(i):
-            copy.start()
-    squares = jnp.zeros((total, 1), F32)
-    for j in range(chips):
-        x, y = mine_ref[j].astype(F32), got_ref[j].astype(F32)
-        squares += jnp.sum(x * x + y * y, axis=-1, keepdims=True)
+    zeros = jnp.zeros(a_ref.shape, F32)
+    sums = (zeros, zeros, jnp.zeros(squares_ref.shape, F32))
+    sums = forward_half(x_ref, gain_ref, gate_ref, up_ref, gate, up, sems, this_core(), sums)
+    a_ref[...], b_ref[...], squares_ref[...] = sums
+
+
+def second_kernel(
+    x_ref, gain_ref, gate_ref, up_ref, a_ref, b_ref, squares_ref, down_ref, counts_ref,
+    send_ref, score_ref, d_gate_ref, d_up_ref, gate, up, sems,
+):
+    total = x_ref.shape[1]
+    width = gate_ref.shape[0]
+    sums = (a_ref[...], b_ref[...], squares_ref[...])
+    a, b, squares = forward_half(
+        x_ref, gain_ref, gate_ref, up_ref, gate, up, sems, 1 - this_core(), sums
+    )
     inv = lax.rsqrt(squares / width + 1e-05)
-    for i, (ref, half, j) in enumerate(order):
-        r = rows(half, j)
-        normed = (ref[j].astype(F32) * inv * gain_ref[:, r].astype(F32)).astype(BF16)
-        for copy in copies(i):
-            copy.wait()
-        a = jnp.dot(normed, gate[r], preferred_element_type=F32)
-        b = jnp.dot(normed, up[r], preferred_element_type=F32)
-        a_ref[...] = a_ref[...] + a if i else a
-        b_ref[...] = b_ref[...] + b if i else b
-    a, b = a_ref[...], b_ref[...]
+    a, b = a * inv, b * inv
     sigma = jax.nn.sigmoid(a)
     active = a * sigma
     down = down_ref[...]
     hidden = (active * b).astype(BF16).astype(F32)
     score_ref[...] = jnp.sum(hidden * down, axis=-1, keepdims=True)
-    d_hidden = valid_ref[...] * down
+    valid, _ = valid_column(counts_ref, total)
+    d_hidden = valid * down
     d_gate = (d_hidden * b * sigma * (1.0 + a * (1.0 - sigma))).astype(BF16)
     d_up = (d_hidden * active).astype(BF16)
-    contract = (((1,), (1,)), ((), ()))
-    for ref, half in ((send_ref, 1 - core), (keep_ref, core)):
-        for j in range(chips):
-            r = rows(half, j)
-            part = lax.dot_general(d_gate, gate[r], contract, preferred_element_type=F32)
-            part += lax.dot_general(d_up, up[r], contract, preferred_element_type=F32)
-            ref[j] = part.astype(ref.dtype)
+    d_gate_ref[...], d_up_ref[...] = d_gate, d_up
+    backward_half(d_gate, d_up, gate, up, send_ref)
+
+
+def third_kernel(d_gate_ref, d_up_ref, gate_ref, up_ref, keep_ref):
+    backward_half(d_gate_ref[...], d_up_ref[...], gate_ref, up_ref, keep_ref)
 
 
 def input_kernel(
-    mine_ref, got_ref, d_mine_ref, d_got_ref, gain_ref, head_ref, valid_ref,
-    score_a_ref, score_b_ref, score_c_ref, member_ref, embed_ref,
+    mine_ref, got_ref, d_mine_ref, d_got_ref, gain_ref, head_ref,
+    score_a_ref, score_b_ref, score_c_ref, counts_ref, embed_ref,
     out_ref, dx_ref, table, sems,
 ):
     chips, total, own = mine_ref.shape
     devices, per, _ = out_ref.shape
     voc = embed_ref.shape[0]
-    requests = member_ref.shape[1]
+    requests = counts_ref.shape[0]
     width = 2 * chips * own
     core = this_core()
     tile = 256
-    starts = [(i, min(tile, voc - i)) for i in range(0, voc, tile)]
-
-    def copy(i):
-        start, size = starts[i]
-        return pltpu.make_async_copy(
-            embed_ref.at[pl.ds(start, size)], table.at[pl.ds(start, size)], sems.at[i]
-        )
-
-    for i in range(len(starts)):
-        copy(i).start()
+    fine = 64
+    stream = Stream([
+        pltpu.make_async_copy(
+            embed_ref.at[pl.ds(i, min(fine, voc - i))],
+            table.at[pl.ds(i, min(fine, voc - i))],
+            sems.at[i // fine],
+        )
+        for i in range(0, voc, fine)
+    ])
     sources = ((mine_ref, d_mine_ref, core), (got_ref, d_got_ref, 1 - core))
     squares = jnp.zeros((total, 1), F32)
     dots = jnp.zeros((total, 1), F32)
@@ -215,7 +290,7 @@
             dots += jnp.sum(g * x, axis=-1, keepdims=True)
     inv = lax.rsqrt(squares / width + 1e-05)
     mean = dots / width
-    valid = valid_ref[...]
+    valid, request = valid_column(counts_ref, total)
     for x_ref, d_ref, half in sources:
         for j in range(chips):
             columns = span((half * chips + j) * own, own)
@@ -223,27 +298,27 @@
             g = d_ref[j].astype(F32) * gain_ref[:, columns].astype(F32)
             dx = inv * g - x * inv * inv * inv * mean
             dx_ref[:, columns] = (dx + valid * head_ref[:, columns].astype(F32)).astype(BF16)
-    score = score_a_ref[...] + score_b_ref[...] + score_c_ref[...]
-    value = jnp.sum(member_ref[...] * (valid * score), axis=0, keepdims=True)
+    score = valid * (score_a_ref[...] + score_b_ref[...] + score_c_ref[...])
+    member = request == lax.broadcasted_iota(jnp.int32, (total, requests), 1)
+    value = jnp.sum(jnp.where(member, score, 0.0), axis=0, keepdims=True)
     pieces = []
     for _ in range(3):
-        piece = value.astype(BF16)
+        piece = value.astype(BF16).astype(F32)
         pieces.append(piece)
-        value = value - piece.astype(F32)
+        value = value - piece
     for i, piece in enumerate(pieces):
         start = voc + i * requests
-        spread = jnp.broadcast_to(piece.astype(F32), (per, requests)).astype(BF16)
+        spread = jnp.broadcast_to(piece, (per, requests)).astype(BF16)
         for d in range(devices):
             out_ref[d, :, start : start + requests] = spread
     contract = (((1,), (1,)), ((), ()))
     dx = dx_ref[...]
-    for i, (start, size) in enumerate(starts):
-        copy(i).wait()
-        part = lax.dot_general(
-            dx, table[start : start + size, :], contract, preferred_element_type=F32
-        )
+    for start in range(0, voc, tile):
+        end = min(start + tile, voc)
+        stream.wait(-(-end // fine))
+        part = lax.dot_general(dx, table[start:end, :], contract, preferred_element_type=F32)
         for d in range(devices):
-            out_ref[d, :, start : start + size] = part[d * per : (d + 1) * per].astype(BF16)
+            out_ref[d, :, start:end] = part[d * per : (d + 1) * per].astype(BF16)
 
 
 def swap_sum(send, keep, devices):
@@ -252,8 +327,7 @@
 
 def sum_and_gather(half, devices):
     total = jnp.sum(exchange_chips(half, devices).astype(F32), axis=0).astype(BF16)
-    held = exchange_chips(jnp.broadcast_to(total[None], half.shape), devices)
-    return held, swap_cores(held, devices)
+    return exchange_chips(jnp.broadcast_to(total[None], half.shape), devices)
 
 
 def pick(blocks, index):
@@ -320,7 +394,6 @@
     total = rows * devices
     request_len = total // requests
     tiled = own % 128 == 0 and hidden % 128 == 0 and total % 16 == 0 and part % 16 == 0
-    head32 = head.astype(F32)
     head_row, gain_row = head.reshape(1, width), norm_gain.reshape(1, width)
     if tiled:
         column = struct((rows, 1), F32)
@@ -331,18 +404,12 @@
         probs32 = jax.nn.softmax(logits.astype(F32), axis=-1)
         blocked = probs32.astype(BF16).reshape(rows, devices, part).transpose(1, 0, 2)
     slices = exchange(blocked).reshape(total, part)
-    down_head = jnp.sum(w_down.astype(F32) * head32[None, :], axis=-1)
-    position = jnp.arange(total, dtype=jnp.int32)
-    member = (position // request_len)[:, None] == jnp.arange(requests, dtype=jnp.int32)[None, :]
-    limit = jnp.sum(jnp.where(member, counts[None, :], 0), axis=-1, keepdims=True)
-    valid = (position[:, None] % request_len < limit).astype(F32)
-    member = member.astype(F32)
-    down_row = down_head.reshape(1, hidden)
     column = struct((total, 1), F32)
     half = (chips, total, own)
     flops = total * part * width
     if tiled:
-        table = [pltpu.VMEM((chips, part, own), BF16), pltpu.SemaphoreType.DMA((chips,))]
+        cuts = 2 if part % 32 == 0 else 1
+        table = [pltpu.VMEM((chips, part, own), BF16), pltpu.SemaphoreType.DMA((cuts * chips,))]
         args = dict(streamed=(1,), flops=flops, scratch=table, room=part * width)
         send, score_a = call(
             functools.partial(half_kernel, True), [struct(half, BF16), column],
@@ -354,37 +421,62 @@
         )
     else:
         send, keep, score_a = plain_half(slices, embed, head_row, devices)
-        score_b = jnp.zeros_like(score_a)
-    x_mine, x_got = sum_and_gather(swap_sum(send, keep, devices), devices)
+    x_mine = sum_and_gather(swap_sum(send, keep, devices), devices)
+    x_got = swap_cores(x_mine, devices)
     if tiled:
-        wide, weight = pltpu.VMEM((total, hidden), F32), pltpu.VMEM((width, hidden), BF16)
-        send, keep, score_c = call(
-            hidden_kernel, [struct(half, BF16), struct(half, F32), column],
-            x_mine, x_got, gain_row, w_gate, w_up, down_row, valid,
-            streamed=(3, 4), flops=8 * total * hidden * width, room=4 * width * hidden,
-            scratch=(weight, weight, wide, wide, pltpu.SemaphoreType.DMA((2, devices))),
+        steps = hidden // 128
+        (down_row,) = call(
+            down_kernel, [struct((1, hidden), F32)], head_row, w_down,
+            streamed=(1,), flops=2 * hidden * width, room=2 * hidden * width,
+            scratch=(pltpu.VMEM((hidden, width), BF16), pltpu.SemaphoreType.DMA((steps,))),
+        )
+        wide = struct((total, hidden), F32)
+        weight = (width // 2, hidden)
+        sems = pltpu.SemaphoreType.DMA((2, chips))
+        args = dict(streamed=(2, 3), flops=2 * total * hidden * width, room=2 * width * hidden)
+        a, b, squares, gate, up = call(
+            first_kernel,
+            [wide, wide, column, pltpu.VMEM(weight, BF16), pltpu.VMEM(weight, BF16)],
+            x_mine, gain_row, w_gate, w_up, scratch=(sems,), **args,
+        )
+        narrow = struct((total, hidden), BF16)
+        send, score_c, d_gate, d_up = call(
+            second_kernel, [struct(half, BF16), column, narrow, narrow],
+            x_got, gain_row, w_gate, w_up, a, b, squares, down_row, counts,
+            scratch=(pltpu.VMEM(weight, BF16), pltpu.VMEM(weight, BF16), sems),
+            scalars=(8,), **args,
+        )
+        (keep,) = call(
+            third_kernel, [struct(half, F32)], d_gate, d_up, gate, up,
+            kept=(2, 3), flops=2 * total * hidden * width,
         )
     else:
+        down_row = jnp.sum(w_down.astype(F32) * head.astype(F32)[None, :], axis=-1)[None]
+        position = jnp.arange(total, dtype=jnp.int32)[:, None]
+        member = position // request_len == jnp.arange(requests, dtype=jnp.int32)[None, :]
+        limit = jnp.sum(jnp.where(member, counts[None, :], 0), axis=-1, keepdims=True)
+        valid = (position % request_len < limit).astype(F32)
         send, keep, score_c = plain_hidden(
             x_mine, x_got, gain_row, w_gate, w_up, down_row, valid, devices
         )
-    d_mine, d_got = sum_and_gather(swap_sum(send, keep, devices), devices)
-    sources = (x_mine, x_got, d_mine, d_got, gain_row, head_row, valid)
+    d_mine = sum_and_gather(swap_sum(send, keep, devices), devices)
+    d_got = swap_cores(d_mine, devices)
+    sources = (x_mine, x_got, d_mine, d_got, gain_row, head_row)
     padded = part + 3 * requests
     if tiled:
         (d_slices,) = call(
             input_kernel, [struct((devices, rows, padded), BF16)],
-            *sources, score_a, score_b, score_c, member, embed,
-            streamed=(11,), flops=2 * flops, room=2 * part * width,
+            *sources, score_a, score_b, score_c, counts, embed,
+            scalars=(9,), streamed=(10,), flops=2 * flops, room=2 * part * width,
             scratch=(
                 pltpu.VMEM((total, width), BF16), pltpu.VMEM((part, width), BF16),
-                pltpu.SemaphoreType.DMA((-(-part // 256),)),
+                pltpu.SemaphoreType.DMA((-(-part // 64),)),
             ),
         )
     else:
-        d_slices = plain_input(*sources, embed).reshape(devices, rows, part)
-        score = valid * (score_a + score_b + score_c)
-        extra = split3(jnp.sum(member * score, axis=0)).reshape(1, 1, requests * 3)
+        d_slices = plain_input(*sources, valid, embed).reshape(devices, rows, part)
+        score = jnp.where(member, valid * (score_a + score_c), 0.0)
+        extra = split3(jnp.sum(score, axis=0)).reshape(1, 1, requests * 3)
         extra = jnp.broadcast_to(extra, (devices, rows, requests * 3))
         d_slices = jnp.concatenate([d_slices, extra], axis=-1)
     back = exchange(d_slices)

time: 112 us -> 116 us (1.036)
  blocking collectives: 20.6 us -> 39.8 us
  waiting for transfers between devices: 29.2 us -> 16.5 us
  Pallas kernels: 34.9 us -> 44.5 us
  starting transfers between devices: 17.8 us -> 11.6 us
  other arithmetic: 5.65 us -> 0.12 us
    all_to_all x2 -> x4, blocking collectives: 20.6 us -> 39.8 us  [exchange_chips(): lax.all_to_all(blocks, 'dp', split_axis=0, concat_axis=0, axis_index_grou...]
    all_to_all x2 -> x0, waiting for transfers between devices: 10.2 us -> none  [exchange_chips(): lax.all_to_all(blocks, 'dp', split_axis=0, concat_axis=0, axis_index_grou...]
    pallas_call x6 -> x9, Pallas kernels: 34.9 us -> 44.5 us  [call(): pl.pallas_call(kernel, out_shape=outs, in_specs=specs, out_specs=[VMEM_SP...]
    all_to_all x2 -> x0, starting transfers between devices: 6.74 us -> none  [exchange_chips(): lax.all_to_all(blocks, 'dp', split_axis=0, concat_axis=0, axis_index_grou...]
    reduce_sum x2 -> x0, other arithmetic: 4.8 us -> none  [the longest x1 4.62 us: body(): down_head = jnp.sum(w_down.astype(F32) * head32[None, :], axis=-1)]
    ppermute x4, waiting for transfers between devices: 3.9 us -> 1.35 us  [swap_cores(): return lax.ppermute(value, 'dp', [(i, i ^ 1) for i in range(devices)])]
  transfers between devices with their start and end apart: 8 -> 6, of which waited for: 7 -> 3; matrix products, arithmetic and copies ran while one was open for 5% -> 1% of each run, Pallas kernels for 4% -> 15%
where the time goes in v6:
time: 116 us; the launch traced here: 115 us
  Pallas kernels  44.5 us (38%)
  blocking collectives  39.8 us (34%)
  waiting for transfers between devices  16.5 us (14%)
  starting transfers between devices  11.6 us (10%)
  local copies, waits for them, and re-layouts  1.72 us (1%)
    pallas_call x9, Pallas kernels, call(): pl.pallas_call(kernel, out_shape=outs, in_specs=specs, out_specs=[VMEM_SP...  44.5 us
    all_to_all x4, blocking collectives, exchange_chips(): lax.all_to_all(blocks, 'dp', split_axis=0, concat_axis=0, axis_index_grou...  39.8 us
    all_to_all x2, waiting for transfers between devices, exchange(): return lax.all_to_all(blocks, 'dp', split_axis=0, concat_axis=0, tiled=True)  15.1 us
    all_to_all x2, starting transfers between devices, exchange(): return lax.all_to_all(blocks, 'dp', split_axis=0, concat_axis=0, tiled=True)  10.9 us
  transfers between devices with their start and end apart: 6, of which 3 were waited for; matrix products, arithmetic and copies ran while one was open for 1% of the time, Pallas kernels for 15%

profile of v6, /device:TPU:0, one launch (start us, length us, event | category | flops | bytes accessed | tf_op | source)
XLA Modules:
  0.0 115.0 jit_solution(1571808866056815745)
XLA Ops:
  0.6 0.0 copy-start
  0.6 0.9 copy-done
  1.5 1.4 %shard_map.95 = (bf16[16,2,2000]{2,1,0:T(2,128)(2,1)}, f32[2,1]{1,0:T(2,128)S(1)}, f32[2,1]{1,0:T(2,128)S(1)}) custom-call(bf16[2,32000]{1,0:T(2,128)(2,1)S(1)} %copy-done), custom_call_target="tpu_custom_call" | custom-call | bytes 128000 | tf_op jit(solution)/shard_map/pallas_call | solution.py:54
  3.0 7.4 %all-to-all-start = ((bf16[16,2,2000]{2,1,0:T(2,128)(2,1)}), bf16[16,2,2000]{2,1,0:T(2,128)(2,1)S(1)}, u32[]{:S(2)}, u32[]{:S(2)}) async-start(bf16[16,2,2000]{2,1,0:T(2,128)(2,1)} %get-tuple-element.22), calls=%async_computation | async-start | bytes 262144 | tf_op jit(solution)/shard_map/all_to_all | solution.py:21
  10.4 0.7 reshape.22.head_ref
  11.1 7.2 %all-to-all-done = bf16[16,2,2000]{2,1,0:T(2,128)(2,1)S(1)} async-done(((bf16[16,2,2000]{2,1,0:T(2,128)(2,1)}), bf16[16,2,2000]{2,1,0:T(2,128)(2,1)S(1)}, u32[]{:S(2)}, u32[]{:S(2)}) %all-to-all-start) | async-done | bytes 128032 | tf_op jit(solution)/shard_map/all_to_all | solution.py:21
  18.3 0.1 reshape.21.slices_ref
  18.4 5.0 %shard_map.97 = (bf16[8,32,256]{2,1,0:T(8,128)(2,1)S(1)}, f32[32,1]{1,0:T(8,128)S(1)}) custom-call(bf16[32,2000]{1,0:T(8,128)(2,1)S(1)} %reshape.21.slices_ref, bf16[2000,4096]{1,0:T(8,128)(2,1)} %embed_ref.5, bf16[1,4096]{1,0:T(2,128)(2,1)S(1)} %reshape.22.head_ref), custom_call_target="tpu_custom_call" | custom-call | flops 262144000 | bytes 16520192 | tf_op jit(solution)/shard_map/pallas_call | solution.py:54
  23.4 0.0 copy-start.3
  23.4 0.1 collective-permute-start
  23.5 5.0 %shard_map.96 = (f32[8,32,256]{2,1,0:T(8,128)S(1)}, f32[32,1]{1,0:T(8,128)S(1)}) custom-call(bf16[32,2000]{1,0:T(8,128)(2,1)S(1)} %reshape.21.slices_ref, bf16[2000,4096]{1,0:T(8,128)(2,1)} %embed_ref.5, bf16[1,4096]{1,0:T(2,128)(2,1)S(1)} %reshape.22.head_ref), custom_call_target="tpu_custom_call" | custom-call | flops 262144000 | bytes 16520192 | tf_op jit(solution)/shard_map/pallas_call | solution.py:54
  28.5 0.0 collective-permute-done
  28.5 10.3 %all_to_all.30 = bf16[8,32,256]{2,1,0:T(8,128)(2,1)S(1)} all-to-all(bf16[8,32,256]{2,1,0:T(8,128)(2,1)S(1)} %add_convert_fusion.1), channel_id=1, replica_groups={{0,2,4,6,8,10,12,14},{1,3,5,7,9,11,13,15},{16,18,20,22,24,26,28,30},{17..., dimensions={0} | all-to-all | bytes 262144 | tf_op jit(solution)/shard_map/all_to_all | solution.py:26
  38.9 9.8 %all_to_all.31.x_ref.mine_ref = bf16[8,32,256]{2,1,0:T(8,128)(2,1)S(1)} all-to-all(bf16[8,32,256]{2,1,0:T(8,128)(2,1)S(1)} %broadcast_in_dim.4), channel_id=1, replica_groups={{0,2,4,6,8,10,12,14},{1,3,5,7,9,11,13,15},{16,18,20,22,24,26,28,30},{17..., dimensions={0} | all-to-all | bytes 262144 | tf_op jit(solution)/shard_map/all_to_all | solution.py:26
  48.7 0.0 collective-permute-start.1
  48.7 5.6 %shard_map.99.down_ref = f32[1,896]{1,0:T(1,128)S(1)} custom-call(bf16[1,4096]{1,0:T(2,128)(2,1)S(1)} %reshape.22.head_ref, bf16[896,4096]{1,0:T(8,128)(2,1)} %down_ref.1), custom_call_target="tpu_custom_call" | custom-call | flops 7340032 | bytes 7348224 | tf_op jit(solution)/shard_map/pallas_call | solution.py:54
  54.4 0.0 copy-start.2
  54.4 4.3 %shard_map.98 = (f32[32,896]{1,0:T(8,128)S(1)}, f32[32,896]{1,0:T(8,128)S(1)}, f32[32,1]{1,0:T(8,128)S(1)}, bf16[2048,896]{1,0:T(8,128)(2,1)S(1)}, bf16[2048,896]{1,0:T(8,128)(2,1)S(1)}) custom-call(bf16[8,32,256]{2,1,0:T(8,128)(2,1)S(1)} %all_to_all.31.x_ref.mine_ref, bf16[1,4096]{1,0:T(2,128)(2,1)S(1)} %reshape.23.gain_ref, bf16[4096,896]{1,0:T(8,128)(2,1)} %gate_ref.3, ...), custom_call_target="tpu_custom_call" | custom-call | flops 234881024 | bytes 14819328 | tf_op jit(solution)/shard_map/pallas_call | solution.py:54
  58.6 0.0 collective-permute-done.1.x_ref.got_ref
  58.7 0.0 copy-done.2
  58.7 7.0 %shard_map.100 = (bf16[8,32,256]{2,1,0:T(8,128)(2,1)S(1)}, f32[32,1]{1,0:T(8,128)S(1)}, bf16[32,896]{1,0:T(8,128)(2,1)S(1)}, bf16[32,896]{1,0:T(8,128)(2,1)S(1)}) custom-call(bf16[8,32,256]{2,1,0:T(8,128)(2,1)S(1)} %collective-permute-done.1.x_ref.got_ref, bf16[1,4096]{1,0:T(2,128)(2,1)S(1)} %reshape.23.gain_ref, bf16[4096,896]{1,0:T(8,128)(2,1)} %gate_ref.3, ...), custom_call_target="tpu_custom_call" | custom-call | flops 234881024 | bytes 15052432 | tf_op jit(solution)/shard_map/pallas_call | solution.py:54
  65.6 0.6 collective-permute-start.2
  66.2 2.2 %shard_map.101 = f32[8,32,256]{2,1,0:T(8,128)S(1)} custom-call(bf16[32,896]{1,0:T(8,128)(2,1)S(1)} %get-tuple-element.28.d_gate_ref, bf16[32,896]{1,0:T(8,128)(2,1)S(1)} %get-tuple-element.29.d_up_ref, bf16[2048,896]{1,0:T(8,128)(2,1)S(1)} %get-tuple-element.30.gate_ref, bf16[2048,896]{1,0:T(8,128)(2,1)S(1)} %get-tuple-element.31.up_ref), custom_call_target="tpu_custom_call" | custom-call | flops 234881024 | bytes 7454720 | tf_op jit(solution)/shard_map/pallas_call | solution.py:54
  68.4 0.0 collective-permute-done.2
  68.5 9.8 %all_to_all.32 = bf16[8,32,256]{2,1,0:T(8,128)(2,1)S(1)} all-to-all(bf16[8,32,256]{2,1,0:T(8,128)(2,1)S(1)} %add_convert_fusion), channel_id=1, replica_groups={{0,2,4,6,8,10,12,14},{1,3,5,7,9,11,13,15},{16,18,20,22,24,26,28,30},{17..., dimensions={0} | all-to-all | bytes 262144 | tf_op jit(solution)/shard_map/all_to_all | solution.py:26
  78.4 9.8 %all_to_all.33.d_mine_ref = bf16[8,32,256]{2,1,0:T(8,128)(2,1)S(1)} all-to-all(bf16[8,32,256]{2,1,0:T(8,128)(2,1)S(1)} %broadcast_in_dim.5), channel_id=1, replica_groups={{0,2,4,6,8,10,12,14},{1,3,5,7,9,11,13,15},{16,18,20,22,24,26,28,30},{17..., dimensions={0} | all-to-all | bytes 262144 | tf_op jit(solution)/shard_map/all_to_all | solution.py:26
  88.2 0.0 collective-permute-start.3
  88.2 1.3 %collective-permute-done.3.d_got_ref = bf16[8,32,256]{2,1,0:T(8,128)(2,1)S(1)} collective-permute-done((bf16[8,32,256]{2,1,0:T(8,128)(2,1)S(1)}, bf16[8,32,256]{2,1,0:T(8,128)(2,1)S(1)}, u32[]{:S(2)}, u32[]{:S(2)}) %collective-permute-start.3) | collective-permute-done | bytes 131104 | tf_op jit(solution)/shard_map/ppermute | solution.py:17
  89.6 12.8 %shard_map.102 = bf16[16,2,2012]{2,1,0:T(2,128)(2,1)} custom-call(bf16[8,32,256]{2,1,0:T(8,128)(2,1)S(1)} %all_to_all.31.x_ref.mine_ref, bf16[8,32,256]{2,1,0:T(8,128)(2,1)S(1)} %collective-permute-done.1.x_ref.got_ref, bf16[8,32,256]{2,1,0:T(8,128)(2,1)S(1)} %all_to_all.33.d_mine_ref, bf16[8,32,256]{2,1,0:T(8,128)(2,1)S(1)} %collective-permute-done.3.d_got_ref, ...), custom_call_target="tpu_custom_call" | custom-call | flops 524288000 | bytes 16925072 | tf_op jit(solution)/shard_map/pallas_call | solution.py:54
  102.4 3.5 %all-to-all-start.5 = ((bf16[16,2,2012]{2,1,0:T(2,128)(2,1)}), bf16[16,2,2012]{2,1,0:T(2,128)(2,1)S(1)}, u32[]{:S(2)}, u32[]{:S(2)}) async-start(bf16[16,2,2012]{2,1,0:T(2,128)(2,1)} %shard_map.102), calls=%async_computation.5 | async-start | bytes 262144 | tf_op jit(solution)/shard_map/all_to_all | solution.py:21
  105.9 7.9 %all-to-all-done.5.back_ref = bf16[16,2,2012]{2,1,0:T(2,128)(2,1)S(1)} async-done(((bf16[16,2,2012]{2,1,0:T(2,128)(2,1)}), bf16[16,2,2012]{2,1,0:T(2,128)(2,1)S(1)}, u32[]{:S(2)}, u32[]{:S(2)}) %all-to-all-start.5) | async-done | bytes 128800 | tf_op jit(solution)/shard_map/all_to_all | solution.py:21
  113.8 1.2 %shard_map.103 = (bf16[2,32000]{1,0:T(2,128)(2,1)}, f32[1,4]{1,0:T(1,128)}) custom-call(bf16[2,32000]{1,0:T(2,128)(2,1)S(1)} %copy-done.1, f32[2,1]{1,0:T(2,128)S(1)} %get-tuple-element.20.top_ref, f32[2,1]{1,0:T(2,128)S(1)} %get-tuple-element.21.scale_ref, bf16[16,2,2012]{2,1,0:T(2,128)(2,1)S(1)} %all-to-all-done.5.back_ref, ...), custom_call_target="tpu_custom_call" | custom-call | bytes 256800 | tf_op jit(solution)/shard_map/pallas_call | solution.py:54
  (11 shorter events, 0.2 us)
Async XLA Ops:
  0.6 0.9 copy-start
  3.0 15.3 %all-to-all-start = ((bf16[16,2,2000]{2,1,0:T(2,128)(2,1)}), bf16[16,2,2000]{2,1,0:T(2,128)(2,1)S(1)}, u32[]{:S(2)}, u32[]{:S(2)}) async-start(bf16[16,2,2000]{2,1,0:T(2,128)(2,1)} %get-tuple-element.22), calls=%async_computation | async-start | bytes 262144 | tf_op jit(solution)/shard_map/all_to_all | solution.py:21
  23.4 25.3 %copy-start.3 = (bf16[4096]{0:T(1024)(128)(2,1)S(1)}, bf16[4096]{0:T(1024)(128)(2,1)}, u32[]{:S(2)}) copy-start(bf16[4096]{0:T(1024)(128)(2,1)} %param.10) | copy-start | bytes 24580
  23.4 5.1 %collective-permute-start = (bf16[8,32,256]{2,1,0:T(8,128)(2,1)S(1)}, bf16[8,32,256]{2,1,0:T(8,128)(2,1)S(1)}, u32[]{:S(2)}, u32[]{:S(2)}) collective-permute-start(bf16[8,32,256]{2,1,0:T(8,128)(2,1)S(1)} %get-tuple-element.24), channel_id=1, source_target_pairs={{0,1},{1,0},{2,3},{3,2},{4,5},{5,4},{6,7},{7,6},{8,9},{9,8},{10,11... | collective-permute-start | bytes 393224 | tf_op jit(solution)/shard_map/ppermute | solution.py:17
  48.7 9.9 %collective-permute-start.1 = (bf16[8,32,256]{2,1,0:T(8,128)(2,1)S(1)}, bf16[8,32,256]{2,1,0:T(8,128)(2,1)S(1)}, u32[]{:S(2)}, u32[]{:S(2)}) collective-permute-start(bf16[8,32,256]{2,1,0:T(8,128)(2,1)S(1)} %all_to_all.31.x_ref.mine_ref), channel_id=1, source_target_pairs={{0,1},{1,0},{2,3},{3,2},{4,5},{5,4},{6,7},{7,6},{8,9},{9,8},{10,11... | collective-permute-start | bytes 393224 | tf_op jit(solution)/shard_map/ppermute | solution.py:17
  54.4 4.3 %copy-start.2 = (s32[4]{0:T(128)S(1)}, s32[4]{0:T(128)}, u32[]{:S(2)}) copy-start(s32[4]{0:T(128)} %counts_ref.3) | copy-start | bytes 52
  65.6 2.8 %collective-permute-start.2 = (bf16[8,32,256]{2,1,0:T(8,128)(2,1)S(1)}, bf16[8,32,256]{2,1,0:T(8,128)(2,1)S(1)}, u32[]{:S(2)}, u32[]{:S(2)}) collective-permute-start(bf16[8,32,256]{2,1,0:T(8,128)(2,1)S(1)} %get-tuple-element.32), channel_id=1, source_target_pairs={{0,1},{1,0},{2,3},{3,2},{4,5},{5,4},{6,7},{7,6},{8,9},{9,8},{10,11... | collective-permute-start | bytes 393224 | tf_op jit(solution)/shard_map/ppermute | solution.py:17
  88.2 1.3 %collective-permute-start.3 = (bf16[8,32,256]{2,1,0:T(8,128)(2,1)S(1)}, bf16[8,32,256]{2,1,0:T(8,128)(2,1)S(1)}, u32[]{:S(2)}, u32[]{:S(2)}) collective-permute-start(bf16[8,32,256]{2,1,0:T(8,128)(2,1)S(1)} %all_to_all.33.d_mine_ref), channel_id=1, source_target_pairs={{0,1},{1,0},{2,3},{3,2},{4,5},{5,4},{6,7},{7,6},{8,9},{9,8},{10,11... | collective-permute-start | bytes 393224 | tf_op jit(solution)/shard_map/ppermute | solution.py:17
  89.6 24.2 %copy-start.1 = (bf16[2,32000]{1,0:T(2,128)(2,1)S(1)}, bf16[2,32000]{1,0:T(2,128)(2,1)}, u32[]{:S(2)}) copy-start(bf16[2,32000]{1,0:T(2,128)(2,1)} %logits_ref.3) | copy-start | bytes 384004
  102.4 11.4 %all-to-all-start.5 = ((bf16[16,2,2012]{2,1,0:T(2,128)(2,1)}), bf16[16,2,2012]{2,1,0:T(2,128)(2,1)S(1)}, u32[]{:S(2)}, u32[]{:S(2)}) async-start(bf16[16,2,2012]{2,1,0:T(2,128)(2,1)} %shard_map.102), calls=%async_computation.5 | async-start | bytes 262144 | tf_op jit(solution)/shard_map/all_to_all | solution.py:21

commit v7 on v6

--- a/solution.py
+++ b/solution.py
@@ -41,7 +41,7 @@
 SMEM_SPEC = pl.BlockSpec(memory_space=pltpu.SMEM)
 
 
-WINDOW = 6
+WINDOW = 128
 
 
 def call(kernel, outs, *args, streamed=(), kept=(), scalars=(), flops=0, scratch=(), room=0):
@@ -136,10 +136,13 @@
     return valid, position // length
 
 
-def half_kernel(other, slices_ref, embed_ref, head_ref, out_ref, score_ref, table, sems):
+def half_kernel(
+    other, slices_ref, embed_ref, head_ref, after_ref, out_ref, score_ref, table, sems
+):
     chips, _, own = out_ref.shape
     part = embed_ref.shape[0]
     cuts = sems.shape[0] // chips
+    del after_ref
     core = this_core()
     half = (1 - core) if other else core
     rows = part // cuts
@@ -166,7 +169,8 @@
     score_ref[...] = score
 
 
-def down_kernel(head_ref, down_ref, out_ref, table, sems):
+def down_kernel(head_ref, down_ref, after_ref, out_ref, table, sems):
+    del after_ref
     steps = sems.shape[0]
     rows = down_ref.shape[0] // steps
     stream = Stream([
@@ -270,7 +274,7 @@
     width = 2 * chips * own
     core = this_core()
     tile = 256
-    fine = 64
+    fine = 32
     stream = Stream([
         pltpu.make_async_copy(
             embed_ref.at[pl.ds(i, min(fine, voc - i))],
@@ -408,28 +412,28 @@
     half = (chips, total, own)
     flops = total * part * width
     if tiled:
-        cuts = 2 if part % 32 == 0 else 1
+        steps = hidden // 128
+        (down_row,) = call(
+            down_kernel, [struct((1, hidden), F32)], head_row, w_down, blocked,
+            streamed=(1,), flops=2 * hidden * width, room=2 * hidden * width,
+            scratch=(pltpu.VMEM((hidden, width), BF16), pltpu.SemaphoreType.DMA((steps,))),
+        )
+        cuts = 5 if part % 80 == 0 else 1
         table = [pltpu.VMEM((chips, part, own), BF16), pltpu.SemaphoreType.DMA((cuts * chips,))]
         args = dict(streamed=(1,), flops=flops, scratch=table, room=part * width)
         send, score_a = call(
             functools.partial(half_kernel, True), [struct(half, BF16), column],
-            slices, embed, head_row, **args,
+            slices, embed, head_row, down_row, **args,
         )
         keep, score_b = call(
             functools.partial(half_kernel, False), [struct(half, F32), column],
-            slices, embed, head_row, **args,
+            slices, embed, head_row, down_row, **args,
         )
     else:
         send, keep, score_a = plain_half(slices, embed, head_row, devices)
     x_mine = sum_and_gather(swap_sum(send, keep, devices), devices)
     x_got = swap_cores(x_mine, devices)
     if tiled:
-        steps = hidden // 128
-        (down_row,) = call(
-            down_kernel, [struct((1, hidden), F32)], head_row, w_down,
-            streamed=(1,), flops=2 * hidden * width, room=2 * hidden * width,
-            scratch=(pltpu.VMEM((hidden, width), BF16), pltpu.SemaphoreType.DMA((steps,))),
-        )
         wide = struct((total, hidden), F32)
         weight = (width // 2, hidden)
         sems = pltpu.SemaphoreType.DMA((2, chips))
@@ -470,7 +474,7 @@
             scalars=(9,), streamed=(10,), flops=2 * flops, room=2 * part * width,
             scratch=(
                 pltpu.VMEM((total, width), BF16), pltpu.VMEM((part, width), BF16),
-                pltpu.SemaphoreType.DMA((-(-part // 64),)),
+                pltpu.SemaphoreType.DMA((-(-part // 32),)),
             ),
         )
     else:

time: 116 us -> 112 us (0.966)
  waiting for transfers between devices: 16.5 us -> 9.93 us
  blocking collectives: 39.8 us -> 42.2 us
    all_to_all x2, waiting for transfers between devices: 15.1 us -> 8.58 us  [exchange(): return lax.all_to_all(blocks, 'dp', split_axis=0, concat_axis=0, tiled=True)]
    all_to_all x4, blocking collectives: 39.8 us -> 42.2 us  [exchange_chips(): lax.all_to_all(blocks, 'dp', split_axis=0, concat_axis=0, axis_index_grou...]
  transfers between devices with their start and end apart: 6 -> 6, of which waited for: 3 -> 3; matrix products, arithmetic and copies ran while one was open for 1% -> 1% of each run, Pallas kernels for 15% -> 16%
where the time goes in v7:
time: 112 us; the launch traced here: 111 us
  Pallas kernels  44.8 us (40%)
  blocking collectives  42.2 us (38%)
  starting transfers between devices  11.6 us (10%)
  waiting for transfers between devices  9.93 us (9%)
  local copies, waits for them, and re-layouts  1.72 us (2%)
    pallas_call x9, Pallas kernels, call(): pl.pallas_call(kernel, out_shape=outs, in_specs=specs, out_specs=[VMEM_SP...  44.8 us
    all_to_all x4, blocking collectives, exchange_chips(): lax.all_to_all(blocks, 'dp', split_axis=0, concat_axis=0, axis_index_grou...  42.2 us
    all_to_all x2, starting transfers between devices, exchange(): return lax.all_to_all(blocks, 'dp', split_axis=0, concat_axis=0, tiled=True)  10.9 us
    all_to_all x2, waiting for transfers between devices, exchange(): return lax.all_to_all(blocks, 'dp', split_axis=0, concat_axis=0, tiled=True)  8.58 us
  transfers between devices with their start and end apart: 6, of which 3 were waited for; matrix products, arithmetic and copies ran while one was open for 1% of the time, Pallas kernels for 16%

profile of v7, /device:TPU:0, one launch (start us, length us, event | category | flops | bytes accessed | tf_op | source)
XLA Modules:
  0.0 111.2 jit_solution(6381666777697061506)
XLA Ops:
  0.6 0.0 copy-start
  0.6 0.9 copy-done
  1.5 1.4 %shard_map.95 = (bf16[16,2,2000]{2,1,0:T(2,128)(2,1)}, f32[2,1]{1,0:T(2,128)S(1)}, f32[2,1]{1,0:T(2,128)S(1)}) custom-call(bf16[2,32000]{1,0:T(2,128)(2,1)S(1)} %copy-done), custom_call_target="tpu_custom_call" | custom-call | bytes 128000 | tf_op jit(solution)/shard_map/pallas_call | solution.py:54
  3.0 7.4 %all-to-all-start = ((bf16[16,2,2000]{2,1,0:T(2,128)(2,1)}), bf16[16,2,2000]{2,1,0:T(2,128)(2,1)S(1)}, u32[]{:S(2)}, u32[]{:S(2)}) async-start(bf16[16,2,2000]{2,1,0:T(2,128)(2,1)} %get-tuple-element.22.after_ref), calls=%async_computation | async-start | bytes 262144 | tf_op jit(solution)/shard_map/all_to_all | solution.py:21
  10.4 0.7 reshape.22.head_ref
  11.1 6.5 %shard_map.96.after_ref.down_ref = f32[1,896]{1,0:T(1,128)S(1)} custom-call(bf16[1,4096]{1,0:T(2,128)(2,1)S(1)} %reshape.22.head_ref, bf16[896,4096]{1,0:T(8,128)(2,1)} %down_ref.1, bf16[16,2,2000]{2,1,0:T(2,128)(2,1)} %get-tuple-element.22.after_ref), custom_call_target="tpu_custom_call" | custom-call | flops 7340032 | bytes 7476224 | tf_op jit(solution)/shard_map/pallas_call | solution.py:54
  17.6 0.7 all-to-all-done
  18.3 0.1 reshape.21.slices_ref
  18.4 5.4 %shard_map.98 = (bf16[8,32,256]{2,1,0:T(8,128)(2,1)S(1)}, f32[32,1]{1,0:T(8,128)S(1)}) custom-call(bf16[32,2000]{1,0:T(8,128)(2,1)S(1)} %reshape.21.slices_ref, bf16[2000,4096]{1,0:T(8,128)(2,1)} %embed_ref.5, bf16[1,4096]{1,0:T(2,128)(2,1)S(1)} %reshape.22.head_ref, f32[1,896]{1,0:T(1,128)S(1)} %shard_map.96.after_ref.down_ref), custom_call_target="tpu_custom_call" | custom-call | flops 262144000 | bytes 16523776 | tf_op jit(solution)/shard_map/pallas_call | solution.py:54
  23.8 0.0 copy-start.3
  23.8 0.1 collective-permute-start
  23.9 5.4 %shard_map.97 = (f32[8,32,256]{2,1,0:T(8,128)S(1)}, f32[32,1]{1,0:T(8,128)S(1)}) custom-call(bf16[32,2000]{1,0:T(8,128)(2,1)S(1)} %reshape.21.slices_ref, bf16[2000,4096]{1,0:T(8,128)(2,1)} %embed_ref.5, bf16[1,4096]{1,0:T(2,128)(2,1)S(1)} %reshape.22.head_ref, f32[1,896]{1,0:T(1,128)S(1)} %shard_map.96.after_ref.down_ref), custom_call_target="tpu_custom_call" | custom-call | flops 262144000 | bytes 16523776 | tf_op jit(solution)/shard_map/pallas_call | solution.py:54
  29.3 0.0 collective-permute-done
  29.4 12.7 %all_to_all.30 = bf16[8,32,256]{2,1,0:T(8,128)(2,1)S(1)} all-to-all(bf16[8,32,256]{2,1,0:T(8,128)(2,1)S(1)} %add_convert_fusion.1), channel_id=1, replica_groups={{0,2,4,6,8,10,12,14},{1,3,5,7,9,11,13,15},{16,18,20,22,24,26,28,30},{17..., dimensions={0} | all-to-all | bytes 262144 | tf_op jit(solution)/shard_map/all_to_all | solution.py:26
  42.0 9.9 %all_to_all.31.x_ref.mine_ref = bf16[8,32,256]{2,1,0:T(8,128)(2,1)S(1)} all-to-all(bf16[8,32,256]{2,1,0:T(8,128)(2,1)S(1)} %broadcast_in_dim.4), channel_id=1, replica_groups={{0,2,4,6,8,10,12,14},{1,3,5,7,9,11,13,15},{16,18,20,22,24,26,28,30},{17..., dimensions={0} | all-to-all | bytes 262144 | tf_op jit(solution)/shard_map/all_to_all | solution.py:26
  51.9 0.0 collective-permute-start.1
  51.9 0.0 copy-start.2
  51.9 3.5 %shard_map.99 = (f32[32,896]{1,0:T(8,128)S(1)}, f32[32,896]{1,0:T(8,128)S(1)}, f32[32,1]{1,0:T(8,128)S(1)}, bf16[2048,896]{1,0:T(8,128)(2,1)S(1)}, bf16[2048,896]{1,0:T(8,128)(2,1)S(1)}) custom-call(bf16[8,32,256]{2,1,0:T(8,128)(2,1)S(1)} %all_to_all.31.x_ref.mine_ref, bf16[1,4096]{1,0:T(2,128)(2,1)S(1)} %reshape.23.gain_ref, bf16[4096,896]{1,0:T(8,128)(2,1)} %gate_ref.3, ...), custom_call_target="tpu_custom_call" | custom-call | flops 234881024 | bytes 14819328 | tf_op jit(solution)/shard_map/pallas_call | solution.py:54
  55.4 0.0 collective-permute-done.1.x_ref.got_ref
  55.5 6.2 %shard_map.100 = (bf16[8,32,256]{2,1,0:T(8,128)(2,1)S(1)}, f32[32,1]{1,0:T(8,128)S(1)}, bf16[32,896]{1,0:T(8,128)(2,1)S(1)}, bf16[32,896]{1,0:T(8,128)(2,1)S(1)}) custom-call(bf16[8,32,256]{2,1,0:T(8,128)(2,1)S(1)} %collective-permute-done.1.x_ref.got_ref, bf16[1,4096]{1,0:T(2,128)(2,1)S(1)} %reshape.23.gain_ref, bf16[4096,896]{1,0:T(8,128)(2,1)} %gate_ref.3, ...), custom_call_target="tpu_custom_call" | custom-call | flops 234881024 | bytes 15052432 | tf_op jit(solution)/shard_map/pallas_call | solution.py:54
  61.7 0.6 collective-permute-start.2
  62.2 2.2 %shard_map.101 = f32[8,32,256]{2,1,0:T(8,128)S(1)} custom-call(bf16[32,896]{1,0:T(8,128)(2,1)S(1)} %get-tuple-element.28.d_gate_ref, bf16[32,896]{1,0:T(8,128)(2,1)S(1)} %get-tuple-element.29.d_up_ref, bf16[2048,896]{1,0:T(8,128)(2,1)S(1)} %get-tuple-element.30.gate_ref, bf16[2048,896]{1,0:T(8,128)(2,1)S(1)} %get-tuple-element.31.up_ref), custom_call_target="tpu_custom_call" | custom-call | flops 234881024 | bytes 7454720 | tf_op jit(solution)/shard_map/pallas_call | solution.py:54
  64.5 0.0 collective-permute-done.2
  64.5 9.8 %all_to_all.32 = bf16[8,32,256]{2,1,0:T(8,128)(2,1)S(1)} all-to-all(bf16[8,32,256]{2,1,0:T(8,128)(2,1)S(1)} %add_convert_fusion), channel_id=1, replica_groups={{0,2,4,6,8,10,12,14},{1,3,5,7,9,11,13,15},{16,18,20,22,24,26,28,30},{17..., dimensions={0} | all-to-all | bytes 262144 | tf_op jit(solution)/shard_map/all_to_all | solution.py:26
  74.4 9.8 %all_to_all.33.d_mine_ref = bf16[8,32,256]{2,1,0:T(8,128)(2,1)S(1)} all-to-all(bf16[8,32,256]{2,1,0:T(8,128)(2,1)S(1)} %broadcast_in_dim.5), channel_id=1, replica_groups={{0,2,4,6,8,10,12,14},{1,3,5,7,9,11,13,15},{16,18,20,22,24,26,28,30},{17..., dimensions={0} | all-to-all | bytes 262144 | tf_op jit(solution)/shard_map/all_to_all | solution.py:26
  84.3 0.0 collective-permute-start.3
  84.3 1.3 %collective-permute-done.3.d_got_ref = bf16[8,32,256]{2,1,0:T(8,128)(2,1)S(1)} collective-permute-done((bf16[8,32,256]{2,1,0:T(8,128)(2,1)S(1)}, bf16[8,32,256]{2,1,0:T(8,128)(2,1)S(1)}, u32[]{:S(2)}, u32[]{:S(2)}) %collective-permute-start.3) | collective-permute-done | bytes 131104 | tf_op jit(solution)/shard_map/ppermute | solution.py:17
  85.6 12.9 %shard_map.102 = bf16[16,2,2012]{2,1,0:T(2,128)(2,1)} custom-call(bf16[8,32,256]{2,1,0:T(8,128)(2,1)S(1)} %all_to_all.31.x_ref.mine_ref, bf16[8,32,256]{2,1,0:T(8,128)(2,1)S(1)} %collective-permute-done.1.x_ref.got_ref, bf16[8,32,256]{2,1,0:T(8,128)(2,1)S(1)} %all_to_all.33.d_mine_ref, bf16[8,32,256]{2,1,0:T(8,128)(2,1)S(1)} %collective-permute-done.3.d_got_ref, ...), custom_call_target="tpu_custom_call" | custom-call | flops 524288000 | bytes 16925072 | tf_op jit(solution)/shard_map/pallas_call | solution.py:54
  98.5 3.5 %all-to-all-start.5 = ((bf16[16,2,2012]{2,1,0:T(2,128)(2,1)}), bf16[16,2,2012]{2,1,0:T(2,128)(2,1)S(1)}, u32[]{:S(2)}, u32[]{:S(2)}) async-start(bf16[16,2,2012]{2,1,0:T(2,128)(2,1)} %shard_map.102), calls=%async_computation.5 | async-start | bytes 262144 | tf_op jit(solution)/shard_map/all_to_all | solution.py:21
  102.1 7.9 %all-to-all-done.5.back_ref = bf16[16,2,2012]{2,1,0:T(2,128)(2,1)S(1)} async-done(((bf16[16,2,2012]{2,1,0:T(2,128)(2,1)}), bf16[16,2,2012]{2,1,0:T(2,128)(2,1)S(1)}, u32[]{:S(2)}, u32[]{:S(2)}) %all-to-all-start.5) | async-done | bytes 128800 | tf_op jit(solution)/shard_map/all_to_all | solution.py:21
  109.9 0.0 copy-done.1
  109.9 1.2 %shard_map.103 = (bf16[2,32000]{1,0:T(2,128)(2,1)}, f32[1,4]{1,0:T(1,128)}) custom-call(bf16[2,32000]{1,0:T(2,128)(2,1)S(1)} %copy-done.1, f32[2,1]{1,0:T(2,128)S(1)} %get-tuple-element.20.top_ref, f32[2,1]{1,0:T(2,128)S(1)} %get-tuple-element.21.scale_ref, bf16[16,2,2012]{2,1,0:T(2,128)(2,1)S(1)} %all-to-all-done.5.back_ref, ...), custom_call_target="tpu_custom_call" | custom-call | bytes 256800 | tf_op jit(solution)/shard_map/pallas_call | solution.py:54
  (11 shorter events, 0.2 us)
Async XLA Ops:
  0.6 0.9 copy-start
  3.0 15.3 %all-to-all-start = ((bf16[16,2,2000]{2,1,0:T(2,128)(2,1)}), bf16[16,2,2000]{2,1,0:T(2,128)(2,1)S(1)}, u32[]{:S(2)}, u32[]{:S(2)}) async-start(bf16[16,2,2000]{2,1,0:T(2,128)(2,1)} %get-tuple-element.22.after_ref), calls=%async_computation | async-start | bytes 262144 | tf_op jit(solution)/shard_map/all_to_all | solution.py:21
  23.8 28.1 %copy-start.3 = (bf16[4096]{0:T(1024)(128)(2,1)S(1)}, bf16[4096]{0:T(1024)(128)(2,1)}, u32[]{:S(2)}) copy-start(bf16[4096]{0:T(1024)(128)(2,1)} %param.10) | copy-start | bytes 24580
  23.8 5.5 %collective-permute-start = (bf16[8,32,256]{2,1,0:T(8,128)(2,1)S(1)}, bf16[8,32,256]{2,1,0:T(8,128)(2,1)S(1)}, u32[]{:S(2)}, u32[]{:S(2)}) collective-permute-start(bf16[8,32,256]{2,1,0:T(8,128)(2,1)S(1)} %get-tuple-element.24), channel_id=1, source_target_pairs={{0,1},{1,0},{2,3},{3,2},{4,5},{5,4},{6,7},{7,6},{8,9},{9,8},{10,11... | collective-permute-start | bytes 393224 | tf_op jit(solution)/shard_map/ppermute | solution.py:17
  51.9 3.5 %collective-permute-start.1 = (bf16[8,32,256]{2,1,0:T(8,128)(2,1)S(1)}, bf16[8,32,256]{2,1,0:T(8,128)(2,1)S(1)}, u32[]{:S(2)}, u32[]{:S(2)}) collective-permute-start(bf16[8,32,256]{2,1,0:T(8,128)(2,1)S(1)} %all_to_all.31.x_ref.mine_ref), channel_id=1, source_target_pairs={{0,1},{1,0},{2,3},{3,2},{4,5},{5,4},{6,7},{7,6},{8,9},{9,8},{10,11... | collective-permute-start | bytes 393224 | tf_op jit(solution)/shard_map/ppermute | solution.py:17
  51.9 3.5 %copy-start.2 = (s32[4]{0:T(128)S(1)}, s32[4]{0:T(128)}, u32[]{:S(2)}) copy-start(s32[4]{0:T(128)} %counts_ref.3) | copy-start | bytes 52
  61.7 2.8 %collective-permute-start.2 = (bf16[8,32,256]{2,1,0:T(8,128)(2,1)S(1)}, bf16[8,32,256]{2,1,0:T(8,128)(2,1)S(1)}, u32[]{:S(2)}, u32[]{:S(2)}) collective-permute-start(bf16[8,32,256]{2,1,0:T(8,128)(2,1)S(1)} %get-tuple-element.32), channel_id=1, source_target_pairs={{0,1},{1,0},{2,3},{3,2},{4,5},{5,4},{6,7},{7,6},{8,9},{9,8},{10,11... | collective-permute-start | bytes 393224 | tf_op jit(solution)/shard_map/ppermute | solution.py:17
  84.3 1.3 %collective-permute-start.3 = (bf16[8,32,256]{2,1,0:T(8,128)(2,1)S(1)}, bf16[8,32,256]{2,1,0:T(8,128)(2,1)S(1)}, u32[]{:S(2)}, u32[]{:S(2)}) collective-permute-start(bf16[8,32,256]{2,1,0:T(8,128)(2,1)S(1)} %all_to_all.33.d_mine_ref), channel_id=1, source_target_pairs={{0,1},{1,0},{2,3},{3,2},{4,5},{5,4},{6,7},{7,6},{8,9},{9,8},{10,11... | collective-permute-start | bytes 393224 | tf_op jit(solution)/shard_map/ppermute | solution.py:17
  85.6 24.3 %copy-start.1 = (bf16[2,32000]{1,0:T(2,128)(2,1)S(1)}, bf16[2,32000]{1,0:T(2,128)(2,1)}, u32[]{:S(2)}) copy-start(bf16[2,32000]{1,0:T(2,128)(2,1)} %logits_ref.3) | copy-start | bytes 384004
  98.5 11.4 %all-to-all-start.5 = ((bf16[16,2,2012]{2,1,0:T(2,128)(2,1)}), bf16[16,2,2012]{2,1,0:T(2,128)(2,1)S(1)}, u32[]{:S(2)}, u32[]{:S(2)}) async-start(bf16[16,2,2012]{2,1,0:T(2,128)(2,1)} %shard_map.102), calls=%async_computation.5 | async-start | bytes 262144 | tf_op jit(solution)/shard_map/all_to_all | solution.py:21

commit v8 on v7

--- a/solution.py
+++ b/solution.py
@@ -137,36 +137,35 @@
 
 
 def half_kernel(
-    other, slices_ref, embed_ref, head_ref, after_ref, out_ref, score_ref, table, sems
+    other, slices_ref, embed_ref, head_ref, after_ref, out_ref, score_ref, table, acc, sems
 ):
-    chips, _, own = out_ref.shape
+    chips, total, own = out_ref.shape
     part = embed_ref.shape[0]
-    cuts = sems.shape[0] // chips
     del after_ref
     core = this_core()
     half = (1 - core) if other else core
-    rows = part // cuts
-
-    def columns(j):
-        return span((half * chips + j) * own, own)
-
+    columns = span(half * chips * own, chips * own)
+    tile, fine = 256, 128
     stream = Stream([
         pltpu.make_async_copy(
-            embed_ref.at[pl.ds(i * rows, rows), columns(j)],
-            table.at[j, pl.ds(i * rows, rows)],
-            sems.at[j * cuts + i],
-        )
-        for j in range(chips)
-        for i in range(cuts)
+            embed_ref.at[pl.ds(i, min(fine, part - i)), columns],
+            table.at[pl.ds(i, min(fine, part - i))],
+            sems.at[i // fine],
+        )
+        for i in range(0, part, fine)
     ])
-    slices = slices_ref[...]
-    score = jnp.zeros(score_ref.shape, F32)
+    for start in range(0, part, tile):
+        end = min(start + tile, part)
+        stream.wait(-(-end // fine))
+        product = jnp.dot(
+            slices_ref[:, start:end], table[start:end], preferred_element_type=F32
+        )
+        acc[...] = acc[...] + product if start else product
+    score_ref[...] = jnp.sum(
+        acc[...] * head_ref[:, columns].astype(F32), axis=-1, keepdims=True
+    )
     for j in range(chips):
-        stream.wait((j + 1) * cuts)
-        part = jnp.dot(slices, table[j], preferred_element_type=F32)
-        score += jnp.sum(part * head_ref[:, columns(j)].astype(F32), axis=-1, keepdims=True)
-        out_ref[j] = part.astype(out_ref.dtype)
-    score_ref[...] = score
+        out_ref[j] = acc[:, j * own : (j + 1) * own].astype(out_ref.dtype)
 
 
 def down_kernel(head_ref, down_ref, after_ref, out_ref, table, sems):
@@ -268,13 +267,12 @@
     out_ref, dx_ref, table, sems,
 ):
     chips, total, own = mine_ref.shape
-    devices, per, _ = out_ref.shape
     voc = embed_ref.shape[0]
     requests = counts_ref.shape[0]
     width = 2 * chips * own
     core = this_core()
     tile = 256
-    fine = 32
+    fine = 64
     stream = Stream([
         pltpu.make_async_copy(
             embed_ref.at[pl.ds(i, min(fine, voc - i))],
@@ -312,17 +310,15 @@
         value = value - piece
     for i, piece in enumerate(pieces):
         start = voc + i * requests
-        spread = jnp.broadcast_to(piece, (per, requests)).astype(BF16)
-        for d in range(devices):
-            out_ref[d, :, start : start + requests] = spread
+        spread = jnp.broadcast_to(piece, (total, requests)).astype(BF16)
+        out_ref[:, start : start + requests] = spread
     contract = (((1,), (1,)), ((), ()))
     dx = dx_ref[...]
     for start in range(0, voc, tile):
         end = min(start + tile, voc)
         stream.wait(-(-end // fine))
         part = lax.dot_general(dx, table[start:end, :], contract, preferred_element_type=F32)
-        for d in range(devices):
-            out_ref[d, :, start:end] = part[d * per : (d + 1) * per].astype(BF16)
+        out_ref[:, start:end] = part.astype(BF16)
 
 
 def swap_sum(send, keep, devices):
@@ -418,8 +414,10 @@
             streamed=(1,), flops=2 * hidden * width, room=2 * hidden * width,
             scratch=(pltpu.VMEM((hidden, width), BF16), pltpu.SemaphoreType.DMA((steps,))),
         )
-        cuts = 5 if part % 80 == 0 else 1
-        table = [pltpu.VMEM((chips, part, own), BF16), pltpu.SemaphoreType.DMA((cuts * chips,))]
+        table = [
+            pltpu.VMEM((part, width // 2), BF16), pltpu.VMEM((total, width // 2), F32),
+            pltpu.SemaphoreType.DMA((-(-part // 128),)),
+        ]
         args = dict(streamed=(1,), flops=flops, scratch=table, room=part * width)
         send, score_a = call(
             functools.partial(half_kernel, True), [struct(half, BF16), column],
@@ -469,21 +467,21 @@
     padded = part + 3 * requests
     if tiled:
         (d_slices,) = call(
-            input_kernel, [struct((devices, rows, padded), BF16)],
+            input_kernel, [struct((total, padded), BF16)],
             *sources, score_a, score_b, score_c, counts, embed,
             scalars=(9,), streamed=(10,), flops=2 * flops, room=2 * part * width,
             scratch=(
                 pltpu.VMEM((total, width), BF16), pltpu.VMEM((part, width), BF16),
-                pltpu.SemaphoreType.DMA((-(-part // 32),)),
+                pltpu.SemaphoreType.DMA((-(-part // 64),)),
             ),
         )
     else:
-        d_slices = plain_input(*sources, valid, embed).reshape(devices, rows, part)
+        d_slices = plain_input(*sources, valid, embed)
         score = jnp.where(member, valid * (score_a + score_c), 0.0)
-        extra = split3(jnp.sum(score, axis=0)).reshape(1, 1, requests * 3)
-        extra = jnp.broadcast_to(extra, (devices, rows, requests * 3))
+        extra = split3(jnp.sum(score, axis=0)).reshape(1, requests * 3)
+        extra = jnp.broadcast_to(extra, (total, requests * 3))
         d_slices = jnp.concatenate([d_slices, extra], axis=-1)
-    back = exchange(d_slices)
+    back = exchange(d_slices.reshape(devices, rows, padded))
     counts32 = counts.astype(F32)
     if tiled:
         guidance, rewards = call(

time: 112 us -> 108 us (0.964)
  Pallas kernels: 44.8 us -> 40.7 us
    pallas_call x9, Pallas kernels: 44.8 us -> 40.7 us  [call(): pl.pallas_call(kernel, out_shape=outs, in_specs=specs, out_specs=[VMEM_SP...]
  transfers between devices with their start and end apart: 6 -> 6, of which waited for: 3 -> 3; matrix products, arithmetic and copies ran while one was open for 1% -> 1% of each run, Pallas kernels for 16% -> 15%
where the time goes in v8:
time: 108 us
  blocking collectives  42.2 us (39%)
  Pallas kernels  40.7 us (38%)
  starting transfers between devices  11.5 us (11%)
  waiting for transfers between devices  9.93 us (9%)
  local copies, waits for them, and re-layouts  2.47 us (2%)
    all_to_all x4, blocking collectives, exchange_chips(): lax.all_to_all(blocks, 'dp', split_axis=0, concat_axis=0, axis_index_grou...  42.2 us
    pallas_call x9, Pallas kernels, call(): pl.pallas_call(kernel, out_shape=outs, in_specs=specs, out_specs=[VMEM_SP...  40.7 us
    all_to_all x2, starting transfers between devices, exchange(): return lax.all_to_all(blocks, 'dp', split_axis=0, concat_axis=0, tiled=True)  10.9 us
    all_to_all x2, waiting for transfers between devices, exchange(): return lax.all_to_all(blocks, 'dp', split_axis=0, concat_axis=0, tiled=True)  8.58 us
  transfers between devices with their start and end apart: 6, of which 3 were waited for; matrix products, arithmetic and copies ran while one was open for 1% of the time, Pallas kernels for 15%

profile of v8, /device:TPU:0, one launch (start us, length us, event | category | flops | bytes accessed | tf_op | source)
XLA Modules:
  0.0 107.7 jit_solution(2954081688308357306)
XLA Ops:
  0.6 0.0 copy-start
  0.6 0.9 copy-done
  1.5 1.4 %shard_map.95 = (bf16[16,2,2000]{2,1,0:T(2,128)(2,1)}, f32[2,1]{1,0:T(2,128)S(1)}, f32[2,1]{1,0:T(2,128)S(1)}) custom-call(bf16[2,32000]{1,0:T(2,128)(2,1)S(1)} %copy-done), custom_call_target="tpu_custom_call" | custom-call | bytes 128000 | tf_op jit(solution)/shard_map/pallas_call | solution.py:54
  3.0 7.4 %all-to-all-start = ((bf16[16,2,2000]{2,1,0:T(2,128)(2,1)}), bf16[16,2,2000]{2,1,0:T(2,128)(2,1)S(1)}, u32[]{:S(2)}, u32[]{:S(2)}) async-start(bf16[16,2,2000]{2,1,0:T(2,128)(2,1)} %get-tuple-element.22.after_ref), calls=%async_computation | async-start | bytes 262144 | tf_op jit(solution)/shard_map/all_to_all | solution.py:21
  10.4 0.7 reshape.25.head_ref
  11.1 6.5 %shard_map.96.after_ref.down_ref = f32[1,896]{1,0:T(1,128)S(1)} custom-call(bf16[1,4096]{1,0:T(2,128)(2,1)S(1)} %reshape.25.head_ref, bf16[896,4096]{1,0:T(8,128)(2,1)} %down_ref.1, bf16[16,2,2000]{2,1,0:T(2,128)(2,1)} %get-tuple-element.22.after_ref), custom_call_target="tpu_custom_call" | custom-call | flops 7340032 | bytes 7476224 | tf_op jit(solution)/shard_map/pallas_call | solution.py:54
  17.6 0.7 all-to-all-done
  18.3 0.1 reshape.24.slices_ref
  18.4 3.8 %shard_map.98 = (bf16[8,32,256]{2,1,0:T(8,128)(2,1)S(1)}, f32[32,1]{1,0:T(8,128)S(1)}) custom-call(bf16[32,2000]{1,0:T(8,128)(2,1)S(1)} %reshape.24.slices_ref, bf16[2000,4096]{1,0:T(8,128)(2,1)} %embed_ref.5, bf16[1,4096]{1,0:T(2,128)(2,1)S(1)} %reshape.25.head_ref, f32[1,896]{1,0:T(1,128)S(1)} %shard_map.96.after_ref.down_ref), custom_call_target="tpu_custom_call" | custom-call | flops 262144000 | bytes 16523776 | tf_op jit(solution)/shard_map/pallas_call | solution.py:54
  22.2 0.0 copy-start.3
  22.2 0.1 collective-permute-start
  22.3 3.8 %shard_map.97 = (f32[8,32,256]{2,1,0:T(8,128)S(1)}, f32[32,1]{1,0:T(8,128)S(1)}) custom-call(bf16[32,2000]{1,0:T(8,128)(2,1)S(1)} %reshape.24.slices_ref, bf16[2000,4096]{1,0:T(8,128)(2,1)} %embed_ref.5, bf16[1,4096]{1,0:T(2,128)(2,1)S(1)} %reshape.25.head_ref, f32[1,896]{1,0:T(1,128)S(1)} %shard_map.96.after_ref.down_ref), custom_call_target="tpu_custom_call" | custom-call | flops 262144000 | bytes 16523776 | tf_op jit(solution)/shard_map/pallas_call | solution.py:54
  26.1 0.0 collective-permute-done
  26.1 12.6 %all_to_all.30 = bf16[8,32,256]{2,1,0:T(8,128)(2,1)S(1)} all-to-all(bf16[8,32,256]{2,1,0:T(8,128)(2,1)S(1)} %add_convert_fusion.1), channel_id=1, replica_groups={{0,2,4,6,8,10,12,14},{1,3,5,7,9,11,13,15},{16,18,20,22,24,26,28,30},{17..., dimensions={0} | all-to-all | bytes 262144 | tf_op jit(solution)/shard_map/all_to_all | solution.py:26
  38.8 9.9 %all_to_all.31.x_ref.mine_ref = bf16[8,32,256]{2,1,0:T(8,128)(2,1)S(1)} all-to-all(bf16[8,32,256]{2,1,0:T(8,128)(2,1)S(1)} %broadcast_in_dim.4), channel_id=1, replica_groups={{0,2,4,6,8,10,12,14},{1,3,5,7,9,11,13,15},{16,18,20,22,24,26,28,30},{17..., dimensions={0} | all-to-all | bytes 262144 | tf_op jit(solution)/shard_map/all_to_all | solution.py:26
  48.7 0.0 collective-permute-start.1
  48.7 0.0 copy-start.2
  48.7 3.5 %shard_map.99 = (f32[32,896]{1,0:T(8,128)S(1)}, f32[32,896]{1,0:T(8,128)S(1)}, f32[32,1]{1,0:T(8,128)S(1)}, bf16[2048,896]{1,0:T(8,128)(2,1)S(1)}, bf16[2048,896]{1,0:T(8,128)(2,1)S(1)}) custom-call(bf16[8,32,256]{2,1,0:T(8,128)(2,1)S(1)} %all_to_all.31.x_ref.mine_ref, bf16[1,4096]{1,0:T(2,128)(2,1)S(1)} %reshape.26.gain_ref, bf16[4096,896]{1,0:T(8,128)(2,1)} %gate_ref.3, ...), custom_call_target="tpu_custom_call" | custom-call | flops 234881024 | bytes 14819328 | tf_op jit(solution)/shard_map/pallas_call | solution.py:54
  52.2 0.0 collective-permute-done.1.x_ref.got_ref
  52.2 6.2 %shard_map.100 = (bf16[8,32,256]{2,1,0:T(8,128)(2,1)S(1)}, f32[32,1]{1,0:T(8,128)S(1)}, bf16[32,896]{1,0:T(8,128)(2,1)S(1)}, bf16[32,896]{1,0:T(8,128)(2,1)S(1)}) custom-call(bf16[8,32,256]{2,1,0:T(8,128)(2,1)S(1)} %collective-permute-done.1.x_ref.got_ref, bf16[1,4096]{1,0:T(2,128)(2,1)S(1)} %reshape.26.gain_ref, bf16[4096,896]{1,0:T(8,128)(2,1)} %gate_ref.3, ...), custom_call_target="tpu_custom_call" | custom-call | flops 234881024 | bytes 15052432 | tf_op jit(solution)/shard_map/pallas_call | solution.py:54
  58.4 0.6 collective-permute-start.2
  59.0 2.2 %shard_map.101 = f32[8,32,256]{2,1,0:T(8,128)S(1)} custom-call(bf16[32,896]{1,0:T(8,128)(2,1)S(1)} %get-tuple-element.28.d_gate_ref, bf16[32,896]{1,0:T(8,128)(2,1)S(1)} %get-tuple-element.29.d_up_ref, bf16[2048,896]{1,0:T(8,128)(2,1)S(1)} %get-tuple-element.30.gate_ref, bf16[2048,896]{1,0:T(8,128)(2,1)S(1)} %get-tuple-element.31.up_ref), custom_call_target="tpu_custom_call" | custom-call | flops 234881024 | bytes 7454720 | tf_op jit(solution)/shard_map/pallas_call | solution.py:54
  61.2 0.0 collective-permute-done.2
  61.3 9.8 %all_to_all.32 = bf16[8,32,256]{2,1,0:T(8,128)(2,1)S(1)} all-to-all(bf16[8,32,256]{2,1,0:T(8,128)(2,1)S(1)} %add_convert_fusion), channel_id=1, replica_groups={{0,2,4,6,8,10,12,14},{1,3,5,7,9,11,13,15},{16,18,20,22,24,26,28,30},{17..., dimensions={0} | all-to-all | bytes 262144 | tf_op jit(solution)/shard_map/all_to_all | solution.py:26
  71.2 9.8 %all_to_all.33.d_mine_ref = bf16[8,32,256]{2,1,0:T(8,128)(2,1)S(1)} all-to-all(bf16[8,32,256]{2,1,0:T(8,128)(2,1)S(1)} %broadcast_in_dim.5), channel_id=1, replica_groups={{0,2,4,6,8,10,12,14},{1,3,5,7,9,11,13,15},{16,18,20,22,24,26,28,30},{17..., dimensions={0} | all-to-all | bytes 262144 | tf_op jit(solution)/shard_map/all_to_all | solution.py:26
  81.0 0.0 collective-permute-start.3
  81.0 1.3 %collective-permute-done.3.d_got_ref = bf16[8,32,256]{2,1,0:T(8,128)(2,1)S(1)} collective-permute-done((bf16[8,32,256]{2,1,0:T(8,128)(2,1)S(1)}, bf16[8,32,256]{2,1,0:T(8,128)(2,1)S(1)}, u32[]{:S(2)}, u32[]{:S(2)}) %collective-permute-start.3) | collective-permute-done | bytes 131104 | tf_op jit(solution)/shard_map/ppermute | solution.py:17
  82.4 11.9 %shard_map.102 = bf16[32,2012]{1,0:T(8,128)(2,1)S(1)} custom-call(bf16[8,32,256]{2,1,0:T(8,128)(2,1)S(1)} %all_to_all.31.x_ref.mine_ref, bf16[8,32,256]{2,1,0:T(8,128)(2,1)S(1)} %collective-permute-done.1.x_ref.got_ref, bf16[8,32,256]{2,1,0:T(8,128)(2,1)S(1)} %all_to_all.33.d_mine_ref, bf16[8,32,256]{2,1,0:T(8,128)(2,1)S(1)} %collective-permute-done.3.d_got_ref, ...), custom_call_target="tpu_custom_call" | custom-call | flops 524288000 | bytes 16925072 | tf_op jit(solution)/shard_map/pallas_call | solution.py:54
  94.3 0.8 reshape.27
  95.1 3.5 %all-to-all-start.5 = ((bf16[16,2,2012]{2,1,0:T(2,128)(2,1)}), bf16[16,2,2012]{2,1,0:T(2,128)(2,1)S(1)}, u32[]{:S(2)}, u32[]{:S(2)}) async-start(bf16[16,2,2012]{2,1,0:T(2,128)(2,1)} %reshape.27), calls=%async_computation.5 | async-start | bytes 262144 | tf_op jit(solution)/shard_map/all_to_all | solution.py:21
  98.6 7.9 %all-to-all-done.5.back_ref = bf16[16,2,2012]{2,1,0:T(2,128)(2,1)S(1)} async-done(((bf16[16,2,2012]{2,1,0:T(2,128)(2,1)}), bf16[16,2,2012]{2,1,0:T(2,128)(2,1)S(1)}, u32[]{:S(2)}, u32[]{:S(2)}) %all-to-all-start.5) | async-done | bytes 128800 | tf_op jit(solution)/shard_map/all_to_all | solution.py:21
  106.5 1.2 %shard_map.103 = (bf16[2,32000]{1,0:T(2,128)(2,1)}, f32[1,4]{1,0:T(1,128)}) custom-call(bf16[2,32000]{1,0:T(2,128)(2,1)S(1)} %copy-done.1, f32[2,1]{1,0:T(2,128)S(1)} %get-tuple-element.20.top_ref, f32[2,1]{1,0:T(2,128)S(1)} %get-tuple-element.21.scale_ref, bf16[16,2,2012]{2,1,0:T(2,128)(2,1)S(1)} %all-to-all-done.5.back_ref, ...), custom_call_target="tpu_custom_call" | custom-call | bytes 256800 | tf_op jit(solution)/shard_map/pallas_call | solution.py:54
  (12 shorter events, 0.2 us)
Async XLA Ops:
  0.6 0.9 copy-start
  3.0 15.3 %all-to-all-start = ((bf16[16,2,2000]{2,1,0:T(2,128)(2,1)}), bf16[16,2,2000]{2,1,0:T(2,128)(2,1)S(1)}, u32[]{:S(2)}, u32[]{:S(2)}) async-start(bf16[16,2,2000]{2,1,0:T(2,128)(2,1)} %get-tuple-element.22.after_ref), calls=%async_computation | async-start | bytes 262144 | tf_op jit(solution)/shard_map/all_to_all | solution.py:21
  22.2 26.5 %copy-start.3 = (bf16[4096]{0:T(1024)(128)(2,1)S(1)}, bf16[4096]{0:T(1024)(128)(2,1)}, u32[]{:S(2)}) copy-start(bf16[4096]{0:T(1024)(128)(2,1)} %param.10) | copy-start | bytes 24580
  22.2 3.9 %collective-permute-start = (bf16[8,32,256]{2,1,0:T(8,128)(2,1)S(1)}, bf16[8,32,256]{2,1,0:T(8,128)(2,1)S(1)}, u32[]{:S(2)}, u32[]{:S(2)}) collective-permute-start(bf16[8,32,256]{2,1,0:T(8,128)(2,1)S(1)} %get-tuple-element.24), channel_id=1, source_target_pairs={{0,1},{1,0},{2,3},{3,2},{4,5},{5,4},{6,7},{7,6},{8,9},{9,8},{10,11... | collective-permute-start | bytes 393224 | tf_op jit(solution)/shard_map/ppermute | solution.py:17
  48.7 3.5 %collective-permute-start.1 = (bf16[8,32,256]{2,1,0:T(8,128)(2,1)S(1)}, bf16[8,32,256]{2,1,0:T(8,128)(2,1)S(1)}, u32[]{:S(2)}, u32[]{:S(2)}) collective-permute-start(bf16[8,32,256]{2,1,0:T(8,128)(2,1)S(1)} %all_to_all.31.x_ref.mine_ref), channel_id=1, source_target_pairs={{0,1},{1,0},{2,3},{3,2},{4,5},{5,4},{6,7},{7,6},{8,9},{9,8},{10,11... | collective-permute-start | bytes 393224 | tf_op jit(solution)/shard_map/ppermute | solution.py:17
  48.7 3.5 %copy-start.2 = (s32[4]{0:T(128)S(1)}, s32[4]{0:T(128)}, u32[]{:S(2)}) copy-start(s32[4]{0:T(128)} %counts_ref.3) | copy-start | bytes 52
  58.4 2.8 %collective-permute-start.2 = (bf16[8,32,256]{2,1,0:T(8,128)(2,1)S(1)}, bf16[8,32,256]{2,1,0:T(8,128)(2,1)S(1)}, u32[]{:S(2)}, u32[]{:S(2)}) collective-permute-start(bf16[8,32,256]{2,1,0:T(8,128)(2,1)S(1)} %get-tuple-element.32), channel_id=1, source_target_pairs={{0,1},{1,0},{2,3},{3,2},{4,5},{5,4},{6,7},{7,6},{8,9},{9,8},{10,11... | collective-permute-start | bytes 393224 | tf_op jit(solution)/shard_map/ppermute | solution.py:17
  81.0 1.3 %collective-permute-start.3 = (bf16[8,32,256]{2,1,0:T(8,128)(2,1)S(1)}, bf16[8,32,256]{2,1,0:T(8,128)(2,1)S(1)}, u32[]{:S(2)}, u32[]{:S(2)}) collective-permute-start(bf16[8,32,256]{2,1,0:T(8,128)(2,1)S(1)} %all_to_all.33.d_mine_ref), channel_id=1, source_target_pairs={{0,1},{1,0},{2,3},{3,2},{4,5},{5,4},{6,7},{7,6},{8,9},{9,8},{10,11... | collective-permute-start | bytes 393224 | tf_op jit(solution)/shard_map/ppermute | solution.py:17
  82.4 24.1 %copy-start.1 = (bf16[2,32000]{1,0:T(2,128)(2,1)S(1)}, bf16[2,32000]{1,0:T(2,128)(2,1)}, u32[]{:S(2)}) copy-start(bf16[2,32000]{1,0:T(2,128)(2,1)} %logits_ref.3) | copy-start | bytes 384004
  95.1 11.4 %all-to-all-start.5 = ((bf16[16,2,2012]{2,1,0:T(2,128)(2,1)}), bf16[16,2,2012]{2,1,0:T(2,128)(2,1)S(1)}, u32[]{:S(2)}, u32[]{:S(2)}) async-start(bf16[16,2,2012]{2,1,0:T(2,128)(2,1)} %reshape.27), calls=%async_computation.5 | async-start | bytes 262144 | tf_op jit(solution)/shard_map/all_to_all | solution.py:21

commit v9 on v8

--- a/solution.py
+++ b/solution.py
@@ -136,12 +136,38 @@
     return valid, position // length
 
 
+def ready_kernel(starts, *refs):
+    count = len(starts)
+    sources, outs, sems = refs[:count], refs[count + 1 : -1], refs[-1]
+    fine = 128
+    copies = [
+        pltpu.make_async_copy(
+            source.at[span(start() + i, fine)], out.at[pl.ds(i, fine)], sems.at[k, i // fine]
+        )
+        for k, (source, out, start) in enumerate(zip(sources, outs, starts))
+        for i in range(0, out.shape[0], fine)
+    ]
+    for copy in copies:
+        copy.start()
+    for copy in copies:
+        copy.wait()
+
+
+def first_rows(rows, sources, starts, after):
+    count = len(sources)
+    return call(
+        functools.partial(ready_kernel, starts),
+        [pltpu.VMEM((rows, a.shape[1]), a.dtype) for a in sources],
+        *sources, after, streamed=range(count),
+        scratch=(pltpu.SemaphoreType.DMA((count, rows // 128)),),
+    )
+
+
 def half_kernel(
-    other, slices_ref, embed_ref, head_ref, after_ref, out_ref, score_ref, table, acc, sems
+    other, slices_ref, ready_ref, embed_ref, head_ref, out_ref, score_ref, table, acc, sems
 ):
     chips, total, own = out_ref.shape
-    part = embed_ref.shape[0]
-    del after_ref
+    part, ready = embed_ref.shape[0], ready_ref.shape[0]
     core = this_core()
     half = (1 - core) if other else core
     columns = span(half * chips * own, chips * own)
@@ -149,18 +175,21 @@
     stream = Stream([
         pltpu.make_async_copy(
             embed_ref.at[pl.ds(i, min(fine, part - i)), columns],
-            table.at[pl.ds(i, min(fine, part - i))],
+            table.at[pl.ds(i - ready, min(fine, part - i))],
             sems.at[i // fine],
         )
-        for i in range(0, part, fine)
+        for i in range(ready, part, fine)
     ])
-    for start in range(0, part, tile):
+    acc[...] = jnp.dot(
+        slices_ref[:, :ready], ready_ref[:, columns], preferred_element_type=F32
+    )
+    for start in range(ready, part, tile):
         end = min(start + tile, part)
-        stream.wait(-(-end // fine))
-        product = jnp.dot(
-            slices_ref[:, start:end], table[start:end], preferred_element_type=F32
-        )
-        acc[...] = acc[...] + product if start else product
+        stream.wait(-(-(end - ready) // fine))
+        acc[...] += jnp.dot(
+            slices_ref[:, start:end], table[start - ready : end - ready],
+            preferred_element_type=F32,
+        )
     score_ref[...] = jnp.sum(
         acc[...] * head_ref[:, columns].astype(F32), axis=-1, keepdims=True
     )
@@ -188,15 +217,25 @@
         out_ref[:, i * rows : (i + 1) * rows] = part[:1]
 
 
-def forward_half(x_ref, gain_ref, gate_ref, up_ref, gate, up, sems, half, sums):
+def weight_rows(j, own, ready, gate, up):
+    skip = ready[0].shape[0] // own if ready else 0
+    if j < skip:
+        return ready, slice(j * own, (j + 1) * own)
+    return (gate, up), slice((j - skip) * own, (j - skip + 1) * own)
+
+
+def forward_half(x_ref, gain_ref, gate_ref, up_ref, gate, up, sems, half, sums, ready=()):
     chips, _, own = x_ref.shape
+    skip = ready[0].shape[0] // own if ready else 0
 
     def rows(j):
         return span((half * chips + j) * own, own)
 
     stream = Stream([
-        pltpu.make_async_copy(source.at[rows(j)], target.at[pl.ds(j * own, own)], sems.at[k, j])
-        for j in range(chips)
+        pltpu.make_async_copy(
+            source.at[rows(j)], target.at[pl.ds((j - skip) * own, own)], sems.at[k, j]
+        )
+        for j in range(skip, chips)
         for k, (source, target) in enumerate(((gate_ref, gate), (up_ref, up)))
     ])
     a, b, squares = sums
@@ -206,29 +245,33 @@
         squares = squares + jnp.sum(x * x, axis=-1, keepdims=True)
         scaled.append((x * gain_ref[:, rows(j)].astype(F32)).astype(BF16))
     for j in range(chips):
-        r = slice(j * own, (j + 1) * own)
-        stream.wait(2 * (j + 1))
-        a = a + jnp.dot(scaled[j], gate[r], preferred_element_type=F32)
-        b = b + jnp.dot(scaled[j], up[r], preferred_element_type=F32)
+        (g, u), r = weight_rows(j, own, ready, gate, up)
+        if j >= skip:
+            stream.wait(2 * (j - skip + 1))
+        a = a + jnp.dot(scaled[j], g[r], preferred_element_type=F32)
+        b = b + jnp.dot(scaled[j], u[r], preferred_element_type=F32)
     return a, b, squares
 
 
-def backward_half(d_gate, d_up, gate, up, out_ref):
+def backward_half(d_gate, d_up, gate, up, out_ref, ready=()):
     chips, _, own = out_ref.shape
     contract = (((1,), (1,)), ((), ()))
     for j in range(chips):
-        r = slice(j * own, (j + 1) * own)
-        part = lax.dot_general(d_gate, gate[r], contract, preferred_element_type=F32)
-        part += lax.dot_general(d_up, up[r], contract, preferred_element_type=F32)
+        (g, u), r = weight_rows(j, own, ready, gate, up)
+        part = lax.dot_general(d_gate, g[r], contract, preferred_element_type=F32)
+        part += lax.dot_general(d_up, u[r], contract, preferred_element_type=F32)
         out_ref[j] = part.astype(out_ref.dtype)
 
 
 def first_kernel(
-    x_ref, gain_ref, gate_ref, up_ref, a_ref, b_ref, squares_ref, gate, up, sems
+    x_ref, gain_ref, gate_ref, up_ref, gate_0, up_0,
+    a_ref, b_ref, squares_ref, gate, up, sems,
 ):
     zeros = jnp.zeros(a_ref.shape, F32)
     sums = (zeros, zeros, jnp.zeros(squares_ref.shape, F32))
-    sums = forward_half(x_ref, gain_ref, gate_ref, up_ref, gate, up, sems, this_core(), sums)
+    sums = forward_half(
+        x_ref, gain_ref, gate_ref, up_ref, gate, up, sems, this_core(), sums, (gate_0, up_0)
+    )
     a_ref[...], b_ref[...], squares_ref[...] = sums
 
 
@@ -257,13 +300,14 @@
     backward_half(d_gate, d_up, gate, up, send_ref)
 
 
-def third_kernel(d_gate_ref, d_up_ref, gate_ref, up_ref, keep_ref):
-    backward_half(d_gate_ref[...], d_up_ref[...], gate_ref, up_ref, keep_ref)
+def third_kernel(d_gate_ref, d_up_ref, gate_0, up_0, gate_ref, up_ref, keep_ref):
+    d_gate, d_up = d_gate_ref[...], d_up_ref[...]
+    backward_half(d_gate, d_up, gate_ref, up_ref, keep_ref, (gate_0, up_0))
 
 
 def input_kernel(
     mine_ref, got_ref, d_mine_ref, d_got_ref, gain_ref, head_ref,
-    score_a_ref, score_b_ref, score_c_ref, counts_ref, embed_ref,
+    score_a_ref, score_b_ref, score_c_ref, counts_ref, ready_ref, embed_ref,
     out_ref, dx_ref, table, sems,
 ):
     chips, total, own = mine_ref.shape
@@ -271,16 +315,19 @@
     requests = counts_ref.shape[0]
     width = 2 * chips * own
     core = this_core()
-    tile = 256
-    fine = 64
-    stream = Stream([
-        pltpu.make_async_copy(
-            embed_ref.at[pl.ds(i, min(fine, voc - i))],
-            table.at[pl.ds(i, min(fine, voc - i))],
-            sems.at[i // fine],
-        )
-        for i in range(0, voc, fine)
-    ])
+    ready = ready_ref.shape[0]
+    tile, fine = 256, 64
+
+    def copy(start, size):
+        return pltpu.make_async_copy(
+            embed_ref.at[pl.ds(start, size)],
+            table.at[pl.ds(start - ready, size)],
+            sems.at[start // fine],
+        )
+
+    pieces_of = range(ready, voc, fine)
+    for start in pieces_of:
+        copy(start, min(fine, voc - start)).start()
     sources = ((mine_ref, d_mine_ref, core), (got_ref, d_got_ref, 1 - core))
     squares = jnp.zeros((total, 1), F32)
     dots = jnp.zeros((total, 1), F32)
@@ -313,21 +360,41 @@
         spread = jnp.broadcast_to(piece, (total, requests)).astype(BF16)
         out_ref[:, start : start + requests] = spread
     contract = (((1,), (1,)), ((), ()))
-    dx = dx_ref[...]
-    for start in range(0, voc, tile):
-        end = min(start + tile, voc)
-        stream.wait(-(-end // fine))
-        part = lax.dot_general(dx, table[start:end, :], contract, preferred_element_type=F32)
-        out_ref[:, start:end] = part.astype(BF16)
+
+    def product(weights):
+        return lax.dot_general(
+            dx_ref[...], weights, contract, preferred_element_type=F32
+        ).astype(BF16)
+
+    out_ref[:, :ready] = product(ready_ref[...])
+
+    def step(j, _):
+        start = pl.multiple_of(j * tile, tile)
+        for i in range(0, tile, fine):
+            copy(pl.multiple_of(start + i, fine), fine).wait()
+        rows = pl.ds(pl.multiple_of(start - ready, tile), tile)
+        out_ref[:, pl.ds(start, tile)] = product(table[rows, :])
+        return 0
+
+    whole = voc // tile
+    lax.fori_loop(ready // tile, whole, step, 0)
+    if voc % tile:
+        last = whole * tile
+        for start in range(last, voc, fine):
+            copy(start, min(fine, voc - start)).wait()
+        out_ref[:, last:voc] = product(table[last - ready :, :])
 
 
 def swap_sum(send, keep, devices):
     return (keep.astype(F32) + swap_cores(send, devices).astype(F32)).astype(BF16)
 
 
-def sum_and_gather(half, devices):
-    total = jnp.sum(exchange_chips(half, devices).astype(F32), axis=0).astype(BF16)
-    return exchange_chips(jnp.broadcast_to(total[None], half.shape), devices)
+def chip_sum(half, devices):
+    return jnp.sum(exchange_chips(half, devices).astype(F32), axis=0).astype(BF16)
+
+
+def chip_gather(total, devices):
+    return exchange_chips(jnp.broadcast_to(total[None], (devices // 2,) + total.shape), devices)
 
 
 def pick(blocks, index):
@@ -393,7 +460,7 @@
     requests = counts.shape[0]
     total = rows * devices
     request_len = total // requests
-    tiled = own % 128 == 0 and hidden % 128 == 0 and total % 16 == 0 and part % 16 == 0
+    tiled = own % 128 == 0 and hidden % 128 == 0 and total % 16 == 0 and part % 16 == 0 and part > 512
     head_row, gain_row = head.reshape(1, width), norm_gain.reshape(1, width)
     if tiled:
         column = struct((rows, 1), F32)
@@ -408,38 +475,51 @@
     half = (chips, total, own)
     flops = total * part * width
     if tiled:
+        (first,) = first_rows(256, [embed], [lambda: 0], blocked)
+        table = [
+            pltpu.VMEM((part - 256, width // 2), BF16), pltpu.VMEM((total, width // 2), F32),
+            pltpu.SemaphoreType.DMA((-(-part // 128),)),
+        ]
+        args = dict(
+            streamed=(2,), kept=(1,), flops=flops, scratch=table, room=part * width
+        )
+        send, score_a = call(
+            functools.partial(half_kernel, True), [struct(half, BF16), column],
+            slices, first, embed, head_row, **args,
+        )
+        keep, score_b = call(
+            functools.partial(half_kernel, False), [struct(half, F32), column],
+            slices, first, embed, head_row, **args,
+        )
+    else:
+        send, keep, score_a = plain_half(slices, embed, head_row, devices)
+    summed = swap_sum(send, keep, devices)
+    if tiled:
         steps = hidden // 128
         (down_row,) = call(
-            down_kernel, [struct((1, hidden), F32)], head_row, w_down, blocked,
+            down_kernel, [struct((1, hidden), F32)], head_row, w_down, summed,
             streamed=(1,), flops=2 * hidden * width, room=2 * hidden * width,
             scratch=(pltpu.VMEM((hidden, width), BF16), pltpu.SemaphoreType.DMA((steps,))),
         )
-        table = [
-            pltpu.VMEM((part, width // 2), BF16), pltpu.VMEM((total, width // 2), F32),
-            pltpu.SemaphoreType.DMA((-(-part // 128),)),
-        ]
-        args = dict(streamed=(1,), flops=flops, scratch=table, room=part * width)
-        send, score_a = call(
-            functools.partial(half_kernel, True), [struct(half, BF16), column],
-            slices, embed, head_row, down_row, **args,
-        )
-        keep, score_b = call(
-            functools.partial(half_kernel, False), [struct(half, F32), column],
-            slices, embed, head_row, down_row, **args,
-        )
     else:
-        send, keep, score_a = plain_half(slices, embed, head_row, devices)
-    x_mine = sum_and_gather(swap_sum(send, keep, devices), devices)
+        down_row = jnp.sum(w_down.astype(F32) * head.astype(F32)[None, :], axis=-1)[None]
+    total_x = chip_sum(summed, devices)
+    if tiled:
+        total_x, down_row = lax.optimization_barrier((total_x, down_row))
+    x_mine = chip_gather(total_x, devices)
     x_got = swap_cores(x_mine, devices)
     if tiled:
+        weights = [w_gate, w_up]
+        starts = [lambda: this_core() * (width // 2)] * 2
+        gate_0, up_0 = first_rows(2 * own, weights, starts, total_x)
         wide = struct((total, hidden), F32)
-        weight = (width // 2, hidden)
+        weight, rest = (width // 2, hidden), (width // 2 - 2 * own, hidden)
         sems = pltpu.SemaphoreType.DMA((2, chips))
         args = dict(streamed=(2, 3), flops=2 * total * hidden * width, room=2 * width * hidden)
         a, b, squares, gate, up = call(
             first_kernel,
-            [wide, wide, column, pltpu.VMEM(weight, BF16), pltpu.VMEM(weight, BF16)],
-            x_mine, gain_row, w_gate, w_up, scratch=(sems,), **args,
+            [wide, wide, column, pltpu.VMEM(rest, BF16), pltpu.VMEM(rest, BF16)],
+            x_mine, gain_row, w_gate, w_up, gate_0, up_0, scratch=(sems,), kept=(4, 5), **args,
         )
         narrow = struct((total, hidden), BF16)
         send, score_c, d_gate, d_up = call(
@@ -449,11 +529,10 @@
             scalars=(8,), **args,
         )
         (keep,) = call(
-            third_kernel, [struct(half, F32)], d_gate, d_up, gate, up,
-            kept=(2, 3), flops=2 * total * hidden * width,
+            third_kernel, [struct(half, F32)], d_gate, d_up, gate_0, up_0, gate, up,
+            kept=(2, 3, 4, 5), flops=2 * total * hidden * width,
         )
     else:
-        down_row = jnp.sum(w_down.astype(F32) * head.astype(F32)[None, :], axis=-1)[None]
         position = jnp.arange(total, dtype=jnp.int32)[:, None]
         member = position // request_len == jnp.arange(requests, dtype=jnp.int32)[None, :]
         limit = jnp.sum(jnp.where(member, counts[None, :], 0), axis=-1, keepdims=True)
@@ -461,17 +540,19 @@
         send, keep, score_c = plain_hidden(
             x_mine, x_got, gain_row, w_gate, w_up, down_row, valid, devices
         )
-    d_mine = sum_and_gather(swap_sum(send, keep, devices), devices)
+    total_d = chip_sum(swap_sum(send, keep, devices), devices)
+    d_mine = chip_gather(total_d, devices)
     d_got = swap_cores(d_mine, devices)
     sources = (x_mine, x_got, d_mine, d_got, gain_row, head_row)
     padded = part + 3 * requests
     if tiled:
+        (first,) = first_rows(256, [embed], [lambda: 0], total_d)
         (d_slices,) = call(
             input_kernel, [struct((total, padded), BF16)],
-            *sources, score_a, score_b, score_c, counts, embed,
-            scalars=(9,), streamed=(10,), flops=2 * flops, room=2 * part * width,
+            *sources, score_a, score_b, score_c, counts, first, embed,
+            scalars=(9,), kept=(10,), streamed=(11,), flops=2 * flops, room=2 * part * width,
             scratch=(
-                pltpu.VMEM((total, width), BF16), pltpu.VMEM((part, width), BF16),
+                pltpu.VMEM((total, width), BF16), pltpu.VMEM((part - 256, width), BF16),
                 pltpu.SemaphoreType.DMA((-(-part // 64),)),
             ),
         )

time: 108 us -> 107 us (level)
  blocking collectives: 42.2 us -> 31.5 us
  waiting for transfers between devices: 9.93 us -> 14.6 us
  starting transfers between devices: 11.5 us -> 14.9 us
    all_to_all x4 -> x3, blocking collectives: 42.2 us -> 31.5 us  [exchange_chips(): lax.all_to_all(blocks, 'dp', split_axis=0, concat_axis=0, axis_index_grou...]
    all_to_all x2, waiting for transfers between devices: 8.58 us -> 13.3 us  [exchange(): return lax.all_to_all(blocks, 'dp', split_axis=0, concat_axis=0, tiled=True)]
    all_to_all x0 -> x1, starting transfers between devices: none -> 3.37 us  [exchange_chips(): lax.all_to_all(blocks, 'dp', split_axis=0, concat_axis=0, axis_index_grou...]
    ppermute x4, waiting for transfers between devices: 1.35 us -> 0.01 us  [swap_cores(): return lax.ppermute(value, 'dp', [(i, i ^ 1) for i in range(devices)])]
    all_to_all x0 -> x1, waiting for transfers between devices: none -> 1.29 us  [exchange_chips(): lax.all_to_all(blocks, 'dp', split_axis=0, concat_axis=0, axis_index_grou...]
    pallas_call x9 -> x12, Pallas kernels: 40.7 us -> 41.5 us  [call(): pl.pallas_call(kernel, out_shape=outs, in_specs=specs, out_specs=[VMEM_SP...]
  transfers between devices with their start and end apart: 6 -> 7, of which waited for: 3 -> 3; matrix products, arithmetic and copies ran while one was open for 1% -> 0% of each run, Pallas kernels for 15% -> 20%
where the time goes in v9:
time: 107 us; the launch traced here: 106 us
  Pallas kernels  41.5 us (39%)
  blocking collectives  31.5 us (29%)
  starting transfers between devices  14.9 us (14%)
  waiting for transfers between devices  14.6 us (14%)
  local copies, waits for them, and re-layouts  1.79 us (2%)
    pallas_call x12, Pallas kernels, call(): pl.pallas_call(kernel, out_shape=outs, in_specs=specs, out_specs=[VMEM_SP...  41.5 us
    all_to_all x3, blocking collectives, exchange_chips(): lax.all_to_all(blocks, 'dp', split_axis=0, concat_axis=0, axis_index_grou...  31.5 us
    all_to_all x2, waiting for transfers between devices, exchange(): return lax.all_to_all(blocks, 'dp', split_axis=0, concat_axis=0, tiled=True)  13.3 us
    all_to_all x2, starting transfers between devices, exchange(): return lax.all_to_all(blocks, 'dp', split_axis=0, concat_axis=0, tiled=True)  10.9 us
    all_to_all x1, starting transfers between devices, exchange_chips(): lax.all_to_all(blocks, 'dp', split_axis=0, concat_axis=0, axis_index_grou...  3.37 us
  transfers between devices with their start and end apart: 7, of which 3 were waited for; matrix products, arithmetic and copies ran while one was open for 0% of the time, Pallas kernels for 20%

profile of v9, /device:TPU:0, one launch (start us, length us, event | category | flops | bytes accessed | tf_op | source)
XLA Modules:
  0.0 105.9 jit_solution(1120857658283701816)
XLA Ops:
  0.6 0.0 copy-start
  0.6 0.9 copy-done
  1.5 1.4 %shard_map.95 = (bf16[16,2,2000]{2,1,0:T(2,128)(2,1)}, f32[2,1]{1,0:T(2,128)S(1)}, f32[2,1]{1,0:T(2,128)S(1)}) custom-call(bf16[2,32000]{1,0:T(2,128)(2,1)S(1)} %copy-done), custom_call_target="tpu_custom_call" | custom-call | bytes 128000 | tf_op jit(solution)/shard_map/pallas_call | solution.py:54
  3.0 7.4 %all-to-all-start = ((bf16[16,2,2000]{2,1,0:T(2,128)(2,1)}), bf16[16,2,2000]{2,1,0:T(2,128)(2,1)S(1)}, u32[]{:S(2)}, u32[]{:S(2)}) async-start(bf16[16,2,2000]{2,1,0:T(2,128)(2,1)} %get-tuple-element.26.refs_1_), calls=%async_computation | async-start | bytes 262144 | tf_op jit(solution)/shard_map/all_to_all | solution.py:21
  10.4 0.0 copy-start.3
  10.4 2.5 %shard_map.96.ready_ref = bf16[256,4096]{1,0:T(8,128)(2,1)S(1)} custom-call(bf16[2000,4096]{1,0:T(8,128)(2,1)} %embed_ref.5, bf16[16,2,2000]{2,1,0:T(2,128)(2,1)} %get-tuple-element.26.refs_1_), custom_call_target="tpu_custom_call" | custom-call | bytes 16512000 | tf_op jit(solution)/shard_map/pallas_call | solution.py:54
  12.9 5.4 %all-to-all-done = bf16[16,2,2000]{2,1,0:T(2,128)(2,1)S(1)} async-done(((bf16[16,2,2000]{2,1,0:T(2,128)(2,1)}), bf16[16,2,2000]{2,1,0:T(2,128)(2,1)S(1)}, u32[]{:S(2)}, u32[]{:S(2)}) %all-to-all-start) | async-done | bytes 128032 | tf_op jit(solution)/shard_map/all_to_all | solution.py:21
  18.3 0.1 reshape.24.slices_ref
  18.4 3.5 %shard_map.98 = (bf16[8,32,256]{2,1,0:T(8,128)(2,1)S(1)}, f32[32,1]{1,0:T(8,128)S(1)}) custom-call(bf16[32,2000]{1,0:T(8,128)(2,1)S(1)} %reshape.24.slices_ref, bf16[256,4096]{1,0:T(8,128)(2,1)S(1)} %shard_map.96.ready_ref, bf16[2000,4096]{1,0:T(8,128)(2,1)} %embed_ref.5, bf16[1,4096]{1,0:T(2,128)(2,1)S(1)} %reshape.25.head_ref), custom_call_target="tpu_custom_call" | custom-call | flops 262144000 | bytes 18617344 | tf_op jit(solution)/shard_map/pallas_call | solution.py:54
  21.9 0.1 collective-permute-start
  22.0 3.5 %shard_map.97 = (f32[8,32,256]{2,1,0:T(8,128)S(1)}, f32[32,1]{1,0:T(8,128)S(1)}) custom-call(bf16[32,2000]{1,0:T(8,128)(2,1)S(1)} %reshape.24.slices_ref, bf16[256,4096]{1,0:T(8,128)(2,1)S(1)} %shard_map.96.ready_ref, bf16[2000,4096]{1,0:T(8,128)(2,1)} %embed_ref.5, bf16[1,4096]{1,0:T(2,128)(2,1)S(1)} %reshape.25.head_ref), custom_call_target="tpu_custom_call" | custom-call | flops 262144000 | bytes 18617344 | tf_op jit(solution)/shard_map/pallas_call | solution.py:54
  25.5 0.0 copy-start.4
  25.5 0.7 add_convert_fusion.1.after_ref
  26.2 3.4 %all-to-all-start.1 = ((bf16[8,32,256]{2,1,0:T(8,128)(2,1)}), bf16[8,32,256]{2,1,0:T(8,128)(2,1)S(1)}, u32[]{:S(2)}, u32[]{:S(2)}) async-start(bf16[8,32,256]{2,1,0:T(8,128)(2,1)} %add_convert_fusion.1.after_ref), calls=%async_computation.1 | async-start | bytes 262144 | tf_op jit(solution)/shard_map/all_to_all | solution.py:26
  29.6 6.6 %shard_map.99.down_ref = f32[1,896]{1,0:T(1,128)S(1)} custom-call(bf16[1,4096]{1,0:T(2,128)(2,1)S(1)} %reshape.25.head_ref, bf16[896,4096]{1,0:T(8,128)(2,1)} %down_ref.1, bf16[8,32,256]{2,1,0:T(8,128)(2,1)} %add_convert_fusion.1.after_ref), custom_call_target="tpu_custom_call" | custom-call | flops 7340032 | bytes 7479296 | tf_op jit(solution)/shard_map/pallas_call | solution.py:54
  36.1 1.3 %all-to-all-done.1 = bf16[8,32,256]{2,1,0:T(8,128)(2,1)S(1)} async-done(((bf16[8,32,256]{2,1,0:T(8,128)(2,1)}), bf16[8,32,256]{2,1,0:T(8,128)(2,1)S(1)}, u32[]{:S(2)}, u32[]{:S(2)}) %all-to-all-start.1) | async-done | bytes 131104 | tf_op jit(solution)/shard_map/all_to_all | solution.py:26
  37.5 11.8 %all_to_all.30.x_ref.mine_ref = bf16[8,32,256]{2,1,0:T(8,128)(2,1)S(1)} all-to-all(bf16[8,32,256]{2,1,0:T(8,128)(2,1)S(1)} %broadcast_in_dim.4), channel_id=1, replica_groups={{0,2,4,6,8,10,12,14},{1,3,5,7,9,11,13,15},{16,18,20,22,24,26,28,30},{17..., dimensions={0} | all-to-all | bytes 262144 | tf_op jit(solution)/shard_map/all_to_all | solution.py:26
  49.3 1.6 %shard_map.100 = (bf16[512,896]{1,0:T(8,128)(2,1)S(1)}, bf16[512,896]{1,0:T(8,128)(2,1)S(1)}) custom-call(bf16[4096,896]{1,0:T(8,128)(2,1)} %gate_ref.3, bf16[4096,896]{1,0:T(8,128)(2,1)} %up_ref.3, bf16[32,256]{1,0:T(8,128)(2,1)S(1)} %reduce_sum.24.refs_2_), custom_call_target="tpu_custom_call" | custom-call | bytes 14696448 | tf_op jit(solution)/shard_map/pallas_call | solution.py:54
  51.0 0.0 copy-start.2
  51.0 3.2 %shard_map.101 = (f32[32,896]{1,0:T(8,128)S(1)}, f32[32,896]{1,0:T(8,128)S(1)}, f32[32,1]{1,0:T(8,128)S(1)}, bf16[1536,896]{1,0:T(8,128)(2,1)S(1)}, bf16[1536,896]{1,0:T(8,128)(2,1)S(1)}) custom-call(bf16[8,32,256]{2,1,0:T(8,128)(2,1)S(1)} %all_to_all.30.x_ref.mine_ref, bf16[1,4096]{1,0:T(2,128)(2,1)S(1)} %reshape.26.gain_ref, bf16[4096,896]{1,0:T(8,128)(2,1)} %gate_ref.3, ...), custom_call_target="tpu_custom_call" | custom-call | flops 234881024 | bytes 16654336 | tf_op jit(solution)/shard_map/pallas_call | solution.py:54
  54.2 6.2 %shard_map.102 = (bf16[8,32,256]{2,1,0:T(8,128)(2,1)S(1)}, f32[32,1]{1,0:T(8,128)S(1)}, bf16[32,896]{1,0:T(8,128)(2,1)S(1)}, bf16[32,896]{1,0:T(8,128)(2,1)S(1)}) custom-call(bf16[8,32,256]{2,1,0:T(8,128)(2,1)S(1)} %collective-permute-done.1.x_ref.got_ref, bf16[1,4096]{1,0:T(2,128)(2,1)S(1)} %reshape.26.gain_ref, bf16[4096,896]{1,0:T(8,128)(2,1)} %gate_ref.3, ...), custom_call_target="tpu_custom_call" | custom-call | flops 234881024 | bytes 15052432 | tf_op jit(solution)/shard_map/pallas_call | solution.py:54
  60.4 0.6 collective-permute-start.2
  60.9 2.2 %shard_map.103 = f32[8,32,256]{2,1,0:T(8,128)S(1)} custom-call(bf16[32,896]{1,0:T(8,128)(2,1)S(1)} %get-tuple-element.36.d_gate_ref, bf16[32,896]{1,0:T(8,128)(2,1)S(1)} %get-tuple-element.37.d_up_ref, bf16[512,896]{1,0:T(8,128)(2,1)S(1)} %get-tuple-element.30.gate_0, bf16[512,896]{1,0:T(8,128)(2,1)S(1)} %get-tuple-element.31.up_0, ...), custom_call_target="tpu_custom_call" | custom-call | flops 234881024 | bytes 7454720 | tf_op jit(solution)/shard_map/pallas_call | solution.py:54
  63.2 9.9 %all_to_all.31 = bf16[8,32,256]{2,1,0:T(8,128)(2,1)S(1)} all-to-all(bf16[8,32,256]{2,1,0:T(8,128)(2,1)S(1)} %add_convert_fusion), channel_id=1, replica_groups={{0,2,4,6,8,10,12,14},{1,3,5,7,9,11,13,15},{16,18,20,22,24,26,28,30},{17..., dimensions={0} | all-to-all | bytes 262144 | tf_op jit(solution)/shard_map/all_to_all | solution.py:26
  73.1 9.8 %all_to_all.32.d_mine_ref = bf16[8,32,256]{2,1,0:T(8,128)(2,1)S(1)} all-to-all(bf16[8,32,256]{2,1,0:T(8,128)(2,1)S(1)} %broadcast_in_dim.5), channel_id=1, replica_groups={{0,2,4,6,8,10,12,14},{1,3,5,7,9,11,13,15},{16,18,20,22,24,26,28,30},{17..., dimensions={0} | all-to-all | bytes 262144 | tf_op jit(solution)/shard_map/all_to_all | solution.py:26
  83.0 1.6 %shard_map.104.ready_ref = bf16[256,4096]{1,0:T(8,128)(2,1)S(1)} custom-call(bf16[2000,4096]{1,0:T(8,128)(2,1)} %embed_ref.5, bf16[32,256]{1,0:T(8,128)(2,1)S(1)} %reduce_sum.25.refs_1_), custom_call_target="tpu_custom_call" | custom-call | bytes 16400384 | tf_op jit(solution)/shard_map/pallas_call | solution.py:54
  84.5 0.0 copy-start.1
  84.6 7.9 %shard_map.105 = bf16[32,2012]{1,0:T(8,128)(2,1)S(1)} custom-call(bf16[8,32,256]{2,1,0:T(8,128)(2,1)S(1)} %all_to_all.30.x_ref.mine_ref, bf16[8,32,256]{2,1,0:T(8,128)(2,1)S(1)} %collective-permute-done.1.x_ref.got_ref, bf16[8,32,256]{2,1,0:T(8,128)(2,1)S(1)} %all_to_all.32.d_mine_ref, bf16[8,32,256]{2,1,0:T(8,128)(2,1)S(1)} %collective-permute-done.3.d_got_ref, ...), custom_call_target="tpu_custom_call" | custom-call | flops 524288000 | bytes 19022224 | tf_op jit(solution)/shard_map/pallas_call | solution.py:54
  92.5 0.8 reshape.27
  93.3 3.5 %all-to-all-start.5 = ((bf16[16,2,2012]{2,1,0:T(2,128)(2,1)}), bf16[16,2,2012]{2,1,0:T(2,128)(2,1)S(1)}, u32[]{:S(2)}, u32[]{:S(2)}) async-start(bf16[16,2,2012]{2,1,0:T(2,128)(2,1)} %reshape.27), calls=%async_computation.5 | async-start | bytes 262144 | tf_op jit(solution)/shard_map/all_to_all | solution.py:21
  96.8 7.9 %all-to-all-done.5.back_ref = bf16[16,2,2012]{2,1,0:T(2,128)(2,1)S(1)} async-done(((bf16[16,2,2012]{2,1,0:T(2,128)(2,1)}), bf16[16,2,2012]{2,1,0:T(2,128)(2,1)S(1)}, u32[]{:S(2)}, u32[]{:S(2)}) %all-to-all-start.5) | async-done | bytes 128800 | tf_op jit(solution)/shard_map/all_to_all | solution.py:21
  104.7 1.2 %shard_map.106 = (bf16[2,32000]{1,0:T(2,128)(2,1)}, f32[1,4]{1,0:T(1,128)}) custom-call(bf16[2,32000]{1,0:T(2,128)(2,1)S(1)} %copy-done.1, f32[2,1]{1,0:T(2,128)S(1)} %get-tuple-element.24.top_ref, f32[2,1]{1,0:T(2,128)S(1)} %get-tuple-element.25.scale_ref, bf16[16,2,2012]{2,1,0:T(2,128)(2,1)S(1)} %all-to-all-done.5.back_ref, ...), custom_call_target="tpu_custom_call" | custom-call | bytes 256800 | tf_op jit(solution)/shard_map/pallas_call | solution.py:54
  (18 shorter events, 0.2 us)
Async XLA Ops:
  0.6 0.9 copy-start
  3.0 15.3 %all-to-all-start = ((bf16[16,2,2000]{2,1,0:T(2,128)(2,1)}), bf16[16,2,2000]{2,1,0:T(2,128)(2,1)S(1)}, u32[]{:S(2)}, u32[]{:S(2)}) async-start(bf16[16,2,2000]{2,1,0:T(2,128)(2,1)} %get-tuple-element.26.refs_1_), calls=%async_computation | async-start | bytes 262144 | tf_op jit(solution)/shard_map/all_to_all | solution.py:21
  10.4 2.5 %copy-start.3 = (bf16[4096]{0:T(1024)(128)(2,1)S(1)}, bf16[4096]{0:T(1024)(128)(2,1)}, u32[]{:S(2)}) copy-start(bf16[4096]{0:T(1024)(128)(2,1)} %param.14) | copy-start | bytes 24580
  21.9 3.6 %collective-permute-start = (bf16[8,32,256]{2,1,0:T(8,128)(2,1)S(1)}, bf16[8,32,256]{2,1,0:T(8,128)(2,1)S(1)}, u32[]{:S(2)}, u32[]{:S(2)}) collective-permute-start(bf16[8,32,256]{2,1,0:T(8,128)(2,1)S(1)} %get-tuple-element.28), channel_id=1, source_target_pairs={{0,1},{1,0},{2,3},{3,2},{4,5},{5,4},{6,7},{7,6},{8,9},{9,8},{10,11... | collective-permute-start | bytes 393224 | tf_op jit(solution)/shard_map/ppermute | solution.py:17
  25.5 23.8 %copy-start.4 = (bf16[4096]{0:T(1024)(128)(2,1)S(1)}, bf16[4096]{0:T(1024)(128)(2,1)}, u32[]{:S(2)}) copy-start(bf16[4096]{0:T(1024)(128)(2,1)} %param.10) | copy-start | bytes 24580
  26.2 11.2 %all-to-all-start.1 = ((bf16[8,32,256]{2,1,0:T(8,128)(2,1)}), bf16[8,32,256]{2,1,0:T(8,128)(2,1)S(1)}, u32[]{:S(2)}, u32[]{:S(2)}) async-start(bf16[8,32,256]{2,1,0:T(8,128)(2,1)} %add_convert_fusion.1.after_ref), calls=%async_computation.1 | async-start | bytes 262144 | tf_op jit(solution)/shard_map/all_to_all | solution.py:26
  49.3 4.9 %collective-permute-start.1 = (bf16[8,32,256]{2,1,0:T(8,128)(2,1)S(1)}, bf16[8,32,256]{2,1,0:T(8,128)(2,1)S(1)}, u32[]{:S(2)}, u32[]{:S(2)}) collective-permute-start(bf16[8,32,256]{2,1,0:T(8,128)(2,1)S(1)} %all_to_all.30.x_ref.mine_ref), channel_id=1, source_target_pairs={{0,1},{1,0},{2,3},{3,2},{4,5},{5,4},{6,7},{7,6},{8,9},{9,8},{10,11... | collective-permute-start | bytes 393224 | tf_op jit(solution)/shard_map/ppermute | solution.py:17
  51.0 3.2 %copy-start.2 = (s32[4]{0:T(128)S(1)}, s32[4]{0:T(128)}, u32[]{:S(2)}) copy-start(s32[4]{0:T(128)} %counts_ref.3) | copy-start | bytes 52
  60.4 2.8 %collective-permute-start.2 = (bf16[8,32,256]{2,1,0:T(8,128)(2,1)S(1)}, bf16[8,32,256]{2,1,0:T(8,128)(2,1)S(1)}, u32[]{:S(2)}, u32[]{:S(2)}) collective-permute-start(bf16[8,32,256]{2,1,0:T(8,128)(2,1)S(1)} %get-tuple-element.40), channel_id=1, source_target_pairs={{0,1},{1,0},{2,3},{3,2},{4,5},{5,4},{6,7},{7,6},{8,9},{9,8},{10,11... | collective-permute-start | bytes 393224 | tf_op jit(solution)/shard_map/ppermute | solution.py:17
  83.0 1.6 %collective-permute-start.3 = (bf16[8,32,256]{2,1,0:T(8,128)(2,1)S(1)}, bf16[8,32,256]{2,1,0:T(8,128)(2,1)S(1)}, u32[]{:S(2)}, u32[]{:S(2)}) collective-permute-start(bf16[8,32,256]{2,1,0:T(8,128)(2,1)S(1)} %all_to_all.32.d_mine_ref), channel_id=1, source_target_pairs={{0,1},{1,0},{2,3},{3,2},{4,5},{5,4},{6,7},{7,6},{8,9},{9,8},{10,11... | collective-permute-start | bytes 393224 | tf_op jit(solution)/shard_map/ppermute | solution.py:17
  84.5 20.1 %copy-start.1 = (bf16[2,32000]{1,0:T(2,128)(2,1)S(1)}, bf16[2,32000]{1,0:T(2,128)(2,1)}, u32[]{:S(2)}) copy-start(bf16[2,32000]{1,0:T(2,128)(2,1)} %logits_ref.3) | copy-start | bytes 384004
  93.3 11.4 %all-to-all-start.5 = ((bf16[16,2,2012]{2,1,0:T(2,128)(2,1)}), bf16[16,2,2012]{2,1,0:T(2,128)(2,1)S(1)}, u32[]{:S(2)}, u32[]{:S(2)}) async-start(bf16[16,2,2012]{2,1,0:T(2,128)(2,1)} %reshape.27), calls=%async_computation.5 | async-start | bytes 262144 | tf_op jit(solution)/shard_map/all_to_all | solution.py:21

commit v10 on v9

--- a/solution.py
+++ b/solution.py
@@ -217,25 +217,17 @@
         out_ref[:, i * rows : (i + 1) * rows] = part[:1]
 
 
-def weight_rows(j, own, ready, gate, up):
-    skip = ready[0].shape[0] // own if ready else 0
-    if j < skip:
-        return ready, slice(j * own, (j + 1) * own)
-    return (gate, up), slice((j - skip) * own, (j - skip + 1) * own)
-
-
-def forward_half(x_ref, gain_ref, gate_ref, up_ref, gate, up, sems, half, sums, ready=()):
+def forward_half(x_ref, gain_ref, gate_ref, up_ref, gate, up, sems, half, sums):
     chips, _, own = x_ref.shape
-    skip = ready[0].shape[0] // own if ready else 0
 
     def rows(j):
         return span((half * chips + j) * own, own)
 
     stream = Stream([
         pltpu.make_async_copy(
-            source.at[rows(j)], target.at[pl.ds((j - skip) * own, own)], sems.at[k, j]
-        )
-        for j in range(skip, chips)
+            source.at[rows(j)], target.at[pl.ds(j * own, own)], sems.at[k, j]
+        )
+        for j in range(chips)
         for k, (source, target) in enumerate(((gate_ref, gate), (up_ref, up)))
     ])
     a, b, squares = sums
@@ -245,39 +237,35 @@
         squares = squares + jnp.sum(x * x, axis=-1, keepdims=True)
         scaled.append((x * gain_ref[:, rows(j)].astype(F32)).astype(BF16))
     for j in range(chips):
-        (g, u), r = weight_rows(j, own, ready, gate, up)
-        if j >= skip:
-            stream.wait(2 * (j - skip + 1))
-        a = a + jnp.dot(scaled[j], g[r], preferred_element_type=F32)
-        b = b + jnp.dot(scaled[j], u[r], preferred_element_type=F32)
+        r = slice(j * own, (j + 1) * own)
+        stream.wait(2 * (j + 1))
+        a = a + jnp.dot(scaled[j], gate[r], preferred_element_type=F32)
+        b = b + jnp.dot(scaled[j], up[r], preferred_element_type=F32)
     return a, b, squares
 
 
-def backward_half(d_gate, d_up, gate, up, out_ref, ready=()):
+def backward_half(d_gate, d_up, gate, up, out_ref):
     chips, _, own = out_ref.shape
     contract = (((1,), (1,)), ((), ()))
     for j in range(chips):
-        (g, u), r = weight_rows(j, own, ready, gate, up)
-        part = lax.dot_general(d_gate, g[r], contract, preferred_element_type=F32)
-        part += lax.dot_general(d_up, u[r], contract, preferred_element_type=F32)
+        r = slice(j * own, (j + 1) * own)
+        part = lax.dot_general(d_gate, gate[r], contract, preferred_element_type=F32)
+        part += lax.dot_general(d_up, up[r], contract, preferred_element_type=F32)
         out_ref[j] = part.astype(out_ref.dtype)
 
 
 def first_kernel(
-    x_ref, gain_ref, gate_ref, up_ref, gate_0, up_0,
-    a_ref, b_ref, squares_ref, gate, up, sems,
+    x_ref, gain_ref, gate_ref, up_ref, a_ref, b_ref, squares_ref, gate, up, sems
 ):
     zeros = jnp.zeros(a_ref.shape, F32)
     sums = (zeros, zeros, jnp.zeros(squares_ref.shape, F32))
-    sums = forward_half(
-        x_ref, gain_ref, gate_ref, up_ref, gate, up, sems, this_core(), sums, (gate_0, up_0)
-    )
+    sums = forward_half(x_ref, gain_ref, gate_ref, up_ref, gate, up, sems, this_core(), sums)
     a_ref[...], b_ref[...], squares_ref[...] = sums
 
 
 def second_kernel(
     x_ref, gain_ref, gate_ref, up_ref, a_ref, b_ref, squares_ref, down_ref, counts_ref,
-    send_ref, score_ref, d_gate_ref, d_up_ref, gate, up, sems,
+    send_ref, score_ref, inv_ref, d_gate_ref, d_up_ref, gate, up, sems,
 ):
     total = x_ref.shape[1]
     width = gate_ref.shape[0]
@@ -286,6 +274,7 @@
         x_ref, gain_ref, gate_ref, up_ref, gate, up, sems, 1 - this_core(), sums
     )
     inv = lax.rsqrt(squares / width + 1e-05)
+    inv_ref[...] = inv
     a, b = a * inv, b * inv
     sigma = jax.nn.sigmoid(a)
     active = a * sigma
@@ -300,89 +289,134 @@
     backward_half(d_gate, d_up, gate, up, send_ref)
 
 
-def third_kernel(d_gate_ref, d_up_ref, gate_0, up_0, gate_ref, up_ref, keep_ref):
-    d_gate, d_up = d_gate_ref[...], d_up_ref[...]
-    backward_half(d_gate, d_up, gate_ref, up_ref, keep_ref, (gate_0, up_0))
+def third_kernel(d_gate_ref, d_up_ref, gate_ref, up_ref, keep_ref):
+    backward_half(d_gate_ref[...], d_up_ref[...], gate_ref, up_ref, keep_ref)
+
+
+def table_steps(lhs_ref, embed_ref, ready, table, sems, columns, first_rows, emit):
+    voc, skip = embed_ref.shape[0], ready.shape[0]
+    tile, fine = 256, 128
+    contract = (((1,), (1,)), ((), ()))
+
+    def copy(start, size):
+        source = embed_ref.at[pl.ds(start, size), columns]
+        return pltpu.make_async_copy(
+            source, table.at[pl.ds(start - skip, size)], sems.at[start // fine]
+        )
+
+    def product(weights):
+        return lax.dot_general(lhs_ref[...], weights, contract, preferred_element_type=F32)
+
+    for start in range(skip, voc, fine):
+        copy(start, min(fine, voc - start)).start()
+    emit(pl.ds(0, skip), product(first_rows()))
+
+    def step(j, _):
+        start = pl.multiple_of(j * tile, tile)
+        for i in range(0, tile, fine):
+            copy(pl.multiple_of(start + i, fine), fine).wait()
+        rows = pl.ds(pl.multiple_of(start - skip, tile), tile)
+        emit(pl.ds(start, tile), product(table[rows, :]))
+        return 0
+
+    whole = voc // tile
+    lax.fori_loop(skip // tile, whole, step, 0)
+    if voc % tile:
+        last = whole * tile
+        for start in range(last, voc, fine):
+            copy(start, min(fine, voc - start)).wait()
+        emit(pl.ds(last, voc - last), product(table[last - skip :, :]))
+
+
+def early_kernel(
+    mine_ref, got_ref, head_ref, after_ref, embed_ref,
+    x_out, head_out, ready, lhs_ref, table, sems, ready_sem,
+):
+    chips, total, own = mine_ref.shape
+    del after_ref
+    core = this_core()
+    bring = pltpu.make_async_copy(embed_ref.at[pl.ds(0, ready.shape[0])], ready, ready_sem)
+    bring.start()
+    for ref, half in ((mine_ref, core), (got_ref, 1 - core)):
+        for j in range(chips):
+            lhs_ref[:total, span((half * chips + j) * own, own)] = ref[j]
+    extra = (lhs_ref.shape[0] - total, head_ref.shape[1])
+    lhs_ref[total:, :] = jnp.broadcast_to(head_ref[...].astype(F32), extra).astype(BF16)
+
+    def rows():
+        bring.wait()
+        return ready[...]
+
+    def emit(rows, part):
+        x_out[:, rows] = part[:total]
+        head_out[:, rows] = part[total : total + 1]
+
+    table_steps(
+        lhs_ref, embed_ref, ready, table, sems, pl.ds(0, embed_ref.shape[1]), rows, emit
+    )
+
+
+def scale_half(d_ref, gain_ref, half, lhs_ref):
+    chips, _, own = d_ref.shape
+    for j in range(chips):
+        gain = gain_ref[:, span((half * chips + j) * own, own)].astype(F32)
+        lhs_ref[:, j * own : (j + 1) * own] = (d_ref[j].astype(F32) * gain).astype(BF16)
+
+
+def own_kernel(d_ref, gain_ref, ready_ref, embed_ref, out_ref, lhs_ref, table, sems):
+    chips, _, own = d_ref.shape
+    half = this_core()
+    columns = span(half * chips * own, chips * own)
+    scale_half(d_ref, gain_ref, half, lhs_ref)
+
+    def emit(rows, part):
+        out_ref[:, rows] = part
+
+    table_steps(
+        lhs_ref, embed_ref, ready_ref, table, sems, columns,
+        lambda: ready_ref[:, columns], emit,
+    )
 
 
 def input_kernel(
-    mine_ref, got_ref, d_mine_ref, d_got_ref, gain_ref, head_ref,
+    mine_ref, got_ref, d_mine_ref, d_got_ref, gain_ref, own_ref, x_ref, head_ref, inv_ref,
     score_a_ref, score_b_ref, score_c_ref, counts_ref, ready_ref, embed_ref,
-    out_ref, dx_ref, table, sems,
+    out_ref, lhs_ref, table, sems,
 ):
     chips, total, own = mine_ref.shape
     voc = embed_ref.shape[0]
     requests = counts_ref.shape[0]
-    width = 2 * chips * own
     core = this_core()
-    ready = ready_ref.shape[0]
-    tile, fine = 256, 64
-
-    def copy(start, size):
-        return pltpu.make_async_copy(
-            embed_ref.at[pl.ds(start, size)],
-            table.at[pl.ds(start - ready, size)],
-            sems.at[start // fine],
-        )
-
-    pieces_of = range(ready, voc, fine)
-    for start in pieces_of:
-        copy(start, min(fine, voc - start)).start()
-    sources = ((mine_ref, d_mine_ref, core), (got_ref, d_got_ref, 1 - core))
-    squares = jnp.zeros((total, 1), F32)
+    half = 1 - core
+    columns = span(half * chips * own, chips * own)
+    scale_half(d_got_ref, gain_ref, half, lhs_ref)
     dots = jnp.zeros((total, 1), F32)
-    for x_ref, d_ref, half in sources:
+    for x, d, h in ((mine_ref, d_mine_ref, core), (got_ref, d_got_ref, half)):
         for j in range(chips):
-            x = x_ref[j].astype(F32)
-            g = d_ref[j].astype(F32) * gain_ref[:, span((half * chips + j) * own, own)].astype(F32)
-            squares += jnp.sum(x * x, axis=-1, keepdims=True)
-            dots += jnp.sum(g * x, axis=-1, keepdims=True)
-    inv = lax.rsqrt(squares / width + 1e-05)
-    mean = dots / width
+            gain = gain_ref[:, span((h * chips + j) * own, own)].astype(F32)
+            g = d[j].astype(F32) * gain
+            dots += jnp.sum(g * x[j].astype(F32), axis=-1, keepdims=True)
+    inv = inv_ref[...]
+    weight = inv * inv * inv * (dots / (2 * chips * own))
     valid, request = valid_column(counts_ref, total)
-    for x_ref, d_ref, half in sources:
-        for j in range(chips):
-            columns = span((half * chips + j) * own, own)
-            x = x_ref[j].astype(F32)
-            g = d_ref[j].astype(F32) * gain_ref[:, columns].astype(F32)
-            dx = inv * g - x * inv * inv * inv * mean
-            dx_ref[:, columns] = (dx + valid * head_ref[:, columns].astype(F32)).astype(BF16)
     score = valid * (score_a_ref[...] + score_b_ref[...] + score_c_ref[...])
     member = request == lax.broadcasted_iota(jnp.int32, (total, requests), 1)
     value = jnp.sum(jnp.where(member, score, 0.0), axis=0, keepdims=True)
-    pieces = []
-    for _ in range(3):
+    for i in range(3):
         piece = value.astype(BF16).astype(F32)
-        pieces.append(piece)
-        value = value - piece
-    for i, piece in enumerate(pieces):
         start = voc + i * requests
         spread = jnp.broadcast_to(piece, (total, requests)).astype(BF16)
         out_ref[:, start : start + requests] = spread
-    contract = (((1,), (1,)), ((), ()))
-
-    def product(weights):
-        return lax.dot_general(
-            dx_ref[...], weights, contract, preferred_element_type=F32
-        ).astype(BF16)
-
-    out_ref[:, :ready] = product(ready_ref[...])
-
-    def step(j, _):
-        start = pl.multiple_of(j * tile, tile)
-        for i in range(0, tile, fine):
-            copy(pl.multiple_of(start + i, fine), fine).wait()
-        rows = pl.ds(pl.multiple_of(start - ready, tile), tile)
-        out_ref[:, pl.ds(start, tile)] = product(table[rows, :])
-        return 0
-
-    whole = voc // tile
-    lax.fori_loop(ready // tile, whole, step, 0)
-    if voc % tile:
-        last = whole * tile
-        for start in range(last, voc, fine):
-            copy(start, min(fine, voc - start)).wait()
-        out_ref[:, last:voc] = product(table[last - ready :, :])
+        value = value - piece
+
+    def emit(rows, part):
+        d_probs = inv * (own_ref[:, rows] + part) - weight * x_ref[:, rows]
+        out_ref[:, rows] = (d_probs + valid * head_ref[:, rows]).astype(BF16)
+
+    table_steps(
+        lhs_ref, embed_ref, ready_ref, table, sems, columns,
+        lambda: ready_ref[:, columns], emit,
+    )
 
 
 def swap_sum(send, keep, devices):
@@ -509,28 +543,25 @@
     x_mine = chip_gather(total_x, devices)
     x_got = swap_cores(x_mine, devices)
     if tiled:
-        weights = [w_gate, w_up]
-        starts = [lambda: this_core() * (width // 2)] * 2
-        gate_0, up_0 = first_rows(2 * own, weights, starts, total_x)
         wide = struct((total, hidden), F32)
-        weight, rest = (width // 2, hidden), (width // 2 - 2 * own, hidden)
+        weight = (width // 2, hidden)
         sems = pltpu.SemaphoreType.DMA((2, chips))
         args = dict(streamed=(2, 3), flops=2 * total * hidden * width, room=2 * width * hidden)
         a, b, squares, gate, up = call(
             first_kernel,
-            [wide, wide, column, pltpu.VMEM(rest, BF16), pltpu.VMEM(rest, BF16)],
-            x_mine, gain_row, w_gate, w_up, gate_0, up_0, scratch=(sems,), kept=(4, 5), **args,
+            [wide, wide, column, pltpu.VMEM(weight, BF16), pltpu.VMEM(weight, BF16)],
+            x_mine, gain_row, w_gate, w_up, scratch=(sems,), **args,
         )
         narrow = struct((total, hidden), BF16)
-        send, score_c, d_gate, d_up = call(
-            second_kernel, [struct(half, BF16), column, narrow, narrow],
+        send, score_c, inv, d_gate, d_up = call(
+            second_kernel, [struct(half, BF16), column, column, narrow, narrow],
             x_got, gain_row, w_gate, w_up, a, b, squares, down_row, counts,
             scratch=(pltpu.VMEM(weight, BF16), pltpu.VMEM(weight, BF16), sems),
             scalars=(8,), **args,
         )
         (keep,) = call(
-            third_kernel, [struct(half, F32)], d_gate, d_up, gate_0, up_0, gate, up,
-            kept=(2, 3, 4, 5), flops=2 * total * hidden * width,
+            third_kernel, [struct(half, F32)], d_gate, d_up, gate, up,
+            kept=(2, 3), flops=2 * total * hidden * width,
         )
     else:
         position = jnp.arange(total, dtype=jnp.int32)[:, None]
@@ -540,24 +571,50 @@
         send, keep, score_c = plain_hidden(
             x_mine, x_got, gain_row, w_gate, w_up, down_row, valid, devices
         )
-    total_d = chip_sum(swap_sum(send, keep, devices), devices)
+    summed_d = swap_sum(send, keep, devices)
+    total_d = chip_sum(summed_d, devices)
+    padded = part + 3 * requests
+    if tiled:
+        ready = 256
+        products = struct((total, part), F32)
+        sems = pltpu.SemaphoreType.DMA((-(-part // 128),))
+        x_product, head_product, first = call(
+            early_kernel,
+            [products, struct((1, part), F32), pltpu.VMEM((ready, width), BF16)],
+            x_mine, x_got, head_row, summed_d, embed,
+            streamed=(4,), flops=2 * flops, room=2 * part * width,
+            scratch=(
+                pltpu.VMEM((total + 16, width), BF16), pltpu.VMEM((part - ready, width), BF16),
+                sems, pltpu.SemaphoreType.DMA,
+            ),
+        )
+        total_d, x_product, head_product, first = lax.optimization_barrier(
+            (total_d, x_product, head_product, first)
+        )
     d_mine = chip_gather(total_d, devices)
     d_got = swap_cores(d_mine, devices)
-    sources = (x_mine, x_got, d_mine, d_got, gain_row, head_row)
-    padded = part + 3 * requests
-    if tiled:
-        (first,) = first_rows(256, [embed], [lambda: 0], total_d)
+    if tiled:
+        args = dict(
+            flops=flops, room=part * width,
+            scratch=(
+                pltpu.VMEM((total, width // 2), BF16),
+                pltpu.VMEM((part - ready, width // 2), BF16), sems,
+            ),
+        )
+        (own_product,) = call(
+            own_kernel, [products], d_mine, gain_row, first, embed,
+            kept=(2,), streamed=(3,), **args,
+        )
         (d_slices,) = call(
             input_kernel, [struct((total, padded), BF16)],
-            *sources, score_a, score_b, score_c, counts, first, embed,
-            scalars=(9,), kept=(10,), streamed=(11,), flops=2 * flops, room=2 * part * width,
-            scratch=(
-                pltpu.VMEM((total, width), BF16), pltpu.VMEM((part - 256, width), BF16),
-                pltpu.SemaphoreType.DMA((-(-part // 64),)),
-            ),
+            x_mine, x_got, d_mine, d_got, gain_row, own_product, x_product, head_product, inv,
+            score_a, score_b, score_c, counts, first, embed,
+            scalars=(12,), kept=(13,), streamed=(14,), **args,
         )
     else:
-        d_slices = plain_input(*sources, valid, embed)
+        d_slices = plain_input(
+            x_mine, x_got, d_mine, d_got, gain_row, head_row, valid, embed
+        )
         score = jnp.where(member, valid * (score_a + score_c), 0.0)
         extra = split3(jnp.sum(score, axis=0)).reshape(1, requests * 3)
         extra = jnp.broadcast_to(extra, (total, requests * 3))

time: 107 us -> 116 us (1.084)
  Pallas kernels: 41.5 us -> 53 us
  blocking collectives: 31.5 us -> 24.9 us
  starting transfers between devices: 14.9 us -> 18.3 us
    pallas_call x12, Pallas kernels: 41.5 us -> 53 us  [call(): pl.pallas_call(kernel, out_shape=outs, in_specs=specs, out_specs=[VMEM_SP...]
    all_to_all x3 -> x2, blocking collectives: 31.5 us -> 24.9 us  [exchange_chips(): lax.all_to_all(blocks, 'dp', split_axis=0, concat_axis=0, axis_index_grou...]
    all_to_all x1 -> x2, starting transfers between devices: 3.37 us -> 6.74 us  [exchange_chips(): lax.all_to_all(blocks, 'dp', split_axis=0, concat_axis=0, axis_index_grou...]
  transfers between devices with their start and end apart: 7 -> 8, of which waited for: 3 -> 3; matrix products, arithmetic and copies ran while one was open for 0% -> 0% of each run, Pallas kernels for 20% -> 31%
where the time goes in v10:
time: 116 us; the launch traced here: 115 us
  Pallas kernels  53 us (46%)
  blocking collectives  24.9 us (21%)
  starting transfers between devices  18.3 us (16%)
  waiting for transfers between devices  14.6 us (13%)
  local copies, waits for them, and re-layouts  1.81 us (2%)
  other arithmetic  1.46 us (1%)
    pallas_call x12, Pallas kernels, call(): pl.pallas_call(kernel, out_shape=outs, in_specs=specs, out_specs=[VMEM_SP...  53 us
    all_to_all x2, blocking collectives, exchange_chips(): lax.all_to_all(blocks, 'dp', split_axis=0, concat_axis=0, axis_index_grou...  24.9 us
    all_to_all x2, waiting for transfers between devices, exchange(): return lax.all_to_all(blocks, 'dp', split_axis=0, concat_axis=0, tiled=True)  13.3 us
    all_to_all x2, starting transfers between devices, exchange(): return lax.all_to_all(blocks, 'dp', split_axis=0, concat_axis=0, tiled=True)  10.9 us
    all_to_all x2, starting transfers between devices, exchange_chips(): lax.all_to_all(blocks, 'dp', split_axis=0, concat_axis=0, axis_index_grou...  6.74 us
  transfers between devices with their start and end apart: 8, of which 3 were waited for; matrix products, arithmetic and copies ran while one was open for 0% of the time, Pallas kernels for 31%

profile of v10, /device:TPU:0, one launch (start us, length us, event | category | flops | bytes accessed | tf_op | source)
XLA Modules:
  0.0 114.9 jit_solution(13714861186897812896)
XLA Ops:
  0.6 0.0 copy-start
  0.6 0.9 copy-done
  1.5 1.4 %shard_map.95 = (bf16[16,2,2000]{2,1,0:T(2,128)(2,1)}, f32[2,1]{1,0:T(2,128)S(1)}, f32[2,1]{1,0:T(2,128)S(1)}) custom-call(bf16[2,32000]{1,0:T(2,128)(2,1)S(1)} %copy-done), custom_call_target="tpu_custom_call" | custom-call | bytes 128000 | tf_op jit(solution)/shard_map/pallas_call | solution.py:54
  3.0 7.4 %all-to-all-start = ((bf16[16,2,2000]{2,1,0:T(2,128)(2,1)}), bf16[16,2,2000]{2,1,0:T(2,128)(2,1)S(1)}, u32[]{:S(2)}, u32[]{:S(2)}) async-start(bf16[16,2,2000]{2,1,0:T(2,128)(2,1)} %get-tuple-element.32.refs_1_), calls=%async_computation | async-start | bytes 262144 | tf_op jit(solution)/shard_map/all_to_all | solution.py:21
  10.4 0.0 copy-start.3
  10.4 2.5 %shard_map.96.ready_ref = bf16[256,4096]{1,0:T(8,128)(2,1)S(1)} custom-call(bf16[2000,4096]{1,0:T(8,128)(2,1)} %embed_ref.9, bf16[16,2,2000]{2,1,0:T(2,128)(2,1)} %get-tuple-element.32.refs_1_), custom_call_target="tpu_custom_call" | custom-call | bytes 16512000 | tf_op jit(solution)/shard_map/pallas_call | solution.py:54
  12.9 5.4 %all-to-all-done = bf16[16,2,2000]{2,1,0:T(2,128)(2,1)S(1)} async-done(((bf16[16,2,2000]{2,1,0:T(2,128)(2,1)}), bf16[16,2,2000]{2,1,0:T(2,128)(2,1)S(1)}, u32[]{:S(2)}, u32[]{:S(2)}) %all-to-all-start) | async-done | bytes 128032 | tf_op jit(solution)/shard_map/all_to_all | solution.py:21
  18.3 0.1 reshape.24.slices_ref
  18.4 3.5 %shard_map.98 = (bf16[8,32,256]{2,1,0:T(8,128)(2,1)S(1)}, f32[32,1]{1,0:T(8,128)S(1)}) custom-call(bf16[32,2000]{1,0:T(8,128)(2,1)S(1)} %reshape.24.slices_ref, bf16[256,4096]{1,0:T(8,128)(2,1)S(1)} %shard_map.96.ready_ref, bf16[2000,4096]{1,0:T(8,128)(2,1)} %embed_ref.9, bf16[1,4096]{1,0:T(2,128)(2,1)S(1)} %reshape.25.head_ref), custom_call_target="tpu_custom_call" | custom-call | flops 262144000 | bytes 18617344 | tf_op jit(solution)/shard_map/pallas_call | solution.py:54
  21.9 0.1 collective-permute-start
  22.0 3.5 %shard_map.97 = (f32[8,32,256]{2,1,0:T(8,128)S(1)}, f32[32,1]{1,0:T(8,128)S(1)}) custom-call(bf16[32,2000]{1,0:T(8,128)(2,1)S(1)} %reshape.24.slices_ref, bf16[256,4096]{1,0:T(8,128)(2,1)S(1)} %shard_map.96.ready_ref, bf16[2000,4096]{1,0:T(8,128)(2,1)} %embed_ref.9, bf16[1,4096]{1,0:T(2,128)(2,1)S(1)} %reshape.25.head_ref), custom_call_target="tpu_custom_call" | custom-call | flops 262144000 | bytes 18617344 | tf_op jit(solution)/shard_map/pallas_call | solution.py:54
  25.5 0.7 add_convert_fusion.1.after_ref
  26.2 3.4 %all-to-all-start.1 = ((bf16[8,32,256]{2,1,0:T(8,128)(2,1)}), bf16[8,32,256]{2,1,0:T(8,128)(2,1)S(1)}, u32[]{:S(2)}, u32[]{:S(2)}) async-start(bf16[8,32,256]{2,1,0:T(8,128)(2,1)} %add_convert_fusion.1.after_ref), calls=%async_computation.1 | async-start | bytes 262144 | tf_op jit(solution)/shard_map/all_to_all | solution.py:26
  29.6 6.6 %shard_map.99.down_ref = f32[1,896]{1,0:T(1,128)S(1)} custom-call(bf16[1,4096]{1,0:T(2,128)(2,1)S(1)} %reshape.25.head_ref, bf16[896,4096]{1,0:T(8,128)(2,1)} %down_ref.1, bf16[8,32,256]{2,1,0:T(8,128)(2,1)} %add_convert_fusion.1.after_ref), custom_call_target="tpu_custom_call" | custom-call | flops 7340032 | bytes 7479296 | tf_op jit(solution)/shard_map/pallas_call | solution.py:54
  36.2 1.3 %all-to-all-done.1 = bf16[8,32,256]{2,1,0:T(8,128)(2,1)S(1)} async-done(((bf16[8,32,256]{2,1,0:T(8,128)(2,1)}), bf16[8,32,256]{2,1,0:T(8,128)(2,1)S(1)}, u32[]{:S(2)}, u32[]{:S(2)}) %all-to-all-start.1) | async-done | bytes 131104 | tf_op jit(solution)/shard_map/all_to_all | solution.py:26
  37.5 11.8 %all_to_all.30.x_ref.mine_ref = bf16[8,32,256]{2,1,0:T(8,128)(2,1)S(1)} all-to-all(bf16[8,32,256]{2,1,0:T(8,128)(2,1)S(1)} %broadcast_in_dim.4), channel_id=1, replica_groups={{0,2,4,6,8,10,12,14},{1,3,5,7,9,11,13,15},{16,18,20,22,24,26,28,30},{17..., dimensions={0} | all-to-all | bytes 262144 | tf_op jit(solution)/shard_map/all_to_all | solution.py:26
  49.3 0.0 copy-start.2
  49.4 3.5 %shard_map.100 = (f32[32,896]{1,0:T(8,128)S(1)}, f32[32,896]{1,0:T(8,128)S(1)}, f32[32,1]{1,0:T(8,128)S(1)}, bf16[2048,896]{1,0:T(8,128)(2,1)S(1)}, bf16[2048,896]{1,0:T(8,128)(2,1)S(1)}) custom-call(bf16[8,32,256]{2,1,0:T(8,128)(2,1)S(1)} %all_to_all.30.x_ref.mine_ref, bf16[1,4096]{1,0:T(2,128)(2,1)S(1)} %reshape.26.gain_ref, bf16[4096,896]{1,0:T(8,128)(2,1)} %gate_ref.3, ...), custom_call_target="tpu_custom_call" | custom-call | flops 234881024 | bytes 14819328 | tf_op jit(solution)/shard_map/pallas_call | solution.py:54
  52.9 6.2 %shard_map.101 = (bf16[8,32,256]{2,1,0:T(8,128)(2,1)S(1)}, f32[32,1]{1,0:T(8,128)S(1)}, f32[32,1]{1,0:T(8,128)S(1)}, bf16[32,896]{1,0:T(8,128)(2,1)S(1)}, bf16[32,896]{1,0:T(8,128)(2,1)S(1)}) custom-call(bf16[8,32,256]{2,1,0:T(8,128)(2,1)S(1)} %collective-permute-done.1.x_ref.got_ref, bf16[1,4096]{1,0:T(2,128)(2,1)S(1)} %reshape.26.gain_ref, ...), custom_call_target="tpu_custom_call" | custom-call | flops 234881024 | bytes 15052432 | tf_op jit(solution)/shard_map/pallas_call | solution.py:54
  59.1 0.6 collective-permute-start.2
  59.6 2.2 %shard_map.102 = f32[8,32,256]{2,1,0:T(8,128)S(1)} custom-call(bf16[32,896]{1,0:T(8,128)(2,1)S(1)} %get-tuple-element.40.d_gate_ref, bf16[32,896]{1,0:T(8,128)(2,1)S(1)} %get-tuple-element.41.d_up_ref, bf16[2048,896]{1,0:T(8,128)(2,1)S(1)} %get-tuple-element.42.gate_ref, bf16[2048,896]{1,0:T(8,128)(2,1)S(1)} %get-tuple-element.43.up_ref), custom_call_target="tpu_custom_call" | custom-call | flops 234881024 | bytes 7454720 | tf_op jit(solution)/shard_map/pallas_call | solution.py:54
  61.9 0.7 add_convert_fusion.after_ref
  62.6 3.4 %all-to-all-start.3 = ((bf16[8,32,256]{2,1,0:T(8,128)(2,1)}), bf16[8,32,256]{2,1,0:T(8,128)(2,1)S(1)}, u32[]{:S(2)}, u32[]{:S(2)}) async-start(bf16[8,32,256]{2,1,0:T(8,128)(2,1)} %add_convert_fusion.after_ref), calls=%async_computation.3 | async-start | bytes 262144 | tf_op jit(solution)/shard_map/all_to_all | solution.py:26
  66.0 12.6 %shard_map.103 = (f32[32,2000]{1,0:T(8,128)S(1)}, f32[1,2000]{1,0:T(1,128)S(1)}, bf16[256,4096]{1,0:T(8,128)(2,1)S(1)}) custom-call(bf16[8,32,256]{2,1,0:T(8,128)(2,1)S(1)} %all_to_all.30.x_ref.mine_ref, bf16[8,32,256]{2,1,0:T(8,128)(2,1)S(1)} %collective-permute-done.1.x_ref.got_ref, bf16[1,4096]{1,0:T(2,128)(2,1)S(1)} %reshape.25.head_ref, ...), custom_call_target="tpu_custom_call" | custom-call | flops 524288000 | bytes 16785408 | tf_op jit(solution)/shard_map/pallas_call | solution.py:54
  78.7 13.1 %all_to_all.31.d_ref.d_mine_ref = bf16[8,32,256]{2,1,0:T(8,128)(2,1)S(1)} all-to-all(bf16[8,32,256]{2,1,0:T(8,128)(2,1)S(1)} %broadcast_in_dim.5), channel_id=1, replica_groups={{0,2,4,6,8,10,12,14},{1,3,5,7,9,11,13,15},{16,18,20,22,24,26,28,30},{17..., dimensions={0} | all-to-all | bytes 262144 | tf_op jit(solution)/shard_map/all_to_all | solution.py:26
  91.8 4.5 %shard_map.104.own_ref = f32[32,2000]{1,0:T(8,128)S(1)} custom-call(bf16[8,32,256]{2,1,0:T(8,128)(2,1)S(1)} %all_to_all.31.d_ref.d_mine_ref, bf16[1,4096]{1,0:T(2,128)(2,1)S(1)} %reshape.26.gain_ref, bf16[256,4096]{1,0:T(8,128)(2,1)S(1)} %get-tuple-element.49.ready_ref, bf16[2000,4096]{1,0:T(8,128)(2,1)} %embed_ref.9), custom_call_target="tpu_custom_call" | custom-call | flops 262144000 | bytes 18620416 | tf_op jit(solution)/shard_map/pallas_call | solution.py:54
  96.3 0.0 copy-start.1
  96.3 5.2 %shard_map.105 = bf16[32,2012]{1,0:T(8,128)(2,1)S(1)} custom-call(bf16[8,32,256]{2,1,0:T(8,128)(2,1)S(1)} %all_to_all.30.x_ref.mine_ref, bf16[8,32,256]{2,1,0:T(8,128)(2,1)S(1)} %collective-permute-done.1.x_ref.got_ref, bf16[8,32,256]{2,1,0:T(8,128)(2,1)S(1)} %all_to_all.31.d_ref.d_mine_ref, bf16[8,32,256]{2,1,0:T(8,128)(2,1)S(1)} %collective-permute-done.3.d_got_ref, ...), custom_call_target="tpu_custom_call" | custom-call | flops 262144000 | bytes 19534160 | tf_op jit(solution)/shard_map/pallas_call | solution.py:54
  101.5 0.8 reshape.27
  102.2 3.5 %all-to-all-start.5 = ((bf16[16,2,2012]{2,1,0:T(2,128)(2,1)}), bf16[16,2,2012]{2,1,0:T(2,128)(2,1)S(1)}, u32[]{:S(2)}, u32[]{:S(2)}) async-start(bf16[16,2,2012]{2,1,0:T(2,128)(2,1)} %reshape.27), calls=%async_computation.5 | async-start | bytes 262144 | tf_op jit(solution)/shard_map/all_to_all | solution.py:21
  105.8 7.9 %all-to-all-done.5.back_ref = bf16[16,2,2012]{2,1,0:T(2,128)(2,1)S(1)} async-done(((bf16[16,2,2012]{2,1,0:T(2,128)(2,1)}), bf16[16,2,2012]{2,1,0:T(2,128)(2,1)S(1)}, u32[]{:S(2)}, u32[]{:S(2)}) %all-to-all-start.5) | async-done | bytes 128800 | tf_op jit(solution)/shard_map/all_to_all | solution.py:21
  113.7 1.2 %shard_map.106 = (bf16[2,32000]{1,0:T(2,128)(2,1)}, f32[1,4]{1,0:T(1,128)}) custom-call(bf16[2,32000]{1,0:T(2,128)(2,1)S(1)} %copy-done.1, f32[2,1]{1,0:T(2,128)S(1)} %get-tuple-element.30.top_ref, f32[2,1]{1,0:T(2,128)S(1)} %get-tuple-element.31.scale_ref, bf16[16,2,2012]{2,1,0:T(2,128)(2,1)S(1)} %all-to-all-done.5.back_ref, ...), custom_call_target="tpu_custom_call" | custom-call | bytes 256800 | tf_op jit(solution)/shard_map/pallas_call | solution.py:54
  (19 shorter events, 0.1 us)
Async XLA Ops:
  0.6 0.9 copy-start
  3.0 15.3 %all-to-all-start = ((bf16[16,2,2000]{2,1,0:T(2,128)(2,1)}), bf16[16,2,2000]{2,1,0:T(2,128)(2,1)S(1)}, u32[]{:S(2)}, u32[]{:S(2)}) async-start(bf16[16,2,2000]{2,1,0:T(2,128)(2,1)} %get-tuple-element.32.refs_1_), calls=%async_computation | async-start | bytes 262144 | tf_op jit(solution)/shard_map/all_to_all | solution.py:21
  10.4 2.5 %copy-start.3 = (bf16[4096]{0:T(1024)(128)(2,1)S(1)}, bf16[4096]{0:T(1024)(128)(2,1)}, u32[]{:S(2)}) copy-start(bf16[4096]{0:T(1024)(128)(2,1)} %param.14) | copy-start | bytes 24580
  21.9 3.6 %collective-permute-start = (bf16[8,32,256]{2,1,0:T(8,128)(2,1)S(1)}, bf16[8,32,256]{2,1,0:T(8,128)(2,1)S(1)}, u32[]{:S(2)}, u32[]{:S(2)}) collective-permute-start(bf16[8,32,256]{2,1,0:T(8,128)(2,1)S(1)} %get-tuple-element.34), channel_id=1, source_target_pairs={{0,1},{1,0},{2,3},{3,2},{4,5},{5,4},{6,7},{7,6},{8,9},{9,8},{10,11... | collective-permute-start | bytes 393224 | tf_op jit(solution)/shard_map/ppermute | solution.py:17
  25.5 23.8 %copy-start.4 = (bf16[4096]{0:T(1024)(128)(2,1)S(1)}, bf16[4096]{0:T(1024)(128)(2,1)}, u32[]{:S(2)}) copy-start(bf16[4096]{0:T(1024)(128)(2,1)} %param.10) | copy-start | bytes 24580
  26.2 11.2 %all-to-all-start.1 = ((bf16[8,32,256]{2,1,0:T(8,128)(2,1)}), bf16[8,32,256]{2,1,0:T(8,128)(2,1)S(1)}, u32[]{:S(2)}, u32[]{:S(2)}) async-start(bf16[8,32,256]{2,1,0:T(8,128)(2,1)} %add_convert_fusion.1.after_ref), calls=%async_computation.1 | async-start | bytes 262144 | tf_op jit(solution)/shard_map/all_to_all | solution.py:26
  49.3 3.5 %collective-permute-start.1 = (bf16[8,32,256]{2,1,0:T(8,128)(2,1)S(1)}, bf16[8,32,256]{2,1,0:T(8,128)(2,1)S(1)}, u32[]{:S(2)}, u32[]{:S(2)}) collective-permute-start(bf16[8,32,256]{2,1,0:T(8,128)(2,1)S(1)} %all_to_all.30.x_ref.mine_ref), channel_id=1, source_target_pairs={{0,1},{1,0},{2,3},{3,2},{4,5},{5,4},{6,7},{7,6},{8,9},{9,8},{10,11... | collective-permute-start | bytes 393224 | tf_op jit(solution)/shard_map/ppermute | solution.py:17
  49.3 3.5 %copy-start.2 = (s32[4]{0:T(128)S(1)}, s32[4]{0:T(128)}, u32[]{:S(2)}) copy-start(s32[4]{0:T(128)} %counts_ref.3) | copy-start | bytes 52
  59.1 2.8 %collective-permute-start.2 = (bf16[8,32,256]{2,1,0:T(8,128)(2,1)S(1)}, bf16[8,32,256]{2,1,0:T(8,128)(2,1)S(1)}, u32[]{:S(2)}, u32[]{:S(2)}) collective-permute-start(bf16[8,32,256]{2,1,0:T(8,128)(2,1)S(1)} %get-tuple-element.44), channel_id=1, source_target_pairs={{0,1},{1,0},{2,3},{3,2},{4,5},{5,4},{6,7},{7,6},{8,9},{9,8},{10,11... | collective-permute-start | bytes 393224 | tf_op jit(solution)/shard_map/ppermute | solution.py:17
  62.6 16.0 %all-to-all-start.3 = ((bf16[8,32,256]{2,1,0:T(8,128)(2,1)}), bf16[8,32,256]{2,1,0:T(8,128)(2,1)S(1)}, u32[]{:S(2)}, u32[]{:S(2)}) async-start(bf16[8,32,256]{2,1,0:T(8,128)(2,1)} %add_convert_fusion.after_ref), calls=%async_computation.3 | async-start | bytes 262144 | tf_op jit(solution)/shard_map/all_to_all | solution.py:26
  91.8 4.5 %collective-permute-start.3 = (bf16[8,32,256]{2,1,0:T(8,128)(2,1)S(1)}, bf16[8,32,256]{2,1,0:T(8,128)(2,1)S(1)}, u32[]{:S(2)}, u32[]{:S(2)}) collective-permute-start(bf16[8,32,256]{2,1,0:T(8,128)(2,1)S(1)} %all_to_all.31.d_ref.d_mine_ref), channel_id=1, source_target_pairs={{0,1},{1,0},{2,3},{3,2},{4,5},{5,4},{6,7},{7,6},{8,9},{9,8},{10,11... | collective-permute-start | bytes 393224 | tf_op jit(solution)/shard_map/ppermute | solution.py:17
  96.3 17.4 %copy-start.1 = (bf16[2,32000]{1,0:T(2,128)(2,1)S(1)}, bf16[2,32000]{1,0:T(2,128)(2,1)}, u32[]{:S(2)}) copy-start(bf16[2,32000]{1,0:T(2,128)(2,1)} %logits_ref.3) | copy-start | bytes 384004
  102.2 11.4 %all-to-all-start.5 = ((bf16[16,2,2012]{2,1,0:T(2,128)(2,1)}), bf16[16,2,2012]{2,1,0:T(2,128)(2,1)S(1)}, u32[]{:S(2)}, u32[]{:S(2)}) async-start(bf16[16,2,2012]{2,1,0:T(2,128)(2,1)} %reshape.27), calls=%async_computation.5 | async-start | bytes 262144 | tf_op jit(solution)/shard_map/all_to_all | solution.py:21

commit v11 on v9

--- a/solution.py
+++ b/solution.py
@@ -199,43 +199,41 @@
 
 def down_kernel(head_ref, down_ref, after_ref, out_ref, table, sems):
     del after_ref
+    width = down_ref.shape[1]
+    lanes = 128
+
+    def copy(j):
+        rows = span(j * lanes, lanes)
+        return pltpu.make_async_copy(down_ref.at[rows], table.at[rows], sems.at[j])
+
     steps = sems.shape[0]
-    rows = down_ref.shape[0] // steps
+    for j in range(steps):
+        copy(j).start()
+
+    def step(j, _):
+        copy(j).wait()
+        rows = span(j * lanes, lanes)
+        total = jnp.zeros((lanes, lanes), F32)
+        for k in range(0, width, lanes):
+            head = head_ref[:, k : k + lanes].astype(F32)
+            total += table[rows, k : k + lanes].astype(F32) * head
+        out_ref[:, rows] = jnp.sum(total.T, axis=0, keepdims=True)
+        return 0
+
+    lax.fori_loop(0, steps, step, 0)
+
+
+def forward_half(x_ref, gain_ref, gate_ref, up_ref, gate, up, sems, half, sums):
+    chips, _, own = x_ref.shape
+
+    def rows(j):
+        return span((half * chips + j) * own, own)
+
     stream = Stream([
         pltpu.make_async_copy(
-            down_ref.at[pl.ds(i * rows, rows)], table.at[pl.ds(i * rows, rows)], sems.at[i]
-        )
-        for i in range(steps)
-    ])
-    head = jnp.broadcast_to(head_ref[...].astype(F32), (16, head_ref.shape[1])).astype(BF16)
-    contract = (((1,), (1,)), ((), ()))
-    for i in range(steps):
-        stream.wait(i + 1)
-        part = lax.dot_general(
-            head, table[i * rows : (i + 1) * rows], contract, preferred_element_type=F32
-        )
-        out_ref[:, i * rows : (i + 1) * rows] = part[:1]
-
-
-def weight_rows(j, own, ready, gate, up):
-    skip = ready[0].shape[0] // own if ready else 0
-    if j < skip:
-        return ready, slice(j * own, (j + 1) * own)
-    return (gate, up), slice((j - skip) * own, (j - skip + 1) * own)
-
-
-def forward_half(x_ref, gain_ref, gate_ref, up_ref, gate, up, sems, half, sums, ready=()):
-    chips, _, own = x_ref.shape
-    skip = ready[0].shape[0] // own if ready else 0
-
-    def rows(j):
-        return span((half * chips + j) * own, own)
-
-    stream = Stream([
-        pltpu.make_async_copy(
-            source.at[rows(j)], target.at[pl.ds((j - skip) * own, own)], sems.at[k, j]
-        )
-        for j in range(skip, chips)
+            source.at[rows(j)], target.at[pl.ds(j * own, own)], sems.at[k, j]
+        )
+        for j in range(chips)
         for k, (source, target) in enumerate(((gate_ref, gate), (up_ref, up)))
     ])
     a, b, squares = sums
@@ -245,33 +243,29 @@
         squares = squares + jnp.sum(x * x, axis=-1, keepdims=True)
         scaled.append((x * gain_ref[:, rows(j)].astype(F32)).astype(BF16))
     for j in range(chips):
-        (g, u), r = weight_rows(j, own, ready, gate, up)
-        if j >= skip:
-            stream.wait(2 * (j - skip + 1))
-        a = a + jnp.dot(scaled[j], g[r], preferred_element_type=F32)
-        b = b + jnp.dot(scaled[j], u[r], preferred_element_type=F32)
+        r = slice(j * own, (j + 1) * own)
+        stream.wait(2 * (j + 1))
+        a = a + jnp.dot(scaled[j], gate[r], preferred_element_type=F32)
+        b = b + jnp.dot(scaled[j], up[r], preferred_element_type=F32)
     return a, b, squares
 
 
-def backward_half(d_gate, d_up, gate, up, out_ref, ready=()):
+def backward_half(d_gate, d_up, gate, up, out_ref):
     chips, _, own = out_ref.shape
     contract = (((1,), (1,)), ((), ()))
     for j in range(chips):
-        (g, u), r = weight_rows(j, own, ready, gate, up)
-        part = lax.dot_general(d_gate, g[r], contract, preferred_element_type=F32)
-        part += lax.dot_general(d_up, u[r], contract, preferred_element_type=F32)
+        r = slice(j * own, (j + 1) * own)
+        part = lax.dot_general(d_gate, gate[r], contract, preferred_element_type=F32)
+        part += lax.dot_general(d_up, up[r], contract, preferred_element_type=F32)
         out_ref[j] = part.astype(out_ref.dtype)
 
 
 def first_kernel(
-    x_ref, gain_ref, gate_ref, up_ref, gate_0, up_0,
-    a_ref, b_ref, squares_ref, gate, up, sems,
+    x_ref, gain_ref, gate_ref, up_ref, a_ref, b_ref, squares_ref, gate, up, sems
 ):
     zeros = jnp.zeros(a_ref.shape, F32)
     sums = (zeros, zeros, jnp.zeros(squares_ref.shape, F32))
-    sums = forward_half(
-        x_ref, gain_ref, gate_ref, up_ref, gate, up, sems, this_core(), sums, (gate_0, up_0)
-    )
+    sums = forward_half(x_ref, gain_ref, gate_ref, up_ref, gate, up, sems, this_core(), sums)
     a_ref[...], b_ref[...], squares_ref[...] = sums
 
 
@@ -300,9 +294,8 @@
     backward_half(d_gate, d_up, gate, up, send_ref)
 
 
-def third_kernel(d_gate_ref, d_up_ref, gate_0, up_0, gate_ref, up_ref, keep_ref):
-    d_gate, d_up = d_gate_ref[...], d_up_ref[...]
-    backward_half(d_gate, d_up, gate_ref, up_ref, keep_ref, (gate_0, up_0))
+def third_kernel(d_gate_ref, d_up_ref, gate_ref, up_ref, keep_ref):
+    backward_half(d_gate_ref[...], d_up_ref[...], gate_ref, up_ref, keep_ref)
 
 
 def input_kernel(
@@ -346,7 +339,8 @@
             x = x_ref[j].astype(F32)
             g = d_ref[j].astype(F32) * gain_ref[:, columns].astype(F32)
             dx = inv * g - x * inv * inv * inv * mean
-            dx_ref[:, columns] = (dx + valid * head_ref[:, columns].astype(F32)).astype(BF16)
+            dx = dx + valid * head_ref[:, columns].astype(F32)
+            dx_ref[columns, :] = dx.T.astype(BF16)
     score = valid * (score_a_ref[...] + score_b_ref[...] + score_c_ref[...])
     member = request == lax.broadcasted_iota(jnp.int32, (total, requests), 1)
     value = jnp.sum(jnp.where(member, score, 0.0), axis=0, keepdims=True)
@@ -359,21 +353,18 @@
         start = voc + i * requests
         spread = jnp.broadcast_to(piece, (total, requests)).astype(BF16)
         out_ref[:, start : start + requests] = spread
-    contract = (((1,), (1,)), ((), ()))
-
-    def product(weights):
-        return lax.dot_general(
-            dx_ref[...], weights, contract, preferred_element_type=F32
-        ).astype(BF16)
-
-    out_ref[:, :ready] = product(ready_ref[...])
+    def product(weights, rows):
+        part = jnp.dot(weights[rows, :], dx_ref[...], preferred_element_type=F32)
+        return part.T.astype(BF16)
+
+    out_ref[:, :ready] = product(ready_ref, pl.ds(0, ready))
 
     def step(j, _):
         start = pl.multiple_of(j * tile, tile)
         for i in range(0, tile, fine):
             copy(pl.multiple_of(start + i, fine), fine).wait()
         rows = pl.ds(pl.multiple_of(start - ready, tile), tile)
-        out_ref[:, pl.ds(start, tile)] = product(table[rows, :])
+        out_ref[:, pl.ds(start, tile)] = product(table, rows)
         return 0
 
     whole = voc // tile
@@ -382,7 +373,7 @@
         last = whole * tile
         for start in range(last, voc, fine):
             copy(start, min(fine, voc - start)).wait()
-        out_ref[:, last:voc] = product(table[last - ready :, :])
+        out_ref[:, last:voc] = product(table, pl.ds(last - ready, voc - last))
 
 
 def swap_sum(send, keep, devices):
@@ -475,7 +466,14 @@
     half = (chips, total, own)
     flops = total * part * width
     if tiled:
-        (first,) = first_rows(256, [embed], [lambda: 0], blocked)
+        (down_row,) = call(
+            down_kernel, [struct((1, hidden), F32)], head_row, w_down, blocked,
+            streamed=(1,), flops=2 * hidden * width, room=2 * hidden * width,
+            scratch=(
+                pltpu.VMEM((hidden, width), BF16), pltpu.SemaphoreType.DMA((hidden // 128,)),
+            ),
+        )
+        (first,) = first_rows(256, [embed], [lambda: 0], down_row)
         table = [
             pltpu.VMEM((part - 256, width // 2), BF16), pltpu.VMEM((total, width // 2), F32),
             pltpu.SemaphoreType.DMA((-(-part // 128),)),
@@ -494,32 +492,17 @@
     else:
         send, keep, score_a = plain_half(slices, embed, head_row, devices)
     summed = swap_sum(send, keep, devices)
-    if tiled:
-        steps = hidden // 128
-        (down_row,) = call(
-            down_kernel, [struct((1, hidden), F32)], head_row, w_down, summed,
-            streamed=(1,), flops=2 * hidden * width, room=2 * hidden * width,
-            scratch=(pltpu.VMEM((hidden, width), BF16), pltpu.SemaphoreType.DMA((steps,))),
-        )
-    else:
-        down_row = jnp.sum(w_down.astype(F32) * head.astype(F32)[None, :], axis=-1)[None]
-    total_x = chip_sum(summed, devices)
-    if tiled:
-        total_x, down_row = lax.optimization_barrier((total_x, down_row))
-    x_mine = chip_gather(total_x, devices)
+    x_mine = chip_gather(chip_sum(summed, devices), devices)
     x_got = swap_cores(x_mine, devices)
     if tiled:
-        weights = [w_gate, w_up]
-        starts = [lambda: this_core() * (width // 2)] * 2
-        gate_0, up_0 = first_rows(2 * own, weights, starts, total_x)
         wide = struct((total, hidden), F32)
-        weight, rest = (width // 2, hidden), (width // 2 - 2 * own, hidden)
+        weight = (width // 2, hidden)
         sems = pltpu.SemaphoreType.DMA((2, chips))
         args = dict(streamed=(2, 3), flops=2 * total * hidden * width, room=2 * width * hidden)
         a, b, squares, gate, up = call(
             first_kernel,
-            [wide, wide, column, pltpu.VMEM(rest, BF16), pltpu.VMEM(rest, BF16)],
-            x_mine, gain_row, w_gate, w_up, gate_0, up_0, scratch=(sems,), kept=(4, 5), **args,
+            [wide, wide, column, pltpu.VMEM(weight, BF16), pltpu.VMEM(weight, BF16)],
+            x_mine, gain_row, w_gate, w_up, scratch=(sems,), **args,
         )
         narrow = struct((total, hidden), BF16)
         send, score_c, d_gate, d_up = call(
@@ -529,10 +512,11 @@
             scalars=(8,), **args,
         )
         (keep,) = call(
-            third_kernel, [struct(half, F32)], d_gate, d_up, gate_0, up_0, gate, up,
-            kept=(2, 3, 4, 5), flops=2 * total * hidden * width,
+            third_kernel, [struct(half, F32)], d_gate, d_up, gate, up,
+            kept=(2, 3), flops=2 * total * hidden * width,
         )
     else:
+        down_row = jnp.sum(w_down.astype(F32) * head.astype(F32)[None, :], axis=-1)[None]
         position = jnp.arange(total, dtype=jnp.int32)[:, None]
         member = position // request_len == jnp.arange(requests, dtype=jnp.int32)[None, :]
         limit = jnp.sum(jnp.where(member, counts[None, :], 0), axis=-1, keepdims=True)
@@ -552,7 +536,7 @@
             *sources, score_a, score_b, score_c, counts, first, embed,
             scalars=(9,), kept=(10,), streamed=(11,), flops=2 * flops, room=2 * part * width,
             scratch=(
-                pltpu.VMEM((total, width), BF16), pltpu.VMEM((part - 256, width), BF16),
+                pltpu.VMEM((width, total), BF16), pltpu.VMEM((part - 256, width), BF16),
                 pltpu.SemaphoreType.DMA((-(-part // 64),)),
             ),
         )

time: 107 us -> 104 us (0.972)
  blocking collectives: 31.5 us -> 41.6 us
  waiting for transfers between devices: 14.6 us -> 9.18 us
  Pallas kernels: 41.5 us -> 37.7 us
  starting transfers between devices: 14.9 us -> 11.5 us
    all_to_all x3 -> x4, blocking collectives: 31.5 us -> 41.6 us  [exchange_chips(): lax.all_to_all(blocks, 'dp', split_axis=0, concat_axis=0, axis_index_grou...]
    all_to_all x2, waiting for transfers between devices: 13.3 us -> 9.17 us  [exchange(): return lax.all_to_all(blocks, 'dp', split_axis=0, concat_axis=0, tiled=True)]
    pallas_call x12 -> x11, Pallas kernels: 41.5 us -> 37.7 us  [call(): pl.pallas_call(kernel, out_shape=outs, in_specs=specs, out_specs=[VMEM_SP...]
    all_to_all x1 -> x0, starting transfers between devices: 3.37 us -> none  [exchange_chips(): lax.all_to_all(blocks, 'dp', split_axis=0, concat_axis=0, axis_index_grou...]
    all_to_all x1 -> x0, waiting for transfers between devices: 1.29 us -> none  [exchange_chips(): lax.all_to_all(blocks, 'dp', split_axis=0, concat_axis=0, axis_index_grou...]
  transfers between devices with their start and end apart: 7 -> 6, of which waited for: 3 -> 2; matrix products, arithmetic and copies ran while one was open for 0% -> 1% of each run, Pallas kernels for 20% -> 16%
where the time goes in v11:
time: 104 us; the launch traced here: 103 us
  blocking collectives  41.6 us (40%)
  Pallas kernels  37.7 us (36%)
  starting transfers between devices  11.5 us (11%)
  waiting for transfers between devices  9.18 us (9%)
  local copies, waits for them, and re-layouts  2.48 us (2%)
    all_to_all x4, blocking collectives, exchange_chips(): lax.all_to_all(blocks, 'dp', split_axis=0, concat_axis=0, axis_index_grou...  41.6 us
    pallas_call x11, Pallas kernels, call(): pl.pallas_call(kernel, out_shape=outs, in_specs=specs, out_specs=[VMEM_SP...  37.7 us
    all_to_all x2, starting transfers between devices, exchange(): return lax.all_to_all(blocks, 'dp', split_axis=0, concat_axis=0, tiled=True)  10.9 us
    all_to_all x2, waiting for transfers between devices, exchange(): return lax.all_to_all(blocks, 'dp', split_axis=0, concat_axis=0, tiled=True)  9.17 us
  transfers between devices with their start and end apart: 6, of which 2 were waited for; matrix products, arithmetic and copies ran while one was open for 1% of the time, Pallas kernels for 16%

profile of v11, /device:TPU:0, one launch (start us, length us, event | category | flops | bytes accessed | tf_op | source)
XLA Modules:
  0.0 103.5 jit_solution(13544538744215114055)
XLA Ops:
  0.6 0.0 copy-start
  0.6 0.9 copy-done
  1.5 1.4 %shard_map.95 = (bf16[16,2,2000]{2,1,0:T(2,128)(2,1)}, f32[2,1]{1,0:T(2,128)S(1)}, f32[2,1]{1,0:T(2,128)S(1)}) custom-call(bf16[2,32000]{1,0:T(2,128)(2,1)S(1)} %copy-done), custom_call_target="tpu_custom_call" | custom-call | bytes 128000 | tf_op jit(solution)/shard_map/pallas_call | solution.py:54
  3.0 7.4 %all-to-all-start = ((bf16[16,2,2000]{2,1,0:T(2,128)(2,1)}), bf16[16,2,2000]{2,1,0:T(2,128)(2,1)S(1)}, u32[]{:S(2)}, u32[]{:S(2)}) async-start(bf16[16,2,2000]{2,1,0:T(2,128)(2,1)} %get-tuple-element.22.after_ref), calls=%async_computation | async-start | bytes 262144 | tf_op jit(solution)/shard_map/all_to_all | solution.py:21
  10.4 0.7 reshape.25.head_ref
  11.1 4.4 %shard_map.96.refs_1_.down_ref = f32[1,896]{1,0:T(1,128)S(1)} custom-call(bf16[1,4096]{1,0:T(2,128)(2,1)S(1)} %reshape.25.head_ref, bf16[896,4096]{1,0:T(8,128)(2,1)} %down_ref.1, bf16[16,2,2000]{2,1,0:T(2,128)(2,1)} %get-tuple-element.22.after_ref), custom_call_target="tpu_custom_call" | custom-call | flops 7340032 | bytes 7476224 | tf_op jit(solution)/shard_map/pallas_call | solution.py:54
  15.4 1.6 %shard_map.97.ready_ref = bf16[256,4096]{1,0:T(8,128)(2,1)S(1)} custom-call(bf16[2000,4096]{1,0:T(8,128)(2,1)} %embed_ref.5, f32[1,896]{1,0:T(1,128)S(1)} %shard_map.96.refs_1_.down_ref), custom_call_target="tpu_custom_call" | custom-call | bytes 16387584 | tf_op jit(solution)/shard_map/pallas_call | solution.py:54
  17.0 1.3 %all-to-all-done = bf16[16,2,2000]{2,1,0:T(2,128)(2,1)S(1)} async-done(((bf16[16,2,2000]{2,1,0:T(2,128)(2,1)}), bf16[16,2,2000]{2,1,0:T(2,128)(2,1)S(1)}, u32[]{:S(2)}, u32[]{:S(2)}) %all-to-all-start) | async-done | bytes 128032 | tf_op jit(solution)/shard_map/all_to_all | solution.py:21
  18.3 0.1 reshape.24.slices_ref
  18.4 3.5 %shard_map.99 = (bf16[8,32,256]{2,1,0:T(8,128)(2,1)S(1)}, f32[32,1]{1,0:T(8,128)S(1)}) custom-call(bf16[32,2000]{1,0:T(8,128)(2,1)S(1)} %reshape.24.slices_ref, bf16[256,4096]{1,0:T(8,128)(2,1)S(1)} %shard_map.97.ready_ref, bf16[2000,4096]{1,0:T(8,128)(2,1)} %embed_ref.5, bf16[1,4096]{1,0:T(2,128)(2,1)S(1)} %reshape.25.head_ref), custom_call_target="tpu_custom_call" | custom-call | flops 262144000 | bytes 18617344 | tf_op jit(solution)/shard_map/pallas_call | solution.py:54
  21.9 0.0 copy-start.3
  21.9 0.1 collective-permute-start
  22.0 3.5 %shard_map.98 = (f32[8,32,256]{2,1,0:T(8,128)S(1)}, f32[32,1]{1,0:T(8,128)S(1)}) custom-call(bf16[32,2000]{1,0:T(8,128)(2,1)S(1)} %reshape.24.slices_ref, bf16[256,4096]{1,0:T(8,128)(2,1)S(1)} %shard_map.97.ready_ref, bf16[2000,4096]{1,0:T(8,128)(2,1)} %embed_ref.5, bf16[1,4096]{1,0:T(2,128)(2,1)S(1)} %reshape.25.head_ref), custom_call_target="tpu_custom_call" | custom-call | flops 262144000 | bytes 18617344 | tf_op jit(solution)/shard_map/pallas_call | solution.py:54
  25.6 12.1 %all_to_all.30 = bf16[8,32,256]{2,1,0:T(8,128)(2,1)S(1)} all-to-all(bf16[8,32,256]{2,1,0:T(8,128)(2,1)S(1)} %add_convert_fusion.1), channel_id=1, replica_groups={{0,2,4,6,8,10,12,14},{1,3,5,7,9,11,13,15},{16,18,20,22,24,26,28,30},{17..., dimensions={0} | all-to-all | bytes 262144 | tf_op jit(solution)/shard_map/all_to_all | solution.py:26
  37.7 9.9 %all_to_all.31.x_ref.mine_ref = bf16[8,32,256]{2,1,0:T(8,128)(2,1)S(1)} all-to-all(bf16[8,32,256]{2,1,0:T(8,128)(2,1)S(1)} %broadcast_in_dim.4), channel_id=1, replica_groups={{0,2,4,6,8,10,12,14},{1,3,5,7,9,11,13,15},{16,18,20,22,24,26,28,30},{17..., dimensions={0} | all-to-all | bytes 262144 | tf_op jit(solution)/shard_map/all_to_all | solution.py:26
  47.5 0.0 copy-start.2
  47.6 3.5 %shard_map.100 = (f32[32,896]{1,0:T(8,128)S(1)}, f32[32,896]{1,0:T(8,128)S(1)}, f32[32,1]{1,0:T(8,128)S(1)}, bf16[2048,896]{1,0:T(8,128)(2,1)S(1)}, bf16[2048,896]{1,0:T(8,128)(2,1)S(1)}) custom-call(bf16[8,32,256]{2,1,0:T(8,128)(2,1)S(1)} %all_to_all.31.x_ref.mine_ref, bf16[1,4096]{1,0:T(2,128)(2,1)S(1)} %reshape.26.gain_ref, bf16[4096,896]{1,0:T(8,128)(2,1)} %gate_ref.3, ...), custom_call_target="tpu_custom_call" | custom-call | flops 234881024 | bytes 14819328 | tf_op jit(solution)/shard_map/pallas_call | solution.py:54
  51.1 0.0 collective-permute-done.1.x_ref.got_ref
  51.1 6.2 %shard_map.101 = (bf16[8,32,256]{2,1,0:T(8,128)(2,1)S(1)}, f32[32,1]{1,0:T(8,128)S(1)}, bf16[32,896]{1,0:T(8,128)(2,1)S(1)}, bf16[32,896]{1,0:T(8,128)(2,1)S(1)}) custom-call(bf16[8,32,256]{2,1,0:T(8,128)(2,1)S(1)} %collective-permute-done.1.x_ref.got_ref, bf16[1,4096]{1,0:T(2,128)(2,1)S(1)} %reshape.26.gain_ref, bf16[4096,896]{1,0:T(8,128)(2,1)} %gate_ref.3, ...), custom_call_target="tpu_custom_call" | custom-call | flops 234881024 | bytes 15052432 | tf_op jit(solution)/shard_map/pallas_call | solution.py:54
  57.3 0.6 collective-permute-start.2
  57.9 2.2 %shard_map.102 = f32[8,32,256]{2,1,0:T(8,128)S(1)} custom-call(bf16[32,896]{1,0:T(8,128)(2,1)S(1)} %get-tuple-element.28.d_gate_ref, bf16[32,896]{1,0:T(8,128)(2,1)S(1)} %get-tuple-element.29.d_up_ref, bf16[2048,896]{1,0:T(8,128)(2,1)S(1)} %get-tuple-element.30.gate_ref, bf16[2048,896]{1,0:T(8,128)(2,1)S(1)} %get-tuple-element.31.up_ref), custom_call_target="tpu_custom_call" | custom-call | flops 234881024 | bytes 7454720 | tf_op jit(solution)/shard_map/pallas_call | solution.py:54
  60.1 0.0 collective-permute-done.2
  60.2 9.8 %all_to_all.32 = bf16[8,32,256]{2,1,0:T(8,128)(2,1)S(1)} all-to-all(bf16[8,32,256]{2,1,0:T(8,128)(2,1)S(1)} %add_convert_fusion), channel_id=1, replica_groups={{0,2,4,6,8,10,12,14},{1,3,5,7,9,11,13,15},{16,18,20,22,24,26,28,30},{17..., dimensions={0} | all-to-all | bytes 262144 | tf_op jit(solution)/shard_map/all_to_all | solution.py:26
  70.0 9.8 %all_to_all.33.d_mine_ref = bf16[8,32,256]{2,1,0:T(8,128)(2,1)S(1)} all-to-all(bf16[8,32,256]{2,1,0:T(8,128)(2,1)S(1)} %broadcast_in_dim.5), channel_id=1, replica_groups={{0,2,4,6,8,10,12,14},{1,3,5,7,9,11,13,15},{16,18,20,22,24,26,28,30},{17..., dimensions={0} | all-to-all | bytes 262144 | tf_op jit(solution)/shard_map/all_to_all | solution.py:26
  79.9 0.0 collective-permute-start.3
  79.9 1.6 %shard_map.103.ready_ref = bf16[256,4096]{1,0:T(8,128)(2,1)S(1)} custom-call(bf16[2000,4096]{1,0:T(8,128)(2,1)} %embed_ref.5, bf16[32,256]{1,0:T(8,128)(2,1)S(1)} %reduce_sum.25.refs_1_), custom_call_target="tpu_custom_call" | custom-call | bytes 16400384 | tf_op jit(solution)/shard_map/pallas_call | solution.py:54
  81.5 0.0 copy-start.1
  81.5 8.6 %shard_map.104 = bf16[32,2012]{1,0:T(8,128)(2,1)S(1)} custom-call(bf16[8,32,256]{2,1,0:T(8,128)(2,1)S(1)} %all_to_all.31.x_ref.mine_ref, bf16[8,32,256]{2,1,0:T(8,128)(2,1)S(1)} %collective-permute-done.1.x_ref.got_ref, bf16[8,32,256]{2,1,0:T(8,128)(2,1)S(1)} %all_to_all.33.d_mine_ref, bf16[8,32,256]{2,1,0:T(8,128)(2,1)S(1)} %collective-permute-done.3.d_got_ref, ...), custom_call_target="tpu_custom_call" | custom-call | flops 524288000 | bytes 19022224 | tf_op jit(solution)/shard_map/pallas_call | solution.py:54
  90.1 0.8 reshape.27
  90.8 3.5 %all-to-all-start.5 = ((bf16[16,2,2012]{2,1,0:T(2,128)(2,1)}), bf16[16,2,2012]{2,1,0:T(2,128)(2,1)S(1)}, u32[]{:S(2)}, u32[]{:S(2)}) async-start(bf16[16,2,2012]{2,1,0:T(2,128)(2,1)} %reshape.27), calls=%async_computation.5 | async-start | bytes 262144 | tf_op jit(solution)/shard_map/all_to_all | solution.py:21
  94.4 7.9 %all-to-all-done.5.back_ref = bf16[16,2,2012]{2,1,0:T(2,128)(2,1)S(1)} async-done(((bf16[16,2,2012]{2,1,0:T(2,128)(2,1)}), bf16[16,2,2012]{2,1,0:T(2,128)(2,1)S(1)}, u32[]{:S(2)}, u32[]{:S(2)}) %all-to-all-start.5) | async-done | bytes 128800 | tf_op jit(solution)/shard_map/all_to_all | solution.py:21
  102.3 1.2 %shard_map.105 = (bf16[2,32000]{1,0:T(2,128)(2,1)}, f32[1,4]{1,0:T(1,128)}) custom-call(bf16[2,32000]{1,0:T(2,128)(2,1)S(1)} %copy-done.1, f32[2,1]{1,0:T(2,128)S(1)} %get-tuple-element.20.top_ref, f32[2,1]{1,0:T(2,128)S(1)} %get-tuple-element.21.scale_ref, bf16[16,2,2012]{2,1,0:T(2,128)(2,1)S(1)} %all-to-all-done.5.back_ref, ...), custom_call_target="tpu_custom_call" | custom-call | bytes 256800 | tf_op jit(solution)/shard_map/pallas_call | solution.py:54
  (14 shorter events, 0.2 us)
Async XLA Ops:
  0.6 0.9 copy-start
  3.0 15.3 %all-to-all-start = ((bf16[16,2,2000]{2,1,0:T(2,128)(2,1)}), bf16[16,2,2000]{2,1,0:T(2,128)(2,1)S(1)}, u32[]{:S(2)}, u32[]{:S(2)}) async-start(bf16[16,2,2000]{2,1,0:T(2,128)(2,1)} %get-tuple-element.22.after_ref), calls=%async_computation | async-start | bytes 262144 | tf_op jit(solution)/shard_map/all_to_all | solution.py:21
  21.9 25.6 %copy-start.3 = (bf16[4096]{0:T(1024)(128)(2,1)S(1)}, bf16[4096]{0:T(1024)(128)(2,1)}, u32[]{:S(2)}) copy-start(bf16[4096]{0:T(1024)(128)(2,1)} %param.10) | copy-start | bytes 24580
  21.9 3.6 %collective-permute-start = (bf16[8,32,256]{2,1,0:T(8,128)(2,1)S(1)}, bf16[8,32,256]{2,1,0:T(8,128)(2,1)S(1)}, u32[]{:S(2)}, u32[]{:S(2)}) collective-permute-start(bf16[8,32,256]{2,1,0:T(8,128)(2,1)S(1)} %get-tuple-element.24), channel_id=1, source_target_pairs={{0,1},{1,0},{2,3},{3,2},{4,5},{5,4},{6,7},{7,6},{8,9},{9,8},{10,11... | collective-permute-start | bytes 393224 | tf_op jit(solution)/shard_map/ppermute | solution.py:17
  47.5 3.5 %collective-permute-start.1 = (bf16[8,32,256]{2,1,0:T(8,128)(2,1)S(1)}, bf16[8,32,256]{2,1,0:T(8,128)(2,1)S(1)}, u32[]{:S(2)}, u32[]{:S(2)}) collective-permute-start(bf16[8,32,256]{2,1,0:T(8,128)(2,1)S(1)} %all_to_all.31.x_ref.mine_ref), channel_id=1, source_target_pairs={{0,1},{1,0},{2,3},{3,2},{4,5},{5,4},{6,7},{7,6},{8,9},{9,8},{10,11... | collective-permute-start | bytes 393224 | tf_op jit(solution)/shard_map/ppermute | solution.py:17
  47.5 3.5 %copy-start.2 = (s32[4]{0:T(128)S(1)}, s32[4]{0:T(128)}, u32[]{:S(2)}) copy-start(s32[4]{0:T(128)} %counts_ref.3) | copy-start | bytes 52
  57.3 2.8 %collective-permute-start.2 = (bf16[8,32,256]{2,1,0:T(8,128)(2,1)S(1)}, bf16[8,32,256]{2,1,0:T(8,128)(2,1)S(1)}, u32[]{:S(2)}, u32[]{:S(2)}) collective-permute-start(bf16[8,32,256]{2,1,0:T(8,128)(2,1)S(1)} %get-tuple-element.32), channel_id=1, source_target_pairs={{0,1},{1,0},{2,3},{3,2},{4,5},{5,4},{6,7},{7,6},{8,9},{9,8},{10,11... | collective-permute-start | bytes 393224 | tf_op jit(solution)/shard_map/ppermute | solution.py:17
  79.9 1.6 %collective-permute-start.3 = (bf16[8,32,256]{2,1,0:T(8,128)(2,1)S(1)}, bf16[8,32,256]{2,1,0:T(8,128)(2,1)S(1)}, u32[]{:S(2)}, u32[]{:S(2)}) collective-permute-start(bf16[8,32,256]{2,1,0:T(8,128)(2,1)S(1)} %all_to_all.33.d_mine_ref), channel_id=1, source_target_pairs={{0,1},{1,0},{2,3},{3,2},{4,5},{5,4},{6,7},{7,6},{8,9},{9,8},{10,11... | collective-permute-start | bytes 393224 | tf_op jit(solution)/shard_map/ppermute | solution.py:17
  81.5 20.8 %copy-start.1 = (bf16[2,32000]{1,0:T(2,128)(2,1)S(1)}, bf16[2,32000]{1,0:T(2,128)(2,1)}, u32[]{:S(2)}) copy-start(bf16[2,32000]{1,0:T(2,128)(2,1)} %logits_ref.3) | copy-start | bytes 384004
  90.8 11.4 %all-to-all-start.5 = ((bf16[16,2,2012]{2,1,0:T(2,128)(2,1)}), bf16[16,2,2012]{2,1,0:T(2,128)(2,1)S(1)}, u32[]{:S(2)}, u32[]{:S(2)}) async-start(bf16[16,2,2012]{2,1,0:T(2,128)(2,1)} %reshape.27), calls=%async_computation.5 | async-start | bytes 262144 | tf_op jit(solution)/shard_map/all_to_all | solution.py:21

commit v12 on v11

--- a/solution.py
+++ b/solution.py
@@ -136,36 +136,37 @@
     return valid, position // length
 
 
-def ready_kernel(starts, *refs):
-    count = len(starts)
-    sources, outs, sems = refs[:count], refs[count + 1 : -1], refs[-1]
+def bring(source_ref, out_ref, sems, columns):
     fine = 128
-    copies = [
+    return [
         pltpu.make_async_copy(
-            source.at[span(start() + i, fine)], out.at[pl.ds(i, fine)], sems.at[k, i // fine]
-        )
-        for k, (source, out, start) in enumerate(zip(sources, outs, starts))
-        for i in range(0, out.shape[0], fine)
+            source_ref.at[pl.ds(i, fine), columns], out_ref.at[pl.ds(i, fine)], sems.at[i // fine]
+        )
+        for i in range(0, out_ref.shape[0], fine)
     ]
+
+
+def ready_kernel(split, source_ref, after_ref, out_ref, sems):
+    del after_ref
+    width = out_ref.shape[1]
+    columns = span((1 - this_core()) * width, width) if split else pl.ds(0, width)
+    copies = bring(source_ref, out_ref, sems, columns)
     for copy in copies:
         copy.start()
     for copy in copies:
         copy.wait()
 
 
-def first_rows(rows, sources, starts, after):
-    count = len(sources)
+def first_rows(rows, source, after, split):
+    width = source.shape[1] // 2 if split else source.shape[1]
     return call(
-        functools.partial(ready_kernel, starts),
-        [pltpu.VMEM((rows, a.shape[1]), a.dtype) for a in sources],
-        *sources, after, streamed=range(count),
-        scratch=(pltpu.SemaphoreType.DMA((count, rows // 128)),),
-    )
-
-
-def half_kernel(
-    other, slices_ref, ready_ref, embed_ref, head_ref, out_ref, score_ref, table, acc, sems
-):
+        functools.partial(ready_kernel, split), [pltpu.VMEM((rows, width), source.dtype)],
+        source, after, streamed=(0,), scratch=(pltpu.SemaphoreType.DMA((rows // 128,)),),
+    )[0]
+
+
+def half_kernel(other, slices_ref, ready_ref, embed_ref, head_ref, out_ref, score_ref, *rest):
+    next_ref, table, acc, sems, next_sems = rest if other else (None, *rest, None)
     chips, total, own = out_ref.shape
     part, ready = embed_ref.shape[0], ready_ref.shape[0]
     core = this_core()
@@ -180,9 +181,12 @@
         )
         for i in range(ready, part, fine)
     ])
-    acc[...] = jnp.dot(
-        slices_ref[:, :ready], ready_ref[:, columns], preferred_element_type=F32
-    )
+    following = []
+    if other:
+        following = bring(embed_ref, next_ref, next_sems, span(core * chips * own, chips * own))
+        for copy in following:
+            copy.start()
+    acc[...] = jnp.dot(slices_ref[:, :ready], ready_ref[...], preferred_element_type=F32)
     for start in range(ready, part, tile):
         end = min(start + tile, part)
         stream.wait(-(-(end - ready) // fine))
@@ -195,6 +199,8 @@
     )
     for j in range(chips):
         out_ref[j] = acc[:, j * own : (j + 1) * own].astype(out_ref.dtype)
+    for copy in following:
+        copy.wait()
 
 
 def down_kernel(head_ref, down_ref, after_ref, out_ref, table, sems):
@@ -223,61 +229,93 @@
     lax.fori_loop(0, steps, step, 0)
 
 
-def forward_half(x_ref, gain_ref, gate_ref, up_ref, gate, up, sems, half, sums):
+def bring_blocks(refs, half, blocks, own, chips, sems):
+    return [
+        pltpu.make_async_copy(
+            source.at[span((half * chips + j) * own, own)],
+            target.at[pl.ds((j - blocks[0]) * own, own)],
+            sems.at[k, j - blocks[0]],
+        )
+        for j in blocks
+        for k, (source, target) in enumerate(refs)
+    ]
+
+
+def forward_half(x_ref, gain_ref, half, sums, weights, wait):
     chips, _, own = x_ref.shape
-
-    def rows(j):
-        return span((half * chips + j) * own, own)
-
-    stream = Stream([
-        pltpu.make_async_copy(
-            source.at[rows(j)], target.at[pl.ds(j * own, own)], sems.at[k, j]
-        )
-        for j in range(chips)
-        for k, (source, target) in enumerate(((gate_ref, gate), (up_ref, up)))
-    ])
     a, b, squares = sums
     scaled = []
     for j in range(chips):
         x = x_ref[j].astype(F32)
         squares = squares + jnp.sum(x * x, axis=-1, keepdims=True)
-        scaled.append((x * gain_ref[:, rows(j)].astype(F32)).astype(BF16))
+        gain = gain_ref[:, span((half * chips + j) * own, own)].astype(F32)
+        scaled.append((x * gain).astype(BF16))
     for j in range(chips):
-        r = slice(j * own, (j + 1) * own)
-        stream.wait(2 * (j + 1))
-        a = a + jnp.dot(scaled[j], gate[r], preferred_element_type=F32)
-        b = b + jnp.dot(scaled[j], up[r], preferred_element_type=F32)
+        wait(j)
+        gate, up = weights(j)
+        a = a + jnp.dot(scaled[j], gate, preferred_element_type=F32)
+        b = b + jnp.dot(scaled[j], up, preferred_element_type=F32)
     return a, b, squares
 
 
-def backward_half(d_gate, d_up, gate, up, out_ref):
-    chips, _, own = out_ref.shape
+def backward_half(d_gate, d_up, weights, out_ref):
     contract = (((1,), (1,)), ((), ()))
-    for j in range(chips):
-        r = slice(j * own, (j + 1) * own)
-        part = lax.dot_general(d_gate, gate[r], contract, preferred_element_type=F32)
-        part += lax.dot_general(d_up, up[r], contract, preferred_element_type=F32)
+    for j in range(out_ref.shape[0]):
+        gate, up = weights(j)
+        part = lax.dot_general(d_gate, gate, contract, preferred_element_type=F32)
+        part += lax.dot_general(d_up, up, contract, preferred_element_type=F32)
         out_ref[j] = part.astype(out_ref.dtype)
 
 
 def first_kernel(
-    x_ref, gain_ref, gate_ref, up_ref, a_ref, b_ref, squares_ref, gate, up, sems
+    x_ref, gain_ref, gate_ref, up_ref,
+    a_ref, b_ref, squares_ref, gate, up, next_gate, next_up, sems, next_sems,
 ):
+    chips, _, own = x_ref.shape
+    core = this_core()
+    refs = ((gate_ref, gate), (up_ref, up))
+    stream = Stream(bring_blocks(refs, core, range(chips), own, chips, sems))
+    refs = ((gate_ref, next_gate), (up_ref, next_up))
+    ahead = range(next_gate.shape[0] // own)
+    following = bring_blocks(refs, 1 - core, ahead, own, chips, next_sems)
+    for copy in following:
+        copy.start()
     zeros = jnp.zeros(a_ref.shape, F32)
     sums = (zeros, zeros, jnp.zeros(squares_ref.shape, F32))
-    sums = forward_half(x_ref, gain_ref, gate_ref, up_ref, gate, up, sems, this_core(), sums)
-    a_ref[...], b_ref[...], squares_ref[...] = sums
+
+    def weights(j):
+        r = slice(j * own, (j + 1) * own)
+        return gate[r], up[r]
+
+    a_ref[...], b_ref[...], squares_ref[...] = forward_half(
+        x_ref, gain_ref, core, sums, weights, lambda j: stream.wait(2 * (j + 1))
+    )
+    for copy in following:
+        copy.wait()
 
 
 def second_kernel(
-    x_ref, gain_ref, gate_ref, up_ref, a_ref, b_ref, squares_ref, down_ref, counts_ref,
+    x_ref, gain_ref, gate_ref, up_ref, first_gate, first_up,
+    a_ref, b_ref, squares_ref, down_ref, counts_ref,
     send_ref, score_ref, d_gate_ref, d_up_ref, gate, up, sems,
 ):
-    total = x_ref.shape[1]
+    chips, total, own = x_ref.shape
     width = gate_ref.shape[0]
+    half = 1 - this_core()
+    skip = first_gate.shape[0] // own
+    refs = ((gate_ref, gate), (up_ref, up))
+    stream = Stream(bring_blocks(refs, half, range(skip, chips), own, chips, sems))
+
+    def weights(j):
+        if j < skip:
+            r = slice(j * own, (j + 1) * own)
+            return first_gate[r], first_up[r]
+        r = slice((j - skip) * own, (j - skip + 1) * own)
+        return gate[r], up[r]
+
     sums = (a_ref[...], b_ref[...], squares_ref[...])
     a, b, squares = forward_half(
-        x_ref, gain_ref, gate_ref, up_ref, gate, up, sems, 1 - this_core(), sums
+        x_ref, gain_ref, half, sums, weights, lambda j: stream.wait(2 * (j - skip + 1))
     )
     inv = lax.rsqrt(squares / width + 1e-05)
     a, b = a * inv, b * inv
@@ -291,11 +329,17 @@
     d_gate = (d_hidden * b * sigma * (1.0 + a * (1.0 - sigma))).astype(BF16)
     d_up = (d_hidden * active).astype(BF16)
     d_gate_ref[...], d_up_ref[...] = d_gate, d_up
-    backward_half(d_gate, d_up, gate, up, send_ref)
+    backward_half(d_gate, d_up, weights, send_ref)
 
 
 def third_kernel(d_gate_ref, d_up_ref, gate_ref, up_ref, keep_ref):
-    backward_half(d_gate_ref[...], d_up_ref[...], gate_ref, up_ref, keep_ref)
+    own = keep_ref.shape[2]
+
+    def weights(j):
+        r = slice(j * own, (j + 1) * own)
+        return gate_ref[r], up_ref[r]
+
+    backward_half(d_gate_ref[...], d_up_ref[...], weights, keep_ref)
 
 
 def input_kernel(
@@ -309,7 +353,7 @@
     width = 2 * chips * own
     core = this_core()
     ready = ready_ref.shape[0]
-    tile, fine = 256, 64
+    tile, fine = 512, 256
 
     def copy(start, size):
         return pltpu.make_async_copy(
@@ -339,8 +383,7 @@
             x = x_ref[j].astype(F32)
             g = d_ref[j].astype(F32) * gain_ref[:, columns].astype(F32)
             dx = inv * g - x * inv * inv * inv * mean
-            dx = dx + valid * head_ref[:, columns].astype(F32)
-            dx_ref[columns, :] = dx.T.astype(BF16)
+            dx_ref[:, columns] = (dx + valid * head_ref[:, columns].astype(F32)).astype(BF16)
     score = valid * (score_a_ref[...] + score_b_ref[...] + score_c_ref[...])
     member = request == lax.broadcasted_iota(jnp.int32, (total, requests), 1)
     value = jnp.sum(jnp.where(member, score, 0.0), axis=0, keepdims=True)
@@ -353,27 +396,30 @@
         start = voc + i * requests
         spread = jnp.broadcast_to(piece, (total, requests)).astype(BF16)
         out_ref[:, start : start + requests] = spread
-    def product(weights, rows):
-        part = jnp.dot(weights[rows, :], dx_ref[...], preferred_element_type=F32)
-        return part.T.astype(BF16)
-
-    out_ref[:, :ready] = product(ready_ref, pl.ds(0, ready))
+    contract = (((1,), (1,)), ((), ()))
+
+    def product(weights):
+        return lax.dot_general(
+            dx_ref[...], weights, contract, preferred_element_type=F32
+        ).astype(BF16)
+
+    out_ref[:, :ready] = product(ready_ref[...])
 
     def step(j, _):
-        start = pl.multiple_of(j * tile, tile)
+        start = pl.multiple_of(ready + j * tile, fine)
         for i in range(0, tile, fine):
             copy(pl.multiple_of(start + i, fine), fine).wait()
-        rows = pl.ds(pl.multiple_of(start - ready, tile), tile)
-        out_ref[:, pl.ds(start, tile)] = product(table, rows)
+        rows = pl.ds(pl.multiple_of(j * tile, tile), tile)
+        out_ref[:, pl.ds(start, tile)] = product(table[rows, :])
         return 0
 
-    whole = voc // tile
-    lax.fori_loop(ready // tile, whole, step, 0)
-    if voc % tile:
-        last = whole * tile
+    whole = (voc - ready) // tile
+    lax.fori_loop(0, whole, step, 0)
+    last = ready + whole * tile
+    if last < voc:
         for start in range(last, voc, fine):
             copy(start, min(fine, voc - start)).wait()
-        out_ref[:, last:voc] = product(table, pl.ds(last - ready, voc - last))
+        out_ref[:, last:voc] = product(table[last - ready :, :])
 
 
 def swap_sum(send, keep, devices):
@@ -473,21 +519,22 @@
                 pltpu.VMEM((hidden, width), BF16), pltpu.SemaphoreType.DMA((hidden // 128,)),
             ),
         )
-        (first,) = first_rows(256, [embed], [lambda: 0], down_row)
-        table = [
-            pltpu.VMEM((part - 256, width // 2), BF16), pltpu.VMEM((total, width // 2), F32),
+        ready = 512
+        first = first_rows(ready, embed, down_row, True)
+        table = (
+            pltpu.VMEM((part - ready, width // 2), BF16), pltpu.VMEM((total, width // 2), F32),
             pltpu.SemaphoreType.DMA((-(-part // 128),)),
-        ]
-        args = dict(
-            streamed=(2,), kept=(1,), flops=flops, scratch=table, room=part * width
-        )
-        send, score_a = call(
-            functools.partial(half_kernel, True), [struct(half, BF16), column],
-            slices, first, embed, head_row, **args,
+        )
+        args = dict(streamed=(2,), kept=(1,), flops=flops, room=part * width)
+        send, score_a, first = call(
+            functools.partial(half_kernel, True),
+            [struct(half, BF16), column, pltpu.VMEM(first.shape, BF16)],
+            slices, first, embed, head_row,
+            scratch=(*table, pltpu.SemaphoreType.DMA((ready // 128,))), **args,
         )
         keep, score_b = call(
             functools.partial(half_kernel, False), [struct(half, F32), column],
-            slices, first, embed, head_row, **args,
+            slices, first, embed, head_row, scratch=table, **args,
         )
     else:
         send, keep, score_a = plain_half(slices, embed, head_row, devices)
@@ -496,20 +543,21 @@
     x_got = swap_cores(x_mine, devices)
     if tiled:
         wide = struct((total, hidden), F32)
-        weight = (width // 2, hidden)
-        sems = pltpu.SemaphoreType.DMA((2, chips))
+        weight = pltpu.VMEM((width // 2, hidden), BF16)
+        ahead = pltpu.VMEM((2 * own, hidden), BF16)
+        rest = pltpu.VMEM((width // 2 - 2 * own, hidden), BF16)
+        sems, next_sems = pltpu.SemaphoreType.DMA((2, chips)), pltpu.SemaphoreType.DMA((2, 2))
         args = dict(streamed=(2, 3), flops=2 * total * hidden * width, room=2 * width * hidden)
-        a, b, squares, gate, up = call(
-            first_kernel,
-            [wide, wide, column, pltpu.VMEM(weight, BF16), pltpu.VMEM(weight, BF16)],
-            x_mine, gain_row, w_gate, w_up, scratch=(sems,), **args,
+        a, b, squares, gate, up, next_gate, next_up = call(
+            first_kernel, [wide, wide, column, weight, weight, ahead, ahead],
+            x_mine, gain_row, w_gate, w_up, scratch=(sems, next_sems), **args,
         )
         narrow = struct((total, hidden), BF16)
         send, score_c, d_gate, d_up = call(
             second_kernel, [struct(half, BF16), column, narrow, narrow],
-            x_got, gain_row, w_gate, w_up, a, b, squares, down_row, counts,
-            scratch=(pltpu.VMEM(weight, BF16), pltpu.VMEM(weight, BF16), sems),
-            scalars=(8,), **args,
+            x_got, gain_row, w_gate, w_up, next_gate, next_up,
+            a, b, squares, down_row, counts,
+            scratch=(rest, rest, sems), kept=(4, 5), scalars=(10,), **args,
         )
         (keep,) = call(
             third_kernel, [struct(half, F32)], d_gate, d_up, gate, up,
@@ -530,14 +578,14 @@
     sources = (x_mine, x_got, d_mine, d_got, gain_row, head_row)
     padded = part + 3 * requests
     if tiled:
-        (first,) = first_rows(256, [embed], [lambda: 0], total_d)
+        first = first_rows(256, embed, total_d, False)
         (d_slices,) = call(
             input_kernel, [struct((total, padded), BF16)],
             *sources, score_a, score_b, score_c, counts, first, embed,
             scalars=(9,), kept=(10,), streamed=(11,), flops=2 * flops, room=2 * part * width,
             scratch=(
-                pltpu.VMEM((width, total), BF16), pltpu.VMEM((part - 256, width), BF16),
-                pltpu.SemaphoreType.DMA((-(-part // 64),)),
+                pltpu.VMEM((total, width), BF16), pltpu.VMEM((part - 256, width), BF16),
+                pltpu.SemaphoreType.DMA((-(-part // 256),)),
             ),
         )
     else:

time: 104 us -> 104 us (level)
  no operation moved by 1% of the time
where the time goes in v12:
time: 104 us; the launch traced here: 103 us
  blocking collectives  41.6 us (40%)
  Pallas kernels  37.6 us (36%)
  starting transfers between devices  11.6 us (11%)
  waiting for transfers between devices  9.18 us (9%)
  local copies, waits for them, and re-layouts  2.48 us (2%)
    all_to_all x4, blocking collectives, exchange_chips(): lax.all_to_all(blocks, 'dp', split_axis=0, concat_axis=0, axis_index_grou...  41.6 us
    pallas_call x11, Pallas kernels, call(): pl.pallas_call(kernel, out_shape=outs, in_specs=specs, out_specs=[VMEM_SP...  37.6 us
    all_to_all x2, starting transfers between devices, exchange(): return lax.all_to_all(blocks, 'dp', split_axis=0, concat_axis=0, tiled=True)  10.9 us
    all_to_all x2, waiting for transfers between devices, exchange(): return lax.all_to_all(blocks, 'dp', split_axis=0, concat_axis=0, tiled=True)  9.17 us
  transfers between devices with their start and end apart: 6, of which 2 were waited for; matrix products, arithmetic and copies ran while one was open for 1% of the time, Pallas kernels for 16%

profile of v12, /device:TPU:0, one launch (start us, length us, event | category | flops | bytes accessed | tf_op | source)
XLA Modules:
  0.0 103.4 jit_solution(13848528410683653933)
XLA Ops:
  0.6 0.0 copy-start
  0.6 0.9 copy-done
  1.5 1.4 %shard_map.95 = (bf16[16,2,2000]{2,1,0:T(2,128)(2,1)}, f32[2,1]{1,0:T(2,128)S(1)}, f32[2,1]{1,0:T(2,128)S(1)}) custom-call(bf16[2,32000]{1,0:T(2,128)(2,1)S(1)} %copy-done), custom_call_target="tpu_custom_call" | custom-call | bytes 128000 | tf_op jit(solution)/shard_map/pallas_call | solution.py:54
  3.0 7.4 %all-to-all-start = ((bf16[16,2,2000]{2,1,0:T(2,128)(2,1)}), bf16[16,2,2000]{2,1,0:T(2,128)(2,1)S(1)}, u32[]{:S(2)}, u32[]{:S(2)}) async-start(bf16[16,2,2000]{2,1,0:T(2,128)(2,1)} %get-tuple-element.25.after_ref), calls=%async_computation | async-start | bytes 262144 | tf_op jit(solution)/shard_map/all_to_all | solution.py:21
  10.4 0.7 reshape.25.head_ref
  11.1 4.4 %shard_map.96.after_ref.down_ref = f32[1,896]{1,0:T(1,128)S(1)} custom-call(bf16[1,4096]{1,0:T(2,128)(2,1)S(1)} %reshape.25.head_ref, bf16[896,4096]{1,0:T(8,128)(2,1)} %down_ref.1, bf16[16,2,2000]{2,1,0:T(2,128)(2,1)} %get-tuple-element.25.after_ref), custom_call_target="tpu_custom_call" | custom-call | flops 7340032 | bytes 7476224 | tf_op jit(solution)/shard_map/pallas_call | solution.py:54
  15.4 1.6 %shard_map.97.ready_ref = bf16[512,2048]{1,0:T(8,128)(2,1)S(1)} custom-call(bf16[2000,4096]{1,0:T(8,128)(2,1)} %embed_ref.5, f32[1,896]{1,0:T(1,128)S(1)} %shard_map.96.after_ref.down_ref), custom_call_target="tpu_custom_call" | custom-call | bytes 16387584 | tf_op jit(solution)/shard_map/pallas_call | solution.py:54
  17.0 1.3 %all-to-all-done = bf16[16,2,2000]{2,1,0:T(2,128)(2,1)S(1)} async-done(((bf16[16,2,2000]{2,1,0:T(2,128)(2,1)}), bf16[16,2,2000]{2,1,0:T(2,128)(2,1)S(1)}, u32[]{:S(2)}, u32[]{:S(2)}) %all-to-all-start) | async-done | bytes 128032 | tf_op jit(solution)/shard_map/all_to_all | solution.py:21
  18.3 0.1 reshape.24.slices_ref
  18.4 3.7 %shard_map.98 = (bf16[8,32,256]{2,1,0:T(8,128)(2,1)S(1)}, f32[32,1]{1,0:T(8,128)S(1)}, bf16[512,2048]{1,0:T(8,128)(2,1)S(1)}) custom-call(bf16[32,2000]{1,0:T(8,128)(2,1)S(1)} %reshape.24.slices_ref, bf16[512,2048]{1,0:T(8,128)(2,1)S(1)} %shard_map.97.ready_ref, bf16[2000,4096]{1,0:T(8,128)(2,1)} %embed_ref.5, bf16[1,4096]{1,0:T(2,128)(2,1)S(1)} %reshape.25.head_ref), custom_call_target="tpu_custom_call" | custom-call | flops 262144000 | bytes 18617344 | tf_op jit(solution)/shard_map/pallas_call | solution.py:54
  22.1 0.1 collective-permute-start
  22.2 0.0 copy-start.3
  22.2 3.2 %shard_map.99 = (f32[8,32,256]{2,1,0:T(8,128)S(1)}, f32[32,1]{1,0:T(8,128)S(1)}) custom-call(bf16[32,2000]{1,0:T(8,128)(2,1)S(1)} %reshape.24.slices_ref, bf16[512,2048]{1,0:T(8,128)(2,1)S(1)} %get-tuple-element.26.ready_ref, bf16[2000,4096]{1,0:T(8,128)(2,1)} %embed_ref.5, bf16[1,4096]{1,0:T(2,128)(2,1)S(1)} %reshape.25.head_ref), custom_call_target="tpu_custom_call" | custom-call | flops 262144000 | bytes 18617344 | tf_op jit(solution)/shard_map/pallas_call | solution.py:54
  25.4 12.1 %all_to_all.30 = bf16[8,32,256]{2,1,0:T(8,128)(2,1)S(1)} all-to-all(bf16[8,32,256]{2,1,0:T(8,128)(2,1)S(1)} %add_convert_fusion.1), channel_id=1, replica_groups={{0,2,4,6,8,10,12,14},{1,3,5,7,9,11,13,15},{16,18,20,22,24,26,28,30},{17..., dimensions={0} | all-to-all | bytes 262144 | tf_op jit(solution)/shard_map/all_to_all | solution.py:26
  37.6 9.9 %all_to_all.31.x_ref.mine_ref = bf16[8,32,256]{2,1,0:T(8,128)(2,1)S(1)} all-to-all(bf16[8,32,256]{2,1,0:T(8,128)(2,1)S(1)} %broadcast_in_dim.4), channel_id=1, replica_groups={{0,2,4,6,8,10,12,14},{1,3,5,7,9,11,13,15},{16,18,20,22,24,26,28,30},{17..., dimensions={0} | all-to-all | bytes 262144 | tf_op jit(solution)/shard_map/all_to_all | solution.py:26
  47.4 0.0 copy-start.2
  47.4 4.0 %shard_map.100 = (f32[32,896]{1,0:T(8,128)S(1)}, f32[32,896]{1,0:T(8,128)S(1)}, f32[32,1]{1,0:T(8,128)S(1)}, bf16[2048,896]{1,0:T(8,128)(2,1)S(1)}, bf16[2048,89...) custom-call(bf16[8,32,256]{2,1,0:T(8,128)(2,1)S(1)} %all_to_all.31.x_ref.mine_ref, ...), custom_call_target="tpu_custom_call" | custom-call | flops 234881024 | bytes 14819328 | tf_op jit(solution)/shard_map/pallas_call | solution.py:54
  51.4 0.0 collective-permute-done.1.x_ref.got_ref
  51.4 5.9 %shard_map.101 = (bf16[8,32,256]{2,1,0:T(8,128)(2,1)S(1)}, f32[32,1]{1,0:T(8,128)S(1)}, bf16[32,896]{1,0:T(8,128)(2,1)S(1)}, bf16[32,896]{1,0:T(8,128)(2,1)S(1)}) custom-call(bf16[8,32,256]{2,1,0:T(8,128)(2,1)S(1)} %collective-permute-done.1.x_ref.got_ref, bf16[1,4096]{1,0:T(2,128)(2,1)S(1)} %reshape.26.gain_ref, bf16[4096,896]{1,0:T(8,128)(2,1)} %gate_ref.3, ...), custom_call_target="tpu_custom_call" | custom-call | flops 234881024 | bytes 16887440 | tf_op jit(solution)/shard_map/pallas_call | solution.py:54
  57.4 0.6 collective-permute-start.2
  58.0 2.2 %shard_map.102 = f32[8,32,256]{2,1,0:T(8,128)S(1)} custom-call(bf16[32,896]{1,0:T(8,128)(2,1)S(1)} %get-tuple-element.34.d_gate_ref, bf16[32,896]{1,0:T(8,128)(2,1)S(1)} %get-tuple-element.35.d_up_ref, bf16[2048,896]{1,0:T(8,128)(2,1)S(1)} %get-tuple-element.36.gate_ref, bf16[2048,896]{1,0:T(8,128)(2,1)S(1)} %get-tuple-element.37.up_ref), custom_call_target="tpu_custom_call" | custom-call | flops 234881024 | bytes 7454720 | tf_op jit(solution)/shard_map/pallas_call | solution.py:54
  60.2 0.0 collective-permute-done.2
  60.3 9.8 %all_to_all.32 = bf16[8,32,256]{2,1,0:T(8,128)(2,1)S(1)} all-to-all(bf16[8,32,256]{2,1,0:T(8,128)(2,1)S(1)} %add_convert_fusion), channel_id=1, replica_groups={{0,2,4,6,8,10,12,14},{1,3,5,7,9,11,13,15},{16,18,20,22,24,26,28,30},{17..., dimensions={0} | all-to-all | bytes 262144 | tf_op jit(solution)/shard_map/all_to_all | solution.py:26
  70.2 9.8 %all_to_all.33.d_mine_ref = bf16[8,32,256]{2,1,0:T(8,128)(2,1)S(1)} all-to-all(bf16[8,32,256]{2,1,0:T(8,128)(2,1)S(1)} %broadcast_in_dim.5), channel_id=1, replica_groups={{0,2,4,6,8,10,12,14},{1,3,5,7,9,11,13,15},{16,18,20,22,24,26,28,30},{17..., dimensions={0} | all-to-all | bytes 262144 | tf_op jit(solution)/shard_map/all_to_all | solution.py:26
  80.0 0.0 collective-permute-start.3
  80.0 1.6 %shard_map.103.ready_ref = bf16[256,4096]{1,0:T(8,128)(2,1)S(1)} custom-call(bf16[2000,4096]{1,0:T(8,128)(2,1)} %embed_ref.5, bf16[32,256]{1,0:T(8,128)(2,1)S(1)} %reduce_sum.25.after_ref), custom_call_target="tpu_custom_call" | custom-call | bytes 16400384 | tf_op jit(solution)/shard_map/pallas_call | solution.py:54
  81.6 0.0 copy-start.1
  81.6 8.4 %shard_map.104 = bf16[32,2012]{1,0:T(8,128)(2,1)S(1)} custom-call(bf16[8,32,256]{2,1,0:T(8,128)(2,1)S(1)} %all_to_all.31.x_ref.mine_ref, bf16[8,32,256]{2,1,0:T(8,128)(2,1)S(1)} %collective-permute-done.1.x_ref.got_ref, bf16[8,32,256]{2,1,0:T(8,128)(2,1)S(1)} %all_to_all.33.d_mine_ref, bf16[8,32,256]{2,1,0:T(8,128)(2,1)S(1)} %collective-permute-done.3.d_got_ref, ...), custom_call_target="tpu_custom_call" | custom-call | flops 524288000 | bytes 19022224 | tf_op jit(solution)/shard_map/pallas_call | solution.py:54
  90.0 0.8 reshape.27
  90.8 3.5 %all-to-all-start.5 = ((bf16[16,2,2012]{2,1,0:T(2,128)(2,1)}), bf16[16,2,2012]{2,1,0:T(2,128)(2,1)S(1)}, u32[]{:S(2)}, u32[]{:S(2)}) async-start(bf16[16,2,2012]{2,1,0:T(2,128)(2,1)} %reshape.27), calls=%async_computation.5 | async-start | bytes 262144 | tf_op jit(solution)/shard_map/all_to_all | solution.py:21
  94.3 7.9 %all-to-all-done.5.back_ref = bf16[16,2,2012]{2,1,0:T(2,128)(2,1)S(1)} async-done(((bf16[16,2,2012]{2,1,0:T(2,128)(2,1)}), bf16[16,2,2012]{2,1,0:T(2,128)(2,1)S(1)}, u32[]{:S(2)}, u32[]{:S(2)}) %all-to-all-start.5) | async-done | bytes 128800 | tf_op jit(solution)/shard_map/all_to_all | solution.py:21
  102.2 1.2 %shard_map.105 = (bf16[2,32000]{1,0:T(2,128)(2,1)}, f32[1,4]{1,0:T(1,128)}) custom-call(bf16[2,32000]{1,0:T(2,128)(2,1)S(1)} %copy-done.1, f32[2,1]{1,0:T(2,128)S(1)} %get-tuple-element.23.top_ref, f32[2,1]{1,0:T(2,128)S(1)} %get-tuple-element.24.scale_ref, bf16[16,2,2012]{2,1,0:T(2,128)(2,1)S(1)} %all-to-all-done.5.back_ref, ...), custom_call_target="tpu_custom_call" | custom-call | bytes 256800 | tf_op jit(solution)/shard_map/pallas_call | solution.py:54
  (14 shorter events, 0.2 us)
Async XLA Ops:
  0.6 0.9 copy-start
  3.0 15.3 %all-to-all-start = ((bf16[16,2,2000]{2,1,0:T(2,128)(2,1)}), bf16[16,2,2000]{2,1,0:T(2,128)(2,1)S(1)}, u32[]{:S(2)}, u32[]{:S(2)}) async-start(bf16[16,2,2000]{2,1,0:T(2,128)(2,1)} %get-tuple-element.25.after_ref), calls=%async_computation | async-start | bytes 262144 | tf_op jit(solution)/shard_map/all_to_all | solution.py:21
  22.1 3.3 %collective-permute-start = (bf16[8,32,256]{2,1,0:T(8,128)(2,1)S(1)}, bf16[8,32,256]{2,1,0:T(8,128)(2,1)S(1)}, u32[]{:S(2)}, u32[]{:S(2)}) collective-permute-start(bf16[8,32,256]{2,1,0:T(8,128)(2,1)S(1)} %get-tuple-element.28), channel_id=1, source_target_pairs={{0,1},{1,0},{2,3},{3,2},{4,5},{5,4},{6,7},{7,6},{8,9},{9,8},{10,11... | collective-permute-start | bytes 393224 | tf_op jit(solution)/shard_map/ppermute | solution.py:17
  22.2 25.3 %copy-start.3 = (bf16[4096]{0:T(1024)(128)(2,1)S(1)}, bf16[4096]{0:T(1024)(128)(2,1)}, u32[]{:S(2)}) copy-start(bf16[4096]{0:T(1024)(128)(2,1)} %param.10) | copy-start | bytes 24580
  47.4 4.0 %collective-permute-start.1 = (bf16[8,32,256]{2,1,0:T(8,128)(2,1)S(1)}, bf16[8,32,256]{2,1,0:T(8,128)(2,1)S(1)}, u32[]{:S(2)}, u32[]{:S(2)}) collective-permute-start(bf16[8,32,256]{2,1,0:T(8,128)(2,1)S(1)} %all_to_all.31.x_ref.mine_ref), channel_id=1, source_target_pairs={{0,1},{1,0},{2,3},{3,2},{4,5},{5,4},{6,7},{7,6},{8,9},{9,8},{10,11... | collective-permute-start | bytes 393224 | tf_op jit(solution)/shard_map/ppermute | solution.py:17
  47.4 4.0 %copy-start.2 = (s32[4]{0:T(128)S(1)}, s32[4]{0:T(128)}, u32[]{:S(2)}) copy-start(s32[4]{0:T(128)} %counts_ref.3) | copy-start | bytes 52
  57.4 2.8 %collective-permute-start.2 = (bf16[8,32,256]{2,1,0:T(8,128)(2,1)S(1)}, bf16[8,32,256]{2,1,0:T(8,128)(2,1)S(1)}, u32[]{:S(2)}, u32[]{:S(2)}) collective-permute-start(bf16[8,32,256]{2,1,0:T(8,128)(2,1)S(1)} %get-tuple-element.38), channel_id=1, source_target_pairs={{0,1},{1,0},{2,3},{3,2},{4,5},{5,4},{6,7},{7,6},{8,9},{9,8},{10,11... | collective-permute-start | bytes 393224 | tf_op jit(solution)/shard_map/ppermute | solution.py:17
  80.0 1.6 %collective-permute-start.3 = (bf16[8,32,256]{2,1,0:T(8,128)(2,1)S(1)}, bf16[8,32,256]{2,1,0:T(8,128)(2,1)S(1)}, u32[]{:S(2)}, u32[]{:S(2)}) collective-permute-start(bf16[8,32,256]{2,1,0:T(8,128)(2,1)S(1)} %all_to_all.33.d_mine_ref), channel_id=1, source_target_pairs={{0,1},{1,0},{2,3},{3,2},{4,5},{5,4},{6,7},{7,6},{8,9},{9,8},{10,11... | collective-permute-start | bytes 393224 | tf_op jit(solution)/shard_map/ppermute | solution.py:17
  81.6 20.6 %copy-start.1 = (bf16[2,32000]{1,0:T(2,128)(2,1)S(1)}, bf16[2,32000]{1,0:T(2,128)(2,1)}, u32[]{:S(2)}) copy-start(bf16[2,32000]{1,0:T(2,128)(2,1)} %logits_ref.3) | copy-start | bytes 384004
  90.8 11.4 %all-to-all-start.5 = ((bf16[16,2,2012]{2,1,0:T(2,128)(2,1)}), bf16[16,2,2012]{2,1,0:T(2,128)(2,1)S(1)}, u32[]{:S(2)}, u32[]{:S(2)}) async-start(bf16[16,2,2012]{2,1,0:T(2,128)(2,1)} %reshape.27), calls=%async_computation.5 | async-start | bytes 262144 | tf_op jit(solution)/shard_map/all_to_all | solution.py:21

commit v13 on v12

--- a/solution.py
+++ b/solution.py
@@ -203,10 +203,13 @@
         copy.wait()
 
 
-def down_kernel(head_ref, down_ref, after_ref, out_ref, table, sems):
+def early_kernel(
+    head_ref, down_ref, embed_ref, gate_ref, up_ref, after_ref,
+    out_ref, first, both, table, sems, first_sems, both_sems,
+):
     del after_ref
-    width = down_ref.shape[1]
-    lanes = 128
+    width, lanes = down_ref.shape[1], 128
+    core = this_core()
 
     def copy(j):
         rows = span(j * lanes, lanes)
@@ -215,6 +218,13 @@
     steps = sems.shape[0]
     for j in range(steps):
         copy(j).start()
+    half = width // 2
+    own = both.shape[0] // 2
+    chips = half // own
+    others = bring(embed_ref, first, first_sems, span((1 - core) * half, half))
+    others += bring_blocks(gate_ref, up_ref, both, core, range(2), own, chips, both_sems)
+    for other in others:
+        other.start()
 
     def step(j, _):
         copy(j).wait()
@@ -227,23 +237,37 @@
         return 0
 
     lax.fori_loop(0, steps, step, 0)
-
-
-def bring_blocks(refs, half, blocks, own, chips, sems):
+    for other in others:
+        other.wait()
+
+
+def bring_blocks(gate_ref, up_ref, both, half, blocks, own, chips, sems):
+    hidden = gate_ref.shape[1]
     return [
         pltpu.make_async_copy(
             source.at[span((half * chips + j) * own, own)],
-            target.at[pl.ds((j - blocks[0]) * own, own)],
+            both.at[pl.ds((j - blocks[0]) * own, own), pl.ds(k * hidden, hidden)],
             sems.at[k, j - blocks[0]],
         )
         for j in blocks
-        for k, (source, target) in enumerate(refs)
+        for k, source in enumerate((gate_ref, up_ref))
     ]
+
+
+def weight_rows(ready, both, own):
+    skip = ready.shape[0] // own
+
+    def weights(j):
+        if j < skip:
+            return ready[j * own : (j + 1) * own]
+        return both[(j - skip) * own : (j - skip + 1) * own]
+
+    return skip, weights
 
 
 def forward_half(x_ref, gain_ref, half, sums, weights, wait):
     chips, _, own = x_ref.shape
-    a, b, squares = sums
+    products, squares = sums
     scaled = []
     for j in range(chips):
         x = x_ref[j].astype(F32)
@@ -252,94 +276,69 @@
         scaled.append((x * gain).astype(BF16))
     for j in range(chips):
         wait(j)
-        gate, up = weights(j)
-        a = a + jnp.dot(scaled[j], gate, preferred_element_type=F32)
-        b = b + jnp.dot(scaled[j], up, preferred_element_type=F32)
-    return a, b, squares
-
-
-def backward_half(d_gate, d_up, weights, out_ref):
+        products = products + jnp.dot(scaled[j], weights(j), preferred_element_type=F32)
+    return products, squares
+
+
+def backward_half(d_both, weights, out_ref):
     contract = (((1,), (1,)), ((), ()))
     for j in range(out_ref.shape[0]):
-        gate, up = weights(j)
-        part = lax.dot_general(d_gate, gate, contract, preferred_element_type=F32)
-        part += lax.dot_general(d_up, up, contract, preferred_element_type=F32)
+        part = lax.dot_general(d_both, weights(j), contract, preferred_element_type=F32)
         out_ref[j] = part.astype(out_ref.dtype)
 
 
 def first_kernel(
-    x_ref, gain_ref, gate_ref, up_ref,
-    a_ref, b_ref, squares_ref, gate, up, next_gate, next_up, sems, next_sems,
+    x_ref, gain_ref, gate_ref, up_ref, ready_ref,
+    products_ref, squares_ref, both, ahead, sems, ahead_sems,
 ):
     chips, _, own = x_ref.shape
     core = this_core()
-    refs = ((gate_ref, gate), (up_ref, up))
-    stream = Stream(bring_blocks(refs, core, range(chips), own, chips, sems))
-    refs = ((gate_ref, next_gate), (up_ref, next_up))
-    ahead = range(next_gate.shape[0] // own)
-    following = bring_blocks(refs, 1 - core, ahead, own, chips, next_sems)
+    skip, weights = weight_rows(ready_ref, both, own)
+    blocks = range(skip, chips)
+    stream = Stream(bring_blocks(gate_ref, up_ref, both, core, blocks, own, chips, sems))
+    blocks = range(ahead.shape[0] // own)
+    following = bring_blocks(gate_ref, up_ref, ahead, 1 - core, blocks, own, chips, ahead_sems)
     for copy in following:
         copy.start()
-    zeros = jnp.zeros(a_ref.shape, F32)
-    sums = (zeros, zeros, jnp.zeros(squares_ref.shape, F32))
-
-    def weights(j):
-        r = slice(j * own, (j + 1) * own)
-        return gate[r], up[r]
-
-    a_ref[...], b_ref[...], squares_ref[...] = forward_half(
-        x_ref, gain_ref, core, sums, weights, lambda j: stream.wait(2 * (j + 1))
+    sums = (jnp.zeros(products_ref.shape, F32), jnp.zeros(squares_ref.shape, F32))
+    products_ref[...], squares_ref[...] = forward_half(
+        x_ref, gain_ref, core, sums, weights, lambda j: stream.wait(2 * (j - skip + 1))
     )
     for copy in following:
         copy.wait()
 
 
 def second_kernel(
-    x_ref, gain_ref, gate_ref, up_ref, first_gate, first_up,
-    a_ref, b_ref, squares_ref, down_ref, counts_ref,
-    send_ref, score_ref, d_gate_ref, d_up_ref, gate, up, sems,
+    x_ref, gain_ref, gate_ref, up_ref, ready_ref, products_ref, squares_ref, down_ref, counts_ref,
+    send_ref, score_ref, d_both_ref, both, sems,
 ):
     chips, total, own = x_ref.shape
-    width = gate_ref.shape[0]
+    width, hidden = gate_ref.shape
     half = 1 - this_core()
-    skip = first_gate.shape[0] // own
-    refs = ((gate_ref, gate), (up_ref, up))
-    stream = Stream(bring_blocks(refs, half, range(skip, chips), own, chips, sems))
-
-    def weights(j):
-        if j < skip:
-            r = slice(j * own, (j + 1) * own)
-            return first_gate[r], first_up[r]
-        r = slice((j - skip) * own, (j - skip + 1) * own)
-        return gate[r], up[r]
-
-    sums = (a_ref[...], b_ref[...], squares_ref[...])
-    a, b, squares = forward_half(
+    skip, weights = weight_rows(ready_ref, both, own)
+    blocks = range(skip, chips)
+    stream = Stream(bring_blocks(gate_ref, up_ref, both, half, blocks, own, chips, sems))
+    sums = (products_ref[...], squares_ref[...])
+    products, squares = forward_half(
         x_ref, gain_ref, half, sums, weights, lambda j: stream.wait(2 * (j - skip + 1))
     )
     inv = lax.rsqrt(squares / width + 1e-05)
-    a, b = a * inv, b * inv
+    a, b = products[:, :hidden] * inv, products[:, hidden:] * inv
     sigma = jax.nn.sigmoid(a)
     active = a * sigma
     down = down_ref[...]
-    hidden = (active * b).astype(BF16).astype(F32)
-    score_ref[...] = jnp.sum(hidden * down, axis=-1, keepdims=True)
+    rounded = (active * b).astype(BF16).astype(F32)
+    score_ref[...] = jnp.sum(rounded * down, axis=-1, keepdims=True)
     valid, _ = valid_column(counts_ref, total)
     d_hidden = valid * down
-    d_gate = (d_hidden * b * sigma * (1.0 + a * (1.0 - sigma))).astype(BF16)
-    d_up = (d_hidden * active).astype(BF16)
-    d_gate_ref[...], d_up_ref[...] = d_gate, d_up
-    backward_half(d_gate, d_up, weights, send_ref)
-
-
-def third_kernel(d_gate_ref, d_up_ref, gate_ref, up_ref, keep_ref):
-    own = keep_ref.shape[2]
-
-    def weights(j):
-        r = slice(j * own, (j + 1) * own)
-        return gate_ref[r], up_ref[r]
-
-    backward_half(d_gate_ref[...], d_up_ref[...], weights, keep_ref)
+    d_both_ref[:, :hidden] = (d_hidden * b * sigma * (1.0 + a * (1.0 - sigma))).astype(BF16)
+    d_both_ref[:, hidden:] = (d_hidden * active).astype(BF16)
+    backward_half(d_both_ref[...], weights, send_ref)
+
+
+def third_kernel(d_both_ref, ready_ref, both_ref, keep_ref):
+    _, weights = weight_rows(ready_ref, both_ref, keep_ref.shape[2])
+    backward_half(d_both_ref[...], weights, keep_ref)
 
 
 def input_kernel(
@@ -353,7 +352,9 @@
     width = 2 * chips * own
     core = this_core()
     ready = ready_ref.shape[0]
-    tile, fine = 512, 256
+    tile, fine, depth = 256, 128, 3
+    steps = (voc - ready) // tile
+    last = ready + steps * tile
 
     def copy(start, size):
         return pltpu.make_async_copy(
@@ -362,9 +363,16 @@
             sems.at[start // fine],
         )
 
-    pieces_of = range(ready, voc, fine)
-    for start in pieces_of:
-        copy(start, min(fine, voc - start)).start()
+    def pieces(start, end):
+        return [copy(start + i, min(fine, end - start - i)) for i in range(0, end - start, fine)]
+
+    def step_pieces(j):
+        start = pl.multiple_of(ready + j * tile, fine)
+        return [copy(pl.multiple_of(start + i, fine), fine) for i in range(0, tile, fine)]
+
+    for j in range(min(depth, steps)):
+        for piece in step_pieces(j):
+            piece.start()
     sources = ((mine_ref, d_mine_ref, core), (got_ref, d_got_ref, 1 - core))
     squares = jnp.zeros((total, 1), F32)
     dots = jnp.zeros((total, 1), F32)
@@ -387,12 +395,12 @@
     score = valid * (score_a_ref[...] + score_b_ref[...] + score_c_ref[...])
     member = request == lax.broadcasted_iota(jnp.int32, (total, requests), 1)
     value = jnp.sum(jnp.where(member, score, 0.0), axis=0, keepdims=True)
-    pieces = []
+    parts = []
     for _ in range(3):
         piece = value.astype(BF16).astype(F32)
-        pieces.append(piece)
+        parts.append(piece)
         value = value - piece
-    for i, piece in enumerate(pieces):
+    for i, piece in enumerate(parts):
         start = voc + i * requests
         spread = jnp.broadcast_to(piece, (total, requests)).astype(BF16)
         out_ref[:, start : start + requests] = spread
@@ -406,19 +414,27 @@
     out_ref[:, :ready] = product(ready_ref[...])
 
     def step(j, _):
-        start = pl.multiple_of(ready + j * tile, fine)
-        for i in range(0, tile, fine):
-            copy(pl.multiple_of(start + i, fine), fine).wait()
+        for piece in step_pieces(j):
+            piece.wait()
+
+        @pl.when(j + depth < steps)
+        def _():
+            for piece in step_pieces(j + depth):
+                piece.start()
+
+        @pl.when(j + depth == steps)
+        def _():
+            for piece in pieces(last, voc):
+                piece.start()
+
         rows = pl.ds(pl.multiple_of(j * tile, tile), tile)
-        out_ref[:, pl.ds(start, tile)] = product(table[rows, :])
+        out_ref[:, pl.ds(pl.multiple_of(ready + j * tile, tile), tile)] = product(table[rows, :])
         return 0
 
-    whole = (voc - ready) // tile
-    lax.fori_loop(0, whole, step, 0)
-    last = ready + whole * tile
+    lax.fori_loop(0, steps, step, 0)
     if last < voc:
-        for start in range(last, voc, fine):
-            copy(start, min(fine, voc - start)).wait()
+        for piece in pieces(last, voc):
+            piece.wait()
         out_ref[:, last:voc] = product(table[last - ready :, :])
 
 
@@ -512,29 +528,38 @@
     half = (chips, total, own)
     flops = total * part * width
     if tiled:
-        (down_row,) = call(
-            down_kernel, [struct((1, hidden), F32)], head_row, w_down, blocked,
-            streamed=(1,), flops=2 * hidden * width, room=2 * hidden * width,
+        ready = 256
+        down_row, first, both_first = call(
+            early_kernel,
+            [
+                struct((1, hidden), F32), pltpu.VMEM((ready, width // 2), BF16),
+                pltpu.VMEM((2 * own, 2 * hidden), BF16),
+            ],
+            head_row, w_down, embed, w_gate, w_up, blocked,
+            streamed=(1, 2, 3, 4), flops=2 * hidden * width, room=2 * hidden * width,
             scratch=(
                 pltpu.VMEM((hidden, width), BF16), pltpu.SemaphoreType.DMA((hidden // 128,)),
+                pltpu.SemaphoreType.DMA((ready // 128,)), pltpu.SemaphoreType.DMA((2, 2)),
             ),
         )
-        ready = 512
-        first = first_rows(ready, embed, down_row, True)
-        table = (
-            pltpu.VMEM((part - ready, width // 2), BF16), pltpu.VMEM((total, width // 2), F32),
-            pltpu.SemaphoreType.DMA((-(-part // 128),)),
-        )
+
+        def table(ready):
+            return (
+                pltpu.VMEM((part - ready, width // 2), BF16),
+                pltpu.VMEM((total, width // 2), F32),
+                pltpu.SemaphoreType.DMA((-(-part // 128),)),
+            )
+
         args = dict(streamed=(2,), kept=(1,), flops=flops, room=part * width)
         send, score_a, first = call(
             functools.partial(half_kernel, True),
-            [struct(half, BF16), column, pltpu.VMEM(first.shape, BF16)],
+            [struct(half, BF16), column, pltpu.VMEM((2 * ready, width // 2), BF16)],
             slices, first, embed, head_row,
-            scratch=(*table, pltpu.SemaphoreType.DMA((ready // 128,))), **args,
+            scratch=(*table(ready), pltpu.SemaphoreType.DMA((ready // 64,))), **args,
         )
         keep, score_b = call(
             functools.partial(half_kernel, False), [struct(half, F32), column],
-            slices, first, embed, head_row, scratch=table, **args,
+            slices, first, embed, head_row, scratch=table(2 * ready), **args,
         )
     else:
         send, keep, score_a = plain_half(slices, embed, head_row, devices)
@@ -542,26 +567,28 @@
     x_mine = chip_gather(chip_sum(summed, devices), devices)
     x_got = swap_cores(x_mine, devices)
     if tiled:
-        wide = struct((total, hidden), F32)
-        weight = pltpu.VMEM((width // 2, hidden), BF16)
-        ahead = pltpu.VMEM((2 * own, hidden), BF16)
-        rest = pltpu.VMEM((width // 2 - 2 * own, hidden), BF16)
-        sems, next_sems = pltpu.SemaphoreType.DMA((2, chips)), pltpu.SemaphoreType.DMA((2, 2))
-        args = dict(streamed=(2, 3), flops=2 * total * hidden * width, room=2 * width * hidden)
-        a, b, squares, gate, up, next_gate, next_up = call(
-            first_kernel, [wide, wide, column, weight, weight, ahead, ahead],
-            x_mine, gain_row, w_gate, w_up, scratch=(sems, next_sems), **args,
-        )
-        narrow = struct((total, hidden), BF16)
-        send, score_c, d_gate, d_up = call(
-            second_kernel, [struct(half, BF16), column, narrow, narrow],
-            x_got, gain_row, w_gate, w_up, next_gate, next_up,
-            a, b, squares, down_row, counts,
-            scratch=(rest, rest, sems), kept=(4, 5), scalars=(10,), **args,
+        weight = (width // 2 - 2 * own, 2 * hidden)
+        sems, ahead_sems = pltpu.SemaphoreType.DMA((2, chips)), pltpu.SemaphoreType.DMA((2, 2))
+        args = dict(
+            streamed=(2, 3), kept=(4,), flops=2 * total * hidden * width, room=2 * width * hidden
+        )
+        products, squares, both, ahead = call(
+            first_kernel,
+            [
+                struct((total, 2 * hidden), F32), column, pltpu.VMEM(weight, BF16),
+                pltpu.VMEM(both_first.shape, BF16),
+            ],
+            x_mine, gain_row, w_gate, w_up, both_first, scratch=(sems, ahead_sems), **args,
+        )
+        send, score_c, d_both = call(
+            second_kernel,
+            [struct(half, BF16), column, struct((total, 2 * hidden), BF16)],
+            x_got, gain_row, w_gate, w_up, ahead, products, squares, down_row, counts,
+            scratch=(pltpu.VMEM(weight, BF16), sems), scalars=(8,), **args,
         )
         (keep,) = call(
-            third_kernel, [struct(half, F32)], d_gate, d_up, gate, up,
-            kept=(2, 3), flops=2 * total * hidden * width,
+            third_kernel, [struct(half, F32)], d_both, both_first, both,
+            kept=(1, 2), flops=2 * total * hidden * width,
         )
     else:
         down_row = jnp.sum(w_down.astype(F32) * head.astype(F32)[None, :], axis=-1)[None]
@@ -585,7 +612,7 @@
             scalars=(9,), kept=(10,), streamed=(11,), flops=2 * flops, room=2 * part * width,
             scratch=(
                 pltpu.VMEM((total, width), BF16), pltpu.VMEM((part - 256, width), BF16),
-                pltpu.SemaphoreType.DMA((-(-part // 256),)),
+                pltpu.SemaphoreType.DMA((-(-part // 128),)),
             ),
         )
     else:

time: 104 us -> 103 us (level)
  Pallas kernels: 37.6 us -> 36.3 us
    pallas_call x11 -> x10, Pallas kernels: 37.6 us -> 36.3 us  [call(): pl.pallas_call(kernel, out_shape=outs, in_specs=specs, out_specs=[VMEM_SP...]
  transfers between devices with their start and end apart: 6 -> 6, of which waited for: 2 -> 2; matrix products, arithmetic and copies ran while one was open for 1% -> 1% of each run, Pallas kernels for 16% -> 15%
where the time goes in v13:
time: 103 us; the launch traced here: 102 us
  blocking collectives  40.6 us (39%)
  Pallas kernels  36.3 us (35%)
  starting transfers between devices  11.5 us (11%)
  waiting for transfers between devices  10.1 us (10%)
  local copies, waits for them, and re-layouts  2.48 us (2%)
    all_to_all x4, blocking collectives, exchange_chips(): lax.all_to_all(blocks, 'dp', split_axis=0, concat_axis=0, axis_index_grou...  40.6 us
    pallas_call x10, Pallas kernels, call(): pl.pallas_call(kernel, out_shape=outs, in_specs=specs, out_specs=[VMEM_SP...  36.3 us
    all_to_all x2, starting transfers between devices, exchange(): return lax.all_to_all(blocks, 'dp', split_axis=0, concat_axis=0, tiled=True)  10.9 us
    all_to_all x2, waiting for transfers between devices, exchange(): return lax.all_to_all(blocks, 'dp', split_axis=0, concat_axis=0, tiled=True)  10.1 us
  transfers between devices with their start and end apart: 6, of which 2 were waited for; matrix products, arithmetic and copies ran while one was open for 1% of the time, Pallas kernels for 15%

profile of v13, /device:TPU:0, one launch (start us, length us, event | category | flops | bytes accessed | tf_op | source)
XLA Modules:
  0.0 102.0 jit_solution(2008591713119688712)
XLA Ops:
  0.6 0.0 copy-start
  0.6 0.9 copy-done
  1.5 1.4 %shard_map.95 = (bf16[16,2,2000]{2,1,0:T(2,128)(2,1)}, f32[2,1]{1,0:T(2,128)S(1)}, f32[2,1]{1,0:T(2,128)S(1)}) custom-call(bf16[2,32000]{1,0:T(2,128)(2,1)S(1)} %copy-done), custom_call_target="tpu_custom_call" | custom-call | bytes 128000 | tf_op jit(solution)/shard_map/pallas_call | solution.py:54
  3.0 7.4 %all-to-all-start = ((bf16[16,2,2000]{2,1,0:T(2,128)(2,1)}), bf16[16,2,2000]{2,1,0:T(2,128)(2,1)S(1)}, u32[]{:S(2)}, u32[]{:S(2)}) async-start(bf16[16,2,2000]{2,1,0:T(2,128)(2,1)} %get-tuple-element.24.after_ref), calls=%async_computation | async-start | bytes 262144 | tf_op jit(solution)/shard_map/all_to_all | solution.py:21
  10.4 0.7 reshape.25.head_ref
  11.1 5.0 %shard_map.96 = (f32[1,896]{1,0:T(1,128)S(1)}, bf16[256,2048]{1,0:T(8,128)(2,1)S(1)}, bf16[512,1792]{1,0:T(8,128)(2,1)S(1)}) custom-call(bf16[1,4096]{1,0:T(2,128)(2,1)S(1)} %reshape.25.head_ref, bf16[896,4096]{1,0:T(8,128)(2,1)} %down_ref.1, bf16[2000,4096]{1,0:T(8,128)(2,1)} %embed_ref.7, bf16[4096,896]{1,0:T(8,128)(2,1)} %gate_ref.5, ...), custom_call_target="tpu_custom_call" | custom-call | flops 7340032 | bytes 38540288 | tf_op jit(solution)/shard_map/pallas_call | solution.py:54
  16.0 2.2 %all-to-all-done = bf16[16,2,2000]{2,1,0:T(2,128)(2,1)S(1)} async-done(((bf16[16,2,2000]{2,1,0:T(2,128)(2,1)}), bf16[16,2,2000]{2,1,0:T(2,128)(2,1)S(1)}, u32[]{:S(2)}, u32[]{:S(2)}) %all-to-all-start) | async-done | bytes 128032 | tf_op jit(solution)/shard_map/all_to_all | solution.py:21
  18.3 0.1 reshape.24.slices_ref
  18.4 4.0 %shard_map.97 = (bf16[8,32,256]{2,1,0:T(8,128)(2,1)S(1)}, f32[32,1]{1,0:T(8,128)S(1)}, bf16[512,2048]{1,0:T(8,128)(2,1)S(1)}) custom-call(bf16[32,2000]{1,0:T(8,128)(2,1)S(1)} %reshape.24.slices_ref, bf16[256,2048]{1,0:T(8,128)(2,1)S(1)} %get-tuple-element.25.ready_ref, bf16[2000,4096]{1,0:T(8,128)(2,1)} %embed_ref.7, bf16[1,4096]{1,0:T(2,128)(2,1)S(1)} %reshape.25.head_ref), custom_call_target="tpu_custom_call" | custom-call | flops 262144000 | bytes 17568768 | tf_op jit(solution)/shard_map/pallas_call | solution.py:54
  22.4 0.1 collective-permute-start
  22.4 0.0 copy-start.3
  22.5 3.2 %shard_map.98 = (f32[8,32,256]{2,1,0:T(8,128)S(1)}, f32[32,1]{1,0:T(8,128)S(1)}) custom-call(bf16[32,2000]{1,0:T(8,128)(2,1)S(1)} %reshape.24.slices_ref, bf16[512,2048]{1,0:T(8,128)(2,1)S(1)} %get-tuple-element.26.ready_ref, bf16[2000,4096]{1,0:T(8,128)(2,1)} %embed_ref.7, bf16[1,4096]{1,0:T(2,128)(2,1)S(1)} %reshape.25.head_ref), custom_call_target="tpu_custom_call" | custom-call | flops 262144000 | bytes 18617344 | tf_op jit(solution)/shard_map/pallas_call | solution.py:54
  25.7 0.0 collective-permute-done
  25.7 11.1 %all_to_all.30 = bf16[8,32,256]{2,1,0:T(8,128)(2,1)S(1)} all-to-all(bf16[8,32,256]{2,1,0:T(8,128)(2,1)S(1)} %add_convert_fusion.1), channel_id=1, replica_groups={{0,2,4,6,8,10,12,14},{1,3,5,7,9,11,13,15},{16,18,20,22,24,26,28,30},{17..., dimensions={0} | all-to-all | bytes 262144 | tf_op jit(solution)/shard_map/all_to_all | solution.py:26
  36.9 9.9 %all_to_all.31.x_ref.mine_ref = bf16[8,32,256]{2,1,0:T(8,128)(2,1)S(1)} all-to-all(bf16[8,32,256]{2,1,0:T(8,128)(2,1)S(1)} %broadcast_in_dim.4), channel_id=1, replica_groups={{0,2,4,6,8,10,12,14},{1,3,5,7,9,11,13,15},{16,18,20,22,24,26,28,30},{17..., dimensions={0} | all-to-all | bytes 262144 | tf_op jit(solution)/shard_map/all_to_all | solution.py:26
  46.7 0.0 collective-permute-start.1
  46.8 0.0 copy-start.2
  46.8 3.7 %shard_map.99 = (f32[32,1792]{1,0:T(8,128)S(1)}, f32[32,1]{1,0:T(8,128)S(1)}, bf16[1536,1792]{1,0:T(8,128)(2,1)S(1)}, bf16[512,1792]{1,0:T(8,128)(2,1)S(1)}) custom-call(bf16[8,32,256]{2,1,0:T(8,128)(2,1)S(1)} %all_to_all.31.x_ref.mine_ref, bf16[1,4096]{1,0:T(2,128)(2,1)S(1)} %reshape.26.gain_ref, bf16[4096,896]{1,0:T(8,128)(2,1)} %gate_ref.5, ...), custom_call_target="tpu_custom_call" | custom-call | flops 234881024 | bytes 16654336 | tf_op jit(solution)/shard_map/pallas_call | solution.py:54
  50.5 0.0 collective-permute-done.1.x_ref.got_ref
  50.5 5.7 %shard_map.100 = (bf16[8,32,256]{2,1,0:T(8,128)(2,1)S(1)}, f32[32,1]{1,0:T(8,128)S(1)}, bf16[32,1792]{1,0:T(8,128)(2,1)S(1)}) custom-call(bf16[8,32,256]{2,1,0:T(8,128)(2,1)S(1)} %collective-permute-done.1.x_ref.got_ref, bf16[1,4096]{1,0:T(2,128)(2,1)S(1)} %reshape.26.gain_ref, bf16[4096,896]{1,0:T(8,128)(2,1)} %gate_ref.5, bf16[4096,896]{1,0:T(8,128)(2,1)} %up_ref.5, ...), custom_call_target="tpu_custom_call" | custom-call | flops 234881024 | bytes 16887440 | tf_op jit(solution)/shard_map/pallas_call | solution.py:54
  56.2 0.6 collective-permute-start.2
  56.8 2.2 %shard_map.101 = f32[8,32,256]{2,1,0:T(8,128)S(1)} custom-call(bf16[32,1792]{1,0:T(8,128)(2,1)S(1)} %get-tuple-element.34.d_both_ref, bf16[512,1792]{1,0:T(8,128)(2,1)S(1)} %get-tuple-element.29.ready_ref, bf16[1536,1792]{1,0:T(8,128)(2,1)S(1)} %get-tuple-element.35.both_ref), custom_call_target="tpu_custom_call" | custom-call | flops 234881024 | bytes 7454720 | tf_op jit(solution)/shard_map/pallas_call | solution.py:54
  59.0 0.0 collective-permute-done.2
  59.1 9.8 %all_to_all.32 = bf16[8,32,256]{2,1,0:T(8,128)(2,1)S(1)} all-to-all(bf16[8,32,256]{2,1,0:T(8,128)(2,1)S(1)} %add_convert_fusion), channel_id=1, replica_groups={{0,2,4,6,8,10,12,14},{1,3,5,7,9,11,13,15},{16,18,20,22,24,26,28,30},{17..., dimensions={0} | all-to-all | bytes 262144 | tf_op jit(solution)/shard_map/all_to_all | solution.py:26
  68.9 9.8 %all_to_all.33.d_mine_ref = bf16[8,32,256]{2,1,0:T(8,128)(2,1)S(1)} all-to-all(bf16[8,32,256]{2,1,0:T(8,128)(2,1)S(1)} %broadcast_in_dim.5), channel_id=1, replica_groups={{0,2,4,6,8,10,12,14},{1,3,5,7,9,11,13,15},{16,18,20,22,24,26,28,30},{17..., dimensions={0} | all-to-all | bytes 262144 | tf_op jit(solution)/shard_map/all_to_all | solution.py:26
  78.8 1.6 %shard_map.102.ready_ref = bf16[256,4096]{1,0:T(8,128)(2,1)S(1)} custom-call(bf16[2000,4096]{1,0:T(8,128)(2,1)} %embed_ref.7, bf16[32,256]{1,0:T(8,128)(2,1)S(1)} %reduce_sum.25.after_ref), custom_call_target="tpu_custom_call" | custom-call | bytes 16400384 | tf_op jit(solution)/shard_map/pallas_call | solution.py:54
  80.4 0.0 copy-start.1
  80.4 8.2 %shard_map.103 = bf16[32,2012]{1,0:T(8,128)(2,1)S(1)} custom-call(bf16[8,32,256]{2,1,0:T(8,128)(2,1)S(1)} %all_to_all.31.x_ref.mine_ref, bf16[8,32,256]{2,1,0:T(8,128)(2,1)S(1)} %collective-permute-done.1.x_ref.got_ref, bf16[8,32,256]{2,1,0:T(8,128)(2,1)S(1)} %all_to_all.33.d_mine_ref, bf16[8,32,256]{2,1,0:T(8,128)(2,1)S(1)} %collective-permute-done.3.d_got_ref, ...), custom_call_target="tpu_custom_call" | custom-call | flops 524288000 | bytes 19022224 | tf_op jit(solution)/shard_map/pallas_call | solution.py:54
  88.6 0.8 reshape.27
  89.4 3.5 %all-to-all-start.5 = ((bf16[16,2,2012]{2,1,0:T(2,128)(2,1)}), bf16[16,2,2012]{2,1,0:T(2,128)(2,1)S(1)}, u32[]{:S(2)}, u32[]{:S(2)}) async-start(bf16[16,2,2012]{2,1,0:T(2,128)(2,1)} %reshape.27), calls=%async_computation.5 | async-start | bytes 262144 | tf_op jit(solution)/shard_map/all_to_all | solution.py:21
  92.9 7.9 %all-to-all-done.5.back_ref = bf16[16,2,2012]{2,1,0:T(2,128)(2,1)S(1)} async-done(((bf16[16,2,2012]{2,1,0:T(2,128)(2,1)}), bf16[16,2,2012]{2,1,0:T(2,128)(2,1)S(1)}, u32[]{:S(2)}, u32[]{:S(2)}) %all-to-all-start.5) | async-done | bytes 128800 | tf_op jit(solution)/shard_map/all_to_all | solution.py:21
  100.8 1.2 %shard_map.104 = (bf16[2,32000]{1,0:T(2,128)(2,1)}, f32[1,4]{1,0:T(1,128)}) custom-call(bf16[2,32000]{1,0:T(2,128)(2,1)S(1)} %copy-done.1, f32[2,1]{1,0:T(2,128)S(1)} %get-tuple-element.22.top_ref, f32[2,1]{1,0:T(2,128)S(1)} %get-tuple-element.23.scale_ref, bf16[16,2,2012]{2,1,0:T(2,128)(2,1)S(1)} %all-to-all-done.5.back_ref, ...), custom_call_target="tpu_custom_call" | custom-call | bytes 256800 | tf_op jit(solution)/shard_map/pallas_call | solution.py:54
  (13 shorter events, 0.2 us)
Async XLA Ops:
  0.6 0.9 copy-start
  3.0 15.3 %all-to-all-start = ((bf16[16,2,2000]{2,1,0:T(2,128)(2,1)}), bf16[16,2,2000]{2,1,0:T(2,128)(2,1)S(1)}, u32[]{:S(2)}, u32[]{:S(2)}) async-start(bf16[16,2,2000]{2,1,0:T(2,128)(2,1)} %get-tuple-element.24.after_ref), calls=%async_computation | async-start | bytes 262144 | tf_op jit(solution)/shard_map/all_to_all | solution.py:21
  22.4 3.3 %collective-permute-start = (bf16[8,32,256]{2,1,0:T(8,128)(2,1)S(1)}, bf16[8,32,256]{2,1,0:T(8,128)(2,1)S(1)}, u32[]{:S(2)}, u32[]{:S(2)}) collective-permute-start(bf16[8,32,256]{2,1,0:T(8,128)(2,1)S(1)} %get-tuple-element.28), channel_id=1, source_target_pairs={{0,1},{1,0},{2,3},{3,2},{4,5},{5,4},{6,7},{7,6},{8,9},{9,8},{10,11... | collective-permute-start | bytes 393224 | tf_op jit(solution)/shard_map/ppermute | solution.py:17
  22.4 24.3 %copy-start.3 = (bf16[4096]{0:T(1024)(128)(2,1)S(1)}, bf16[4096]{0:T(1024)(128)(2,1)}, u32[]{:S(2)}) copy-start(bf16[4096]{0:T(1024)(128)(2,1)} %param.10) | copy-start | bytes 24580
  46.7 3.7 %collective-permute-start.1 = (bf16[8,32,256]{2,1,0:T(8,128)(2,1)S(1)}, bf16[8,32,256]{2,1,0:T(8,128)(2,1)S(1)}, u32[]{:S(2)}, u32[]{:S(2)}) collective-permute-start(bf16[8,32,256]{2,1,0:T(8,128)(2,1)S(1)} %all_to_all.31.x_ref.mine_ref), channel_id=1, source_target_pairs={{0,1},{1,0},{2,3},{3,2},{4,5},{5,4},{6,7},{7,6},{8,9},{9,8},{10,11... | collective-permute-start | bytes 393224 | tf_op jit(solution)/shard_map/ppermute | solution.py:17
  46.8 3.7 %copy-start.2 = (s32[4]{0:T(128)S(1)}, s32[4]{0:T(128)}, u32[]{:S(2)}) copy-start(s32[4]{0:T(128)} %counts_ref.3) | copy-start | bytes 52
  56.2 2.8 %collective-permute-start.2 = (bf16[8,32,256]{2,1,0:T(8,128)(2,1)S(1)}, bf16[8,32,256]{2,1,0:T(8,128)(2,1)S(1)}, u32[]{:S(2)}, u32[]{:S(2)}) collective-permute-start(bf16[8,32,256]{2,1,0:T(8,128)(2,1)S(1)} %get-tuple-element.36), channel_id=1, source_target_pairs={{0,1},{1,0},{2,3},{3,2},{4,5},{5,4},{6,7},{7,6},{8,9},{9,8},{10,11... | collective-permute-start | bytes 393224 | tf_op jit(solution)/shard_map/ppermute | solution.py:17
  78.8 1.6 %collective-permute-start.3 = (bf16[8,32,256]{2,1,0:T(8,128)(2,1)S(1)}, bf16[8,32,256]{2,1,0:T(8,128)(2,1)S(1)}, u32[]{:S(2)}, u32[]{:S(2)}) collective-permute-start(bf16[8,32,256]{2,1,0:T(8,128)(2,1)S(1)} %all_to_all.33.d_mine_ref), channel_id=1, source_target_pairs={{0,1},{1,0},{2,3},{3,2},{4,5},{5,4},{6,7},{7,6},{8,9},{9,8},{10,11... | collective-permute-start | bytes 393224 | tf_op jit(solution)/shard_map/ppermute | solution.py:17
  80.4 20.4 %copy-start.1 = (bf16[2,32000]{1,0:T(2,128)(2,1)S(1)}, bf16[2,32000]{1,0:T(2,128)(2,1)}, u32[]{:S(2)}) copy-start(bf16[2,32000]{1,0:T(2,128)(2,1)} %logits_ref.3) | copy-start | bytes 384004
  89.4 11.4 %all-to-all-start.5 = ((bf16[16,2,2012]{2,1,0:T(2,128)(2,1)}), bf16[16,2,2012]{2,1,0:T(2,128)(2,1)S(1)}, u32[]{:S(2)}, u32[]{:S(2)}) async-start(bf16[16,2,2012]{2,1,0:T(2,128)(2,1)} %reshape.27), calls=%async_computation.5 | async-start | bytes 262144 | tf_op jit(solution)/shard_map/all_to_all | solution.py:21

commit v14 on v13

--- a/solution.py
+++ b/solution.py
@@ -92,25 +92,20 @@
     return pl.ds(pl.multiple_of(start, size), size)
 
 
-def softmax_kernel(logits_ref, out_ref, top_ref, scale_ref):
+def softmax_kernel(logits_ref, out_ref, probs_ref):
     devices, _, part = out_ref.shape
     x = logits_ref[...].astype(F32)
-    top = jnp.max(x, axis=-1, keepdims=True)
-    e = jnp.exp(x - top)
-    scale = 1.0 / jnp.sum(e, axis=-1, keepdims=True)
-    probs = e * scale
+    e = jnp.exp(x - jnp.max(x, axis=-1, keepdims=True))
+    probs = e * (1.0 / jnp.sum(e, axis=-1, keepdims=True))
+    probs_ref[...] = probs
     for d in range(devices):
         out_ref[d] = probs[:, d * part : (d + 1) * part].astype(BF16)
-    top_ref[...] = top
-    scale_ref[...] = scale
-
-
-def final_kernel(
-    logits_ref, top_ref, scale_ref, back_ref, counts_ref, out_ref, rewards_ref, d_ref
-):
+
+
+def final_kernel(probs_ref, back_ref, counts_ref, out_ref, rewards_ref, d_ref):
     devices, _, padded = back_ref.shape
     part = out_ref.shape[1] // devices
-    requests = counts_ref.shape[1]
+    requests = counts_ref.shape[0]
     sums = jnp.zeros((1, requests), F32)
     for d in range(devices):
         block = back_ref[d].astype(F32)
@@ -118,9 +113,12 @@
         for i in range(3):
             start = part + i * requests
             sums += block[:1, start : start + requests]
-    rewards_ref[...] = sums / counts_ref[...]
-    probs = jnp.exp(logits_ref[...].astype(F32) - top_ref[...]) * scale_ref[...]
-    d_probs = d_ref[...]
+    lane = lax.broadcasted_iota(jnp.int32, (1, requests), 1)
+    counts = jnp.ones((1, requests), F32)
+    for r in range(requests):
+        counts = jnp.where(lane == r, counts_ref[r].astype(F32), counts)
+    rewards_ref[...] = sums / counts
+    probs, d_probs = probs_ref[...], d_ref[...]
     mean = jnp.sum(probs * d_probs, axis=-1, keepdims=True)
     out_ref[...] = (math.sqrt(VOC) * (probs * (d_probs - mean))).astype(BF16)
 
@@ -204,10 +202,10 @@
 
 
 def early_kernel(
-    head_ref, down_ref, embed_ref, gate_ref, up_ref, after_ref,
+    head_ref, down_ref, embed_ref, gate_ref, up_ref, after_ref, greeting_ref,
     out_ref, first, both, table, sems, first_sems, both_sems,
 ):
-    del after_ref
+    del after_ref, greeting_ref
     width, lanes = down_ref.shape[1], 128
     core = this_core()
 
@@ -269,11 +267,13 @@
     chips, _, own = x_ref.shape
     products, squares = sums
     scaled = []
+    wide = jnp.zeros(x_ref.shape[1:], F32)
     for j in range(chips):
         x = x_ref[j].astype(F32)
-        squares = squares + jnp.sum(x * x, axis=-1, keepdims=True)
+        wide = wide + x * x
         gain = gain_ref[:, span((half * chips + j) * own, own)].astype(F32)
         scaled.append((x * gain).astype(BF16))
+    squares = squares + jnp.sum(wide, axis=-1, keepdims=True)
     for j in range(chips):
         wait(j)
         products = products + jnp.dot(scaled[j], weights(j), preferred_element_type=F32)
@@ -310,7 +310,7 @@
 
 def second_kernel(
     x_ref, gain_ref, gate_ref, up_ref, ready_ref, products_ref, squares_ref, down_ref, counts_ref,
-    send_ref, score_ref, d_both_ref, both, sems,
+    send_ref, score_ref, inv_ref, d_both_ref, both, sems,
 ):
     chips, total, own = x_ref.shape
     width, hidden = gate_ref.shape
@@ -323,6 +323,7 @@
         x_ref, gain_ref, half, sums, weights, lambda j: stream.wait(2 * (j - skip + 1))
     )
     inv = lax.rsqrt(squares / width + 1e-05)
+    inv_ref[...] = inv
     a, b = products[:, :hidden] * inv, products[:, hidden:] * inv
     sigma = jax.nn.sigmoid(a)
     active = a * sigma
@@ -342,7 +343,7 @@
 
 
 def input_kernel(
-    mine_ref, got_ref, d_mine_ref, d_got_ref, gain_ref, head_ref,
+    mine_ref, got_ref, d_mine_ref, d_got_ref, gain_ref, head_ref, inv_ref,
     score_a_ref, score_b_ref, score_c_ref, counts_ref, ready_ref, embed_ref,
     out_ref, dx_ref, table, sems,
 ):
@@ -352,7 +353,7 @@
     width = 2 * chips * own
     core = this_core()
     ready = ready_ref.shape[0]
-    tile, fine, depth = 256, 128, 3
+    tile, fine = 256, 64
     steps = (voc - ready) // tile
     last = ready + steps * tile
 
@@ -370,27 +371,23 @@
         start = pl.multiple_of(ready + j * tile, fine)
         return [copy(pl.multiple_of(start + i, fine), fine) for i in range(0, tile, fine)]
 
-    for j in range(min(depth, steps)):
-        for piece in step_pieces(j):
-            piece.start()
+    for piece in pieces(ready, voc):
+        piece.start()
     sources = ((mine_ref, d_mine_ref, core), (got_ref, d_got_ref, 1 - core))
-    squares = jnp.zeros((total, 1), F32)
-    dots = jnp.zeros((total, 1), F32)
+    wide = jnp.zeros((total, own), F32)
     for x_ref, d_ref, half in sources:
         for j in range(chips):
-            x = x_ref[j].astype(F32)
-            g = d_ref[j].astype(F32) * gain_ref[:, span((half * chips + j) * own, own)].astype(F32)
-            squares += jnp.sum(x * x, axis=-1, keepdims=True)
-            dots += jnp.sum(g * x, axis=-1, keepdims=True)
-    inv = lax.rsqrt(squares / width + 1e-05)
-    mean = dots / width
+            gain = gain_ref[:, span((half * chips + j) * own, own)].astype(F32)
+            wide += d_ref[j].astype(F32) * gain * x_ref[j].astype(F32)
+    inv = inv_ref[...]
+    weight = inv * inv * inv * (jnp.sum(wide, axis=-1, keepdims=True) / width)
     valid, request = valid_column(counts_ref, total)
     for x_ref, d_ref, half in sources:
         for j in range(chips):
             columns = span((half * chips + j) * own, own)
             x = x_ref[j].astype(F32)
             g = d_ref[j].astype(F32) * gain_ref[:, columns].astype(F32)
-            dx = inv * g - x * inv * inv * inv * mean
+            dx = inv * g - x * weight
             dx_ref[:, columns] = (dx + valid * head_ref[:, columns].astype(F32)).astype(BF16)
     score = valid * (score_a_ref[...] + score_b_ref[...] + score_c_ref[...])
     member = request == lax.broadcasted_iota(jnp.int32, (total, requests), 1)
@@ -417,16 +414,6 @@
         for piece in step_pieces(j):
             piece.wait()
 
-        @pl.when(j + depth < steps)
-        def _():
-            for piece in step_pieces(j + depth):
-                piece.start()
-
-        @pl.when(j + depth == steps)
-        def _():
-            for piece in pieces(last, voc):
-                piece.start()
-
         rows = pl.ds(pl.multiple_of(j * tile, tile), tile)
         out_ref[:, pl.ds(pl.multiple_of(ready + j * tile, tile), tile)] = product(table[rows, :])
         return 0
@@ -516,9 +503,11 @@
     tiled = own % 128 == 0 and hidden % 128 == 0 and total % 16 == 0 and part % 16 == 0 and part > 512
     head_row, gain_row = head.reshape(1, width), norm_gain.reshape(1, width)
     if tiled:
-        column = struct((rows, 1), F32)
-        blocked, top, scale = call(
-            softmax_kernel, [struct((devices, rows, part), BF16), column, column], logits
+        around = [(i, (i + devices // 4) % devices) for i in range(devices)]
+        greeting = lax.ppermute(gain_row[:, :128], "dp", around)
+        blocked, probs = call(
+            softmax_kernel,
+            [struct((devices, rows, part), BF16), pltpu.VMEM((rows, voc), F32)], logits,
         )
     else:
         probs32 = jax.nn.softmax(logits.astype(F32), axis=-1)
@@ -535,7 +524,7 @@
                 struct((1, hidden), F32), pltpu.VMEM((ready, width // 2), BF16),
                 pltpu.VMEM((2 * own, 2 * hidden), BF16),
             ],
-            head_row, w_down, embed, w_gate, w_up, blocked,
+            head_row, w_down, embed, w_gate, w_up, blocked, greeting,
             streamed=(1, 2, 3, 4), flops=2 * hidden * width, room=2 * hidden * width,
             scratch=(
                 pltpu.VMEM((hidden, width), BF16), pltpu.SemaphoreType.DMA((hidden // 128,)),
@@ -580,9 +569,9 @@
             ],
             x_mine, gain_row, w_gate, w_up, both_first, scratch=(sems, ahead_sems), **args,
         )
-        send, score_c, d_both = call(
+        send, score_c, inv, d_both = call(
             second_kernel,
-            [struct(half, BF16), column, struct((total, 2 * hidden), BF16)],
+            [struct(half, BF16), column, column, struct((total, 2 * hidden), BF16)],
             x_got, gain_row, w_gate, w_up, ahead, products, squares, down_row, counts,
             scratch=(pltpu.VMEM(weight, BF16), sems), scalars=(8,), **args,
         )
@@ -602,36 +591,35 @@
     total_d = chip_sum(swap_sum(send, keep, devices), devices)
     d_mine = chip_gather(total_d, devices)
     d_got = swap_cores(d_mine, devices)
-    sources = (x_mine, x_got, d_mine, d_got, gain_row, head_row)
     padded = part + 3 * requests
     if tiled:
         first = first_rows(256, embed, total_d, False)
         (d_slices,) = call(
             input_kernel, [struct((total, padded), BF16)],
-            *sources, score_a, score_b, score_c, counts, first, embed,
-            scalars=(9,), kept=(10,), streamed=(11,), flops=2 * flops, room=2 * part * width,
+            x_mine, x_got, d_mine, d_got, gain_row, head_row, inv,
+            score_a, score_b, score_c, counts, first, embed,
+            scalars=(10,), kept=(11,), streamed=(12,), flops=2 * flops, room=2 * part * width,
             scratch=(
                 pltpu.VMEM((total, width), BF16), pltpu.VMEM((part - 256, width), BF16),
-                pltpu.SemaphoreType.DMA((-(-part // 128),)),
+                pltpu.SemaphoreType.DMA((-(-part // 64),)),
             ),
         )
     else:
-        d_slices = plain_input(*sources, valid, embed)
+        d_slices = plain_input(x_mine, x_got, d_mine, d_got, gain_row, head_row, valid, embed)
         score = jnp.where(member, valid * (score_a + score_c), 0.0)
         extra = split3(jnp.sum(score, axis=0)).reshape(1, requests * 3)
         extra = jnp.broadcast_to(extra, (total, requests * 3))
         d_slices = jnp.concatenate([d_slices, extra], axis=-1)
     back = exchange(d_slices.reshape(devices, rows, padded))
-    counts32 = counts.astype(F32)
     if tiled:
         guidance, rewards = call(
             final_kernel, [struct((rows, voc), BF16), struct((1, requests), F32)],
-            logits, top, scale, back, counts32.reshape(1, requests),
+            probs, back, counts, kept=(0,), scalars=(2,),
             scratch=(pltpu.VMEM((rows, voc), F32),),
         )
         return (guidance, rewards.reshape(requests))
     sums = jnp.sum(back[:, 0, part:].astype(F32).reshape(devices, requests, 3), axis=(0, 2))
-    rewards = sums / counts32
+    rewards = sums / counts.astype(F32)
     d_probs = back[:, :, :part].transpose(1, 0, 2).reshape(rows, voc).astype(F32)
     d_logits = probs32 * (d_probs - jnp.sum(probs32 * d_probs, axis=-1, keepdims=True))
     guidance = (math.sqrt(VOC) * d_logits).astype(BF16)

time: 103 us -> 105 us (1.019)
  blocking collectives: 40.6 us -> 50.7 us
  waiting for transfers between devices: 10.1 us -> 3.62 us
  starting transfers between devices: 11.5 us -> 10 us
    all_to_all x0 -> x1, blocking collectives: none -> 10.5 us  [exchange(): return lax.all_to_all(blocks, 'dp', split_axis=0, concat_axis=0, tiled=True)]
    all_to_all x2 -> x1, waiting for transfers between devices: 10.1 us -> 0.01 us  [exchange(): return lax.all_to_all(blocks, 'dp', split_axis=0, concat_axis=0, tiled=True)]
    ppermute x0 -> x1, waiting for transfers between devices: none -> 3.61 us  [body(): greeting = lax.ppermute(gain_row[:, :128], 'dp', around)]
    all_to_all x2 -> x1, starting transfers between devices: 10.9 us -> 7.39 us  [exchange(): return lax.all_to_all(blocks, 'dp', split_axis=0, concat_axis=0, tiled=True)]
    ppermute x0 -> x1, starting transfers between devices: none -> 1.98 us  [body(): greeting = lax.ppermute(gain_row[:, :128], 'dp', around)]
  transfers between devices with their start and end apart: 6 -> 6, of which waited for: 2 -> 1; matrix products, arithmetic and copies ran while one was open for 1% -> 1% of each run, Pallas kernels for 15% -> 15%
where the time goes in v14:
time: 105 us; the launch traced here: 104 us
  blocking collectives  50.7 us (48%)
  Pallas kernels  36.4 us (35%)
  starting transfers between devices  10 us (10%)
  waiting for transfers between devices  3.62 us (3%)
  local copies, waits for them, and re-layouts  2.51 us (2%)
    all_to_all x4, blocking collectives, exchange_chips(): lax.all_to_all(blocks, 'dp', split_axis=0, concat_axis=0, axis_index_grou...  40.2 us
    pallas_call x10, Pallas kernels, call(): pl.pallas_call(kernel, out_shape=outs, in_specs=specs, out_specs=[VMEM_SP...  36.4 us
    all_to_all x1, blocking collectives, exchange(): return lax.all_to_all(blocks, 'dp', split_axis=0, concat_axis=0, tiled=True)  10.5 us
    all_to_all x1, starting transfers between devices, exchange(): return lax.all_to_all(blocks, 'dp', split_axis=0, concat_axis=0, tiled=True)  7.39 us
    ppermute x1, waiting for transfers between devices, body(): greeting = lax.ppermute(gain_row[:, :128], 'dp', around)  3.61 us
  transfers between devices with their start and end apart: 6, of which 1 were waited for; matrix products, arithmetic and copies ran while one was open for 1% of the time, Pallas kernels for 15%

profile of v14, /device:TPU:0, one launch (start us, length us, event | category | flops | bytes accessed | tf_op | source)
XLA Modules:
  0.0 104.2 jit_solution(1535531183226248085)
XLA Ops:
  0.6 0.9 copy-done
  1.5 1.4 %shard_map.95 = (bf16[16,2,2000]{2,1,0:T(2,128)(2,1)}, f32[2,32000]{1,0:T(2,128)S(1)}) custom-call(bf16[2,32000]{1,0:T(2,128)(2,1)S(1)} %copy-done), custom_call_target="tpu_custom_call" | custom-call | bytes 128000 | tf_op jit(solution)/shard_map/pallas_call | solution.py:54
  2.9 7.4 %all-to-all-start = ((bf16[16,2,2000]{2,1,0:T(2,128)(2,1)}), bf16[16,2,2000]{2,1,0:T(2,128)(2,1)S(1)}, u32[]{:S(2)}, u32[]{:S(2)}) async-start(bf16[16,2,2000]{2,1,0:T(2,128)(2,1)} %get-tuple-element.23.after_ref), calls=%async_computation | async-start | bytes 262144 | tf_op jit(solution)/shard_map/all_to_all | solution.py:21
  10.3 0.7 reshape.23.gain_ref
  11.1 2.0 %collective-permute-start = (bf16[1,128]{1,0:T(2,128)(2,1)S(1)}, bf16[1,128]{1,0:T(2,128)(2,1)S(1)}, u32[]{:S(2)}, u32[]{:S(2)}) collective-permute-start(bf16[1,128]{1,0:T(2,128)(2,1)S(1)} %slice.4), channel_id=1, source_target_pairs={{0,4},{1,5},{2,6},{3,7},{4,8},{5,9},{6,10},{7,11},{8,12},{9,13},{1... | collective-permute-start | bytes 776 | tf_op jit(solution)/shard_map/ppermute | solution.py:507
  13.0 0.7 reshape.22.head_ref
  13.8 3.6 %collective-permute-done.greeting_ref = bf16[1,128]{1,0:T(2,128)(2,1)S(1)} collective-permute-done((bf16[1,128]{1,0:T(2,128)(2,1)S(1)}, bf16[1,128]{1,0:T(2,128)(2,1)S(1)}, u32[]{:S(2)}, u32[]{:S(2)}) %collective-permute-start) | collective-permute-done | bytes 288 | tf_op jit(solution)/shard_map/ppermute | solution.py:507
  17.4 5.0 %shard_map.96 = (f32[1,896]{1,0:T(1,128)S(1)}, bf16[256,2048]{1,0:T(8,128)(2,1)S(1)}, bf16[512,1792]{1,0:T(8,128)(2,1)S(1)}) custom-call(bf16[1,4096]{1,0:T(2,128)(2,1)S(1)} %reshape.22.head_ref, bf16[896,4096]{1,0:T(8,128)(2,1)} %down_ref.1, bf16[2000,4096]{1,0:T(8,128)(2,1)} %embed_ref.7, bf16[4096,896]{1,0:T(8,128)(2,1)} %gate_ref.5, ...), custom_call_target="tpu_custom_call" | custom-call | flops 7340032 | bytes 38540544 | tf_op jit(solution)/shard_map/pallas_call | solution.py:54
  22.3 0.0 all-to-all-done
  22.3 0.1 reshape.21.slices_ref
  22.4 4.0 %shard_map.97 = (bf16[8,32,256]{2,1,0:T(8,128)(2,1)S(1)}, f32[32,1]{1,0:T(8,128)S(1)}, bf16[512,2048]{1,0:T(8,128)(2,1)S(1)}) custom-call(bf16[32,2000]{1,0:T(8,128)(2,1)S(1)} %reshape.21.slices_ref, bf16[256,2048]{1,0:T(8,128)(2,1)S(1)} %get-tuple-element.24.ready_ref, bf16[2000,4096]{1,0:T(8,128)(2,1)} %embed_ref.7, bf16[1,4096]{1,0:T(2,128)(2,1)S(1)} %reshape.22.head_ref), custom_call_target="tpu_custom_call" | custom-call | flops 262144000 | bytes 17568768 | tf_op jit(solution)/shard_map/pallas_call | solution.py:54
  26.4 0.1 collective-permute-start.1
  26.5 3.2 %shard_map.98 = (f32[8,32,256]{2,1,0:T(8,128)S(1)}, f32[32,1]{1,0:T(8,128)S(1)}) custom-call(bf16[32,2000]{1,0:T(8,128)(2,1)S(1)} %reshape.21.slices_ref, bf16[512,2048]{1,0:T(8,128)(2,1)S(1)} %get-tuple-element.25.ready_ref, bf16[2000,4096]{1,0:T(8,128)(2,1)} %embed_ref.7, bf16[1,4096]{1,0:T(2,128)(2,1)S(1)} %reshape.22.head_ref), custom_call_target="tpu_custom_call" | custom-call | flops 262144000 | bytes 18617344 | tf_op jit(solution)/shard_map/pallas_call | solution.py:54
  29.7 0.0 collective-permute-done.1
  29.8 10.6 %all_to_all.30 = bf16[8,32,256]{2,1,0:T(8,128)(2,1)S(1)} all-to-all(bf16[8,32,256]{2,1,0:T(8,128)(2,1)S(1)} %add_convert_fusion.1), channel_id=1, replica_groups={{0,2,4,6,8,10,12,14},{1,3,5,7,9,11,13,15},{16,18,20,22,24,26,28,30},{17..., dimensions={0} | all-to-all | bytes 262144 | tf_op jit(solution)/shard_map/all_to_all | solution.py:26
  40.5 9.9 %all_to_all.31.x_ref.mine_ref = bf16[8,32,256]{2,1,0:T(8,128)(2,1)S(1)} all-to-all(bf16[8,32,256]{2,1,0:T(8,128)(2,1)S(1)} %broadcast_in_dim.4), channel_id=1, replica_groups={{0,2,4,6,8,10,12,14},{1,3,5,7,9,11,13,15},{16,18,20,22,24,26,28,30},{17..., dimensions={0} | all-to-all | bytes 262144 | tf_op jit(solution)/shard_map/all_to_all | solution.py:26
  50.3 0.0 collective-permute-start.2
  50.3 3.7 %shard_map.99 = (f32[32,1792]{1,0:T(8,128)S(1)}, f32[32,1]{1,0:T(8,128)S(1)}, bf16[1536,1792]{1,0:T(8,128)(2,1)S(1)}, bf16[512,1792]{1,0:T(8,128)(2,1)S(1)}) custom-call(bf16[8,32,256]{2,1,0:T(8,128)(2,1)S(1)} %all_to_all.31.x_ref.mine_ref, bf16[1,4096]{1,0:T(2,128)(2,1)S(1)} %reshape.23.gain_ref, bf16[4096,896]{1,0:T(8,128)(2,1)} %gate_ref.5, ...), custom_call_target="tpu_custom_call" | custom-call | flops 234881024 | bytes 16654336 | tf_op jit(solution)/shard_map/pallas_call | solution.py:54
  54.1 0.0 collective-permute-done.2.x_ref.got_ref
  54.1 5.8 %shard_map.100 = (bf16[8,32,256]{2,1,0:T(8,128)(2,1)S(1)}, f32[32,1]{1,0:T(8,128)S(1)}, f32[32,1]{1,0:T(8,128)S(1)}, bf16[32,1792]{1,0:T(8,128)(2,1)S(1)}) custom-call(bf16[8,32,256]{2,1,0:T(8,128)(2,1)S(1)} %collective-permute-done.2.x_ref.got_ref, bf16[1,4096]{1,0:T(2,128)(2,1)S(1)} %reshape.23.gain_ref, bf16[4096,896]{1,0:T(8,128)(2,1)} %gate_ref.5, ...), custom_call_target="tpu_custom_call" | custom-call | flops 234881024 | bytes 16887440 | tf_op jit(solution)/shard_map/pallas_call | solution.py:54
  59.8 0.6 collective-permute-start.3
  60.4 2.2 %shard_map.101 = f32[8,32,256]{2,1,0:T(8,128)S(1)} custom-call(bf16[32,1792]{1,0:T(8,128)(2,1)S(1)} %get-tuple-element.33.d_both_ref, bf16[512,1792]{1,0:T(8,128)(2,1)S(1)} %get-tuple-element.28.ready_ref, bf16[1536,1792]{1,0:T(8,128)(2,1)S(1)} %get-tuple-element.34.both_ref), custom_call_target="tpu_custom_call" | custom-call | flops 234881024 | bytes 7454720 | tf_op jit(solution)/shard_map/pallas_call | solution.py:54
  62.6 0.0 collective-permute-done.3
  62.7 9.8 %all_to_all.32 = bf16[8,32,256]{2,1,0:T(8,128)(2,1)S(1)} all-to-all(bf16[8,32,256]{2,1,0:T(8,128)(2,1)S(1)} %add_convert_fusion), channel_id=1, replica_groups={{0,2,4,6,8,10,12,14},{1,3,5,7,9,11,13,15},{16,18,20,22,24,26,28,30},{17..., dimensions={0} | all-to-all | bytes 262144 | tf_op jit(solution)/shard_map/all_to_all | solution.py:26
  72.6 9.8 %all_to_all.33.d_mine_ref = bf16[8,32,256]{2,1,0:T(8,128)(2,1)S(1)} all-to-all(bf16[8,32,256]{2,1,0:T(8,128)(2,1)S(1)} %broadcast_in_dim.5), channel_id=1, replica_groups={{0,2,4,6,8,10,12,14},{1,3,5,7,9,11,13,15},{16,18,20,22,24,26,28,30},{17..., dimensions={0} | all-to-all | bytes 262144 | tf_op jit(solution)/shard_map/all_to_all | solution.py:26
  82.4 0.0 collective-permute-start.4
  82.4 1.6 %shard_map.102.ready_ref = bf16[256,4096]{1,0:T(8,128)(2,1)S(1)} custom-call(bf16[2000,4096]{1,0:T(8,128)(2,1)} %embed_ref.7, bf16[32,256]{1,0:T(8,128)(2,1)S(1)} %reduce_sum.25.after_ref), custom_call_target="tpu_custom_call" | custom-call | bytes 16400384 | tf_op jit(solution)/shard_map/pallas_call | solution.py:54
  84.0 0.0 collective-permute-done.4.d_got_ref
  84.0 7.8 %shard_map.103 = bf16[32,2012]{1,0:T(8,128)(2,1)S(1)} custom-call(bf16[8,32,256]{2,1,0:T(8,128)(2,1)S(1)} %all_to_all.31.x_ref.mine_ref, bf16[8,32,256]{2,1,0:T(8,128)(2,1)S(1)} %collective-permute-done.2.x_ref.got_ref, bf16[8,32,256]{2,1,0:T(8,128)(2,1)S(1)} %all_to_all.33.d_mine_ref, bf16[8,32,256]{2,1,0:T(8,128)(2,1)S(1)} %collective-permute-done.4.d_got_ref, ...), custom_call_target="tpu_custom_call" | custom-call | flops 524288000 | bytes 19022352 | tf_op jit(solution)/shard_map/pallas_call | solution.py:54
  91.8 0.1 reshape.24
  91.9 10.5 %all_to_all.34.back_ref = bf16[16,2,2012]{2,1,0:T(2,128)(2,1)S(1)} all-to-all(bf16[16,2,2012]{2,1,0:T(2,128)(2,1)S(1)} %reshape.24), channel_id=1, replica_groups=mesh['groups'=2,'dp'=16] {'dp'}, dimensions={0} | all-to-all | bytes 257536 | tf_op jit(solution)/shard_map/all_to_all | solution.py:21
  102.4 1.8 %shard_map.104 = (bf16[2,32000]{1,0:T(2,128)(2,1)}, f32[1,4]{1,0:T(1,128)}) custom-call(f32[2,32000]{1,0:T(2,128)S(1)} %get-tuple-element.22.probs_ref, bf16[16,2,2012]{2,1,0:T(2,128)(2,1)S(1)} %all_to_all.34.back_ref, s32[4]{0:T(128)S(1)} %copy-done.1), custom_call_target="tpu_custom_call" | custom-call | bytes 384784 | tf_op jit(solution)/shard_map/pallas_call | solution.py:54
  (10 shorter events, 0.1 us)
Async XLA Ops:
  0.6 0.9 copy-start
  2.9 19.4 %all-to-all-start = ((bf16[16,2,2000]{2,1,0:T(2,128)(2,1)}), bf16[16,2,2000]{2,1,0:T(2,128)(2,1)S(1)}, u32[]{:S(2)}, u32[]{:S(2)}) async-start(bf16[16,2,2000]{2,1,0:T(2,128)(2,1)} %get-tuple-element.23.after_ref), calls=%async_computation | async-start | bytes 262144 | tf_op jit(solution)/shard_map/all_to_all | solution.py:21
  11.1 6.3 %collective-permute-start = (bf16[1,128]{1,0:T(2,128)(2,1)S(1)}, bf16[1,128]{1,0:T(2,128)(2,1)S(1)}, u32[]{:S(2)}, u32[]{:S(2)}) collective-permute-start(bf16[1,128]{1,0:T(2,128)(2,1)S(1)} %slice.4), channel_id=1, source_target_pairs={{0,4},{1,5},{2,6},{3,7},{4,8},{5,9},{6,10},{7,11},{8,12},{9,13},{1... | collective-permute-start | bytes 776 | tf_op jit(solution)/shard_map/ppermute | solution.py:507
  26.4 3.3 %collective-permute-start.1 = (bf16[8,32,256]{2,1,0:T(8,128)(2,1)S(1)}, bf16[8,32,256]{2,1,0:T(8,128)(2,1)S(1)}, u32[]{:S(2)}, u32[]{:S(2)}) collective-permute-start(bf16[8,32,256]{2,1,0:T(8,128)(2,1)S(1)} %get-tuple-element.27), channel_id=1, source_target_pairs={{0,1},{1,0},{2,3},{3,2},{4,5},{5,4},{6,7},{7,6},{8,9},{9,8},{10,11... | collective-permute-start | bytes 393224 | tf_op jit(solution)/shard_map/ppermute | solution.py:17
  50.3 3.7 %collective-permute-start.2 = (bf16[8,32,256]{2,1,0:T(8,128)(2,1)S(1)}, bf16[8,32,256]{2,1,0:T(8,128)(2,1)S(1)}, u32[]{:S(2)}, u32[]{:S(2)}) collective-permute-start(bf16[8,32,256]{2,1,0:T(8,128)(2,1)S(1)} %all_to_all.31.x_ref.mine_ref), channel_id=1, source_target_pairs={{0,1},{1,0},{2,3},{3,2},{4,5},{5,4},{6,7},{7,6},{8,9},{9,8},{10,11... | collective-permute-start | bytes 393224 | tf_op jit(solution)/shard_map/ppermute | solution.py:17
  50.3 3.7 %copy-start.1 = (s32[4]{0:T(128)S(1)}, s32[4]{0:T(128)}, u32[]{:S(2)}) copy-start(s32[4]{0:T(128)} %counts_ref.5) | copy-start | bytes 52
  59.8 2.8 %collective-permute-start.3 = (bf16[8,32,256]{2,1,0:T(8,128)(2,1)S(1)}, bf16[8,32,256]{2,1,0:T(8,128)(2,1)S(1)}, u32[]{:S(2)}, u32[]{:S(2)}) collective-permute-start(bf16[8,32,256]{2,1,0:T(8,128)(2,1)S(1)} %get-tuple-element.35), channel_id=1, source_target_pairs={{0,1},{1,0},{2,3},{3,2},{4,5},{5,4},{6,7},{7,6},{8,9},{9,8},{10,11... | collective-permute-start | bytes 393224 | tf_op jit(solution)/shard_map/ppermute | solution.py:17
  82.4 1.6 %collective-permute-start.4 = (bf16[8,32,256]{2,1,0:T(8,128)(2,1)S(1)}, bf16[8,32,256]{2,1,0:T(8,128)(2,1)S(1)}, u32[]{:S(2)}, u32[]{:S(2)}) collective-permute-start(bf16[8,32,256]{2,1,0:T(8,128)(2,1)S(1)} %all_to_all.33.d_mine_ref), channel_id=1, source_target_pairs={{0,1},{1,0},{2,3},{3,2},{4,5},{5,4},{6,7},{7,6},{8,9},{9,8},{10,11... | collective-permute-start | bytes 393224 | tf_op jit(solution)/shard_map/ppermute | solution.py:17

commit v15 on v14

--- a/solution.py
+++ b/solution.py
@@ -105,7 +105,7 @@
 def final_kernel(probs_ref, back_ref, counts_ref, out_ref, rewards_ref, d_ref):
     devices, _, padded = back_ref.shape
     part = out_ref.shape[1] // devices
-    requests = counts_ref.shape[0]
+    requests = counts_ref.shape[1]
     sums = jnp.zeros((1, requests), F32)
     for d in range(devices):
         block = back_ref[d].astype(F32)
@@ -113,11 +113,7 @@
         for i in range(3):
             start = part + i * requests
             sums += block[:1, start : start + requests]
-    lane = lax.broadcasted_iota(jnp.int32, (1, requests), 1)
-    counts = jnp.ones((1, requests), F32)
-    for r in range(requests):
-        counts = jnp.where(lane == r, counts_ref[r].astype(F32), counts)
-    rewards_ref[...] = sums / counts
+    rewards_ref[...] = sums / counts_ref[...]
     probs, d_probs = probs_ref[...], d_ref[...]
     mean = jnp.sum(probs * d_probs, axis=-1, keepdims=True)
     out_ref[...] = (math.sqrt(VOC) * (probs * (d_probs - mean))).astype(BF16)
@@ -131,7 +127,7 @@
     for r in range(requests):
         inside = (position >= r * length) & (position < r * length + counts_ref[r])
         valid = jnp.where(inside, 1.0, valid)
-    return valid, position // length
+    return valid
 
 
 def bring(source_ref, out_ref, sems, columns):
@@ -202,8 +198,8 @@
 
 
 def early_kernel(
-    head_ref, down_ref, embed_ref, gate_ref, up_ref, after_ref, greeting_ref,
-    out_ref, first, both, table, sems, first_sems, both_sems,
+    head_ref, down_ref, embed_ref, gate_ref, up_ref, counts_ref, after_ref, greeting_ref,
+    out_ref, valid_ref, counts_row, first, both, table, sems, first_sems, both_sems,
 ):
     del after_ref, greeting_ref
     width, lanes = down_ref.shape[1], 128
@@ -223,6 +219,12 @@
     others += bring_blocks(gate_ref, up_ref, both, core, range(2), own, chips, both_sems)
     for other in others:
         other.start()
+    valid_ref[...] = valid_column(counts_ref, valid_ref.shape[0])
+    lane = lax.broadcasted_iota(jnp.int32, counts_row.shape, 1)
+    counts = jnp.ones(counts_row.shape, F32)
+    for r in range(counts_row.shape[1]):
+        counts = jnp.where(lane == r, counts_ref[r].astype(F32), counts)
+    counts_row[...] = counts
 
     def step(j, _):
         copy(j).wait()
@@ -309,7 +311,7 @@
 
 
 def second_kernel(
-    x_ref, gain_ref, gate_ref, up_ref, ready_ref, products_ref, squares_ref, down_ref, counts_ref,
+    x_ref, gain_ref, gate_ref, up_ref, ready_ref, products_ref, squares_ref, down_ref, valid_ref,
     send_ref, score_ref, inv_ref, d_both_ref, both, sems,
 ):
     chips, total, own = x_ref.shape
@@ -330,8 +332,7 @@
     down = down_ref[...]
     rounded = (active * b).astype(BF16).astype(F32)
     score_ref[...] = jnp.sum(rounded * down, axis=-1, keepdims=True)
-    valid, _ = valid_column(counts_ref, total)
-    d_hidden = valid * down
+    d_hidden = valid_ref[...] * down
     d_both_ref[:, :hidden] = (d_hidden * b * sigma * (1.0 + a * (1.0 - sigma))).astype(BF16)
     d_both_ref[:, hidden:] = (d_hidden * active).astype(BF16)
     backward_half(d_both_ref[...], weights, send_ref)
@@ -344,12 +345,12 @@
 
 def input_kernel(
     mine_ref, got_ref, d_mine_ref, d_got_ref, gain_ref, head_ref, inv_ref,
-    score_a_ref, score_b_ref, score_c_ref, counts_ref, ready_ref, embed_ref,
+    score_a_ref, score_b_ref, score_c_ref, valid_ref, counts_ref, ready_ref, embed_ref,
     out_ref, dx_ref, table, sems,
 ):
     chips, total, own = mine_ref.shape
     voc = embed_ref.shape[0]
-    requests = counts_ref.shape[0]
+    requests = counts_ref.shape[1]
     width = 2 * chips * own
     core = this_core()
     ready = ready_ref.shape[0]
@@ -381,7 +382,8 @@
             wide += d_ref[j].astype(F32) * gain * x_ref[j].astype(F32)
     inv = inv_ref[...]
     weight = inv * inv * inv * (jnp.sum(wide, axis=-1, keepdims=True) / width)
-    valid, request = valid_column(counts_ref, total)
+    valid = valid_ref[...]
+    request = lax.broadcasted_iota(jnp.int32, (total, requests), 0) // (total // requests)
     for x_ref, d_ref, half in sources:
         for j in range(chips):
             columns = span((half * chips + j) * own, own)
@@ -504,7 +506,7 @@
     head_row, gain_row = head.reshape(1, width), norm_gain.reshape(1, width)
     if tiled:
         around = [(i, (i + devices // 4) % devices) for i in range(devices)]
-        greeting = lax.ppermute(gain_row[:, :128], "dp", around)
+        greeting = lax.ppermute(counts, "dp", around)
         blocked, probs = call(
             softmax_kernel,
             [struct((devices, rows, part), BF16), pltpu.VMEM((rows, voc), F32)], logits,
@@ -512,43 +514,41 @@
     else:
         probs32 = jax.nn.softmax(logits.astype(F32), axis=-1)
         blocked = probs32.astype(BF16).reshape(rows, devices, part).transpose(1, 0, 2)
+    if tiled:
+        blocked, greeting = lax.optimization_barrier((blocked, greeting))
     slices = exchange(blocked).reshape(total, part)
     column = struct((total, 1), F32)
     half = (chips, total, own)
     flops = total * part * width
     if tiled:
         ready = 256
-        down_row, first, both_first = call(
+        down_row, valid, counts_row, first, both_first = call(
             early_kernel,
             [
-                struct((1, hidden), F32), pltpu.VMEM((ready, width // 2), BF16),
+                struct((1, hidden), F32), column, struct((1, requests), F32), pltpu.VMEM((ready, width // 2), BF16),
                 pltpu.VMEM((2 * own, 2 * hidden), BF16),
             ],
-            head_row, w_down, embed, w_gate, w_up, blocked, greeting,
-            streamed=(1, 2, 3, 4), flops=2 * hidden * width, room=2 * hidden * width,
+            head_row, w_down, embed, w_gate, w_up, counts, blocked, greeting,
+            streamed=(1, 2, 3, 4), scalars=(5,), flops=2 * hidden * width, room=2 * hidden * width,
             scratch=(
                 pltpu.VMEM((hidden, width), BF16), pltpu.SemaphoreType.DMA((hidden // 128,)),
                 pltpu.SemaphoreType.DMA((ready // 128,)), pltpu.SemaphoreType.DMA((2, 2)),
             ),
         )
-
-        def table(ready):
-            return (
-                pltpu.VMEM((part - ready, width // 2), BF16),
-                pltpu.VMEM((total, width // 2), F32),
-                pltpu.SemaphoreType.DMA((-(-part // 128),)),
-            )
-
+        table = (
+            pltpu.VMEM((part - ready, width // 2), BF16), pltpu.VMEM((total, width // 2), F32),
+            pltpu.SemaphoreType.DMA((-(-part // 128),)),
+        )
         args = dict(streamed=(2,), kept=(1,), flops=flops, room=part * width)
         send, score_a, first = call(
             functools.partial(half_kernel, True),
-            [struct(half, BF16), column, pltpu.VMEM((2 * ready, width // 2), BF16)],
+            [struct(half, BF16), column, pltpu.VMEM((ready, width // 2), BF16)],
             slices, first, embed, head_row,
-            scratch=(*table(ready), pltpu.SemaphoreType.DMA((ready // 64,))), **args,
+            scratch=(*table, pltpu.SemaphoreType.DMA((ready // 128,))), **args,
         )
         keep, score_b = call(
             functools.partial(half_kernel, False), [struct(half, F32), column],
-            slices, first, embed, head_row, scratch=table(2 * ready), **args,
+            slices, first, embed, head_row, scratch=table, **args,
         )
     else:
         send, keep, score_a = plain_half(slices, embed, head_row, devices)
@@ -572,8 +572,8 @@
         send, score_c, inv, d_both = call(
             second_kernel,
             [struct(half, BF16), column, column, struct((total, 2 * hidden), BF16)],
-            x_got, gain_row, w_gate, w_up, ahead, products, squares, down_row, counts,
-            scratch=(pltpu.VMEM(weight, BF16), sems), scalars=(8,), **args,
+            x_got, gain_row, w_gate, w_up, ahead, products, squares, down_row, valid,
+            scratch=(pltpu.VMEM(weight, BF16), sems), **args,
         )
         (keep,) = call(
             third_kernel, [struct(half, F32)], d_both, both_first, both,
@@ -597,8 +597,8 @@
         (d_slices,) = call(
             input_kernel, [struct((total, padded), BF16)],
             x_mine, x_got, d_mine, d_got, gain_row, head_row, inv,
-            score_a, score_b, score_c, counts, first, embed,
-            scalars=(10,), kept=(11,), streamed=(12,), flops=2 * flops, room=2 * part * width,
+            score_a, score_b, score_c, valid, counts_row, first, embed,
+            kept=(12,), streamed=(13,), flops=2 * flops, room=2 * part * width,
             scratch=(
                 pltpu.VMEM((total, width), BF16), pltpu.VMEM((part - 256, width), BF16),
                 pltpu.SemaphoreType.DMA((-(-part // 64),)),
@@ -614,7 +614,7 @@
     if tiled:
         guidance, rewards = call(
             final_kernel, [struct((rows, voc), BF16), struct((1, requests), F32)],
-            probs, back, counts, kept=(0,), scalars=(2,),
+            probs, back, counts_row, kept=(0,),
             scratch=(pltpu.VMEM((rows, voc), F32),),
         )
         return (guidance, rewards.reshape(requests))

time: 105 us -> 101 us (0.962)
  starting transfers between devices: 10 us -> 8.08 us
  Pallas kernels: 36.4 us -> 34.7 us
  blocking collectives: 50.7 us -> 51.8 us
    all_to_all x1, starting transfers between devices: 7.39 us -> 4.35 us  [exchange(): return lax.all_to_all(blocks, 'dp', split_axis=0, concat_axis=0, tiled=True)]
    ppermute x1, waiting for transfers between devices: 3.61 us -> 1.37 us  [body(): greeting = lax.ppermute(counts, 'dp', around)]
    pallas_call x10, Pallas kernels: 36.4 us -> 34.7 us  [call(): pl.pallas_call(kernel, out_shape=outs, in_specs=specs, out_specs=[VMEM_SP...]
    all_to_all x1, waiting for transfers between devices: 0.01 us -> 1.58 us  [exchange(): return lax.all_to_all(blocks, 'dp', split_axis=0, concat_axis=0, tiled=True)]
    all_to_all x4, blocking collectives: 40.2 us -> 41.3 us  [exchange_chips(): lax.all_to_all(blocks, 'dp', split_axis=0, concat_axis=0, axis_index_grou...]
    ppermute x1, starting transfers between devices: 1.98 us -> 3.08 us  [body(): greeting = lax.ppermute(counts, 'dp', around)]
  transfers between devices with their start and end apart: 6 -> 6, of which waited for: 1 -> 2; matrix products, arithmetic and copies ran while one was open for 1% -> 1% of each run, Pallas kernels for 15% -> 17%
where the time goes in v15:
time: 101 us
  blocking collectives  51.8 us (51%)
  Pallas kernels  34.7 us (34%)
  starting transfers between devices  8.08 us (8%)
  waiting for transfers between devices  2.96 us (3%)
  local copies, waits for them, and re-layouts  2.47 us (2%)
    all_to_all x4, blocking collectives, exchange_chips(): lax.all_to_all(blocks, 'dp', split_axis=0, concat_axis=0, axis_index_grou...  41.3 us
    pallas_call x10, Pallas kernels, call(): pl.pallas_call(kernel, out_shape=outs, in_specs=specs, out_specs=[VMEM_SP...  34.7 us
    all_to_all x1, blocking collectives, exchange(): return lax.all_to_all(blocks, 'dp', split_axis=0, concat_axis=0, tiled=True)  10.5 us
    all_to_all x1, starting transfers between devices, exchange(): return lax.all_to_all(blocks, 'dp', split_axis=0, concat_axis=0, tiled=True)  4.35 us
    ppermute x1, starting transfers between devices, body(): greeting = lax.ppermute(counts, 'dp', around)  3.08 us
  transfers between devices with their start and end apart: 6, of which 2 were waited for; matrix products, arithmetic and copies ran while one was open for 1% of the time, Pallas kernels for 17%

profile of v15, /device:TPU:0, one launch (start us, length us, event | category | flops | bytes accessed | tf_op | source)
XLA Modules:
  0.0 101.0 jit_solution(13602160115112713313)
XLA Ops:
  0.6 3.1 %collective-permute-start = (s32[4]{0:T(128)}, s32[4]{0:T(128)S(1)}, u32[]{:S(2)}, u32[]{:S(2)}) collective-permute-start(s32[4]{0:T(128)} %counts_ref.1), channel_id=1, source_target_pairs={{0,4},{1,5},{2,6},{3,7},{4,8},{5,9},{6,10},{7,11},{8,12},{9,13},{1... | collective-permute-start | bytes 56 | tf_op jit(solution)/shard_map/ppermute | solution.py:509
  3.7 0.9 copy-done
  4.6 1.4 %shard_map.95 = (bf16[16,2,2000]{2,1,0:T(2,128)(2,1)}, f32[2,32000]{1,0:T(2,128)S(1)}) custom-call(bf16[2,32000]{1,0:T(2,128)(2,1)S(1)} %copy-done), custom_call_target="tpu_custom_call" | custom-call | bytes 128000 | tf_op jit(solution)/shard_map/pallas_call | solution.py:54
  6.0 1.4 %collective-permute-done.greeting_ref = s32[4]{0:T(128)S(1)} collective-permute-done((s32[4]{0:T(128)}, s32[4]{0:T(128)S(1)}, u32[]{:S(2)}, u32[]{:S(2)}) %collective-permute-start) | collective-permute-done | bytes 48 | tf_op jit(solution)/shard_map/ppermute | solution.py:509
  7.4 4.4 %all-to-all-start = ((bf16[16,2,2000]{2,1,0:T(2,128)(2,1)}), bf16[16,2,2000]{2,1,0:T(2,128)(2,1)S(1)}, u32[]{:S(2)}, u32[]{:S(2)}) async-start(bf16[16,2,2000]{2,1,0:T(2,128)(2,1)} %get-tuple-element.28.after_ref), calls=%async_computation | async-start | bytes 262144 | tf_op jit(solution)/shard_map/all_to_all | solution.py:21
  11.8 0.7 reshape.22.head_ref
  12.5 0.0 copy-start.1
  12.5 0.6 copy-done.1
  13.1 5.0 %shard_map.96 = (f32[1,896]{1,0:T(1,128)S(1)}, f32[32,1]{1,0:T(8,128)S(1)}, f32[1,4]{1,0:T(1,128)S(1)}, bf16[256,2048]{1,0:T(8,128)(2,1)S(1)}, bf16[512,1792]{1,0:T(8,128)(2,1)S(1)}) custom-call(bf16[1,4096]{1,0:T(2,128)(2,1)S(1)} %reshape.22.head_ref, bf16[896,4096]{1,0:T(8,128)(2,1)} %down_ref.1, bf16[2000,4096]{1,0:T(8,128)(2,1)} %embed_ref.7, ...), custom_call_target="tpu_custom_call" | custom-call | flops 7340032 | bytes 38540320 | tf_op jit(solution)/shard_map/pallas_call | solution.py:54
  18.1 1.6 %all-to-all-done = bf16[16,2,2000]{2,1,0:T(2,128)(2,1)S(1)} async-done(((bf16[16,2,2000]{2,1,0:T(2,128)(2,1)}), bf16[16,2,2000]{2,1,0:T(2,128)(2,1)S(1)}, u32[]{:S(2)}, u32[]{:S(2)}) %all-to-all-start) | async-done | bytes 128032 | tf_op jit(solution)/shard_map/all_to_all | solution.py:21
  19.7 0.1 reshape.21.slices_ref
  19.8 3.7 %shard_map.97 = (bf16[8,32,256]{2,1,0:T(8,128)(2,1)S(1)}, f32[32,1]{1,0:T(8,128)S(1)}, bf16[256,2048]{1,0:T(8,128)(2,1)S(1)}) custom-call(bf16[32,2000]{1,0:T(8,128)(2,1)S(1)} %reshape.21.slices_ref, bf16[256,2048]{1,0:T(8,128)(2,1)S(1)} %get-tuple-element.30.ready_ref, bf16[2000,4096]{1,0:T(8,128)(2,1)} %embed_ref.7, bf16[1,4096]{1,0:T(2,128)(2,1)S(1)} %reshape.22.head_ref), custom_call_target="tpu_custom_call" | custom-call | flops 262144000 | bytes 17568768 | tf_op jit(solution)/shard_map/pallas_call | solution.py:54
  23.4 0.1 collective-permute-start.1
  23.5 0.0 copy-start.2
  23.5 3.5 %shard_map.98 = (f32[8,32,256]{2,1,0:T(8,128)S(1)}, f32[32,1]{1,0:T(8,128)S(1)}) custom-call(bf16[32,2000]{1,0:T(8,128)(2,1)S(1)} %reshape.21.slices_ref, bf16[256,2048]{1,0:T(8,128)(2,1)S(1)} %get-tuple-element.31.ready_ref, bf16[2000,4096]{1,0:T(8,128)(2,1)} %embed_ref.7, bf16[1,4096]{1,0:T(2,128)(2,1)S(1)} %reshape.22.head_ref), custom_call_target="tpu_custom_call" | custom-call | flops 262144000 | bytes 17568768 | tf_op jit(solution)/shard_map/pallas_call | solution.py:54
  27.1 0.0 collective-permute-done.1
  27.1 11.8 %all_to_all.30 = bf16[8,32,256]{2,1,0:T(8,128)(2,1)S(1)} all-to-all(bf16[8,32,256]{2,1,0:T(8,128)(2,1)S(1)} %add_convert_fusion.1), channel_id=1, replica_groups={{0,2,4,6,8,10,12,14},{1,3,5,7,9,11,13,15},{16,18,20,22,24,26,28,30},{17..., dimensions={0} | all-to-all | bytes 262144 | tf_op jit(solution)/shard_map/all_to_all | solution.py:26
  38.9 9.9 %all_to_all.31.x_ref.mine_ref = bf16[8,32,256]{2,1,0:T(8,128)(2,1)S(1)} all-to-all(bf16[8,32,256]{2,1,0:T(8,128)(2,1)S(1)} %broadcast_in_dim.4), channel_id=1, replica_groups={{0,2,4,6,8,10,12,14},{1,3,5,7,9,11,13,15},{16,18,20,22,24,26,28,30},{17..., dimensions={0} | all-to-all | bytes 262144 | tf_op jit(solution)/shard_map/all_to_all | solution.py:26
  48.8 3.7 %shard_map.99 = (f32[32,1792]{1,0:T(8,128)S(1)}, f32[32,1]{1,0:T(8,128)S(1)}, bf16[1536,1792]{1,0:T(8,128)(2,1)S(1)}, bf16[512,1792]{1,0:T(8,128)(2,1)S(1)}) custom-call(bf16[8,32,256]{2,1,0:T(8,128)(2,1)S(1)} %all_to_all.31.x_ref.mine_ref, bf16[1,4096]{1,0:T(2,128)(2,1)S(1)} %reshape.23.gain_ref, bf16[4096,896]{1,0:T(8,128)(2,1)} %gate_ref.5, ...), custom_call_target="tpu_custom_call" | custom-call | flops 234881024 | bytes 16654336 | tf_op jit(solution)/shard_map/pallas_call | solution.py:54
  52.5 0.0 collective-permute-done.2.x_ref.got_ref
  52.5 5.2 %shard_map.100 = (bf16[8,32,256]{2,1,0:T(8,128)(2,1)S(1)}, f32[32,1]{1,0:T(8,128)S(1)}, f32[32,1]{1,0:T(8,128)S(1)}, bf16[32,1792]{1,0:T(8,128)(2,1)S(1)}) custom-call(bf16[8,32,256]{2,1,0:T(8,128)(2,1)S(1)} %collective-permute-done.2.x_ref.got_ref, bf16[1,4096]{1,0:T(2,128)(2,1)S(1)} %reshape.23.gain_ref, bf16[4096,896]{1,0:T(8,128)(2,1)} %gate_ref.5, ...), custom_call_target="tpu_custom_call" | custom-call | flops 234881024 | bytes 16887552 | tf_op jit(solution)/shard_map/pallas_call | solution.py:54
  57.8 0.6 collective-permute-start.3
  58.3 2.2 %shard_map.101 = f32[8,32,256]{2,1,0:T(8,128)S(1)} custom-call(bf16[32,1792]{1,0:T(8,128)(2,1)S(1)} %get-tuple-element.40.d_both_ref, bf16[512,1792]{1,0:T(8,128)(2,1)S(1)} %get-tuple-element.34.ready_ref, bf16[1536,1792]{1,0:T(8,128)(2,1)S(1)} %get-tuple-element.41.both_ref), custom_call_target="tpu_custom_call" | custom-call | flops 234881024 | bytes 7454720 | tf_op jit(solution)/shard_map/pallas_call | solution.py:54
  60.6 9.8 %all_to_all.32 = bf16[8,32,256]{2,1,0:T(8,128)(2,1)S(1)} all-to-all(bf16[8,32,256]{2,1,0:T(8,128)(2,1)S(1)} %add_convert_fusion), channel_id=1, replica_groups={{0,2,4,6,8,10,12,14},{1,3,5,7,9,11,13,15},{16,18,20,22,24,26,28,30},{17..., dimensions={0} | all-to-all | bytes 262144 | tf_op jit(solution)/shard_map/all_to_all | solution.py:26
  70.5 9.8 %all_to_all.33.d_mine_ref = bf16[8,32,256]{2,1,0:T(8,128)(2,1)S(1)} all-to-all(bf16[8,32,256]{2,1,0:T(8,128)(2,1)S(1)} %broadcast_in_dim.5), channel_id=1, replica_groups={{0,2,4,6,8,10,12,14},{1,3,5,7,9,11,13,15},{16,18,20,22,24,26,28,30},{17..., dimensions={0} | all-to-all | bytes 262144 | tf_op jit(solution)/shard_map/all_to_all | solution.py:26
  80.3 0.0 collective-permute-start.4
  80.3 1.6 %shard_map.102.ready_ref = bf16[256,4096]{1,0:T(8,128)(2,1)S(1)} custom-call(bf16[2000,4096]{1,0:T(8,128)(2,1)} %embed_ref.7, bf16[32,256]{1,0:T(8,128)(2,1)S(1)} %reduce_sum.25.after_ref), custom_call_target="tpu_custom_call" | custom-call | bytes 16400384 | tf_op jit(solution)/shard_map/pallas_call | solution.py:54
  81.9 0.0 collective-permute-done.4.d_got_ref
  81.9 7.2 %shard_map.103 = bf16[32,2012]{1,0:T(8,128)(2,1)S(1)} custom-call(bf16[8,32,256]{2,1,0:T(8,128)(2,1)S(1)} %all_to_all.31.x_ref.mine_ref, bf16[8,32,256]{2,1,0:T(8,128)(2,1)S(1)} %collective-permute-done.2.x_ref.got_ref, bf16[8,32,256]{2,1,0:T(8,128)(2,1)S(1)} %all_to_all.33.d_mine_ref, bf16[8,32,256]{2,1,0:T(8,128)(2,1)S(1)} %collective-permute-done.4.d_got_ref, ...), custom_call_target="tpu_custom_call" | custom-call | flops 524288000 | bytes 19022480 | tf_op jit(solution)/shard_map/pallas_call | solution.py:54
  89.1 0.1 reshape.24
  89.2 10.5 %all_to_all.34.back_ref = bf16[16,2,2012]{2,1,0:T(2,128)(2,1)S(1)} all-to-all(bf16[16,2,2012]{2,1,0:T(2,128)(2,1)S(1)} %reshape.24), channel_id=1, replica_groups=mesh['groups'=2,'dp'=16] {'dp'}, dimensions={0} | all-to-all | bytes 257536 | tf_op jit(solution)/shard_map/all_to_all | solution.py:21
  99.8 1.2 %shard_map.104 = (bf16[2,32000]{1,0:T(2,128)(2,1)}, f32[1,4]{1,0:T(1,128)}) custom-call(f32[2,32000]{1,0:T(2,128)S(1)} %get-tuple-element.26.probs_ref, bf16[16,2,2012]{2,1,0:T(2,128)(2,1)S(1)} %all_to_all.34.back_ref, f32[1,4]{1,0:T(1,128)S(1)} %get-tuple-element.47.counts_ref), custom_call_target="tpu_custom_call" | custom-call | bytes 384784 | tf_op jit(solution)/shard_map/pallas_call | solution.py:54
  (11 shorter events, 0.2 us)
Async XLA Ops:
  0.6 6.8 %collective-permute-start = (s32[4]{0:T(128)}, s32[4]{0:T(128)S(1)}, u32[]{:S(2)}, u32[]{:S(2)}) collective-permute-start(s32[4]{0:T(128)} %counts_ref.1), channel_id=1, source_target_pairs={{0,4},{1,5},{2,6},{3,7},{4,8},{5,9},{6,10},{7,11},{8,12},{9,13},{1... | collective-permute-start | bytes 56 | tf_op jit(solution)/shard_map/ppermute | solution.py:509
  3.7 0.9 copy-start
  7.4 12.3 %all-to-all-start = ((bf16[16,2,2000]{2,1,0:T(2,128)(2,1)}), bf16[16,2,2000]{2,1,0:T(2,128)(2,1)S(1)}, u32[]{:S(2)}, u32[]{:S(2)}) async-start(bf16[16,2,2000]{2,1,0:T(2,128)(2,1)} %get-tuple-element.28.after_ref), calls=%async_computation | async-start | bytes 262144 | tf_op jit(solution)/shard_map/all_to_all | solution.py:21
  12.5 0.7 copy-start.1
  23.4 3.6 %collective-permute-start.1 = (bf16[8,32,256]{2,1,0:T(8,128)(2,1)S(1)}, bf16[8,32,256]{2,1,0:T(8,128)(2,1)S(1)}, u32[]{:S(2)}, u32[]{:S(2)}) collective-permute-start(bf16[8,32,256]{2,1,0:T(8,128)(2,1)S(1)} %get-tuple-element.33), channel_id=1, source_target_pairs={{0,1},{1,0},{2,3},{3,2},{4,5},{5,4},{6,7},{7,6},{8,9},{9,8},{10,11... | collective-permute-start | bytes 393224 | tf_op jit(solution)/shard_map/ppermute | solution.py:17
  23.5 25.3 %copy-start.2 = (bf16[4096]{0:T(1024)(128)(2,1)S(1)}, bf16[4096]{0:T(1024)(128)(2,1)}, u32[]{:S(2)}) copy-start(bf16[4096]{0:T(1024)(128)(2,1)} %param.10) | copy-start | bytes 24580
  48.8 3.7 %collective-permute-start.2 = (bf16[8,32,256]{2,1,0:T(8,128)(2,1)S(1)}, bf16[8,32,256]{2,1,0:T(8,128)(2,1)S(1)}, u32[]{:S(2)}, u32[]{:S(2)}) collective-permute-start(bf16[8,32,256]{2,1,0:T(8,128)(2,1)S(1)} %all_to_all.31.x_ref.mine_ref), channel_id=1, source_target_pairs={{0,1},{1,0},{2,3},{3,2},{4,5},{5,4},{6,7},{7,6},{8,9},{9,8},{10,11... | collective-permute-start | bytes 393224 | tf_op jit(solution)/shard_map/ppermute | solution.py:17
  57.8 2.8 %collective-permute-start.3 = (bf16[8,32,256]{2,1,0:T(8,128)(2,1)S(1)}, bf16[8,32,256]{2,1,0:T(8,128)(2,1)S(1)}, u32[]{:S(2)}, u32[]{:S(2)}) collective-permute-start(bf16[8,32,256]{2,1,0:T(8,128)(2,1)S(1)} %get-tuple-element.42), channel_id=1, source_target_pairs={{0,1},{1,0},{2,3},{3,2},{4,5},{5,4},{6,7},{7,6},{8,9},{9,8},{10,11... | collective-permute-start | bytes 393224 | tf_op jit(solution)/shard_map/ppermute | solution.py:17
  80.3 1.6 %collective-permute-start.4 = (bf16[8,32,256]{2,1,0:T(8,128)(2,1)S(1)}, bf16[8,32,256]{2,1,0:T(8,128)(2,1)S(1)}, u32[]{:S(2)}, u32[]{:S(2)}) collective-permute-start(bf16[8,32,256]{2,1,0:T(8,128)(2,1)S(1)} %all_to_all.33.d_mine_ref), channel_id=1, source_target_pairs={{0,1},{1,0},{2,3},{3,2},{4,5},{5,4},{6,7},{7,6},{8,9},{9,8},{10,11... | collective-permute-start | bytes 393224 | tf_op jit(solution)/shard_map/ppermute | solution.py:17

commit v16 on v15

--- a/solution.py
+++ b/solution.py
@@ -119,15 +119,13 @@
     out_ref[...] = (math.sqrt(VOC) * (probs * (d_probs - mean))).astype(BF16)
 
 
-def valid_column(counts_ref, total):
-    requests = counts_ref.shape[0]
+def valid_column(counts, total):
+    requests = counts.shape[1]
     length = total // requests
-    position = lax.broadcasted_iota(jnp.int32, (total, 1), 0)
-    valid = jnp.zeros((total, 1), F32)
-    for r in range(requests):
-        inside = (position >= r * length) & (position < r * length + counts_ref[r])
-        valid = jnp.where(inside, 1.0, valid)
-    return valid
+    position = lax.broadcasted_iota(jnp.int32, (total, requests), 0)
+    start = length * lax.broadcasted_iota(jnp.int32, (total, requests), 1)
+    inside = (position >= start) & (position < start + counts)
+    return jnp.sum(jnp.where(inside, 1.0, 0.0), axis=-1, keepdims=True)
 
 
 def bring(source_ref, out_ref, sems, columns):
@@ -198,10 +196,10 @@
 
 
 def early_kernel(
-    head_ref, down_ref, embed_ref, gate_ref, up_ref, counts_ref, after_ref, greeting_ref,
-    out_ref, valid_ref, counts_row, first, both, table, sems, first_sems, both_sems,
+    head_ref, down_ref, embed_ref, gate_ref, up_ref, after_ref,
+    out_ref, first, both, table, sems, first_sems, both_sems,
 ):
-    del after_ref, greeting_ref
+    del after_ref
     width, lanes = down_ref.shape[1], 128
     core = this_core()
 
@@ -219,20 +217,14 @@
     others += bring_blocks(gate_ref, up_ref, both, core, range(2), own, chips, both_sems)
     for other in others:
         other.start()
-    valid_ref[...] = valid_column(counts_ref, valid_ref.shape[0])
-    lane = lax.broadcasted_iota(jnp.int32, counts_row.shape, 1)
-    counts = jnp.ones(counts_row.shape, F32)
-    for r in range(counts_row.shape[1]):
-        counts = jnp.where(lane == r, counts_ref[r].astype(F32), counts)
-    counts_row[...] = counts
+    head = head_ref[...].astype(F32).reshape(1, width)
 
     def step(j, _):
         copy(j).wait()
         rows = span(j * lanes, lanes)
         total = jnp.zeros((lanes, lanes), F32)
         for k in range(0, width, lanes):
-            head = head_ref[:, k : k + lanes].astype(F32)
-            total += table[rows, k : k + lanes].astype(F32) * head
+            total += table[rows, k : k + lanes].astype(F32) * head[:, k : k + lanes]
         out_ref[:, rows] = jnp.sum(total.T, axis=0, keepdims=True)
         return 0
 
@@ -290,8 +282,8 @@
 
 
 def first_kernel(
-    x_ref, gain_ref, gate_ref, up_ref, ready_ref,
-    products_ref, squares_ref, both, ahead, sems, ahead_sems,
+    x_ref, gain_ref, gate_ref, up_ref, ready_ref, counts_ref,
+    products_ref, squares_ref, valid_ref, counts_row, both, ahead, sems, ahead_sems,
 ):
     chips, _, own = x_ref.shape
     core = this_core()
@@ -302,6 +294,9 @@
     following = bring_blocks(gate_ref, up_ref, ahead, 1 - core, blocks, own, chips, ahead_sems)
     for copy in following:
         copy.start()
+    counts = counts_ref[...]
+    valid_ref[...] = valid_column(counts, valid_ref.shape[0])
+    counts_row[...] = counts.astype(F32)
     sums = (jnp.zeros(products_ref.shape, F32), jnp.zeros(squares_ref.shape, F32))
     products_ref[...], squares_ref[...] = forward_half(
         x_ref, gain_ref, core, sums, weights, lambda j: stream.wait(2 * (j - skip + 1))
@@ -505,8 +500,6 @@
     tiled = own % 128 == 0 and hidden % 128 == 0 and total % 16 == 0 and part % 16 == 0 and part > 512
     head_row, gain_row = head.reshape(1, width), norm_gain.reshape(1, width)
     if tiled:
-        around = [(i, (i + devices // 4) % devices) for i in range(devices)]
-        greeting = lax.ppermute(counts, "dp", around)
         blocked, probs = call(
             softmax_kernel,
             [struct((devices, rows, part), BF16), pltpu.VMEM((rows, voc), F32)], logits,
@@ -514,22 +507,20 @@
     else:
         probs32 = jax.nn.softmax(logits.astype(F32), axis=-1)
         blocked = probs32.astype(BF16).reshape(rows, devices, part).transpose(1, 0, 2)
-    if tiled:
-        blocked, greeting = lax.optimization_barrier((blocked, greeting))
     slices = exchange(blocked).reshape(total, part)
     column = struct((total, 1), F32)
     half = (chips, total, own)
     flops = total * part * width
     if tiled:
         ready = 256
-        down_row, valid, counts_row, first, both_first = call(
+        down_row, first, both_first = call(
             early_kernel,
             [
-                struct((1, hidden), F32), column, struct((1, requests), F32), pltpu.VMEM((ready, width // 2), BF16),
+                struct((1, hidden), F32), pltpu.VMEM((ready, width // 2), BF16),
                 pltpu.VMEM((2 * own, 2 * hidden), BF16),
             ],
-            head_row, w_down, embed, w_gate, w_up, counts, blocked, greeting,
-            streamed=(1, 2, 3, 4), scalars=(5,), flops=2 * hidden * width, room=2 * hidden * width,
+            head, w_down, embed, w_gate, w_up, blocked,
+            streamed=(1, 2, 3, 4), flops=2 * hidden * width, room=2 * hidden * width,
             scratch=(
                 pltpu.VMEM((hidden, width), BF16), pltpu.SemaphoreType.DMA((hidden // 128,)),
                 pltpu.SemaphoreType.DMA((ready // 128,)), pltpu.SemaphoreType.DMA((2, 2)),
@@ -561,13 +552,14 @@
         args = dict(
             streamed=(2, 3), kept=(4,), flops=2 * total * hidden * width, room=2 * width * hidden
         )
-        products, squares, both, ahead = call(
+        products, squares, valid, counts_row, both, ahead = call(
             first_kernel,
             [
-                struct((total, 2 * hidden), F32), column, pltpu.VMEM(weight, BF16),
-                pltpu.VMEM(both_first.shape, BF16),
+                struct((total, 2 * hidden), F32), column, column, struct((1, requests), F32),
+                pltpu.VMEM(weight, BF16), pltpu.VMEM(both_first.shape, BF16),
             ],
-            x_mine, gain_row, w_gate, w_up, both_first, scratch=(sems, ahead_sems), **args,
+            x_mine, gain_row, w_gate, w_up, both_first, counts.reshape(1, requests),
+            scratch=(sems, ahead_sems), **args,
         )
         send, score_c, inv, d_both = call(
             second_kernel,

time: 101 us -> 100 us (0.990)
  waiting for transfers between devices: 2.96 us -> 1.54 us
    ppermute x1 -> x0, starting transfers between devices: 3.08 us -> none  [body(): greeting = lax.ppermute(counts, 'dp', around)]
    all_to_all x1, starting transfers between devices: 4.35 us -> 7.39 us  [exchange(): return lax.all_to_all(blocks, 'dp', split_axis=0, concat_axis=0, tiled=True)]
    ppermute x1 -> x0, waiting for transfers between devices: 1.37 us -> none  [body(): greeting = lax.ppermute(counts, 'dp', around)]
  transfers between devices with their start and end apart: 6 -> 5, of which waited for: 2 -> 1; matrix products, arithmetic and copies ran while one was open for 1% -> 1% of each run, Pallas kernels for 17% -> 16%
where the time goes in v16:
time: 100 us; the launch traced here: 99.6 us
  blocking collectives  51.9 us (52%)
  Pallas kernels  34.7 us (35%)
  starting transfers between devices  8.03 us (8%)
  local copies, waits for them, and re-layouts  2.51 us (3%)
  waiting for transfers between devices  1.54 us (2%)
    all_to_all x4, blocking collectives, exchange_chips(): lax.all_to_all(blocks, 'dp', split_axis=0, concat_axis=0, axis_index_grou...  41.3 us
    pallas_call x10, Pallas kernels, call(): pl.pallas_call(kernel, out_shape=outs, in_specs=specs, out_specs=[VMEM_SP...  34.7 us
    all_to_all x1, blocking collectives, exchange(): return lax.all_to_all(blocks, 'dp', split_axis=0, concat_axis=0, tiled=True)  10.5 us
    all_to_all x1, starting transfers between devices, exchange(): return lax.all_to_all(blocks, 'dp', split_axis=0, concat_axis=0, tiled=True)  7.39 us
  transfers between devices with their start and end apart: 5, of which 1 were waited for; matrix products, arithmetic and copies ran while one was open for 1% of the time, Pallas kernels for 16%

profile of v16, /device:TPU:0, one launch (start us, length us, event | category | flops | bytes accessed | tf_op | source)
XLA Modules:
  0.0 99.6 jit_solution(8746278461337364756)
XLA Ops:
  0.6 0.9 copy-done
  1.5 1.4 %shard_map.95 = (bf16[16,2,2000]{2,1,0:T(2,128)(2,1)}, f32[2,32000]{1,0:T(2,128)S(1)}) custom-call(bf16[2,32000]{1,0:T(2,128)(2,1)S(1)} %copy-done), custom_call_target="tpu_custom_call" | custom-call | bytes 128000 | tf_op jit(solution)/shard_map/pallas_call | solution.py:54
  2.9 7.4 %all-to-all-start = ((bf16[16,2,2000]{2,1,0:T(2,128)(2,1)}), bf16[16,2,2000]{2,1,0:T(2,128)(2,1)S(1)}, u32[]{:S(2)}, u32[]{:S(2)}) async-start(bf16[16,2,2000]{2,1,0:T(2,128)(2,1)} %get-tuple-element.25.after_ref), calls=%async_computation | async-start | bytes 262144 | tf_op jit(solution)/shard_map/all_to_all | solution.py:21
  10.3 0.7 reshape.25.head_ref
  11.0 0.0 copy-start.1
  11.1 0.7 copy-done.1
  11.7 5.0 %shard_map.96 = (f32[1,896]{1,0:T(1,128)S(1)}, bf16[256,2048]{1,0:T(8,128)(2,1)S(1)}, bf16[512,1792]{1,0:T(8,128)(2,1)S(1)}) custom-call(bf16[4096]{0:T(1024)(128)(2,1)S(1)} %copy-done.1, bf16[896,4096]{1,0:T(8,128)(2,1)} %down_ref.1, bf16[2000,4096]{1,0:T(8,128)(2,1)} %embed_ref.7, bf16[4096,896]{1,0:T(8,128)(2,1)} %gate_ref.5, bf16[4096,896]{1,0:T(8,128)(2,1)} %up_ref.5, ...), custom_call_target="tpu_custom_call" | custom-call | flops 7340032 | bytes 38540288 | tf_op jit(solution)/shard_map/pallas_call | solution.py:54
  16.7 1.5 %all-to-all-done = bf16[16,2,2000]{2,1,0:T(2,128)(2,1)S(1)} async-done(((bf16[16,2,2000]{2,1,0:T(2,128)(2,1)}), bf16[16,2,2000]{2,1,0:T(2,128)(2,1)S(1)}, u32[]{:S(2)}, u32[]{:S(2)}) %all-to-all-start) | async-done | bytes 128032 | tf_op jit(solution)/shard_map/all_to_all | solution.py:21
  18.3 0.1 reshape.24.slices_ref
  18.3 3.7 %shard_map.97 = (bf16[8,32,256]{2,1,0:T(8,128)(2,1)S(1)}, f32[32,1]{1,0:T(8,128)S(1)}, bf16[256,2048]{1,0:T(8,128)(2,1)S(1)}) custom-call(bf16[32,2000]{1,0:T(8,128)(2,1)S(1)} %reshape.24.slices_ref, bf16[256,2048]{1,0:T(8,128)(2,1)S(1)} %get-tuple-element.26.ready_ref, bf16[2000,4096]{1,0:T(8,128)(2,1)} %embed_ref.7, bf16[1,4096]{1,0:T(2,128)(2,1)S(1)} %reshape.25.head_ref), custom_call_target="tpu_custom_call" | custom-call | flops 262144000 | bytes 17568768 | tf_op jit(solution)/shard_map/pallas_call | solution.py:54
  22.0 0.1 collective-permute-start
  22.1 0.0 copy-start.3
  22.1 0.0 copy-start.2
  22.1 3.5 %shard_map.98 = (f32[8,32,256]{2,1,0:T(8,128)S(1)}, f32[32,1]{1,0:T(8,128)S(1)}) custom-call(bf16[32,2000]{1,0:T(8,128)(2,1)S(1)} %reshape.24.slices_ref, bf16[256,2048]{1,0:T(8,128)(2,1)S(1)} %get-tuple-element.27.ready_ref, bf16[2000,4096]{1,0:T(8,128)(2,1)} %embed_ref.7, bf16[1,4096]{1,0:T(2,128)(2,1)S(1)} %reshape.25.head_ref), custom_call_target="tpu_custom_call" | custom-call | flops 262144000 | bytes 17568768 | tf_op jit(solution)/shard_map/pallas_call | solution.py:54
  25.7 0.0 collective-permute-done
  25.7 11.8 %all_to_all.30 = bf16[8,32,256]{2,1,0:T(8,128)(2,1)S(1)} all-to-all(bf16[8,32,256]{2,1,0:T(8,128)(2,1)S(1)} %add_convert_fusion.1), channel_id=1, replica_groups={{0,2,4,6,8,10,12,14},{1,3,5,7,9,11,13,15},{16,18,20,22,24,26,28,30},{17..., dimensions={0} | all-to-all | bytes 262144 | tf_op jit(solution)/shard_map/all_to_all | solution.py:26
  37.6 9.9 %all_to_all.31.x_ref.mine_ref = bf16[8,32,256]{2,1,0:T(8,128)(2,1)S(1)} all-to-all(bf16[8,32,256]{2,1,0:T(8,128)(2,1)S(1)} %broadcast_in_dim.4), channel_id=1, replica_groups={{0,2,4,6,8,10,12,14},{1,3,5,7,9,11,13,15},{16,18,20,22,24,26,28,30},{17..., dimensions={0} | all-to-all | bytes 262144 | tf_op jit(solution)/shard_map/all_to_all | solution.py:26
  47.4 0.0 collective-permute-start.1
  47.4 3.7 %shard_map.99 = (f32[32,1792]{1,0:T(8,128)S(1)}, f32[32,1]{1,0:T(8,128)S(1)}, f32[32,1]{1,0:T(8,128)S(1)}, f32[1,4]{1,0:T(1,128)S(1)}, bf16[1536,1792]{1,0:T(8,128)(2,1)S(1)}, /*index=5*/bf16[512,1792]{1,0:T(8,128)(2,1)S(1)}) custom-call(bf16[8,32,256]{2,1,0:T(8,128)(2,1)S(1)} %all_to_all.31.x_ref.mine_ref, bf16[1,4096]{1,0:T(2,128)(2,1)S(1)} %reshape.26.gain_ref, ...), custom_call_target="tpu_custom_call" | custom-call | flops 234881024 | bytes 16654352 | tf_op jit(solution)/shard_map/pallas_call | solution.py:54
  51.2 0.0 collective-permute-done.1.x_ref.got_ref
  51.2 5.2 %shard_map.100 = (bf16[8,32,256]{2,1,0:T(8,128)(2,1)S(1)}, f32[32,1]{1,0:T(8,128)S(1)}, f32[32,1]{1,0:T(8,128)S(1)}, bf16[32,1792]{1,0:T(8,128)(2,1)S(1)}) custom-call(bf16[8,32,256]{2,1,0:T(8,128)(2,1)S(1)} %collective-permute-done.1.x_ref.got_ref, bf16[1,4096]{1,0:T(2,128)(2,1)S(1)} %reshape.26.gain_ref, bf16[4096,896]{1,0:T(8,128)(2,1)} %gate_ref.5, ...), custom_call_target="tpu_custom_call" | custom-call | flops 234881024 | bytes 16887552 | tf_op jit(solution)/shard_map/pallas_call | solution.py:54
  56.4 0.6 collective-permute-start.2
  57.0 2.2 %shard_map.101 = f32[8,32,256]{2,1,0:T(8,128)S(1)} custom-call(bf16[32,1792]{1,0:T(8,128)(2,1)S(1)} %get-tuple-element.36.d_both_ref, bf16[512,1792]{1,0:T(8,128)(2,1)S(1)} %get-tuple-element.30.ready_ref, bf16[1536,1792]{1,0:T(8,128)(2,1)S(1)} %get-tuple-element.37.both_ref), custom_call_target="tpu_custom_call" | custom-call | flops 234881024 | bytes 7454720 | tf_op jit(solution)/shard_map/pallas_call | solution.py:54
  59.2 0.0 collective-permute-done.2
  59.2 9.8 %all_to_all.32 = bf16[8,32,256]{2,1,0:T(8,128)(2,1)S(1)} all-to-all(bf16[8,32,256]{2,1,0:T(8,128)(2,1)S(1)} %add_convert_fusion), channel_id=1, replica_groups={{0,2,4,6,8,10,12,14},{1,3,5,7,9,11,13,15},{16,18,20,22,24,26,28,30},{17..., dimensions={0} | all-to-all | bytes 262144 | tf_op jit(solution)/shard_map/all_to_all | solution.py:26
  69.1 9.8 %all_to_all.33.d_mine_ref = bf16[8,32,256]{2,1,0:T(8,128)(2,1)S(1)} all-to-all(bf16[8,32,256]{2,1,0:T(8,128)(2,1)S(1)} %broadcast_in_dim.5), channel_id=1, replica_groups={{0,2,4,6,8,10,12,14},{1,3,5,7,9,11,13,15},{16,18,20,22,24,26,28,30},{17..., dimensions={0} | all-to-all | bytes 262144 | tf_op jit(solution)/shard_map/all_to_all | solution.py:26
  79.0 0.0 collective-permute-start.3
  79.0 1.6 %shard_map.102.ready_ref = bf16[256,4096]{1,0:T(8,128)(2,1)S(1)} custom-call(bf16[2000,4096]{1,0:T(8,128)(2,1)} %embed_ref.7, bf16[32,256]{1,0:T(8,128)(2,1)S(1)} %reduce_sum.25.after_ref), custom_call_target="tpu_custom_call" | custom-call | bytes 16400384 | tf_op jit(solution)/shard_map/pallas_call | solution.py:54
  80.5 7.2 %shard_map.103 = bf16[32,2012]{1,0:T(8,128)(2,1)S(1)} custom-call(bf16[8,32,256]{2,1,0:T(8,128)(2,1)S(1)} %all_to_all.31.x_ref.mine_ref, bf16[8,32,256]{2,1,0:T(8,128)(2,1)S(1)} %collective-permute-done.1.x_ref.got_ref, bf16[8,32,256]{2,1,0:T(8,128)(2,1)S(1)} %all_to_all.33.d_mine_ref, bf16[8,32,256]{2,1,0:T(8,128)(2,1)S(1)} %collective-permute-done.3.d_got_ref, ...), custom_call_target="tpu_custom_call" | custom-call | flops 524288000 | bytes 19022480 | tf_op jit(solution)/shard_map/pallas_call | solution.py:54
  87.8 0.1 reshape.28
  87.9 10.5 %all_to_all.34.back_ref = bf16[16,2,2012]{2,1,0:T(2,128)(2,1)S(1)} all-to-all(bf16[16,2,2012]{2,1,0:T(2,128)(2,1)S(1)} %reshape.28), channel_id=1, replica_groups=mesh['groups'=2,'dp'=16] {'dp'}, dimensions={0} | all-to-all | bytes 257536 | tf_op jit(solution)/shard_map/all_to_all | solution.py:21
  98.4 1.2 %shard_map.104 = (bf16[2,32000]{1,0:T(2,128)(2,1)}, f32[1,4]{1,0:T(1,128)}) custom-call(f32[2,32000]{1,0:T(2,128)S(1)} %get-tuple-element.24.probs_ref, bf16[16,2,2012]{2,1,0:T(2,128)(2,1)S(1)} %all_to_all.34.back_ref, f32[1,4]{1,0:T(1,128)S(1)} %get-tuple-element.43.counts_ref), custom_call_target="tpu_custom_call" | custom-call | bytes 384784 | tf_op jit(solution)/shard_map/pallas_call | solution.py:54
  (11 shorter events, 0.2 us)
Async XLA Ops:
  0.6 0.9 copy-start
  2.9 15.3 %all-to-all-start = ((bf16[16,2,2000]{2,1,0:T(2,128)(2,1)}), bf16[16,2,2000]{2,1,0:T(2,128)(2,1)S(1)}, u32[]{:S(2)}, u32[]{:S(2)}) async-start(bf16[16,2,2000]{2,1,0:T(2,128)(2,1)} %get-tuple-element.25.after_ref), calls=%async_computation | async-start | bytes 262144 | tf_op jit(solution)/shard_map/all_to_all | solution.py:21
  11.0 0.7 copy-start.1
  22.0 3.6 %collective-permute-start = (bf16[8,32,256]{2,1,0:T(8,128)(2,1)S(1)}, bf16[8,32,256]{2,1,0:T(8,128)(2,1)S(1)}, u32[]{:S(2)}, u32[]{:S(2)}) collective-permute-start(bf16[8,32,256]{2,1,0:T(8,128)(2,1)S(1)} %get-tuple-element.29), channel_id=1, source_target_pairs={{0,1},{1,0},{2,3},{3,2},{4,5},{5,4},{6,7},{7,6},{8,9},{9,8},{10,11... | collective-permute-start | bytes 393224 | tf_op jit(solution)/shard_map/ppermute | solution.py:17
  22.1 25.3 %copy-start.3 = (bf16[4096]{0:T(1024)(128)(2,1)S(1)}, bf16[4096]{0:T(1024)(128)(2,1)}, u32[]{:S(2)}) copy-start(bf16[4096]{0:T(1024)(128)(2,1)} %param.10) | copy-start | bytes 24580
  22.1 25.3 %copy-start.2 = (s32[4]{0:T(128)S(1)}, s32[4]{0:T(128)}, u32[]{:S(2)}) copy-start(s32[4]{0:T(128)} %param.15) | copy-start | bytes 52
  47.4 3.8 %collective-permute-start.1 = (bf16[8,32,256]{2,1,0:T(8,128)(2,1)S(1)}, bf16[8,32,256]{2,1,0:T(8,128)(2,1)S(1)}, u32[]{:S(2)}, u32[]{:S(2)}) collective-permute-start(bf16[8,32,256]{2,1,0:T(8,128)(2,1)S(1)} %all_to_all.31.x_ref.mine_ref), channel_id=1, source_target_pairs={{0,1},{1,0},{2,3},{3,2},{4,5},{5,4},{6,7},{7,6},{8,9},{9,8},{10,11... | collective-permute-start | bytes 393224 | tf_op jit(solution)/shard_map/ppermute | solution.py:17
  56.4 2.8 %collective-permute-start.2 = (bf16[8,32,256]{2,1,0:T(8,128)(2,1)S(1)}, bf16[8,32,256]{2,1,0:T(8,128)(2,1)S(1)}, u32[]{:S(2)}, u32[]{:S(2)}) collective-permute-start(bf16[8,32,256]{2,1,0:T(8,128)(2,1)S(1)} %get-tuple-element.38), channel_id=1, source_target_pairs={{0,1},{1,0},{2,3},{3,2},{4,5},{5,4},{6,7},{7,6},{8,9},{9,8},{10,11... | collective-permute-start | bytes 393224 | tf_op jit(solution)/shard_map/ppermute | solution.py:17
  79.0 1.6 %collective-permute-start.3 = (bf16[8,32,256]{2,1,0:T(8,128)(2,1)S(1)}, bf16[8,32,256]{2,1,0:T(8,128)(2,1)S(1)}, u32[]{:S(2)}, u32[]{:S(2)}) collective-permute-start(bf16[8,32,256]{2,1,0:T(8,128)(2,1)S(1)} %all_to_all.33.d_mine_ref), channel_id=1, source_target_pairs={{0,1},{1,0},{2,3},{3,2},{4,5},{5,4},{6,7},{7,6},{8,9},{9,8},{10,11... | collective-permute-start | bytes 393224 | tf_op jit(solution)/shard_map/ppermute | solution.py:17

commit v17 on v16

--- a/solution.py
+++ b/solution.py
@@ -92,7 +92,8 @@
     return pl.ds(pl.multiple_of(start, size), size)
 
 
-def softmax_kernel(logits_ref, out_ref, probs_ref):
+def softmax_kernel(logits_ref, beside_ref, out_ref, probs_ref):
+    del beside_ref
     devices, _, part = out_ref.shape
     x = logits_ref[...].astype(F32)
     e = jnp.exp(x - jnp.max(x, axis=-1, keepdims=True))
@@ -138,25 +139,6 @@
     ]
 
 
-def ready_kernel(split, source_ref, after_ref, out_ref, sems):
-    del after_ref
-    width = out_ref.shape[1]
-    columns = span((1 - this_core()) * width, width) if split else pl.ds(0, width)
-    copies = bring(source_ref, out_ref, sems, columns)
-    for copy in copies:
-        copy.start()
-    for copy in copies:
-        copy.wait()
-
-
-def first_rows(rows, source, after, split):
-    width = source.shape[1] // 2 if split else source.shape[1]
-    return call(
-        functools.partial(ready_kernel, split), [pltpu.VMEM((rows, width), source.dtype)],
-        source, after, streamed=(0,), scratch=(pltpu.SemaphoreType.DMA((rows // 128,)),),
-    )[0]
-
-
 def half_kernel(other, slices_ref, ready_ref, embed_ref, head_ref, out_ref, score_ref, *rest):
     next_ref, table, acc, sems, next_sems = rest if other else (None, *rest, None)
     chips, total, own = out_ref.shape
@@ -186,9 +168,9 @@
             slices_ref[:, start:end], table[start - ready : end - ready],
             preferred_element_type=F32,
         )
-    score_ref[...] = jnp.sum(
-        acc[...] * head_ref[:, columns].astype(F32), axis=-1, keepdims=True
-    )
+    head = head_ref[...].astype(F32).reshape(1, 2 * chips * own)
+    head = jnp.where(half == 0, head[:, : chips * own], head[:, chips * own :])
+    score_ref[...] = jnp.sum(acc[...] * head, axis=-1, keepdims=True)
     for j in range(chips):
         out_ref[j] = acc[:, j * own : (j + 1) * own].astype(out_ref.dtype)
     for copy in following:
@@ -333,15 +315,20 @@
     backward_half(d_both_ref[...], weights, send_ref)
 
 
-def third_kernel(d_both_ref, ready_ref, both_ref, keep_ref):
+def third_kernel(d_both_ref, ready_ref, both_ref, embed_ref, keep_ref, first, sems):
+    following = bring(embed_ref, first, sems, pl.ds(0, embed_ref.shape[1]))
+    for copy in following:
+        copy.start()
     _, weights = weight_rows(ready_ref, both_ref, keep_ref.shape[2])
     backward_half(d_both_ref[...], weights, keep_ref)
+    for copy in following:
+        copy.wait()
 
 
 def input_kernel(
     mine_ref, got_ref, d_mine_ref, d_got_ref, gain_ref, head_ref, inv_ref,
     score_a_ref, score_b_ref, score_c_ref, valid_ref, counts_ref, ready_ref, embed_ref,
-    out_ref, dx_ref, table, sems,
+    out_ref, dx_ref, head_row, table, sems,
 ):
     chips, total, own = mine_ref.shape
     voc = embed_ref.shape[0]
@@ -369,6 +356,7 @@
 
     for piece in pieces(ready, voc):
         piece.start()
+    head_row[...] = head_ref[...].astype(F32).reshape(1, width)
     sources = ((mine_ref, d_mine_ref, core), (got_ref, d_got_ref, 1 - core))
     wide = jnp.zeros((total, own), F32)
     for x_ref, d_ref, half in sources:
@@ -385,7 +373,7 @@
             x = x_ref[j].astype(F32)
             g = d_ref[j].astype(F32) * gain_ref[:, columns].astype(F32)
             dx = inv * g - x * weight
-            dx_ref[:, columns] = (dx + valid * head_ref[:, columns].astype(F32)).astype(BF16)
+            dx_ref[:, columns] = (dx + valid * head_row[:, columns]).astype(BF16)
     score = valid * (score_a_ref[...] + score_b_ref[...] + score_c_ref[...])
     member = request == lax.broadcasted_iota(jnp.int32, (total, requests), 1)
     value = jnp.sum(jnp.where(member, score, 0.0), axis=0, keepdims=True)
@@ -502,7 +490,7 @@
     if tiled:
         blocked, probs = call(
             softmax_kernel,
-            [struct((devices, rows, part), BF16), pltpu.VMEM((rows, voc), F32)], logits,
+            [struct((devices, rows, part), BF16), pltpu.VMEM((rows, voc), F32)], logits, head,
         )
     else:
         probs32 = jax.nn.softmax(logits.astype(F32), axis=-1)
@@ -534,12 +522,12 @@
         send, score_a, first = call(
             functools.partial(half_kernel, True),
             [struct(half, BF16), column, pltpu.VMEM((ready, width // 2), BF16)],
-            slices, first, embed, head_row,
+            slices, first, embed, head,
             scratch=(*table, pltpu.SemaphoreType.DMA((ready // 128,))), **args,
         )
         keep, score_b = call(
             functools.partial(half_kernel, False), [struct(half, F32), column],
-            slices, first, embed, head_row, scratch=table, **args,
+            slices, first, embed, head, scratch=table, **args,
         )
     else:
         send, keep, score_a = plain_half(slices, embed, head_row, devices)
@@ -567,9 +555,11 @@
             x_got, gain_row, w_gate, w_up, ahead, products, squares, down_row, valid,
             scratch=(pltpu.VMEM(weight, BF16), sems), **args,
         )
-        (keep,) = call(
-            third_kernel, [struct(half, F32)], d_both, both_first, both,
-            kept=(1, 2), flops=2 * total * hidden * width,
+        keep, first = call(
+            third_kernel, [struct(half, F32), pltpu.VMEM((ready, width), BF16)],
+            d_both, both_first, both, embed,
+            kept=(1, 2), streamed=(3,), flops=2 * total * hidden * width,
+            scratch=(pltpu.SemaphoreType.DMA((ready // 128,)),),
         )
     else:
         down_row = jnp.sum(w_down.astype(F32) * head.astype(F32)[None, :], axis=-1)[None]
@@ -585,14 +575,14 @@
     d_got = swap_cores(d_mine, devices)
     padded = part + 3 * requests
     if tiled:
-        first = first_rows(256, embed, total_d, False)
         (d_slices,) = call(
             input_kernel, [struct((total, padded), BF16)],
-            x_mine, x_got, d_mine, d_got, gain_row, head_row, inv,
+            x_mine, x_got, d_mine, d_got, gain_row, head, inv,
             score_a, score_b, score_c, valid, counts_row, first, embed,
             kept=(12,), streamed=(13,), flops=2 * flops, room=2 * part * width,
             scratch=(
-                pltpu.VMEM((total, width), BF16), pltpu.VMEM((part - 256, width), BF16),
+                pltpu.VMEM((total, width), BF16), pltpu.VMEM((1, width), F32),
+                pltpu.VMEM((part - ready, width), BF16),
                 pltpu.SemaphoreType.DMA((-(-part // 64),)),
             ),
         )

time: 100 us -> 104 us (1.040)
  local copies, waits for them, and re-layouts: 2.51 us -> 5.42 us
  waiting for transfers between devices: 1.54 us -> 3.58 us
    unnamed x8 -> x16, local copies, waits for them, and re-layouts: 1.6 us -> 5.22 us
    ppermute x4, waiting for transfers between devices: 0.01 us -> 1.35 us  [swap_cores(): return lax.ppermute(value, 'dp', [(i, i ^ 1) for i in range(devices)])]
    pallas_call x10 -> x9, Pallas kernels: 34.7 us -> 34.3 us  [call(): pl.pallas_call(kernel, out_shape=outs, in_specs=specs, out_specs=[VMEM_SP...]
  transfers between devices with their start and end apart: 5 -> 5, of which waited for: 1 -> 2; matrix products, arithmetic and copies ran while one was open for 1% -> 0% of each run, Pallas kernels for 16% -> 15%
where the time goes in v17:
time: 104 us; the launch traced here: 103 us
  blocking collectives  51.2 us (49%)
  Pallas kernels  34.3 us (33%)
  starting transfers between devices  8.03 us (8%)
  local copies, waits for them, and re-layouts  5.42 us (5%)
  waiting for transfers between devices  3.58 us (3%)
    all_to_all x4, blocking collectives, exchange_chips(): lax.all_to_all(blocks, 'dp', split_axis=0, concat_axis=0, axis_index_grou...  40.6 us
    pallas_call x9, Pallas kernels, call(): pl.pallas_call(kernel, out_shape=outs, in_specs=specs, out_specs=[VMEM_SP...  34.3 us
    all_to_all x1, blocking collectives, exchange(): return lax.all_to_all(blocks, 'dp', split_axis=0, concat_axis=0, tiled=True)  10.5 us
    all_to_all x1, starting transfers between devices, exchange(): return lax.all_to_all(blocks, 'dp', split_axis=0, concat_axis=0, tiled=True)  7.39 us
    unnamed x16, local copies, waits for them, and re-layouts  5.22 us
    all_to_all x1, waiting for transfers between devices, exchange(): return lax.all_to_all(blocks, 'dp', split_axis=0, concat_axis=0, tiled=True)  2.23 us
  transfers between devices with their start and end apart: 5, of which 2 were waited for; matrix products, arithmetic and copies ran while one was open for 0% of the time, Pallas kernels for 15%

profile of v17, /device:TPU:0, one launch (start us, length us, event | category | flops | bytes accessed | tf_op | source)
XLA Modules:
  0.0 103.4 jit_solution(2867036298021503636)
XLA Ops:
  0.6 0.0 copy-start.2
  0.6 0.7 copy-done.2
  1.3 0.9 copy-done.5
  2.2 1.4 %shard_map.95 = (bf16[16,2,2000]{2,1,0:T(2,128)(2,1)}, f32[2,32000]{1,0:T(2,128)S(1)}) custom-call(bf16[2,32000]{1,0:T(2,128)(2,1)S(1)} %copy-done.5, bf16[4096]{0:T(1024)(128)(2,1)S(1)} %copy-done.2), custom_call_target="tpu_custom_call" | custom-call | bytes 136192 | tf_op jit(solution)/shard_map/pallas_call | solution.py:54
  3.7 7.4 %all-to-all-start = ((bf16[16,2,2000]{2,1,0:T(2,128)(2,1)}), bf16[16,2,2000]{2,1,0:T(2,128)(2,1)S(1)}, u32[]{:S(2)}, u32[]{:S(2)}) async-start(bf16[16,2,2000]{2,1,0:T(2,128)(2,1)} %get-tuple-element.27.after_ref), calls=%async_computation | async-start | bytes 262144 | tf_op jit(solution)/shard_map/all_to_all | solution.py:21
  11.1 0.0 copy-start.3
  11.1 0.7 copy-done.3
  11.8 5.0 %shard_map.96 = (f32[1,896]{1,0:T(1,128)S(1)}, bf16[256,2048]{1,0:T(8,128)(2,1)S(1)}, bf16[512,1792]{1,0:T(8,128)(2,1)S(1)}) custom-call(bf16[4096]{0:T(1024)(128)(2,1)S(1)} %copy-done.3, bf16[896,4096]{1,0:T(8,128)(2,1)} %down_ref.1, bf16[2000,4096]{1,0:T(8,128)(2,1)} %embed_ref.9, bf16[4096,896]{1,0:T(8,128)(2,1)} %gate_ref.5, bf16[4096,896]{1,0:T(8,128)(2,1)} %up_ref.5, ...), custom_call_target="tpu_custom_call" | custom-call | flops 7340032 | bytes 38540288 | tf_op jit(solution)/shard_map/pallas_call | solution.py:54
  16.8 2.2 %all-to-all-done = bf16[16,2,2000]{2,1,0:T(2,128)(2,1)S(1)} async-done(((bf16[16,2,2000]{2,1,0:T(2,128)(2,1)}), bf16[16,2,2000]{2,1,0:T(2,128)(2,1)S(1)}, u32[]{:S(2)}, u32[]{:S(2)}) %all-to-all-start) | async-done | bytes 128032 | tf_op jit(solution)/shard_map/all_to_all | solution.py:21
  19.0 0.1 reshape.21.slices_ref
  19.1 3.7 %shard_map.97 = (bf16[8,32,256]{2,1,0:T(8,128)(2,1)S(1)}, f32[32,1]{1,0:T(8,128)S(1)}, bf16[256,2048]{1,0:T(8,128)(2,1)S(1)}) custom-call(bf16[32,2000]{1,0:T(8,128)(2,1)S(1)} %reshape.21.slices_ref, bf16[256,2048]{1,0:T(8,128)(2,1)S(1)} %get-tuple-element.28.ready_ref, bf16[2000,4096]{1,0:T(8,128)(2,1)} %embed_ref.9, bf16[4096]{0:T(1024)(128)(2,1)S(1)} %copy-done.4), custom_call_target="tpu_custom_call" | custom-call | flops 262144000 | bytes 17568768 | tf_op jit(solution)/shard_map/pallas_call | solution.py:54
  22.8 0.1 collective-permute-start
  22.8 0.0 copy-start.7
  22.9 0.0 copy-start.6
  22.9 3.5 %shard_map.98 = (f32[8,32,256]{2,1,0:T(8,128)S(1)}, f32[32,1]{1,0:T(8,128)S(1)}) custom-call(bf16[32,2000]{1,0:T(8,128)(2,1)S(1)} %reshape.21.slices_ref, bf16[256,2048]{1,0:T(8,128)(2,1)S(1)} %get-tuple-element.29.ready_ref, bf16[2000,4096]{1,0:T(8,128)(2,1)} %embed_ref.9, bf16[4096]{0:T(1024)(128)(2,1)S(1)} %copy-done.4), custom_call_target="tpu_custom_call" | custom-call | flops 262144000 | bytes 17568768 | tf_op jit(solution)/shard_map/pallas_call | solution.py:54
  26.4 11.1 %all_to_all.30 = bf16[8,32,256]{2,1,0:T(8,128)(2,1)S(1)} all-to-all(bf16[8,32,256]{2,1,0:T(8,128)(2,1)S(1)} %add_convert_fusion.1), channel_id=1, replica_groups={{0,2,4,6,8,10,12,14},{1,3,5,7,9,11,13,15},{16,18,20,22,24,26,28,30},{17..., dimensions={0} | all-to-all | bytes 262144 | tf_op jit(solution)/shard_map/all_to_all | solution.py:26
  37.6 9.9 %all_to_all.31.x_ref.mine_ref = bf16[8,32,256]{2,1,0:T(8,128)(2,1)S(1)} all-to-all(bf16[8,32,256]{2,1,0:T(8,128)(2,1)S(1)} %broadcast_in_dim.4), channel_id=1, replica_groups={{0,2,4,6,8,10,12,14},{1,3,5,7,9,11,13,15},{16,18,20,22,24,26,28,30},{17..., dimensions={0} | all-to-all | bytes 262144 | tf_op jit(solution)/shard_map/all_to_all | solution.py:26
  47.4 0.0 collective-permute-start.1
  47.5 3.7 %shard_map.99 = (f32[32,1792]{1,0:T(8,128)S(1)}, f32[32,1]{1,0:T(8,128)S(1)}, f32[32,1]{1,0:T(8,128)S(1)}, f32[1,4]{1,0:T(1,128)S(1)}, bf16[1536,1792]{1,0:T(8,128)(2,1)S(1)}, /*index=5*/bf16[512,1792]{1,0:T(8,128)(2,1)S(1)}) custom-call(bf16[8,32,256]{2,1,0:T(8,128)(2,1)S(1)} %all_to_all.31.x_ref.mine_ref, bf16[1,4096]{1,0:T(2,128)(2,1)S(1)} %reshape.22.gain_ref, ...), custom_call_target="tpu_custom_call" | custom-call | flops 234881024 | bytes 16654352 | tf_op jit(solution)/shard_map/pallas_call | solution.py:54
  51.2 5.2 %shard_map.100 = (bf16[8,32,256]{2,1,0:T(8,128)(2,1)S(1)}, f32[32,1]{1,0:T(8,128)S(1)}, f32[32,1]{1,0:T(8,128)S(1)}, bf16[32,1792]{1,0:T(8,128)(2,1)S(1)}) custom-call(bf16[8,32,256]{2,1,0:T(8,128)(2,1)S(1)} %collective-permute-done.1.x_ref.got_ref, bf16[1,4096]{1,0:T(2,128)(2,1)S(1)} %reshape.22.gain_ref, bf16[4096,896]{1,0:T(8,128)(2,1)} %gate_ref.5, ...), custom_call_target="tpu_custom_call" | custom-call | flops 234881024 | bytes 16887552 | tf_op jit(solution)/shard_map/pallas_call | solution.py:54
  56.4 0.6 collective-permute-start.2
  57.0 3.3 %shard_map.101 = (f32[8,32,256]{2,1,0:T(8,128)S(1)}, bf16[256,4096]{1,0:T(8,128)(2,1)S(1)}) custom-call(bf16[32,1792]{1,0:T(8,128)(2,1)S(1)} %get-tuple-element.38.d_both_ref, bf16[512,1792]{1,0:T(8,128)(2,1)S(1)} %get-tuple-element.32.ready_ref, bf16[1536,1792]{1,0:T(8,128)(2,1)S(1)} %get-tuple-element.39.both_ref, bf16[2000,4096]{1,0:T(8,128)(2,1)} %embed_ref.9), custom_call_target="tpu_custom_call" | custom-call | flops 234881024 | bytes 23838720 | tf_op jit(solution)/shard_map/pallas_call | solution.py:54
  60.3 1.3 %copy-done = bf16[256,4096]{1,0:T(8,128)(2,1)} copy-done((bf16[256,4096]{1,0:T(8,128)(2,1)}, bf16[256,4096]{1,0:T(8,128)(2,1)S(1)}, u32[]{:S(2)}) %copy-start) | copy-done | bytes 2097176
  61.6 0.0 collective-permute-done.2
  61.7 9.8 %all_to_all.32 = bf16[8,32,256]{2,1,0:T(8,128)(2,1)S(1)} all-to-all(bf16[8,32,256]{2,1,0:T(8,128)(2,1)S(1)} %add_convert_fusion), channel_id=1, replica_groups={{0,2,4,6,8,10,12,14},{1,3,5,7,9,11,13,15},{16,18,20,22,24,26,28,30},{17..., dimensions={0} | all-to-all | bytes 262144 | tf_op jit(solution)/shard_map/all_to_all | solution.py:26
  71.5 9.8 %all_to_all.33.d_mine_ref = bf16[8,32,256]{2,1,0:T(8,128)(2,1)S(1)} all-to-all(bf16[8,32,256]{2,1,0:T(8,128)(2,1)S(1)} %broadcast_in_dim.5), channel_id=1, replica_groups={{0,2,4,6,8,10,12,14},{1,3,5,7,9,11,13,15},{16,18,20,22,24,26,28,30},{17..., dimensions={0} | all-to-all | bytes 262144 | tf_op jit(solution)/shard_map/all_to_all | solution.py:26
  81.4 1.3 %collective-permute-done.3.d_got_ref = bf16[8,32,256]{2,1,0:T(8,128)(2,1)S(1)} collective-permute-done((bf16[8,32,256]{2,1,0:T(8,128)(2,1)S(1)}, bf16[8,32,256]{2,1,0:T(8,128)(2,1)S(1)}, u32[]{:S(2)}, u32[]{:S(2)}) %collective-permute-start.3) | collective-permute-done | bytes 131104 | tf_op jit(solution)/shard_map/ppermute | solution.py:17
  82.7 1.6 %copy-done.1 = bf16[256,4096]{1,0:T(8,128)(2,1)S(1)} copy-done((bf16[256,4096]{1,0:T(8,128)(2,1)S(1)}, bf16[256,4096]{1,0:T(8,128)(2,1)}, u32[]{:S(2)}) %copy-start.1) | copy-done | bytes 2097176
  84.3 7.2 %shard_map.102 = bf16[32,2012]{1,0:T(8,128)(2,1)S(1)} custom-call(bf16[8,32,256]{2,1,0:T(8,128)(2,1)S(1)} %all_to_all.31.x_ref.mine_ref, bf16[8,32,256]{2,1,0:T(8,128)(2,1)S(1)} %collective-permute-done.1.x_ref.got_ref, bf16[8,32,256]{2,1,0:T(8,128)(2,1)S(1)} %all_to_all.33.d_mine_ref, bf16[8,32,256]{2,1,0:T(8,128)(2,1)S(1)} %collective-permute-done.3.d_got_ref, ...), custom_call_target="tpu_custom_call" | custom-call | flops 524288000 | bytes 19022480 | tf_op jit(solution)/shard_map/pallas_call | solution.py:54
  91.6 0.1 reshape.24
  91.7 10.5 %all_to_all.34.back_ref = bf16[16,2,2012]{2,1,0:T(2,128)(2,1)S(1)} all-to-all(bf16[16,2,2012]{2,1,0:T(2,128)(2,1)S(1)} %reshape.24), channel_id=1, replica_groups=mesh['groups'=2,'dp'=16] {'dp'}, dimensions={0} | all-to-all | bytes 257536 | tf_op jit(solution)/shard_map/all_to_all | solution.py:21
  102.2 1.2 %shard_map.103 = (bf16[2,32000]{1,0:T(2,128)(2,1)}, f32[1,4]{1,0:T(1,128)}) custom-call(f32[2,32000]{1,0:T(2,128)S(1)} %get-tuple-element.26.probs_ref, bf16[16,2,2012]{2,1,0:T(2,128)(2,1)S(1)} %all_to_all.34.back_ref, f32[1,4]{1,0:T(1,128)S(1)} %get-tuple-element.46.counts_ref), custom_call_target="tpu_custom_call" | custom-call | bytes 384784 | tf_op jit(solution)/shard_map/pallas_call | solution.py:54
  (17 shorter events, 0.2 us)
Async XLA Ops:
  0.6 0.7 copy-start.2
  1.3 0.9 copy-start.5
  3.7 15.3 %all-to-all-start = ((bf16[16,2,2000]{2,1,0:T(2,128)(2,1)}), bf16[16,2,2000]{2,1,0:T(2,128)(2,1)S(1)}, u32[]{:S(2)}, u32[]{:S(2)}) async-start(bf16[16,2,2000]{2,1,0:T(2,128)(2,1)} %get-tuple-element.27.after_ref), calls=%async_computation | async-start | bytes 262144 | tf_op jit(solution)/shard_map/all_to_all | solution.py:21
  11.1 0.7 copy-start.3
  11.8 7.3 %copy-start.4 = (bf16[4096]{0:T(1024)(128)(2,1)S(1)}, bf16[4096]{0:T(1024)(128)(2,1)}, u32[]{:S(2)}) copy-start(bf16[4096]{0:T(1024)(128)(2,1)} %head_ref.7) | copy-start | bytes 24580
  22.8 3.6 %collective-permute-start = (bf16[8,32,256]{2,1,0:T(8,128)(2,1)S(1)}, bf16[8,32,256]{2,1,0:T(8,128)(2,1)S(1)}, u32[]{:S(2)}, u32[]{:S(2)}) collective-permute-start(bf16[8,32,256]{2,1,0:T(8,128)(2,1)S(1)} %get-tuple-element.31), channel_id=1, source_target_pairs={{0,1},{1,0},{2,3},{3,2},{4,5},{5,4},{6,7},{7,6},{8,9},{9,8},{10,11... | collective-permute-start | bytes 393224 | tf_op jit(solution)/shard_map/ppermute | solution.py:17
  22.8 24.6 %copy-start.7 = (bf16[4096]{0:T(1024)(128)(2,1)S(1)}, bf16[4096]{0:T(1024)(128)(2,1)}, u32[]{:S(2)}) copy-start(bf16[4096]{0:T(1024)(128)(2,1)} %param.10) | copy-start | bytes 24580
  22.9 24.6 %copy-start.6 = (s32[4]{0:T(128)S(1)}, s32[4]{0:T(128)}, u32[]{:S(2)}) copy-start(s32[4]{0:T(128)} %param.15) | copy-start | bytes 52
  47.4 3.8 %collective-permute-start.1 = (bf16[8,32,256]{2,1,0:T(8,128)(2,1)S(1)}, bf16[8,32,256]{2,1,0:T(8,128)(2,1)S(1)}, u32[]{:S(2)}, u32[]{:S(2)}) collective-permute-start(bf16[8,32,256]{2,1,0:T(8,128)(2,1)S(1)} %all_to_all.31.x_ref.mine_ref), channel_id=1, source_target_pairs={{0,1},{1,0},{2,3},{3,2},{4,5},{5,4},{6,7},{7,6},{8,9},{9,8},{10,11... | collective-permute-start | bytes 393224 | tf_op jit(solution)/shard_map/ppermute | solution.py:17
  56.4 5.2 %collective-permute-start.2 = (bf16[8,32,256]{2,1,0:T(8,128)(2,1)S(1)}, bf16[8,32,256]{2,1,0:T(8,128)(2,1)S(1)}, u32[]{:S(2)}, u32[]{:S(2)}) collective-permute-start(bf16[8,32,256]{2,1,0:T(8,128)(2,1)S(1)} %get-tuple-element.41), channel_id=1, source_target_pairs={{0,1},{1,0},{2,3},{3,2},{4,5},{5,4},{6,7},{7,6},{8,9},{9,8},{10,11... | collective-permute-start | bytes 393224 | tf_op jit(solution)/shard_map/ppermute | solution.py:17
  60.3 1.3 %copy-start = (bf16[256,4096]{1,0:T(8,128)(2,1)}, bf16[256,4096]{1,0:T(8,128)(2,1)S(1)}, u32[]{:S(2)}) copy-start(bf16[256,4096]{1,0:T(8,128)(2,1)S(1)} %get-tuple-element.47.ready_ref) | copy-start | bytes 6291460
  81.4 1.3 %collective-permute-start.3 = (bf16[8,32,256]{2,1,0:T(8,128)(2,1)S(1)}, bf16[8,32,256]{2,1,0:T(8,128)(2,1)S(1)}, u32[]{:S(2)}, u32[]{:S(2)}) collective-permute-start(bf16[8,32,256]{2,1,0:T(8,128)(2,1)S(1)} %all_to_all.33.d_mine_ref), channel_id=1, source_target_pairs={{0,1},{1,0},{2,3},{3,2},{4,5},{5,4},{6,7},{7,6},{8,9},{9,8},{10,11... | collective-permute-start | bytes 393224 | tf_op jit(solution)/shard_map/ppermute | solution.py:17
  82.7 1.6 %copy-start.1 = (bf16[256,4096]{1,0:T(8,128)(2,1)S(1)}, bf16[256,4096]{1,0:T(8,128)(2,1)}, u32[]{:S(2)}) copy-start(bf16[256,4096]{1,0:T(8,128)(2,1)} %copy-done) | copy-start | bytes 6291460

commit v18 on v16

--- a/solution.py
+++ b/solution.py
@@ -197,7 +197,7 @@
 
 def early_kernel(
     head_ref, down_ref, embed_ref, gate_ref, up_ref, after_ref,
-    out_ref, first, both, table, sems, first_sems, both_sems,
+    out_ref, head_row, first, both, table, head_copy, sems, first_sems, both_sems, head_sem,
 ):
     del after_ref
     width, lanes = down_ref.shape[1], 128
@@ -208,6 +208,8 @@
         return pltpu.make_async_copy(down_ref.at[rows], table.at[rows], sems.at[j])
 
     steps = sems.shape[0]
+    bring_head = pltpu.make_async_copy(head_ref, head_copy, head_sem)
+    bring_head.start()
     for j in range(steps):
         copy(j).start()
     half = width // 2
@@ -217,7 +219,9 @@
     others += bring_blocks(gate_ref, up_ref, both, core, range(2), own, chips, both_sems)
     for other in others:
         other.start()
-    head = head_ref[...].astype(F32).reshape(1, width)
+    bring_head.wait()
+    head = head_copy[...].astype(F32).reshape(1, width)
+    head_row[...] = head
 
     def step(j, _):
         copy(j).wait()
@@ -513,17 +517,20 @@
     flops = total * part * width
     if tiled:
         ready = 256
-        down_row, first, both_first = call(
+        down_row, head32, first, both_first = call(
             early_kernel,
             [
-                struct((1, hidden), F32), pltpu.VMEM((ready, width // 2), BF16),
+                struct((1, hidden), F32), struct((1, width), F32),
+                pltpu.VMEM((ready, width // 2), BF16),
                 pltpu.VMEM((2 * own, 2 * hidden), BF16),
             ],
             head, w_down, embed, w_gate, w_up, blocked,
-            streamed=(1, 2, 3, 4), flops=2 * hidden * width, room=2 * hidden * width,
+            streamed=(0, 1, 2, 3, 4), flops=2 * hidden * width, room=2 * hidden * width,
             scratch=(
-                pltpu.VMEM((hidden, width), BF16), pltpu.SemaphoreType.DMA((hidden // 128,)),
+                pltpu.VMEM((hidden, width), BF16), pltpu.VMEM((width,), BF16),
+                pltpu.SemaphoreType.DMA((hidden // 128,)),
                 pltpu.SemaphoreType.DMA((ready // 128,)), pltpu.SemaphoreType.DMA((2, 2)),
+                pltpu.SemaphoreType.DMA,
             ),
         )
         table = (
@@ -534,12 +541,12 @@
         send, score_a, first = call(
             functools.partial(half_kernel, True),
             [struct(half, BF16), column, pltpu.VMEM((ready, width // 2), BF16)],
-            slices, first, embed, head_row,
+            slices, first, embed, head32,
             scratch=(*table, pltpu.SemaphoreType.DMA((ready // 128,))), **args,
         )
         keep, score_b = call(
             functools.partial(half_kernel, False), [struct(half, F32), column],
-            slices, first, embed, head_row, scratch=table, **args,
+            slices, first, embed, head32, scratch=table, **args,
         )
     else:
         send, keep, score_a = plain_half(slices, embed, head_row, devices)
@@ -588,7 +595,7 @@
         first = first_rows(256, embed, total_d, False)
         (d_slices,) = call(
             input_kernel, [struct((total, padded), BF16)],
-            x_mine, x_got, d_mine, d_got, gain_row, head_row, inv,
+            x_mine, x_got, d_mine, d_got, gain_row, head32, inv,
             score_a, score_b, score_c, valid, counts_row, first, embed,
             kept=(12,), streamed=(13,), flops=2 * flops, room=2 * part * width,
             scratch=(

time: 100 us -> 100 us (level)
  local copies, waits for them, and re-layouts: 2.51 us -> 1.11 us
  Pallas kernels: 34.7 us -> 36.1 us
    pallas_call x10, Pallas kernels: 34.7 us -> 36.1 us  [call(): pl.pallas_call(kernel, out_shape=outs, in_specs=specs, out_specs=[VMEM_SP...]
  transfers between devices with their start and end apart: 5 -> 5, of which waited for: 1 -> 1; matrix products, arithmetic and copies ran while one was open for 1% -> 0% of each run, Pallas kernels for 16% -> 17%
where the time goes in v18:
time: 100 us; the launch traced here: 99.5 us
  blocking collectives  51.7 us (52%)
  Pallas kernels  36.1 us (36%)
  starting transfers between devices  8.03 us (8%)
  waiting for transfers between devices  1.66 us (2%)
  local copies, waits for them, and re-layouts  1.11 us (1%)
    all_to_all x4, blocking collectives, exchange_chips(): lax.all_to_all(blocks, 'dp', split_axis=0, concat_axis=0, axis_index_grou...  41.2 us
    pallas_call x10, Pallas kernels, call(): pl.pallas_call(kernel, out_shape=outs, in_specs=specs, out_specs=[VMEM_SP...  36.1 us
    all_to_all x1, blocking collectives, exchange(): return lax.all_to_all(blocks, 'dp', split_axis=0, concat_axis=0, tiled=True)  10.5 us
    all_to_all x1, starting transfers between devices, exchange(): return lax.all_to_all(blocks, 'dp', split_axis=0, concat_axis=0, tiled=True)  7.39 us
  transfers between devices with their start and end apart: 5, of which 1 were waited for; matrix products, arithmetic and copies ran while one was open for 0% of the time, Pallas kernels for 17%

profile of v18, /device:TPU:0, one launch (start us, length us, event | category | flops | bytes accessed | tf_op | source)
XLA Modules:
  0.0 99.5 jit_solution(8903071434808845499)
XLA Ops:
  0.6 0.0 copy-start
  0.6 0.9 copy-done
  1.5 1.4 %shard_map.95 = (bf16[16,2,2000]{2,1,0:T(2,128)(2,1)}, f32[2,32000]{1,0:T(2,128)S(1)}) custom-call(bf16[2,32000]{1,0:T(2,128)(2,1)S(1)} %copy-done), custom_call_target="tpu_custom_call" | custom-call | bytes 128000 | tf_op jit(solution)/shard_map/pallas_call | solution.py:54
  2.9 7.4 %all-to-all-start = ((bf16[16,2,2000]{2,1,0:T(2,128)(2,1)}), bf16[16,2,2000]{2,1,0:T(2,128)(2,1)S(1)}, u32[]{:S(2)}, u32[]{:S(2)}) async-start(bf16[16,2,2000]{2,1,0:T(2,128)(2,1)} %get-tuple-element.26.after_ref), calls=%async_computation | async-start | bytes 262144 | tf_op jit(solution)/shard_map/all_to_all | solution.py:21
  10.3 6.3 %shard_map.96 = (f32[1,896]{1,0:T(1,128)S(1)}, f32[1,4096]{1,0:T(1,128)S(1)}, bf16[256,2048]{1,0:T(8,128)(2,1)S(1)}, bf16[512,1792]{1,0:T(8,128)(2,1)S(1)}) custom-call(bf16[4096]{0:T(1024)(128)(2,1)} %head_ref.1, bf16[896,4096]{1,0:T(8,128)(2,1)} %down_ref.1, bf16[2000,4096]{1,0:T(8,128)(2,1)} %embed_ref.7, bf16[4096,896]{1,0:T(8,128)(2,1)} %gate_ref.5, ...), custom_call_target="tpu_custom_call" | custom-call | flops 7340032 | bytes 38540288 | tf_op jit(solution)/shard_map/pallas_call | solution.py:54
  16.6 1.6 %all-to-all-done = bf16[16,2,2000]{2,1,0:T(2,128)(2,1)S(1)} async-done(((bf16[16,2,2000]{2,1,0:T(2,128)(2,1)}), bf16[16,2,2000]{2,1,0:T(2,128)(2,1)S(1)}, u32[]{:S(2)}, u32[]{:S(2)}) %all-to-all-start) | async-done | bytes 128032 | tf_op jit(solution)/shard_map/all_to_all | solution.py:21
  18.3 0.1 reshape.21.slices_ref
  18.3 3.7 %shard_map.97 = (bf16[8,32,256]{2,1,0:T(8,128)(2,1)S(1)}, f32[32,1]{1,0:T(8,128)S(1)}, bf16[256,2048]{1,0:T(8,128)(2,1)S(1)}) custom-call(bf16[32,2000]{1,0:T(8,128)(2,1)S(1)} %reshape.21.slices_ref, bf16[256,2048]{1,0:T(8,128)(2,1)S(1)} %get-tuple-element.27.ready_ref, bf16[2000,4096]{1,0:T(8,128)(2,1)} %embed_ref.7, f32[1,4096]{1,0:T(1,128)S(1)} %get-tuple-element.28.head_ref), custom_call_target="tpu_custom_call" | custom-call | flops 262144000 | bytes 17576960 | tf_op jit(solution)/shard_map/pallas_call | solution.py:54
  22.0 0.1 collective-permute-start
  22.1 0.0 copy-start.2
  22.1 0.0 copy-start.1
  22.1 3.5 %shard_map.98 = (f32[8,32,256]{2,1,0:T(8,128)S(1)}, f32[32,1]{1,0:T(8,128)S(1)}) custom-call(bf16[32,2000]{1,0:T(8,128)(2,1)S(1)} %reshape.21.slices_ref, bf16[256,2048]{1,0:T(8,128)(2,1)S(1)} %get-tuple-element.29.ready_ref, bf16[2000,4096]{1,0:T(8,128)(2,1)} %embed_ref.7, f32[1,4096]{1,0:T(1,128)S(1)} %get-tuple-element.28.head_ref), custom_call_target="tpu_custom_call" | custom-call | flops 262144000 | bytes 17576960 | tf_op jit(solution)/shard_map/pallas_call | solution.py:54
  25.7 0.0 collective-permute-done
  25.7 11.7 %all_to_all.30 = bf16[8,32,256]{2,1,0:T(8,128)(2,1)S(1)} all-to-all(bf16[8,32,256]{2,1,0:T(8,128)(2,1)S(1)} %add_convert_fusion.1), channel_id=1, replica_groups={{0,2,4,6,8,10,12,14},{1,3,5,7,9,11,13,15},{16,18,20,22,24,26,28,30},{17..., dimensions={0} | all-to-all | bytes 262144 | tf_op jit(solution)/shard_map/all_to_all | solution.py:26
  37.4 9.9 %all_to_all.31.x_ref.mine_ref = bf16[8,32,256]{2,1,0:T(8,128)(2,1)S(1)} all-to-all(bf16[8,32,256]{2,1,0:T(8,128)(2,1)S(1)} %broadcast_in_dim.4), channel_id=1, replica_groups={{0,2,4,6,8,10,12,14},{1,3,5,7,9,11,13,15},{16,18,20,22,24,26,28,30},{17..., dimensions={0} | all-to-all | bytes 262144 | tf_op jit(solution)/shard_map/all_to_all | solution.py:26
  47.3 0.0 collective-permute-start.1
  47.3 0.0 copy-done.2
  47.3 3.7 %shard_map.99 = (f32[32,1792]{1,0:T(8,128)S(1)}, f32[32,1]{1,0:T(8,128)S(1)}, f32[32,1]{1,0:T(8,128)S(1)}, f32[1,4]{1,0:T(1,128)S(1)}, bf16[1536,1792]{1,0:T(8,128)(2,1)S(1)}, /*index=5*/bf16[512,1792]{1,0:T(8,128)(2,1)S(1)}) custom-call(bf16[8,32,256]{2,1,0:T(8,128)(2,1)S(1)} %all_to_all.31.x_ref.mine_ref, bf16[1,4096]{1,0:T(2,128)(2,1)S(1)} %reshape.22.gain_ref, ...), custom_call_target="tpu_custom_call" | custom-call | flops 234881024 | bytes 16654352 | tf_op jit(solution)/shard_map/pallas_call | solution.py:54
  51.1 0.0 collective-permute-done.1.x_ref.got_ref
  51.1 5.2 %shard_map.100 = (bf16[8,32,256]{2,1,0:T(8,128)(2,1)S(1)}, f32[32,1]{1,0:T(8,128)S(1)}, f32[32,1]{1,0:T(8,128)S(1)}, bf16[32,1792]{1,0:T(8,128)(2,1)S(1)}) custom-call(bf16[8,32,256]{2,1,0:T(8,128)(2,1)S(1)} %collective-permute-done.1.x_ref.got_ref, bf16[1,4096]{1,0:T(2,128)(2,1)S(1)} %reshape.22.gain_ref, bf16[4096,896]{1,0:T(8,128)(2,1)} %gate_ref.5, ...), custom_call_target="tpu_custom_call" | custom-call | flops 234881024 | bytes 16887552 | tf_op jit(solution)/shard_map/pallas_call | solution.py:54
  56.3 0.6 collective-permute-start.2
  56.9 2.2 %shard_map.101 = f32[8,32,256]{2,1,0:T(8,128)S(1)} custom-call(bf16[32,1792]{1,0:T(8,128)(2,1)S(1)} %get-tuple-element.38.d_both_ref, bf16[512,1792]{1,0:T(8,128)(2,1)S(1)} %get-tuple-element.32.ready_ref, bf16[1536,1792]{1,0:T(8,128)(2,1)S(1)} %get-tuple-element.39.both_ref), custom_call_target="tpu_custom_call" | custom-call | flops 234881024 | bytes 7454720 | tf_op jit(solution)/shard_map/pallas_call | solution.py:54
  59.1 0.0 collective-permute-done.2
  59.1 9.8 %all_to_all.32 = bf16[8,32,256]{2,1,0:T(8,128)(2,1)S(1)} all-to-all(bf16[8,32,256]{2,1,0:T(8,128)(2,1)S(1)} %add_convert_fusion), channel_id=1, replica_groups={{0,2,4,6,8,10,12,14},{1,3,5,7,9,11,13,15},{16,18,20,22,24,26,28,30},{17..., dimensions={0} | all-to-all | bytes 262144 | tf_op jit(solution)/shard_map/all_to_all | solution.py:26
  69.0 9.8 %all_to_all.33.d_mine_ref = bf16[8,32,256]{2,1,0:T(8,128)(2,1)S(1)} all-to-all(bf16[8,32,256]{2,1,0:T(8,128)(2,1)S(1)} %broadcast_in_dim.5), channel_id=1, replica_groups={{0,2,4,6,8,10,12,14},{1,3,5,7,9,11,13,15},{16,18,20,22,24,26,28,30},{17..., dimensions={0} | all-to-all | bytes 262144 | tf_op jit(solution)/shard_map/all_to_all | solution.py:26
  78.9 0.0 collective-permute-start.3
  78.9 1.6 %shard_map.102.ready_ref = bf16[256,4096]{1,0:T(8,128)(2,1)S(1)} custom-call(bf16[2000,4096]{1,0:T(8,128)(2,1)} %embed_ref.7, bf16[32,256]{1,0:T(8,128)(2,1)S(1)} %reduce_sum.25.after_ref), custom_call_target="tpu_custom_call" | custom-call | bytes 16400384 | tf_op jit(solution)/shard_map/pallas_call | solution.py:54
  80.4 0.0 collective-permute-done.3.d_got_ref
  80.4 7.2 %shard_map.103 = bf16[32,2012]{1,0:T(8,128)(2,1)S(1)} custom-call(bf16[8,32,256]{2,1,0:T(8,128)(2,1)S(1)} %all_to_all.31.x_ref.mine_ref, bf16[8,32,256]{2,1,0:T(8,128)(2,1)S(1)} %collective-permute-done.1.x_ref.got_ref, bf16[8,32,256]{2,1,0:T(8,128)(2,1)S(1)} %all_to_all.33.d_mine_ref, bf16[8,32,256]{2,1,0:T(8,128)(2,1)S(1)} %collective-permute-done.3.d_got_ref, ...), custom_call_target="tpu_custom_call" | custom-call | flops 524288000 | bytes 19030672 | tf_op jit(solution)/shard_map/pallas_call | solution.py:54
  87.7 0.1 reshape.24
  87.8 10.5 %all_to_all.34.back_ref = bf16[16,2,2012]{2,1,0:T(2,128)(2,1)S(1)} all-to-all(bf16[16,2,2012]{2,1,0:T(2,128)(2,1)S(1)} %reshape.24), channel_id=1, replica_groups=mesh['groups'=2,'dp'=16] {'dp'}, dimensions={0} | all-to-all | bytes 257536 | tf_op jit(solution)/shard_map/all_to_all | solution.py:21
  98.3 1.2 %shard_map.104 = (bf16[2,32000]{1,0:T(2,128)(2,1)}, f32[1,4]{1,0:T(1,128)}) custom-call(f32[2,32000]{1,0:T(2,128)S(1)} %get-tuple-element.25.probs_ref, bf16[16,2,2012]{2,1,0:T(2,128)(2,1)S(1)} %all_to_all.34.back_ref, f32[1,4]{1,0:T(1,128)S(1)} %get-tuple-element.45.counts_ref), custom_call_target="tpu_custom_call" | custom-call | bytes 384784 | tf_op jit(solution)/shard_map/pallas_call | solution.py:54
  (8 shorter events, 0.2 us)
Async XLA Ops:
  0.6 0.9 copy-start
  2.9 15.3 %all-to-all-start = ((bf16[16,2,2000]{2,1,0:T(2,128)(2,1)}), bf16[16,2,2000]{2,1,0:T(2,128)(2,1)S(1)}, u32[]{:S(2)}, u32[]{:S(2)}) async-start(bf16[16,2,2000]{2,1,0:T(2,128)(2,1)} %get-tuple-element.26.after_ref), calls=%async_computation | async-start | bytes 262144 | tf_op jit(solution)/shard_map/all_to_all | solution.py:21
  22.0 3.6 %collective-permute-start = (bf16[8,32,256]{2,1,0:T(8,128)(2,1)S(1)}, bf16[8,32,256]{2,1,0:T(8,128)(2,1)S(1)}, u32[]{:S(2)}, u32[]{:S(2)}) collective-permute-start(bf16[8,32,256]{2,1,0:T(8,128)(2,1)S(1)} %get-tuple-element.31), channel_id=1, source_target_pairs={{0,1},{1,0},{2,3},{3,2},{4,5},{5,4},{6,7},{7,6},{8,9},{9,8},{10,11... | collective-permute-start | bytes 393224 | tf_op jit(solution)/shard_map/ppermute | solution.py:17
  22.1 25.2 %copy-start.2 = (bf16[4096]{0:T(1024)(128)(2,1)S(1)}, bf16[4096]{0:T(1024)(128)(2,1)}, u32[]{:S(2)}) copy-start(bf16[4096]{0:T(1024)(128)(2,1)} %param.10) | copy-start | bytes 24580
  22.1 25.2 %copy-start.1 = (s32[4]{0:T(128)S(1)}, s32[4]{0:T(128)}, u32[]{:S(2)}) copy-start(s32[4]{0:T(128)} %param.15) | copy-start | bytes 52
  47.3 3.8 %collective-permute-start.1 = (bf16[8,32,256]{2,1,0:T(8,128)(2,1)S(1)}, bf16[8,32,256]{2,1,0:T(8,128)(2,1)S(1)}, u32[]{:S(2)}, u32[]{:S(2)}) collective-permute-start(bf16[8,32,256]{2,1,0:T(8,128)(2,1)S(1)} %all_to_all.31.x_ref.mine_ref), channel_id=1, source_target_pairs={{0,1},{1,0},{2,3},{3,2},{4,5},{5,4},{6,7},{7,6},{8,9},{9,8},{10,11... | collective-permute-start | bytes 393224 | tf_op jit(solution)/shard_map/ppermute | solution.py:17
  56.3 2.8 %collective-permute-start.2 = (bf16[8,32,256]{2,1,0:T(8,128)(2,1)S(1)}, bf16[8,32,256]{2,1,0:T(8,128)(2,1)S(1)}, u32[]{:S(2)}, u32[]{:S(2)}) collective-permute-start(bf16[8,32,256]{2,1,0:T(8,128)(2,1)S(1)} %get-tuple-element.40), channel_id=1, source_target_pairs={{0,1},{1,0},{2,3},{3,2},{4,5},{5,4},{6,7},{7,6},{8,9},{9,8},{10,11... | collective-permute-start | bytes 393224 | tf_op jit(solution)/shard_map/ppermute | solution.py:17
  78.9 1.6 %collective-permute-start.3 = (bf16[8,32,256]{2,1,0:T(8,128)(2,1)S(1)}, bf16[8,32,256]{2,1,0:T(8,128)(2,1)S(1)}, u32[]{:S(2)}, u32[]{:S(2)}) collective-permute-start(bf16[8,32,256]{2,1,0:T(8,128)(2,1)S(1)} %all_to_all.33.d_mine_ref), channel_id=1, source_target_pairs={{0,1},{1,0},{2,3},{3,2},{4,5},{5,4},{6,7},{7,6},{8,9},{9,8},{10,11... | collective-permute-start | bytes 393224 | tf_op jit(solution)/shard_map/ppermute | solution.py:17

commit v19 on v18

--- a/solution.py
+++ b/solution.py
@@ -157,10 +157,14 @@
     )[0]
 
 
-def half_kernel(other, slices_ref, ready_ref, embed_ref, head_ref, out_ref, score_ref, *rest):
-    next_ref, table, acc, sems, next_sems = rest if other else (None, *rest, None)
+def half_kernel(other, slices_ref, embed_ref, head_ref, *rest):
+    if other:
+        ready_ref = None
+        out_ref, score_ref, next_ref, table, acc, sems, next_sems = rest
+    else:
+        ready_ref, out_ref, score_ref, table, acc, sems = rest
     chips, total, own = out_ref.shape
-    part, ready = embed_ref.shape[0], ready_ref.shape[0]
+    part, ready = embed_ref.shape[0], 0 if other else ready_ref.shape[0]
     core = this_core()
     half = (1 - core) if other else core
     columns = span(half * chips * own, chips * own)
@@ -178,7 +182,9 @@
         following = bring(embed_ref, next_ref, next_sems, span(core * chips * own, chips * own))
         for copy in following:
             copy.start()
-    acc[...] = jnp.dot(slices_ref[:, :ready], ready_ref[...], preferred_element_type=F32)
+        acc[...] = jnp.zeros_like(acc)
+    else:
+        acc[...] = jnp.dot(slices_ref[:, :ready], ready_ref[...], preferred_element_type=F32)
     for start in range(ready, part, tile):
         end = min(start + tile, part)
         stream.wait(-(-(end - ready) // fine))
@@ -196,12 +202,10 @@
 
 
 def early_kernel(
-    head_ref, down_ref, embed_ref, gate_ref, up_ref, after_ref,
-    out_ref, head_row, first, both, table, head_copy, sems, first_sems, both_sems, head_sem,
+    head_ref, down_ref, after_ref, out_ref, head_row, table, head_copy, sems, head_sem
 ):
     del after_ref
     width, lanes = down_ref.shape[1], 128
-    core = this_core()
 
     def copy(j):
         rows = span(j * lanes, lanes)
@@ -212,13 +216,6 @@
     bring_head.start()
     for j in range(steps):
         copy(j).start()
-    half = width // 2
-    own = both.shape[0] // 2
-    chips = half // own
-    others = bring(embed_ref, first, first_sems, span((1 - core) * half, half))
-    others += bring_blocks(gate_ref, up_ref, both, core, range(2), own, chips, both_sems)
-    for other in others:
-        other.start()
     bring_head.wait()
     head = head_copy[...].astype(F32).reshape(1, width)
     head_row[...] = head
@@ -233,8 +230,6 @@
         return 0
 
     lax.fori_loop(0, steps, step, 0)
-    for other in others:
-        other.wait()
 
 
 def bring_blocks(gate_ref, up_ref, both, half, blocks, own, chips, sems):
@@ -251,7 +246,7 @@
 
 
 def weight_rows(ready, both, own):
-    skip = ready.shape[0] // own
+    skip = ready.shape[0] // own if ready is not None else 0
 
     def weights(j):
         if j < skip:
@@ -286,12 +281,12 @@
 
 
 def first_kernel(
-    x_ref, gain_ref, gate_ref, up_ref, ready_ref, counts_ref,
+    x_ref, gain_ref, gate_ref, up_ref, counts_ref,
     products_ref, squares_ref, valid_ref, counts_row, both, ahead, sems, ahead_sems,
 ):
     chips, _, own = x_ref.shape
     core = this_core()
-    skip, weights = weight_rows(ready_ref, both, own)
+    skip, weights = weight_rows(None, both, own)
     blocks = range(skip, chips)
     stream = Stream(bring_blocks(gate_ref, up_ref, both, core, blocks, own, chips, sems))
     blocks = range(ahead.shape[0] // own)
@@ -337,8 +332,8 @@
     backward_half(d_both_ref[...], weights, send_ref)
 
 
-def third_kernel(d_both_ref, ready_ref, both_ref, keep_ref):
-    _, weights = weight_rows(ready_ref, both_ref, keep_ref.shape[2])
+def third_kernel(d_both_ref, both_ref, keep_ref):
+    _, weights = weight_rows(None, both_ref, keep_ref.shape[2])
     backward_half(d_both_ref[...], weights, keep_ref)
 
 
@@ -517,36 +512,33 @@
     flops = total * part * width
     if tiled:
         ready = 256
-        down_row, head32, first, both_first = call(
-            early_kernel,
-            [
-                struct((1, hidden), F32), struct((1, width), F32),
-                pltpu.VMEM((ready, width // 2), BF16),
-                pltpu.VMEM((2 * own, 2 * hidden), BF16),
-            ],
-            head, w_down, embed, w_gate, w_up, blocked,
-            streamed=(0, 1, 2, 3, 4), flops=2 * hidden * width, room=2 * hidden * width,
+        down_row, head32 = call(
+            early_kernel, [struct((1, hidden), F32), struct((1, width), F32)],
+            head, w_down, blocked,
+            streamed=(0, 1), flops=2 * hidden * width, room=2 * hidden * width,
             scratch=(
                 pltpu.VMEM((hidden, width), BF16), pltpu.VMEM((width,), BF16),
-                pltpu.SemaphoreType.DMA((hidden // 128,)),
-                pltpu.SemaphoreType.DMA((ready // 128,)), pltpu.SemaphoreType.DMA((2, 2)),
-                pltpu.SemaphoreType.DMA,
+                pltpu.SemaphoreType.DMA((hidden // 128,)), pltpu.SemaphoreType.DMA,
             ),
         )
-        table = (
-            pltpu.VMEM((part - ready, width // 2), BF16), pltpu.VMEM((total, width // 2), F32),
-            pltpu.SemaphoreType.DMA((-(-part // 128),)),
-        )
-        args = dict(streamed=(2,), kept=(1,), flops=flops, room=part * width)
+        ready = 256
+        args = dict(streamed=(1,), flops=flops, room=part * width)
+        acc = pltpu.VMEM((total, width // 2), F32)
+        sems = pltpu.SemaphoreType.DMA((-(-part // 128),))
         send, score_a, first = call(
             functools.partial(half_kernel, True),
             [struct(half, BF16), column, pltpu.VMEM((ready, width // 2), BF16)],
-            slices, first, embed, head32,
-            scratch=(*table, pltpu.SemaphoreType.DMA((ready // 128,))), **args,
+            slices, embed, head32,
+            scratch=(
+                pltpu.VMEM((part, width // 2), BF16), acc, sems,
+                pltpu.SemaphoreType.DMA((ready // 128,)),
+            ),
+            **args,
         )
         keep, score_b = call(
             functools.partial(half_kernel, False), [struct(half, F32), column],
-            slices, first, embed, head32, scratch=table, **args,
+            slices, embed, head32, first, kept=(3,),
+            scratch=(pltpu.VMEM((part - ready, width // 2), BF16), acc, sems), **args,
         )
     else:
         send, keep, score_a = plain_half(slices, embed, head_row, devices)
@@ -554,29 +546,26 @@
     x_mine = chip_gather(chip_sum(summed, devices), devices)
     x_got = swap_cores(x_mine, devices)
     if tiled:
-        weight = (width // 2 - 2 * own, 2 * hidden)
         sems, ahead_sems = pltpu.SemaphoreType.DMA((2, chips)), pltpu.SemaphoreType.DMA((2, 2))
-        args = dict(
-            streamed=(2, 3), kept=(4,), flops=2 * total * hidden * width, room=2 * width * hidden
-        )
+        args = dict(streamed=(2, 3), flops=2 * total * hidden * width, room=2 * width * hidden)
         products, squares, valid, counts_row, both, ahead = call(
             first_kernel,
             [
                 struct((total, 2 * hidden), F32), column, column, struct((1, requests), F32),
-                pltpu.VMEM(weight, BF16), pltpu.VMEM(both_first.shape, BF16),
+                pltpu.VMEM((width // 2, 2 * hidden), BF16), pltpu.VMEM((2 * own, 2 * hidden), BF16),
             ],
-            x_mine, gain_row, w_gate, w_up, both_first, counts.reshape(1, requests),
+            x_mine, gain_row, w_gate, w_up, counts.reshape(1, requests),
             scratch=(sems, ahead_sems), **args,
         )
         send, score_c, inv, d_both = call(
             second_kernel,
             [struct(half, BF16), column, column, struct((total, 2 * hidden), BF16)],
             x_got, gain_row, w_gate, w_up, ahead, products, squares, down_row, valid,
-            scratch=(pltpu.VMEM(weight, BF16), sems), **args,
+            scratch=(pltpu.VMEM((width // 2 - 2 * own, 2 * hidden), BF16), sems), kept=(4,), **args,
         )
         (keep,) = call(
-            third_kernel, [struct(half, F32)], d_both, both_first, both,
-            kept=(1, 2), flops=2 * total * hidden * width,
+            third_kernel, [struct(half, F32)], d_both, both,
+            kept=(1,), flops=2 * total * hidden * width,
         )
     else:
         down_row = jnp.sum(w_down.astype(F32) * head.astype(F32)[None, :], axis=-1)[None]

time: 100 us -> 100 us (level)
  no operation moved by 1% of the time
where the time goes in v19:
time: 100 us; the launch traced here: 99.5 us
  blocking collectives  51.1 us (51%)
  Pallas kernels  36 us (36%)
  starting transfers between devices  8.07 us (8%)
  waiting for transfers between devices  2.27 us (2%)
  local copies, waits for them, and re-layouts  1.11 us (1%)
    all_to_all x4, blocking collectives, exchange_chips(): lax.all_to_all(blocks, 'dp', split_axis=0, concat_axis=0, axis_index_grou...  40.6 us
    pallas_call x10, Pallas kernels, call(): pl.pallas_call(kernel, out_shape=outs, in_specs=specs, out_specs=[VMEM_SP...  36 us
    all_to_all x1, blocking collectives, exchange(): return lax.all_to_all(blocks, 'dp', split_axis=0, concat_axis=0, tiled=True)  10.5 us
    all_to_all x1, starting transfers between devices, exchange(): return lax.all_to_all(blocks, 'dp', split_axis=0, concat_axis=0, tiled=True)  7.39 us
    all_to_all x1, waiting for transfers between devices, exchange(): return lax.all_to_all(blocks, 'dp', split_axis=0, concat_axis=0, tiled=True)  2.26 us
  transfers between devices with their start and end apart: 5, of which 1 were waited for; matrix products, arithmetic and copies ran while one was open for 0% of the time, Pallas kernels for 17%

profile of v19, /device:TPU:0, one launch (start us, length us, event | category | flops | bytes accessed | tf_op | source)
XLA Modules:
  0.0 99.5 jit_solution(12261115187036156790)
XLA Ops:
  0.6 0.0 copy-start
  0.6 0.9 copy-done
  1.5 1.4 %shard_map.95 = (bf16[16,2,2000]{2,1,0:T(2,128)(2,1)}, f32[2,32000]{1,0:T(2,128)S(1)}) custom-call(bf16[2,32000]{1,0:T(2,128)(2,1)S(1)} %copy-done), custom_call_target="tpu_custom_call" | custom-call | bytes 128000 | tf_op jit(solution)/shard_map/pallas_call | solution.py:54
  2.9 7.4 %all-to-all-start = ((bf16[16,2,2000]{2,1,0:T(2,128)(2,1)}), bf16[16,2,2000]{2,1,0:T(2,128)(2,1)S(1)}, u32[]{:S(2)}, u32[]{:S(2)}) async-start(bf16[16,2,2000]{2,1,0:T(2,128)(2,1)} %get-tuple-element.24.after_ref), calls=%async_computation | async-start | bytes 262144 | tf_op jit(solution)/shard_map/all_to_all | solution.py:21
  10.3 5.7 %shard_map.96 = (f32[1,896]{1,0:T(1,128)S(1)}, f32[1,4096]{1,0:T(1,128)S(1)}) custom-call(bf16[4096]{0:T(1024)(128)(2,1)} %head_ref.1, bf16[896,4096]{1,0:T(8,128)(2,1)} %down_ref.1, bf16[16,2,2000]{2,1,0:T(2,128)(2,1)} %get-tuple-element.24.after_ref), custom_call_target="tpu_custom_call" | custom-call | flops 7340032 | bytes 7476224 | tf_op jit(solution)/shard_map/pallas_call | solution.py:54
  16.0 2.3 %all-to-all-done = bf16[16,2,2000]{2,1,0:T(2,128)(2,1)S(1)} async-done(((bf16[16,2,2000]{2,1,0:T(2,128)(2,1)}), bf16[16,2,2000]{2,1,0:T(2,128)(2,1)S(1)}, u32[]{:S(2)}, u32[]{:S(2)}) %all-to-all-start) | async-done | bytes 128032 | tf_op jit(solution)/shard_map/all_to_all | solution.py:21
  18.3 0.1 reshape.21.slices_ref
  18.3 4.0 %shard_map.97 = (bf16[8,32,256]{2,1,0:T(8,128)(2,1)S(1)}, f32[32,1]{1,0:T(8,128)S(1)}, bf16[256,2048]{1,0:T(8,128)(2,1)S(1)}) custom-call(bf16[32,2000]{1,0:T(8,128)(2,1)S(1)} %reshape.21.slices_ref, bf16[2000,4096]{1,0:T(8,128)(2,1)} %embed_ref.5, f32[1,4096]{1,0:T(1,128)S(1)} %get-tuple-element.25.head_ref), custom_call_target="tpu_custom_call" | custom-call | flops 262144000 | bytes 16528384 | tf_op jit(solution)/shard_map/pallas_call | solution.py:54
  22.3 0.1 collective-permute-start
  22.4 0.0 copy-start.2
  22.4 0.0 copy-start.1
  22.4 3.5 %shard_map.98 = (f32[8,32,256]{2,1,0:T(8,128)S(1)}, f32[32,1]{1,0:T(8,128)S(1)}) custom-call(bf16[32,2000]{1,0:T(8,128)(2,1)S(1)} %reshape.21.slices_ref, bf16[2000,4096]{1,0:T(8,128)(2,1)} %embed_ref.5, f32[1,4096]{1,0:T(1,128)S(1)} %get-tuple-element.25.head_ref, bf16[256,2048]{1,0:T(8,128)(2,1)S(1)} %get-tuple-element.26.rest_0_), custom_call_target="tpu_custom_call" | custom-call | flops 262144000 | bytes 17576960 | tf_op jit(solution)/shard_map/pallas_call | solution.py:54
  25.9 0.0 collective-permute-done
  26.0 11.1 %all_to_all.30 = bf16[8,32,256]{2,1,0:T(8,128)(2,1)S(1)} all-to-all(bf16[8,32,256]{2,1,0:T(8,128)(2,1)S(1)} %add_convert_fusion.1), channel_id=1, replica_groups={{0,2,4,6,8,10,12,14},{1,3,5,7,9,11,13,15},{16,18,20,22,24,26,28,30},{17..., dimensions={0} | all-to-all | bytes 262144 | tf_op jit(solution)/shard_map/all_to_all | solution.py:26
  37.1 9.9 %all_to_all.31.x_ref.mine_ref = bf16[8,32,256]{2,1,0:T(8,128)(2,1)S(1)} all-to-all(bf16[8,32,256]{2,1,0:T(8,128)(2,1)S(1)} %broadcast_in_dim.4), channel_id=1, replica_groups={{0,2,4,6,8,10,12,14},{1,3,5,7,9,11,13,15},{16,18,20,22,24,26,28,30},{17..., dimensions={0} | all-to-all | bytes 262144 | tf_op jit(solution)/shard_map/all_to_all | solution.py:26
  47.0 0.0 collective-permute-start.1
  47.0 0.0 copy-done.2
  47.0 4.0 %shard_map.99 = (f32[32,1792]{1,0:T(8,128)S(1)}, f32[32,1]{1,0:T(8,128)S(1)}, f32[32,1]{1,0:T(8,128)S(1)}, f32[1,4]{1,0:T(1,128)S(1)}, bf16[2048,1792]{1,0:T(8,128)(2,1)S(1)}, /*index=5*/bf16[512,1792]{1,0:T(8,128)(2,1)S(1)}) custom-call(bf16[8,32,256]{2,1,0:T(8,128)(2,1)S(1)} %all_to_all.31.x_ref.mine_ref, bf16[1,4096]{1,0:T(2,128)(2,1)S(1)} %reshape.22.gain_ref, ...), custom_call_target="tpu_custom_call" | custom-call | flops 234881024 | bytes 14819344 | tf_op jit(solution)/shard_map/pallas_call | solution.py:54
  51.0 0.0 collective-permute-done.1.x_ref.got_ref
  51.0 5.2 %shard_map.100 = (bf16[8,32,256]{2,1,0:T(8,128)(2,1)S(1)}, f32[32,1]{1,0:T(8,128)S(1)}, f32[32,1]{1,0:T(8,128)S(1)}, bf16[32,1792]{1,0:T(8,128)(2,1)S(1)}) custom-call(bf16[8,32,256]{2,1,0:T(8,128)(2,1)S(1)} %collective-permute-done.1.x_ref.got_ref, bf16[1,4096]{1,0:T(2,128)(2,1)S(1)} %reshape.22.gain_ref, bf16[4096,896]{1,0:T(8,128)(2,1)} %gate_ref.3, ...), custom_call_target="tpu_custom_call" | custom-call | flops 234881024 | bytes 16887552 | tf_op jit(solution)/shard_map/pallas_call | solution.py:54
  56.3 0.6 collective-permute-start.2
  56.9 2.2 %shard_map.101 = f32[8,32,256]{2,1,0:T(8,128)S(1)} custom-call(bf16[32,1792]{1,0:T(8,128)(2,1)S(1)} %get-tuple-element.34.d_both_ref, bf16[2048,1792]{1,0:T(8,128)(2,1)S(1)} %get-tuple-element.35.both_ref), custom_call_target="tpu_custom_call" | custom-call | flops 234881024 | bytes 7454720 | tf_op jit(solution)/shard_map/pallas_call | solution.py:54
  59.1 0.0 collective-permute-done.2
  59.1 9.8 %all_to_all.32 = bf16[8,32,256]{2,1,0:T(8,128)(2,1)S(1)} all-to-all(bf16[8,32,256]{2,1,0:T(8,128)(2,1)S(1)} %add_convert_fusion), channel_id=1, replica_groups={{0,2,4,6,8,10,12,14},{1,3,5,7,9,11,13,15},{16,18,20,22,24,26,28,30},{17..., dimensions={0} | all-to-all | bytes 262144 | tf_op jit(solution)/shard_map/all_to_all | solution.py:26
  69.0 9.8 %all_to_all.33.d_mine_ref = bf16[8,32,256]{2,1,0:T(8,128)(2,1)S(1)} all-to-all(bf16[8,32,256]{2,1,0:T(8,128)(2,1)S(1)} %broadcast_in_dim.5), channel_id=1, replica_groups={{0,2,4,6,8,10,12,14},{1,3,5,7,9,11,13,15},{16,18,20,22,24,26,28,30},{17..., dimensions={0} | all-to-all | bytes 262144 | tf_op jit(solution)/shard_map/all_to_all | solution.py:26
  78.9 0.0 collective-permute-start.3
  78.9 1.6 %shard_map.102.ready_ref = bf16[256,4096]{1,0:T(8,128)(2,1)S(1)} custom-call(bf16[2000,4096]{1,0:T(8,128)(2,1)} %embed_ref.5, bf16[32,256]{1,0:T(8,128)(2,1)S(1)} %reduce_sum.25.after_ref), custom_call_target="tpu_custom_call" | custom-call | bytes 16400384 | tf_op jit(solution)/shard_map/pallas_call | solution.py:54
  80.4 0.0 collective-permute-done.3.d_got_ref
  80.4 7.2 %shard_map.103 = bf16[32,2012]{1,0:T(8,128)(2,1)S(1)} custom-call(bf16[8,32,256]{2,1,0:T(8,128)(2,1)S(1)} %all_to_all.31.x_ref.mine_ref, bf16[8,32,256]{2,1,0:T(8,128)(2,1)S(1)} %collective-permute-done.1.x_ref.got_ref, bf16[8,32,256]{2,1,0:T(8,128)(2,1)S(1)} %all_to_all.33.d_mine_ref, bf16[8,32,256]{2,1,0:T(8,128)(2,1)S(1)} %collective-permute-done.3.d_got_ref, ...), custom_call_target="tpu_custom_call" | custom-call | flops 524288000 | bytes 19030672 | tf_op jit(solution)/shard_map/pallas_call | solution.py:54
  87.7 0.1 reshape.24
  87.8 10.5 %all_to_all.34.back_ref = bf16[16,2,2012]{2,1,0:T(2,128)(2,1)S(1)} all-to-all(bf16[16,2,2012]{2,1,0:T(2,128)(2,1)S(1)} %reshape.24), channel_id=1, replica_groups=mesh['groups'=2,'dp'=16] {'dp'}, dimensions={0} | all-to-all | bytes 257536 | tf_op jit(solution)/shard_map/all_to_all | solution.py:21
  98.3 1.2 %shard_map.104 = (bf16[2,32000]{1,0:T(2,128)(2,1)}, f32[1,4]{1,0:T(1,128)}) custom-call(f32[2,32000]{1,0:T(2,128)S(1)} %get-tuple-element.23.probs_ref, bf16[16,2,2012]{2,1,0:T(2,128)(2,1)S(1)} %all_to_all.34.back_ref, f32[1,4]{1,0:T(1,128)S(1)} %get-tuple-element.41.counts_ref), custom_call_target="tpu_custom_call" | custom-call | bytes 384784 | tf_op jit(solution)/shard_map/pallas_call | solution.py:54
  (8 shorter events, 0.2 us)
Async XLA Ops:
  0.6 0.9 copy-start
  2.9 15.3 %all-to-all-start = ((bf16[16,2,2000]{2,1,0:T(2,128)(2,1)}), bf16[16,2,2000]{2,1,0:T(2,128)(2,1)S(1)}, u32[]{:S(2)}, u32[]{:S(2)}) async-start(bf16[16,2,2000]{2,1,0:T(2,128)(2,1)} %get-tuple-element.24.after_ref), calls=%async_computation | async-start | bytes 262144 | tf_op jit(solution)/shard_map/all_to_all | solution.py:21
  22.3 3.6 %collective-permute-start = (bf16[8,32,256]{2,1,0:T(8,128)(2,1)S(1)}, bf16[8,32,256]{2,1,0:T(8,128)(2,1)S(1)}, u32[]{:S(2)}, u32[]{:S(2)}) collective-permute-start(bf16[8,32,256]{2,1,0:T(8,128)(2,1)S(1)} %get-tuple-element.28), channel_id=1, source_target_pairs={{0,1},{1,0},{2,3},{3,2},{4,5},{5,4},{6,7},{7,6},{8,9},{9,8},{10,11... | collective-permute-start | bytes 393224 | tf_op jit(solution)/shard_map/ppermute | solution.py:17
  22.4 24.6 %copy-start.2 = (bf16[4096]{0:T(1024)(128)(2,1)S(1)}, bf16[4096]{0:T(1024)(128)(2,1)}, u32[]{:S(2)}) copy-start(bf16[4096]{0:T(1024)(128)(2,1)} %param.10) | copy-start | bytes 24580
  22.4 24.6 %copy-start.1 = (s32[4]{0:T(128)S(1)}, s32[4]{0:T(128)}, u32[]{:S(2)}) copy-start(s32[4]{0:T(128)} %param.15) | copy-start | bytes 52
  47.0 4.0 %collective-permute-start.1 = (bf16[8,32,256]{2,1,0:T(8,128)(2,1)S(1)}, bf16[8,32,256]{2,1,0:T(8,128)(2,1)S(1)}, u32[]{:S(2)}, u32[]{:S(2)}) collective-permute-start(bf16[8,32,256]{2,1,0:T(8,128)(2,1)S(1)} %all_to_all.31.x_ref.mine_ref), channel_id=1, source_target_pairs={{0,1},{1,0},{2,3},{3,2},{4,5},{5,4},{6,7},{7,6},{8,9},{9,8},{10,11... | collective-permute-start | bytes 393224 | tf_op jit(solution)/shard_map/ppermute | solution.py:17
  56.3 2.8 %collective-permute-start.2 = (bf16[8,32,256]{2,1,0:T(8,128)(2,1)S(1)}, bf16[8,32,256]{2,1,0:T(8,128)(2,1)S(1)}, u32[]{:S(2)}, u32[]{:S(2)}) collective-permute-start(bf16[8,32,256]{2,1,0:T(8,128)(2,1)S(1)} %get-tuple-element.36), channel_id=1, source_target_pairs={{0,1},{1,0},{2,3},{3,2},{4,5},{5,4},{6,7},{7,6},{8,9},{9,8},{10,11... | collective-permute-start | bytes 393224 | tf_op jit(solution)/shard_map/ppermute | solution.py:17
  78.9 1.6 %collective-permute-start.3 = (bf16[8,32,256]{2,1,0:T(8,128)(2,1)S(1)}, bf16[8,32,256]{2,1,0:T(8,128)(2,1)S(1)}, u32[]{:S(2)}, u32[]{:S(2)}) collective-permute-start(bf16[8,32,256]{2,1,0:T(8,128)(2,1)S(1)} %all_to_all.33.d_mine_ref), channel_id=1, source_target_pairs={{0,1},{1,0},{2,3},{3,2},{4,5},{5,4},{6,7},{7,6},{8,9},{9,8},{10,11... | collective-permute-start | bytes 393224 | tf_op jit(solution)/shard_map/ppermute | solution.py:17

commit v20 on v19

--- a/solution.py
+++ b/solution.py
@@ -206,12 +206,13 @@
 ):
     del after_ref
     width, lanes = down_ref.shape[1], 128
+    steps = sems.shape[0]
+    skip = lax.axis_index("groups") * (down_ref.shape[0] // lanes - steps)
 
     def copy(j):
-        rows = span(j * lanes, lanes)
-        return pltpu.make_async_copy(down_ref.at[rows], table.at[rows], sems.at[j])
-
-    steps = sems.shape[0]
+        source = down_ref.at[span((skip + j) * lanes, lanes)]
+        return pltpu.make_async_copy(source, table.at[span(j * lanes, lanes)], sems.at[j])
+
     bring_head = pltpu.make_async_copy(head_ref, head_copy, head_sem)
     bring_head.start()
     for j in range(steps):
@@ -305,7 +306,7 @@
 
 
 def second_kernel(
-    x_ref, gain_ref, gate_ref, up_ref, ready_ref, products_ref, squares_ref, down_ref, valid_ref,
+    x_ref, gain_ref, gate_ref, up_ref, ready_ref, products_ref, squares_ref, down_a, down_b, valid_ref,
     send_ref, score_ref, inv_ref, d_both_ref, both, sems,
 ):
     chips, total, own = x_ref.shape
@@ -323,7 +324,10 @@
     a, b = products[:, :hidden] * inv, products[:, hidden:] * inv
     sigma = jax.nn.sigmoid(a)
     active = a * sigma
-    down = down_ref[...]
+    first_group = lax.axis_index("groups") == 0
+    down = jnp.where(first_group, down_a[...], down_b[...])
+    rest = jnp.where(first_group, down_b[...], down_a[...])
+    down = jnp.concatenate([down, rest[:, 2 * rest.shape[1] - hidden :]], axis=-1)
     rounded = (active * b).astype(BF16).astype(F32)
     score_ref[...] = jnp.sum(rounded * down, axis=-1, keepdims=True)
     d_hidden = valid_ref[...] * down
@@ -497,6 +501,7 @@
     total = rows * devices
     request_len = total // requests
     tiled = own % 128 == 0 and hidden % 128 == 0 and total % 16 == 0 and part % 16 == 0 and part > 512
+    tiled = tiled and lax.axis_size("groups") == 2
     head_row, gain_row = head.reshape(1, width), norm_gain.reshape(1, width)
     if tiled:
         blocked, probs = call(
@@ -512,15 +517,17 @@
     flops = total * part * width
     if tiled:
         ready = 256
-        down_row, head32 = call(
-            early_kernel, [struct((1, hidden), F32), struct((1, width), F32)],
+        steps = -(-hidden // 256)
+        down_a, head32 = call(
+            early_kernel, [struct((1, steps * 128), F32), struct((1, width), F32)],
             head, w_down, blocked,
             streamed=(0, 1), flops=2 * hidden * width, room=2 * hidden * width,
             scratch=(
-                pltpu.VMEM((hidden, width), BF16), pltpu.VMEM((width,), BF16),
-                pltpu.SemaphoreType.DMA((hidden // 128,)), pltpu.SemaphoreType.DMA,
+                pltpu.VMEM((steps * 128, width), BF16), pltpu.VMEM((width,), BF16),
+                pltpu.SemaphoreType.DMA((steps,)), pltpu.SemaphoreType.DMA,
             ),
         )
+        down_b = lax.ppermute(down_a, "groups", [(0, 1), (1, 0)])
         ready = 256
         args = dict(streamed=(1,), flops=flops, room=part * width)
         acc = pltpu.VMEM((total, width // 2), F32)
@@ -560,7 +567,7 @@
         send, score_c, inv, d_both = call(
             second_kernel,
             [struct(half, BF16), column, column, struct((total, 2 * hidden), BF16)],
-            x_got, gain_row, w_gate, w_up, ahead, products, squares, down_row, valid,
+            x_got, gain_row, w_gate, w_up, ahead, products, squares, down_a, down_b, valid,
             scratch=(pltpu.VMEM((width // 2 - 2 * own, 2 * hidden), BF16), sems), kept=(4,), **args,
         )
         (keep,) = call(

time: 100 us -> 101 us (1.010)
  waiting for transfers between devices: 2.27 us -> 4.48 us
  Pallas kernels: 36 us -> 33.8 us
  starting transfers between devices: 8.07 us -> 9.28 us
    pallas_call x10, Pallas kernels: 36 us -> 33.8 us  [call(): pl.pallas_call(kernel, out_shape=outs, in_specs=specs, out_specs=[VMEM_SP...]
    all_to_all x1, waiting for transfers between devices: 2.26 us -> 4.47 us  [exchange(): return lax.all_to_all(blocks, 'dp', split_axis=0, concat_axis=0, tiled=True)]
    ppermute x0 -> x1, starting transfers between devices: none -> 1.49 us  [body(): down_b = lax.ppermute(down_a, 'groups', [(0, 1), (1, 0)])]
  transfers between devices with their start and end apart: 5 -> 6, of which waited for: 1 -> 1; matrix products, arithmetic and copies ran while one was open for 0% -> 0% of each run, Pallas kernels for 17% -> 15%
where the time goes in v20:
time: 101 us; the launch traced here: 100 us
  blocking collectives  50.6 us (50%)
  Pallas kernels  33.8 us (33%)
  starting transfers between devices  9.28 us (9%)
  waiting for transfers between devices  4.48 us (4%)
  local copies, waits for them, and re-layouts  1.11 us (1%)
    all_to_all x4, blocking collectives, exchange_chips(): lax.all_to_all(blocks, 'dp', split_axis=0, concat_axis=0, axis_index_grou...  40 us
    pallas_call x10, Pallas kernels, call(): pl.pallas_call(kernel, out_shape=outs, in_specs=specs, out_specs=[VMEM_SP...  33.8 us
    all_to_all x1, blocking collectives, exchange(): return lax.all_to_all(blocks, 'dp', split_axis=0, concat_axis=0, tiled=True)  10.5 us
    all_to_all x1, starting transfers between devices, exchange(): return lax.all_to_all(blocks, 'dp', split_axis=0, concat_axis=0, tiled=True)  7.39 us
    all_to_all x1, waiting for transfers between devices, exchange(): return lax.all_to_all(blocks, 'dp', split_axis=0, concat_axis=0, tiled=True)  4.47 us
  transfers between devices with their start and end apart: 6, of which 1 were waited for; matrix products, arithmetic and copies ran while one was open for 0% of the time, Pallas kernels for 15%

profile of v20, /device:TPU:0, one launch (start us, length us, event | category | flops | bytes accessed | tf_op | source)
XLA Modules:
  0.0 100.2 jit_solution(12285582170743467150)
XLA Ops:
  0.6 0.9 copy-done
  1.5 1.4 %shard_map.95 = (bf16[16,2,2000]{2,1,0:T(2,128)(2,1)}, f32[2,32000]{1,0:T(2,128)S(1)}) custom-call(bf16[2,32000]{1,0:T(2,128)(2,1)S(1)} %copy-done), custom_call_target="tpu_custom_call" | custom-call | bytes 128000 | tf_op jit(solution)/shard_map/pallas_call | solution.py:54
  2.9 7.4 %all-to-all-start = ((bf16[16,2,2000]{2,1,0:T(2,128)(2,1)}), bf16[16,2,2000]{2,1,0:T(2,128)(2,1)S(1)}, u32[]{:S(2)}, u32[]{:S(2)}) async-start(bf16[16,2,2000]{2,1,0:T(2,128)(2,1)} %get-tuple-element.24.after_ref), calls=%async_computation | async-start | bytes 262144 | tf_op jit(solution)/shard_map/all_to_all | solution.py:21
  10.3 3.5 %shard_map.96 = (f32[1,512]{1,0:T(1,128)S(1)}, f32[1,4096]{1,0:T(1,128)S(1)}) custom-call(bf16[4096]{0:T(1024)(128)(2,1)} %head_ref.1, bf16[896,4096]{1,0:T(8,128)(2,1)} %down_ref.1, bf16[16,2,2000]{2,1,0:T(2,128)(2,1)} %get-tuple-element.24.after_ref), custom_call_target="tpu_custom_call" | custom-call | flops 7340032 | bytes 7476224 | tf_op jit(solution)/shard_map/pallas_call | solution.py:54
  13.8 4.5 %all-to-all-done = bf16[16,2,2000]{2,1,0:T(2,128)(2,1)S(1)} async-done(((bf16[16,2,2000]{2,1,0:T(2,128)(2,1)}), bf16[16,2,2000]{2,1,0:T(2,128)(2,1)S(1)}, u32[]{:S(2)}, u32[]{:S(2)}) %all-to-all-start) | async-done | bytes 128032 | tf_op jit(solution)/shard_map/all_to_all | solution.py:21
  18.3 0.1 reshape.21.slices_ref
  18.3 4.0 %shard_map.97 = (bf16[8,32,256]{2,1,0:T(8,128)(2,1)S(1)}, f32[32,1]{1,0:T(8,128)S(1)}, bf16[256,2048]{1,0:T(8,128)(2,1)S(1)}) custom-call(bf16[32,2000]{1,0:T(8,128)(2,1)S(1)} %reshape.21.slices_ref, bf16[2000,4096]{1,0:T(8,128)(2,1)} %embed_ref.5, f32[1,4096]{1,0:T(1,128)S(1)} %get-tuple-element.25.head_ref), custom_call_target="tpu_custom_call" | custom-call | flops 262144000 | bytes 16528384 | tf_op jit(solution)/shard_map/pallas_call | solution.py:54
  22.3 0.1 collective-permute-start
  22.4 0.0 copy-start.2
  22.4 0.0 copy-start.1
  22.4 3.5 %shard_map.98 = (f32[8,32,256]{2,1,0:T(8,128)S(1)}, f32[32,1]{1,0:T(8,128)S(1)}) custom-call(bf16[32,2000]{1,0:T(8,128)(2,1)S(1)} %reshape.21.slices_ref, bf16[2000,4096]{1,0:T(8,128)(2,1)} %embed_ref.5, f32[1,4096]{1,0:T(1,128)S(1)} %get-tuple-element.25.head_ref, bf16[256,2048]{1,0:T(8,128)(2,1)S(1)} %get-tuple-element.26.rest_0_), custom_call_target="tpu_custom_call" | custom-call | flops 262144000 | bytes 17576960 | tf_op jit(solution)/shard_map/pallas_call | solution.py:54
  25.9 0.0 collective-permute-done
  26.0 10.3 %all_to_all.30 = bf16[8,32,256]{2,1,0:T(8,128)(2,1)S(1)} all-to-all(bf16[8,32,256]{2,1,0:T(8,128)(2,1)S(1)} %add_convert_fusion.1), channel_id=1, replica_groups={{0,2,4,6,8,10,12,14},{1,3,5,7,9,11,13,15},{16,18,20,22,24,26,28,30},{17..., dimensions={0} | all-to-all | bytes 262144 | tf_op jit(solution)/shard_map/all_to_all | solution.py:26
  36.3 9.8 %all_to_all.31.x_ref.mine_ref = bf16[8,32,256]{2,1,0:T(8,128)(2,1)S(1)} all-to-all(bf16[8,32,256]{2,1,0:T(8,128)(2,1)S(1)} %broadcast_in_dim.4), channel_id=1, replica_groups={{0,2,4,6,8,10,12,14},{1,3,5,7,9,11,13,15},{16,18,20,22,24,26,28,30},{17..., dimensions={0} | all-to-all | bytes 262144 | tf_op jit(solution)/shard_map/all_to_all | solution.py:26
  46.2 0.0 collective-permute-start.1
  46.2 1.5 %collective-permute-start.2 = (f32[1,512]{1,0:T(1,128)S(1)}, f32[1,512]{1,0:T(1,128)S(1)}, u32[]{:S(2)}, u32[]{:S(2)}) collective-permute-start(f32[1,512]{1,0:T(1,128)S(1)} %get-tuple-element.32.down_a), channel_id=1, source_target_pairs={{0,16},{16,0},{1,17},{17,1},{2,18},{18,2},{3,19},{19,3},{4,20},{20... | collective-permute-start | bytes 6152 | tf_op jit(solution)/shard_map/ppermute | solution.py:530
  47.7 4.0 %shard_map.99 = (f32[32,1792]{1,0:T(8,128)S(1)}, f32[32,1]{1,0:T(8,128)S(1)}, f32[32,1]{1,0:T(8,128)S(1)}, f32[1,4]{1,0:T(1,128)S(1)}, bf16[2048,1792]{1,0:T(8,128)(2,1)S(1)}, /*index=5*/bf16[512,1792]{1,0:T(8,128)(2,1)S(1)}) custom-call(bf16[8,32,256]{2,1,0:T(8,128)(2,1)S(1)} %all_to_all.31.x_ref.mine_ref, bf16[1,4096]{1,0:T(2,128)(2,1)S(1)} %reshape.22.gain_ref, ...), custom_call_target="tpu_custom_call" | custom-call | flops 234881024 | bytes 14819344 | tf_op jit(solution)/shard_map/pallas_call | solution.py:54
  51.7 0.0 collective-permute-done.2.down_b
  51.7 0.0 collective-permute-done.1.x_ref.got_ref
  51.7 5.2 %shard_map.100 = (bf16[8,32,256]{2,1,0:T(8,128)(2,1)S(1)}, f32[32,1]{1,0:T(8,128)S(1)}, f32[32,1]{1,0:T(8,128)S(1)}, bf16[32,1792]{1,0:T(8,128)(2,1)S(1)}) custom-call(bf16[8,32,256]{2,1,0:T(8,128)(2,1)S(1)} %collective-permute-done.1.x_ref.got_ref, bf16[1,4096]{1,0:T(2,128)(2,1)S(1)} %reshape.22.gain_ref, bf16[4096,896]{1,0:T(8,128)(2,1)} %gate_ref.3, ...), custom_call_target="tpu_custom_call" | custom-call | flops 234881024 | bytes 16888064 | tf_op jit(solution)/shard_map/pallas_call | solution.py:54
  57.0 0.3 collective-permute-start.3
  57.3 2.2 %shard_map.101 = f32[8,32,256]{2,1,0:T(8,128)S(1)} custom-call(bf16[32,1792]{1,0:T(8,128)(2,1)S(1)} %get-tuple-element.34.d_both_ref, bf16[2048,1792]{1,0:T(8,128)(2,1)S(1)} %get-tuple-element.35.both_ref), custom_call_target="tpu_custom_call" | custom-call | flops 234881024 | bytes 7454720 | tf_op jit(solution)/shard_map/pallas_call | solution.py:54
  59.5 0.0 collective-permute-done.3
  59.5 10.1 %all_to_all.32 = bf16[8,32,256]{2,1,0:T(8,128)(2,1)S(1)} all-to-all(bf16[8,32,256]{2,1,0:T(8,128)(2,1)S(1)} %add_convert_fusion), channel_id=1, replica_groups={{0,2,4,6,8,10,12,14},{1,3,5,7,9,11,13,15},{16,18,20,22,24,26,28,30},{17..., dimensions={0} | all-to-all | bytes 262144 | tf_op jit(solution)/shard_map/all_to_all | solution.py:26
  69.7 9.8 %all_to_all.33.d_mine_ref = bf16[8,32,256]{2,1,0:T(8,128)(2,1)S(1)} all-to-all(bf16[8,32,256]{2,1,0:T(8,128)(2,1)S(1)} %broadcast_in_dim.5), channel_id=1, replica_groups={{0,2,4,6,8,10,12,14},{1,3,5,7,9,11,13,15},{16,18,20,22,24,26,28,30},{17..., dimensions={0} | all-to-all | bytes 262144 | tf_op jit(solution)/shard_map/all_to_all | solution.py:26
  79.5 0.0 collective-permute-start.4
  79.5 1.6 %shard_map.102.ready_ref = bf16[256,4096]{1,0:T(8,128)(2,1)S(1)} custom-call(bf16[2000,4096]{1,0:T(8,128)(2,1)} %embed_ref.5, bf16[32,256]{1,0:T(8,128)(2,1)S(1)} %reduce_sum.25.after_ref), custom_call_target="tpu_custom_call" | custom-call | bytes 16400384 | tf_op jit(solution)/shard_map/pallas_call | solution.py:54
  81.1 0.0 collective-permute-done.4.d_got_ref
  81.1 7.2 %shard_map.103 = bf16[32,2012]{1,0:T(8,128)(2,1)S(1)} custom-call(bf16[8,32,256]{2,1,0:T(8,128)(2,1)S(1)} %all_to_all.31.x_ref.mine_ref, bf16[8,32,256]{2,1,0:T(8,128)(2,1)S(1)} %collective-permute-done.1.x_ref.got_ref, bf16[8,32,256]{2,1,0:T(8,128)(2,1)S(1)} %all_to_all.33.d_mine_ref, bf16[8,32,256]{2,1,0:T(8,128)(2,1)S(1)} %collective-permute-done.4.d_got_ref, ...), custom_call_target="tpu_custom_call" | custom-call | flops 524288000 | bytes 19030672 | tf_op jit(solution)/shard_map/pallas_call | solution.py:54
  88.3 0.1 reshape.24
  88.4 10.5 %all_to_all.34.back_ref = bf16[16,2,2012]{2,1,0:T(2,128)(2,1)S(1)} all-to-all(bf16[16,2,2012]{2,1,0:T(2,128)(2,1)S(1)} %reshape.24), channel_id=1, replica_groups=mesh['groups'=2,'dp'=16] {'dp'}, dimensions={0} | all-to-all | bytes 257536 | tf_op jit(solution)/shard_map/all_to_all | solution.py:21
  99.0 1.2 %shard_map.104 = (bf16[2,32000]{1,0:T(2,128)(2,1)}, f32[1,4]{1,0:T(1,128)}) custom-call(f32[2,32000]{1,0:T(2,128)S(1)} %get-tuple-element.23.probs_ref, bf16[16,2,2012]{2,1,0:T(2,128)(2,1)S(1)} %all_to_all.34.back_ref, f32[1,4]{1,0:T(1,128)S(1)} %get-tuple-element.41.counts_ref), custom_call_target="tpu_custom_call" | custom-call | bytes 384784 | tf_op jit(solution)/shard_map/pallas_call | solution.py:54
  (10 shorter events, 0.2 us)
Async XLA Ops:
  0.6 0.9 copy-start
  2.9 15.3 %all-to-all-start = ((bf16[16,2,2000]{2,1,0:T(2,128)(2,1)}), bf16[16,2,2000]{2,1,0:T(2,128)(2,1)S(1)}, u32[]{:S(2)}, u32[]{:S(2)}) async-start(bf16[16,2,2000]{2,1,0:T(2,128)(2,1)} %get-tuple-element.24.after_ref), calls=%async_computation | async-start | bytes 262144 | tf_op jit(solution)/shard_map/all_to_all | solution.py:21
  22.3 3.6 %collective-permute-start = (bf16[8,32,256]{2,1,0:T(8,128)(2,1)S(1)}, bf16[8,32,256]{2,1,0:T(8,128)(2,1)S(1)}, u32[]{:S(2)}, u32[]{:S(2)}) collective-permute-start(bf16[8,32,256]{2,1,0:T(8,128)(2,1)S(1)} %get-tuple-element.28), channel_id=1, source_target_pairs={{0,1},{1,0},{2,3},{3,2},{4,5},{5,4},{6,7},{7,6},{8,9},{9,8},{10,11... | collective-permute-start | bytes 393224 | tf_op jit(solution)/shard_map/ppermute | solution.py:17
  22.4 25.3 %copy-start.2 = (bf16[4096]{0:T(1024)(128)(2,1)S(1)}, bf16[4096]{0:T(1024)(128)(2,1)}, u32[]{:S(2)}) copy-start(bf16[4096]{0:T(1024)(128)(2,1)} %param.10) | copy-start | bytes 24580
  22.4 25.3 %copy-start.1 = (s32[4]{0:T(128)S(1)}, s32[4]{0:T(128)}, u32[]{:S(2)}) copy-start(s32[4]{0:T(128)} %param.15) | copy-start | bytes 52
  46.2 5.5 %collective-permute-start.1 = (bf16[8,32,256]{2,1,0:T(8,128)(2,1)S(1)}, bf16[8,32,256]{2,1,0:T(8,128)(2,1)S(1)}, u32[]{:S(2)}, u32[]{:S(2)}) collective-permute-start(bf16[8,32,256]{2,1,0:T(8,128)(2,1)S(1)} %all_to_all.31.x_ref.mine_ref), channel_id=1, source_target_pairs={{0,1},{1,0},{2,3},{3,2},{4,5},{5,4},{6,7},{7,6},{8,9},{9,8},{10,11... | collective-permute-start | bytes 393224 | tf_op jit(solution)/shard_map/ppermute | solution.py:17
  46.2 5.5 %collective-permute-start.2 = (f32[1,512]{1,0:T(1,128)S(1)}, f32[1,512]{1,0:T(1,128)S(1)}, u32[]{:S(2)}, u32[]{:S(2)}) collective-permute-start(f32[1,512]{1,0:T(1,128)S(1)} %get-tuple-element.32.down_a), channel_id=1, source_target_pairs={{0,16},{16,0},{1,17},{17,1},{2,18},{18,2},{3,19},{19,3},{4,20},{20... | collective-permute-start | bytes 6152 | tf_op jit(solution)/shard_map/ppermute | solution.py:530
  57.0 2.5 %collective-permute-start.3 = (bf16[8,32,256]{2,1,0:T(8,128)(2,1)S(1)}, bf16[8,32,256]{2,1,0:T(8,128)(2,1)S(1)}, u32[]{:S(2)}, u32[]{:S(2)}) collective-permute-start(bf16[8,32,256]{2,1,0:T(8,128)(2,1)S(1)} %get-tuple-element.36), channel_id=1, source_target_pairs={{0,1},{1,0},{2,3},{3,2},{4,5},{5,4},{6,7},{7,6},{8,9},{9,8},{10,11... | collective-permute-start | bytes 393224 | tf_op jit(solution)/shard_map/ppermute | solution.py:17
  79.5 1.6 %collective-permute-start.4 = (bf16[8,32,256]{2,1,0:T(8,128)(2,1)S(1)}, bf16[8,32,256]{2,1,0:T(8,128)(2,1)S(1)}, u32[]{:S(2)}, u32[]{:S(2)}) collective-permute-start(bf16[8,32,256]{2,1,0:T(8,128)(2,1)S(1)} %all_to_all.33.d_mine_ref), channel_id=1, source_target_pairs={{0,1},{1,0},{2,3},{3,2},{4,5},{5,4},{6,7},{7,6},{8,9},{9,8},{10,11... | collective-permute-start | bytes 393224 | tf_op jit(solution)/shard_map/ppermute | solution.py:17

commit v21 on v20

--- a/solution.py
+++ b/solution.py
@@ -159,12 +159,11 @@
 
 def half_kernel(other, slices_ref, embed_ref, head_ref, *rest):
     if other:
-        ready_ref = None
-        out_ref, score_ref, next_ref, table, acc, sems, next_sems = rest
+        ready_ref, out_ref, score_ref, next_ref, table, acc, sems, next_sems = rest
     else:
         ready_ref, out_ref, score_ref, table, acc, sems = rest
     chips, total, own = out_ref.shape
-    part, ready = embed_ref.shape[0], 0 if other else ready_ref.shape[0]
+    part, ready = embed_ref.shape[0], ready_ref.shape[0]
     core = this_core()
     half = (1 - core) if other else core
     columns = span(half * chips * own, chips * own)
@@ -182,9 +181,7 @@
         following = bring(embed_ref, next_ref, next_sems, span(core * chips * own, chips * own))
         for copy in following:
             copy.start()
-        acc[...] = jnp.zeros_like(acc)
-    else:
-        acc[...] = jnp.dot(slices_ref[:, :ready], ready_ref[...], preferred_element_type=F32)
+    acc[...] = jnp.dot(slices_ref[:, :ready], ready_ref[...], preferred_element_type=F32)
     for start in range(ready, part, tile):
         end = min(start + tile, part)
         stream.wait(-(-(end - ready) // fine))
@@ -202,7 +199,8 @@
 
 
 def early_kernel(
-    head_ref, down_ref, after_ref, out_ref, head_row, table, head_copy, sems, head_sem
+    head_ref, down_ref, embed_ref, after_ref,
+    out_ref, head_row, first, table, head_copy, sems, head_sem, first_sems,
 ):
     del after_ref
     width, lanes = down_ref.shape[1], 128
@@ -217,6 +215,10 @@
     bring_head.start()
     for j in range(steps):
         copy(j).start()
+    half = first.shape[1]
+    others = bring(embed_ref, first, first_sems, span((1 - this_core()) * half, half))
+    for other in others:
+        other.start()
     bring_head.wait()
     head = head_copy[...].astype(F32).reshape(1, width)
     head_row[...] = head
@@ -231,6 +233,8 @@
         return 0
 
     lax.fori_loop(0, steps, step, 0)
+    for other in others:
+        other.wait()
 
 
 def bring_blocks(gate_ref, up_ref, both, half, blocks, own, chips, sems):
@@ -517,35 +521,32 @@
     flops = total * part * width
     if tiled:
         ready = 256
-        steps = -(-hidden // 256)
-        down_a, head32 = call(
-            early_kernel, [struct((1, steps * 128), F32), struct((1, width), F32)],
-            head, w_down, blocked,
-            streamed=(0, 1), flops=2 * hidden * width, room=2 * hidden * width,
+        steps, ready = -(-hidden // 256), 256
+        ahead = pltpu.VMEM((ready, width // 2), BF16)
+        ahead_sems = pltpu.SemaphoreType.DMA((ready // 128,))
+        down_a, head32, first = call(
+            early_kernel, [struct((1, steps * 128), F32), struct((1, width), F32), ahead],
+            head, w_down, embed, blocked,
+            streamed=(0, 1, 2), flops=2 * hidden * width, room=2 * hidden * width,
             scratch=(
                 pltpu.VMEM((steps * 128, width), BF16), pltpu.VMEM((width,), BF16),
-                pltpu.SemaphoreType.DMA((steps,)), pltpu.SemaphoreType.DMA,
+                pltpu.SemaphoreType.DMA((steps,)), pltpu.SemaphoreType.DMA, ahead_sems,
             ),
         )
         down_b = lax.ppermute(down_a, "groups", [(0, 1), (1, 0)])
-        ready = 256
-        args = dict(streamed=(1,), flops=flops, room=part * width)
-        acc = pltpu.VMEM((total, width // 2), F32)
-        sems = pltpu.SemaphoreType.DMA((-(-part // 128),))
+        args = dict(streamed=(1,), kept=(3,), flops=flops, room=part * width)
+        scratch = (
+            pltpu.VMEM((part - ready, width // 2), BF16), pltpu.VMEM((total, width // 2), F32),
+            pltpu.SemaphoreType.DMA((-(-part // 128),)),
+        )
         send, score_a, first = call(
-            functools.partial(half_kernel, True),
-            [struct(half, BF16), column, pltpu.VMEM((ready, width // 2), BF16)],
-            slices, embed, head32,
-            scratch=(
-                pltpu.VMEM((part, width // 2), BF16), acc, sems,
-                pltpu.SemaphoreType.DMA((ready // 128,)),
-            ),
-            **args,
-        )
+            functools.partial(half_kernel, True), [struct(half, BF16), column, ahead],
+            slices, embed, head32, first, scratch=(*scratch, ahead_sems), **args,
+        )
+        send, down_b = lax.optimization_barrier((send, down_b))
         keep, score_b = call(
             functools.partial(half_kernel, False), [struct(half, F32), column],
-            slices, embed, head32, first, kept=(3,),
-            scratch=(pltpu.VMEM((part - ready, width // 2), BF16), acc, sems), **args,
+            slices, embed, head32, first, scratch=scratch, **args,
         )
     else:
         send, keep, score_a = plain_half(slices, embed, head_row, devices)

time: 101 us -> 99.5 us (0.985)
  waiting for transfers between devices: 4.48 us -> 2.5 us
    all_to_all x1, waiting for transfers between devices: 4.47 us -> 2.48 us  [exchange(): return lax.all_to_all(blocks, 'dp', split_axis=0, concat_axis=0, tiled=True)]
  transfers between devices with their start and end apart: 6 -> 6, of which waited for: 1 -> 1; matrix products, arithmetic and copies ran while one was open for 0% -> 0% of each run, Pallas kernels for 15% -> 19%
where the time goes in v21:
time: 99.5 us; the launch traced here: 99 us
  blocking collectives  50.9 us (51%)
  Pallas kernels  33.9 us (34%)
  starting transfers between devices  9.66 us (10%)
  waiting for transfers between devices  2.5 us (3%)
  local copies, waits for them, and re-layouts  1.11 us (1%)
    all_to_all x4, blocking collectives, exchange_chips(): lax.all_to_all(blocks, 'dp', split_axis=0, concat_axis=0, axis_index_grou...  40.4 us
    pallas_call x10, Pallas kernels, call(): pl.pallas_call(kernel, out_shape=outs, in_specs=specs, out_specs=[VMEM_SP...  33.9 us
    all_to_all x1, blocking collectives, exchange(): return lax.all_to_all(blocks, 'dp', split_axis=0, concat_axis=0, tiled=True)  10.5 us
    all_to_all x1, starting transfers between devices, exchange(): return lax.all_to_all(blocks, 'dp', split_axis=0, concat_axis=0, tiled=True)  7.39 us
    all_to_all x1, waiting for transfers between devices, exchange(): return lax.all_to_all(blocks, 'dp', split_axis=0, concat_axis=0, tiled=True)  2.48 us
  transfers between devices with their start and end apart: 6, of which 1 were waited for; matrix products, arithmetic and copies ran while one was open for 0% of the time, Pallas kernels for 19%

profile of v21, /device:TPU:0, one launch (start us, length us, event | category | flops | bytes accessed | tf_op | source)
XLA Modules:
  0.0 99.0 jit_solution(6913064020682093335)
XLA Ops:
  0.6 0.9 copy-done
  1.5 1.4 %shard_map.95 = (bf16[16,2,2000]{2,1,0:T(2,128)(2,1)}, f32[2,32000]{1,0:T(2,128)S(1)}) custom-call(bf16[2,32000]{1,0:T(2,128)(2,1)S(1)} %copy-done), custom_call_target="tpu_custom_call" | custom-call | bytes 128000 | tf_op jit(solution)/shard_map/pallas_call | solution.py:54
  2.9 7.4 %all-to-all-start = ((bf16[16,2,2000]{2,1,0:T(2,128)(2,1)}), bf16[16,2,2000]{2,1,0:T(2,128)(2,1)S(1)}, u32[]{:S(2)}, u32[]{:S(2)}) async-start(bf16[16,2,2000]{2,1,0:T(2,128)(2,1)} %get-tuple-element.27.after_ref), calls=%async_computation | async-start | bytes 262144 | tf_op jit(solution)/shard_map/all_to_all | solution.py:21
  10.3 3.8 %shard_map.96 = (f32[1,512]{1,0:T(1,128)S(1)}, f32[1,4096]{1,0:T(1,128)S(1)}, bf16[256,2048]{1,0:T(8,128)(2,1)S(1)}) custom-call(bf16[4096]{0:T(1024)(128)(2,1)} %head_ref.1, bf16[896,4096]{1,0:T(8,128)(2,1)} %down_ref.1, bf16[2000,4096]{1,0:T(8,128)(2,1)} %embed_ref.7, bf16[16,2,2000]{2,1,0:T(2,128)(2,1)} %get-tuple-element.27.after_ref), custom_call_target="tpu_custom_call" | custom-call | flops 7340032 | bytes 23860224 | tf_op jit(solution)/shard_map/pallas_call | solution.py:54
  14.2 1.6 %collective-permute-start = (f32[1,512]{1,0:T(1,128)S(1)}, f32[1,512]{1,0:T(1,128)S(1)}, u32[]{:S(2)}, u32[]{:S(2)}) collective-permute-start(f32[1,512]{1,0:T(1,128)S(1)} %get-tuple-element.33.down_a), channel_id=1, source_target_pairs={{0,16},{16,0},{1,17},{17,1},{2,18},{18,2},{3,19},{19,3},{4,20},{20... | collective-permute-start | bytes 6152 | tf_op jit(solution)/shard_map/ppermute | solution.py:536
  15.8 2.5 %all-to-all-done = bf16[16,2,2000]{2,1,0:T(2,128)(2,1)S(1)} async-done(((bf16[16,2,2000]{2,1,0:T(2,128)(2,1)}), bf16[16,2,2000]{2,1,0:T(2,128)(2,1)S(1)}, u32[]{:S(2)}, u32[]{:S(2)}) %all-to-all-start) | async-done | bytes 128032 | tf_op jit(solution)/shard_map/all_to_all | solution.py:21
  18.3 0.1 reshape.21.slices_ref
  18.3 3.7 %shard_map.97 = (bf16[8,32,256]{2,1,0:T(8,128)(2,1)S(1)}, f32[32,1]{1,0:T(8,128)S(1)}, bf16[256,2048]{1,0:T(8,128)(2,1)S(1)}) custom-call(bf16[32,2000]{1,0:T(8,128)(2,1)S(1)} %reshape.21.slices_ref, bf16[2000,4096]{1,0:T(8,128)(2,1)} %embed_ref.7, f32[1,4096]{1,0:T(1,128)S(1)} %get-tuple-element.28.head_ref, bf16[256,2048]{1,0:T(8,128)(2,1)S(1)} %get-tuple-element.29.rest_0_), custom_call_target="tpu_custom_call" | custom-call | flops 262144000 | bytes 17576960 | tf_op jit(solution)/shard_map/pallas_call | solution.py:54
  22.0 0.0 collective-permute-done.down_b
  22.0 0.1 collective-permute-start.1
  22.1 0.0 copy-start.2
  22.1 0.0 copy-start.1
  22.1 3.5 %shard_map.98 = (f32[8,32,256]{2,1,0:T(8,128)S(1)}, f32[32,1]{1,0:T(8,128)S(1)}) custom-call(bf16[32,2000]{1,0:T(8,128)(2,1)S(1)} %reshape.21.slices_ref, bf16[2000,4096]{1,0:T(8,128)(2,1)} %embed_ref.7, f32[1,4096]{1,0:T(1,128)S(1)} %get-tuple-element.28.head_ref, bf16[256,2048]{1,0:T(8,128)(2,1)S(1)} %get-tuple-element.30.rest_0_), custom_call_target="tpu_custom_call" | custom-call | flops 262144000 | bytes 17576960 | tf_op jit(solution)/shard_map/pallas_call | solution.py:54
  25.7 0.0 collective-permute-done.1
  25.7 10.8 %all_to_all.30 = bf16[8,32,256]{2,1,0:T(8,128)(2,1)S(1)} all-to-all(bf16[8,32,256]{2,1,0:T(8,128)(2,1)S(1)} %add_convert_fusion.1), channel_id=1, replica_groups={{0,2,4,6,8,10,12,14},{1,3,5,7,9,11,13,15},{16,18,20,22,24,26,28,30},{17..., dimensions={0} | all-to-all | bytes 262144 | tf_op jit(solution)/shard_map/all_to_all | solution.py:26
  36.6 9.9 %all_to_all.31.x_ref.mine_ref = bf16[8,32,256]{2,1,0:T(8,128)(2,1)S(1)} all-to-all(bf16[8,32,256]{2,1,0:T(8,128)(2,1)S(1)} %broadcast_in_dim.4), channel_id=1, replica_groups={{0,2,4,6,8,10,12,14},{1,3,5,7,9,11,13,15},{16,18,20,22,24,26,28,30},{17..., dimensions={0} | all-to-all | bytes 262144 | tf_op jit(solution)/shard_map/all_to_all | solution.py:26
  46.5 0.0 collective-permute-start.2
  46.5 4.0 %shard_map.99 = (f32[32,1792]{1,0:T(8,128)S(1)}, f32[32,1]{1,0:T(8,128)S(1)}, f32[32,1]{1,0:T(8,128)S(1)}, f32[1,4]{1,0:T(1,128)S(1)}, bf16[2048,1792]{1,0:T(8,128)(2,1)S(1)}, /*index=5*/bf16[512,1792]{1,0:T(8,128)(2,1)S(1)}) custom-call(bf16[8,32,256]{2,1,0:T(8,128)(2,1)S(1)} %all_to_all.31.x_ref.mine_ref, bf16[1,4096]{1,0:T(2,128)(2,1)S(1)} %reshape.22.gain_ref, ...), custom_call_target="tpu_custom_call" | custom-call | flops 234881024 | bytes 14819344 | tf_op jit(solution)/shard_map/pallas_call | solution.py:54
  50.5 0.0 collective-permute-done.2.x_ref.got_ref
  50.5 5.2 %shard_map.100 = (bf16[8,32,256]{2,1,0:T(8,128)(2,1)S(1)}, f32[32,1]{1,0:T(8,128)S(1)}, f32[32,1]{1,0:T(8,128)S(1)}, bf16[32,1792]{1,0:T(8,128)(2,1)S(1)}) custom-call(bf16[8,32,256]{2,1,0:T(8,128)(2,1)S(1)} %collective-permute-done.2.x_ref.got_ref, bf16[1,4096]{1,0:T(2,128)(2,1)S(1)} %reshape.22.gain_ref, bf16[4096,896]{1,0:T(8,128)(2,1)} %gate_ref.3, ...), custom_call_target="tpu_custom_call" | custom-call | flops 234881024 | bytes 16888064 | tf_op jit(solution)/shard_map/pallas_call | solution.py:54
  55.7 0.6 collective-permute-start.3
  56.4 2.2 %shard_map.101 = f32[8,32,256]{2,1,0:T(8,128)S(1)} custom-call(bf16[32,1792]{1,0:T(8,128)(2,1)S(1)} %get-tuple-element.40.d_both_ref, bf16[2048,1792]{1,0:T(8,128)(2,1)S(1)} %get-tuple-element.41.both_ref), custom_call_target="tpu_custom_call" | custom-call | flops 234881024 | bytes 7454720 | tf_op jit(solution)/shard_map/pallas_call | solution.py:54
  58.6 0.0 collective-permute-done.3
  58.6 9.8 %all_to_all.32 = bf16[8,32,256]{2,1,0:T(8,128)(2,1)S(1)} all-to-all(bf16[8,32,256]{2,1,0:T(8,128)(2,1)S(1)} %add_convert_fusion), channel_id=1, replica_groups={{0,2,4,6,8,10,12,14},{1,3,5,7,9,11,13,15},{16,18,20,22,24,26,28,30},{17..., dimensions={0} | all-to-all | bytes 262144 | tf_op jit(solution)/shard_map/all_to_all | solution.py:26
  68.5 9.8 %all_to_all.33.d_mine_ref = bf16[8,32,256]{2,1,0:T(8,128)(2,1)S(1)} all-to-all(bf16[8,32,256]{2,1,0:T(8,128)(2,1)S(1)} %broadcast_in_dim.5), channel_id=1, replica_groups={{0,2,4,6,8,10,12,14},{1,3,5,7,9,11,13,15},{16,18,20,22,24,26,28,30},{17..., dimensions={0} | all-to-all | bytes 262144 | tf_op jit(solution)/shard_map/all_to_all | solution.py:26
  78.3 0.0 collective-permute-start.4
  78.3 1.6 %shard_map.102.ready_ref = bf16[256,4096]{1,0:T(8,128)(2,1)S(1)} custom-call(bf16[2000,4096]{1,0:T(8,128)(2,1)} %embed_ref.7, bf16[32,256]{1,0:T(8,128)(2,1)S(1)} %reduce_sum.25.after_ref), custom_call_target="tpu_custom_call" | custom-call | bytes 16400384 | tf_op jit(solution)/shard_map/pallas_call | solution.py:54
  79.9 0.0 collective-permute-done.4.d_got_ref
  79.9 7.2 %shard_map.103 = bf16[32,2012]{1,0:T(8,128)(2,1)S(1)} custom-call(bf16[8,32,256]{2,1,0:T(8,128)(2,1)S(1)} %all_to_all.31.x_ref.mine_ref, bf16[8,32,256]{2,1,0:T(8,128)(2,1)S(1)} %collective-permute-done.2.x_ref.got_ref, bf16[8,32,256]{2,1,0:T(8,128)(2,1)S(1)} %all_to_all.33.d_mine_ref, bf16[8,32,256]{2,1,0:T(8,128)(2,1)S(1)} %collective-permute-done.4.d_got_ref, ...), custom_call_target="tpu_custom_call" | custom-call | flops 524288000 | bytes 19030672 | tf_op jit(solution)/shard_map/pallas_call | solution.py:54
  87.2 0.1 reshape.24
  87.3 10.5 %all_to_all.34.back_ref = bf16[16,2,2012]{2,1,0:T(2,128)(2,1)S(1)} all-to-all(bf16[16,2,2012]{2,1,0:T(2,128)(2,1)S(1)} %reshape.24), channel_id=1, replica_groups=mesh['groups'=2,'dp'=16] {'dp'}, dimensions={0} | all-to-all | bytes 257536 | tf_op jit(solution)/shard_map/all_to_all | solution.py:21
  97.8 1.2 %shard_map.104 = (bf16[2,32000]{1,0:T(2,128)(2,1)}, f32[1,4]{1,0:T(1,128)}) custom-call(f32[2,32000]{1,0:T(2,128)S(1)} %get-tuple-element.26.probs_ref, bf16[16,2,2012]{2,1,0:T(2,128)(2,1)S(1)} %all_to_all.34.back_ref, f32[1,4]{1,0:T(1,128)S(1)} %get-tuple-element.47.counts_ref), custom_call_target="tpu_custom_call" | custom-call | bytes 384784 | tf_op jit(solution)/shard_map/pallas_call | solution.py:54
  (10 shorter events, 0.2 us)
Async XLA Ops:
  0.6 0.9 copy-start
  2.9 15.3 %all-to-all-start = ((bf16[16,2,2000]{2,1,0:T(2,128)(2,1)}), bf16[16,2,2000]{2,1,0:T(2,128)(2,1)S(1)}, u32[]{:S(2)}, u32[]{:S(2)}) async-start(bf16[16,2,2000]{2,1,0:T(2,128)(2,1)} %get-tuple-element.27.after_ref), calls=%async_computation | async-start | bytes 262144 | tf_op jit(solution)/shard_map/all_to_all | solution.py:21
  14.2 7.8 %collective-permute-start = (f32[1,512]{1,0:T(1,128)S(1)}, f32[1,512]{1,0:T(1,128)S(1)}, u32[]{:S(2)}, u32[]{:S(2)}) collective-permute-start(f32[1,512]{1,0:T(1,128)S(1)} %get-tuple-element.33.down_a), channel_id=1, source_target_pairs={{0,16},{16,0},{1,17},{17,1},{2,18},{18,2},{3,19},{19,3},{4,20},{20... | collective-permute-start | bytes 6152 | tf_op jit(solution)/shard_map/ppermute | solution.py:536
  22.0 3.6 %collective-permute-start.1 = (bf16[8,32,256]{2,1,0:T(8,128)(2,1)S(1)}, bf16[8,32,256]{2,1,0:T(8,128)(2,1)S(1)}, u32[]{:S(2)}, u32[]{:S(2)}) collective-permute-start(bf16[8,32,256]{2,1,0:T(8,128)(2,1)S(1)} %get-tuple-element.34), channel_id=1, source_target_pairs={{0,1},{1,0},{2,3},{3,2},{4,5},{5,4},{6,7},{7,6},{8,9},{9,8},{10,11... | collective-permute-start | bytes 393224 | tf_op jit(solution)/shard_map/ppermute | solution.py:17
  22.1 24.4 %copy-start.2 = (bf16[4096]{0:T(1024)(128)(2,1)S(1)}, bf16[4096]{0:T(1024)(128)(2,1)}, u32[]{:S(2)}) copy-start(bf16[4096]{0:T(1024)(128)(2,1)} %param.10) | copy-start | bytes 24580
  22.1 24.4 %copy-start.1 = (s32[4]{0:T(128)S(1)}, s32[4]{0:T(128)}, u32[]{:S(2)}) copy-start(s32[4]{0:T(128)} %param.15) | copy-start | bytes 52
  46.5 4.0 %collective-permute-start.2 = (bf16[8,32,256]{2,1,0:T(8,128)(2,1)S(1)}, bf16[8,32,256]{2,1,0:T(8,128)(2,1)S(1)}, u32[]{:S(2)}, u32[]{:S(2)}) collective-permute-start(bf16[8,32,256]{2,1,0:T(8,128)(2,1)S(1)} %all_to_all.31.x_ref.mine_ref), channel_id=1, source_target_pairs={{0,1},{1,0},{2,3},{3,2},{4,5},{5,4},{6,7},{7,6},{8,9},{9,8},{10,11... | collective-permute-start | bytes 393224 | tf_op jit(solution)/shard_map/ppermute | solution.py:17
  55.7 2.8 %collective-permute-start.3 = (bf16[8,32,256]{2,1,0:T(8,128)(2,1)S(1)}, bf16[8,32,256]{2,1,0:T(8,128)(2,1)S(1)}, u32[]{:S(2)}, u32[]{:S(2)}) collective-permute-start(bf16[8,32,256]{2,1,0:T(8,128)(2,1)S(1)} %get-tuple-element.42), channel_id=1, source_target_pairs={{0,1},{1,0},{2,3},{3,2},{4,5},{5,4},{6,7},{7,6},{8,9},{9,8},{10,11... | collective-permute-start | bytes 393224 | tf_op jit(solution)/shard_map/ppermute | solution.py:17
  78.3 1.6 %collective-permute-start.4 = (bf16[8,32,256]{2,1,0:T(8,128)(2,1)S(1)}, bf16[8,32,256]{2,1,0:T(8,128)(2,1)S(1)}, u32[]{:S(2)}, u32[]{:S(2)}) collective-permute-start(bf16[8,32,256]{2,1,0:T(8,128)(2,1)S(1)} %all_to_all.33.d_mine_ref), channel_id=1, source_target_pairs={{0,1},{1,0},{2,3},{3,2},{4,5},{5,4},{6,7},{7,6},{8,9},{9,8},{10,11... | collective-permute-start | bytes 393224 | tf_op jit(solution)/shard_map/ppermute | solution.py:17

commit v22 on v18

--- a/solution.py
+++ b/solution.py
@@ -164,7 +164,7 @@
     core = this_core()
     half = (1 - core) if other else core
     columns = span(half * chips * own, chips * own)
-    tile, fine = 256, 128
+    tile, fine = 512, 128
     stream = Stream([
         pltpu.make_async_copy(
             embed_ref.at[pl.ds(i, min(fine, part - i)), columns],
@@ -253,10 +253,10 @@
 def weight_rows(ready, both, own):
     skip = ready.shape[0] // own
 
-    def weights(j):
+    def weights(j, count=1):
         if j < skip:
-            return ready[j * own : (j + 1) * own]
-        return both[(j - skip) * own : (j - skip + 1) * own]
+            return ready[j * own : (j + count) * own]
+        return both[(j - skip) * own : (j - skip + count) * own]
 
     return skip, weights
 
@@ -272,9 +272,10 @@
         gain = gain_ref[:, span((half * chips + j) * own, own)].astype(F32)
         scaled.append((x * gain).astype(BF16))
     squares = squares + jnp.sum(wide, axis=-1, keepdims=True)
-    for j in range(chips):
-        wait(j)
-        products = products + jnp.dot(scaled[j], weights(j), preferred_element_type=F32)
+    for j in range(0, chips, 2):
+        wait(j + 1)
+        pair = jnp.concatenate(scaled[j : j + 2], axis=-1)
+        products = products + jnp.dot(pair, weights(j, 2), preferred_element_type=F32)
     return products, squares
 
 
@@ -501,7 +502,7 @@
     requests = counts.shape[0]
     total = rows * devices
     request_len = total // requests
-    tiled = own % 128 == 0 and hidden % 128 == 0 and total % 16 == 0 and part % 16 == 0 and part > 512
+    tiled = chips % 2 == 0 and own % 128 == 0 and hidden % 128 == 0 and total % 16 == 0 and part % 16 == 0 and part > 512
     head_row, gain_row = head.reshape(1, width), norm_gain.reshape(1, width)
     if tiled:
         blocked, probs = call(

time: 100 us -> 100 us (level)
  no operation moved by 1% of the time
where the time goes in v22:
time: 100 us; the launch traced here: 99.9 us
  blocking collectives  51.7 us (52%)
  Pallas kernels  36.4 us (36%)
  starting transfers between devices  8.03 us (8%)
  waiting for transfers between devices  1.66 us (2%)
  local copies, waits for them, and re-layouts  1.11 us (1%)
    all_to_all x4, blocking collectives, exchange_chips(): lax.all_to_all(blocks, 'dp', split_axis=0, concat_axis=0, axis_index_grou...  41.2 us
    pallas_call x10, Pallas kernels, call(): pl.pallas_call(kernel, out_shape=outs, in_specs=specs, out_specs=[VMEM_SP...  36.4 us
    all_to_all x1, blocking collectives, exchange(): return lax.all_to_all(blocks, 'dp', split_axis=0, concat_axis=0, tiled=True)  10.5 us
    all_to_all x1, starting transfers between devices, exchange(): return lax.all_to_all(blocks, 'dp', split_axis=0, concat_axis=0, tiled=True)  7.39 us
  transfers between devices with their start and end apart: 5, of which 1 were waited for; matrix products, arithmetic and copies ran while one was open for 0% of the time, Pallas kernels for 17%

profile of v22, /device:TPU:0, one launch (start us, length us, event | category | flops | bytes accessed | tf_op | source)
XLA Modules:
  0.0 99.9 jit_solution(13514938752559801048)
XLA Ops:
  0.6 0.0 copy-start
  0.6 0.9 copy-done
  1.5 1.4 %shard_map.95 = (bf16[16,2,2000]{2,1,0:T(2,128)(2,1)}, f32[2,32000]{1,0:T(2,128)S(1)}) custom-call(bf16[2,32000]{1,0:T(2,128)(2,1)S(1)} %copy-done), custom_call_target="tpu_custom_call" | custom-call | bytes 128000 | tf_op jit(solution)/shard_map/pallas_call | solution.py:54
  2.9 7.4 %all-to-all-start = ((bf16[16,2,2000]{2,1,0:T(2,128)(2,1)}), bf16[16,2,2000]{2,1,0:T(2,128)(2,1)S(1)}, u32[]{:S(2)}, u32[]{:S(2)}) async-start(bf16[16,2,2000]{2,1,0:T(2,128)(2,1)} %get-tuple-element.26.after_ref), calls=%async_computation | async-start | bytes 262144 | tf_op jit(solution)/shard_map/all_to_all | solution.py:21
  10.3 6.3 %shard_map.96 = (f32[1,896]{1,0:T(1,128)S(1)}, f32[1,4096]{1,0:T(1,128)S(1)}, bf16[256,2048]{1,0:T(8,128)(2,1)S(1)}, bf16[512,1792]{1,0:T(8,128)(2,1)S(1)}) custom-call(bf16[4096]{0:T(1024)(128)(2,1)} %head_ref.1, bf16[896,4096]{1,0:T(8,128)(2,1)} %down_ref.1, bf16[2000,4096]{1,0:T(8,128)(2,1)} %embed_ref.7, bf16[4096,896]{1,0:T(8,128)(2,1)} %gate_ref.5, ...), custom_call_target="tpu_custom_call" | custom-call | flops 7340032 | bytes 38540288 | tf_op jit(solution)/shard_map/pallas_call | solution.py:54
  16.6 1.6 %all-to-all-done = bf16[16,2,2000]{2,1,0:T(2,128)(2,1)S(1)} async-done(((bf16[16,2,2000]{2,1,0:T(2,128)(2,1)}), bf16[16,2,2000]{2,1,0:T(2,128)(2,1)S(1)}, u32[]{:S(2)}, u32[]{:S(2)}) %all-to-all-start) | async-done | bytes 128032 | tf_op jit(solution)/shard_map/all_to_all | solution.py:21
  18.3 0.1 reshape.21.slices_ref
  18.3 3.7 %shard_map.97 = (bf16[8,32,256]{2,1,0:T(8,128)(2,1)S(1)}, f32[32,1]{1,0:T(8,128)S(1)}, bf16[256,2048]{1,0:T(8,128)(2,1)S(1)}) custom-call(bf16[32,2000]{1,0:T(8,128)(2,1)S(1)} %reshape.21.slices_ref, bf16[256,2048]{1,0:T(8,128)(2,1)S(1)} %get-tuple-element.27.ready_ref, bf16[2000,4096]{1,0:T(8,128)(2,1)} %embed_ref.7, f32[1,4096]{1,0:T(1,128)S(1)} %get-tuple-element.28.head_ref), custom_call_target="tpu_custom_call" | custom-call | flops 262144000 | bytes 17576960 | tf_op jit(solution)/shard_map/pallas_call | solution.py:54
  22.0 0.1 collective-permute-start
  22.1 0.0 copy-start.2
  22.1 0.0 copy-start.1
  22.1 3.7 %shard_map.98 = (f32[8,32,256]{2,1,0:T(8,128)S(1)}, f32[32,1]{1,0:T(8,128)S(1)}) custom-call(bf16[32,2000]{1,0:T(8,128)(2,1)S(1)} %reshape.21.slices_ref, bf16[256,2048]{1,0:T(8,128)(2,1)S(1)} %get-tuple-element.29.ready_ref, bf16[2000,4096]{1,0:T(8,128)(2,1)} %embed_ref.7, f32[1,4096]{1,0:T(1,128)S(1)} %get-tuple-element.28.head_ref), custom_call_target="tpu_custom_call" | custom-call | flops 262144000 | bytes 17576960 | tf_op jit(solution)/shard_map/pallas_call | solution.py:54
  25.8 0.0 collective-permute-done
  25.9 11.7 %all_to_all.30 = bf16[8,32,256]{2,1,0:T(8,128)(2,1)S(1)} all-to-all(bf16[8,32,256]{2,1,0:T(8,128)(2,1)S(1)} %add_convert_fusion.1), channel_id=1, replica_groups={{0,2,4,6,8,10,12,14},{1,3,5,7,9,11,13,15},{16,18,20,22,24,26,28,30},{17..., dimensions={0} | all-to-all | bytes 262144 | tf_op jit(solution)/shard_map/all_to_all | solution.py:26
  37.6 9.9 %all_to_all.31.x_ref.mine_ref = bf16[8,32,256]{2,1,0:T(8,128)(2,1)S(1)} all-to-all(bf16[8,32,256]{2,1,0:T(8,128)(2,1)S(1)} %broadcast_in_dim.4), channel_id=1, replica_groups={{0,2,4,6,8,10,12,14},{1,3,5,7,9,11,13,15},{16,18,20,22,24,26,28,30},{17..., dimensions={0} | all-to-all | bytes 262144 | tf_op jit(solution)/shard_map/all_to_all | solution.py:26
  47.4 0.0 collective-permute-start.1
  47.5 0.0 copy-done.1
  47.5 3.7 %shard_map.99 = (f32[32,1792]{1,0:T(8,128)S(1)}, f32[32,1]{1,0:T(8,128)S(1)}, f32[32,1]{1,0:T(8,128)S(1)}, f32[1,4]{1,0:T(1,128)S(1)}, bf16[1536,1792]{1,0:T(8,128)(2,1)S(1)}, /*index=5*/bf16[512,1792]{1,0:T(8,128)(2,1)S(1)}) custom-call(bf16[8,32,256]{2,1,0:T(8,128)(2,1)S(1)} %all_to_all.31.x_ref.mine_ref, bf16[1,4096]{1,0:T(2,128)(2,1)S(1)} %reshape.22.gain_ref, ...), custom_call_target="tpu_custom_call" | custom-call | flops 234881024 | bytes 16654352 | tf_op jit(solution)/shard_map/pallas_call | solution.py:54
  51.2 0.0 collective-permute-done.1.x_ref.got_ref
  51.2 5.4 %shard_map.100 = (bf16[8,32,256]{2,1,0:T(8,128)(2,1)S(1)}, f32[32,1]{1,0:T(8,128)S(1)}, f32[32,1]{1,0:T(8,128)S(1)}, bf16[32,1792]{1,0:T(8,128)(2,1)S(1)}) custom-call(bf16[8,32,256]{2,1,0:T(8,128)(2,1)S(1)} %collective-permute-done.1.x_ref.got_ref, bf16[1,4096]{1,0:T(2,128)(2,1)S(1)} %reshape.22.gain_ref, bf16[4096,896]{1,0:T(8,128)(2,1)} %gate_ref.5, ...), custom_call_target="tpu_custom_call" | custom-call | flops 234881024 | bytes 16887552 | tf_op jit(solution)/shard_map/pallas_call | solution.py:54
  56.6 0.6 collective-permute-start.2
  57.2 2.2 %shard_map.101 = f32[8,32,256]{2,1,0:T(8,128)S(1)} custom-call(bf16[32,1792]{1,0:T(8,128)(2,1)S(1)} %get-tuple-element.38.d_both_ref, bf16[512,1792]{1,0:T(8,128)(2,1)S(1)} %get-tuple-element.32.ready_ref, bf16[1536,1792]{1,0:T(8,128)(2,1)S(1)} %get-tuple-element.39.both_ref), custom_call_target="tpu_custom_call" | custom-call | flops 234881024 | bytes 7454720 | tf_op jit(solution)/shard_map/pallas_call | solution.py:54
  59.4 0.0 collective-permute-done.2
  59.5 9.8 %all_to_all.32 = bf16[8,32,256]{2,1,0:T(8,128)(2,1)S(1)} all-to-all(bf16[8,32,256]{2,1,0:T(8,128)(2,1)S(1)} %add_convert_fusion), channel_id=1, replica_groups={{0,2,4,6,8,10,12,14},{1,3,5,7,9,11,13,15},{16,18,20,22,24,26,28,30},{17..., dimensions={0} | all-to-all | bytes 262144 | tf_op jit(solution)/shard_map/all_to_all | solution.py:26
  69.3 9.8 %all_to_all.33.d_mine_ref = bf16[8,32,256]{2,1,0:T(8,128)(2,1)S(1)} all-to-all(bf16[8,32,256]{2,1,0:T(8,128)(2,1)S(1)} %broadcast_in_dim.5), channel_id=1, replica_groups={{0,2,4,6,8,10,12,14},{1,3,5,7,9,11,13,15},{16,18,20,22,24,26,28,30},{17..., dimensions={0} | all-to-all | bytes 262144 | tf_op jit(solution)/shard_map/all_to_all | solution.py:26
  79.2 0.0 collective-permute-start.3
  79.2 1.6 %shard_map.102.ready_ref = bf16[256,4096]{1,0:T(8,128)(2,1)S(1)} custom-call(bf16[2000,4096]{1,0:T(8,128)(2,1)} %embed_ref.7, bf16[32,256]{1,0:T(8,128)(2,1)S(1)} %reduce_sum.25.after_ref), custom_call_target="tpu_custom_call" | custom-call | bytes 16400384 | tf_op jit(solution)/shard_map/pallas_call | solution.py:54
  80.7 0.0 collective-permute-done.3.d_got_ref
  80.8 7.2 %shard_map.103 = bf16[32,2012]{1,0:T(8,128)(2,1)S(1)} custom-call(bf16[8,32,256]{2,1,0:T(8,128)(2,1)S(1)} %all_to_all.31.x_ref.mine_ref, bf16[8,32,256]{2,1,0:T(8,128)(2,1)S(1)} %collective-permute-done.1.x_ref.got_ref, bf16[8,32,256]{2,1,0:T(8,128)(2,1)S(1)} %all_to_all.33.d_mine_ref, bf16[8,32,256]{2,1,0:T(8,128)(2,1)S(1)} %collective-permute-done.3.d_got_ref, ...), custom_call_target="tpu_custom_call" | custom-call | flops 524288000 | bytes 19030672 | tf_op jit(solution)/shard_map/pallas_call | solution.py:54
  88.0 0.1 reshape.24
  88.1 10.5 %all_to_all.34.back_ref = bf16[16,2,2012]{2,1,0:T(2,128)(2,1)S(1)} all-to-all(bf16[16,2,2012]{2,1,0:T(2,128)(2,1)S(1)} %reshape.24), channel_id=1, replica_groups=mesh['groups'=2,'dp'=16] {'dp'}, dimensions={0} | all-to-all | bytes 257536 | tf_op jit(solution)/shard_map/all_to_all | solution.py:21
  98.6 1.2 %shard_map.104 = (bf16[2,32000]{1,0:T(2,128)(2,1)}, f32[1,4]{1,0:T(1,128)}) custom-call(f32[2,32000]{1,0:T(2,128)S(1)} %get-tuple-element.25.probs_ref, bf16[16,2,2012]{2,1,0:T(2,128)(2,1)S(1)} %all_to_all.34.back_ref, f32[1,4]{1,0:T(1,128)S(1)} %get-tuple-element.45.counts_ref), custom_call_target="tpu_custom_call" | custom-call | bytes 384784 | tf_op jit(solution)/shard_map/pallas_call | solution.py:54
  (8 shorter events, 0.2 us)
Async XLA Ops:
  0.6 0.9 copy-start
  2.9 15.3 %all-to-all-start = ((bf16[16,2,2000]{2,1,0:T(2,128)(2,1)}), bf16[16,2,2000]{2,1,0:T(2,128)(2,1)S(1)}, u32[]{:S(2)}, u32[]{:S(2)}) async-start(bf16[16,2,2000]{2,1,0:T(2,128)(2,1)} %get-tuple-element.26.after_ref), calls=%async_computation | async-start | bytes 262144 | tf_op jit(solution)/shard_map/all_to_all | solution.py:21
  22.0 3.8 %collective-permute-start = (bf16[8,32,256]{2,1,0:T(8,128)(2,1)S(1)}, bf16[8,32,256]{2,1,0:T(8,128)(2,1)S(1)}, u32[]{:S(2)}, u32[]{:S(2)}) collective-permute-start(bf16[8,32,256]{2,1,0:T(8,128)(2,1)S(1)} %get-tuple-element.31), channel_id=1, source_target_pairs={{0,1},{1,0},{2,3},{3,2},{4,5},{5,4},{6,7},{7,6},{8,9},{9,8},{10,11... | collective-permute-start | bytes 393224 | tf_op jit(solution)/shard_map/ppermute | solution.py:17
  22.1 25.3 %copy-start.2 = (bf16[4096]{0:T(1024)(128)(2,1)S(1)}, bf16[4096]{0:T(1024)(128)(2,1)}, u32[]{:S(2)}) copy-start(bf16[4096]{0:T(1024)(128)(2,1)} %param.10) | copy-start | bytes 24580
  22.1 25.3 %copy-start.1 = (s32[4]{0:T(128)S(1)}, s32[4]{0:T(128)}, u32[]{:S(2)}) copy-start(s32[4]{0:T(128)} %param.15) | copy-start | bytes 52
  47.4 3.7 %collective-permute-start.1 = (bf16[8,32,256]{2,1,0:T(8,128)(2,1)S(1)}, bf16[8,32,256]{2,1,0:T(8,128)(2,1)S(1)}, u32[]{:S(2)}, u32[]{:S(2)}) collective-permute-start(bf16[8,32,256]{2,1,0:T(8,128)(2,1)S(1)} %all_to_all.31.x_ref.mine_ref), channel_id=1, source_target_pairs={{0,1},{1,0},{2,3},{3,2},{4,5},{5,4},{6,7},{7,6},{8,9},{9,8},{10,11... | collective-permute-start | bytes 393224 | tf_op jit(solution)/shard_map/ppermute | solution.py:17
  56.6 2.8 %collective-permute-start.2 = (bf16[8,32,256]{2,1,0:T(8,128)(2,1)S(1)}, bf16[8,32,256]{2,1,0:T(8,128)(2,1)S(1)}, u32[]{:S(2)}, u32[]{:S(2)}) collective-permute-start(bf16[8,32,256]{2,1,0:T(8,128)(2,1)S(1)} %get-tuple-element.40), channel_id=1, source_target_pairs={{0,1},{1,0},{2,3},{3,2},{4,5},{5,4},{6,7},{7,6},{8,9},{9,8},{10,11... | collective-permute-start | bytes 393224 | tf_op jit(solution)/shard_map/ppermute | solution.py:17
  79.2 1.6 %collective-permute-start.3 = (bf16[8,32,256]{2,1,0:T(8,128)(2,1)S(1)}, bf16[8,32,256]{2,1,0:T(8,128)(2,1)S(1)}, u32[]{:S(2)}, u32[]{:S(2)}) collective-permute-start(bf16[8,32,256]{2,1,0:T(8,128)(2,1)S(1)} %all_to_all.33.d_mine_ref), channel_id=1, source_target_pairs={{0,1},{1,0},{2,3},{3,2},{4,5},{5,4},{6,7},{7,6},{8,9},{9,8},{10,11... | collective-permute-start | bytes 393224 | tf_op jit(solution)/shard_map/ppermute | solution.py:17

commit v23 on v18

--- a/solution.py
+++ b/solution.py
@@ -353,7 +353,7 @@
     width = 2 * chips * own
     core = this_core()
     ready = ready_ref.shape[0]
-    tile, fine = 256, 64
+    tile, fine = 256, 128
     steps = (voc - ready) // tile
     last = ready + steps * tile
 
@@ -600,7 +600,7 @@
             kept=(12,), streamed=(13,), flops=2 * flops, room=2 * part * width,
             scratch=(
                 pltpu.VMEM((total, width), BF16), pltpu.VMEM((part - 256, width), BF16),
-                pltpu.SemaphoreType.DMA((-(-part // 64),)),
+                pltpu.SemaphoreType.DMA((-(-part // 128),)),
             ),
         )
     else:

time: 100 us -> 99.9 us (level)
  no operation moved by 1% of the time
where the time goes in v23:
time: 99.9 us; the launch traced here: 99.4 us
  blocking collectives  51.7 us (52%)
  Pallas kernels  35.9 us (36%)
  starting transfers between devices  8.03 us (8%)
  waiting for transfers between devices  1.66 us (2%)
  local copies, waits for them, and re-layouts  1.11 us (1%)
    all_to_all x4, blocking collectives, exchange_chips(): lax.all_to_all(blocks, 'dp', split_axis=0, concat_axis=0, axis_index_grou...  41.2 us
    pallas_call x10, Pallas kernels, call(): pl.pallas_call(kernel, out_shape=outs, in_specs=specs, out_specs=[VMEM_SP...  35.9 us
    all_to_all x1, blocking collectives, exchange(): return lax.all_to_all(blocks, 'dp', split_axis=0, concat_axis=0, tiled=True)  10.5 us
    all_to_all x1, starting transfers between devices, exchange(): return lax.all_to_all(blocks, 'dp', split_axis=0, concat_axis=0, tiled=True)  7.39 us
  transfers between devices with their start and end apart: 5, of which 1 were waited for; matrix products, arithmetic and copies ran while one was open for 0% of the time, Pallas kernels for 17%

profile of v23, /device:TPU:0, one launch (start us, length us, event | category | flops | bytes accessed | tf_op | source)
XLA Modules:
  0.0 99.4 jit_solution(13912562765399170087)
XLA Ops:
  0.6 0.0 copy-start
  0.6 0.9 copy-done
  1.5 1.4 %shard_map.95 = (bf16[16,2,2000]{2,1,0:T(2,128)(2,1)}, f32[2,32000]{1,0:T(2,128)S(1)}) custom-call(bf16[2,32000]{1,0:T(2,128)(2,1)S(1)} %copy-done), custom_call_target="tpu_custom_call" | custom-call | bytes 128000 | tf_op jit(solution)/shard_map/pallas_call | solution.py:54
  2.9 7.4 %all-to-all-start = ((bf16[16,2,2000]{2,1,0:T(2,128)(2,1)}), bf16[16,2,2000]{2,1,0:T(2,128)(2,1)S(1)}, u32[]{:S(2)}, u32[]{:S(2)}) async-start(bf16[16,2,2000]{2,1,0:T(2,128)(2,1)} %get-tuple-element.26.after_ref), calls=%async_computation | async-start | bytes 262144 | tf_op jit(solution)/shard_map/all_to_all | solution.py:21
  10.3 6.3 %shard_map.96 = (f32[1,896]{1,0:T(1,128)S(1)}, f32[1,4096]{1,0:T(1,128)S(1)}, bf16[256,2048]{1,0:T(8,128)(2,1)S(1)}, bf16[512,1792]{1,0:T(8,128)(2,1)S(1)}) custom-call(bf16[4096]{0:T(1024)(128)(2,1)} %head_ref.1, bf16[896,4096]{1,0:T(8,128)(2,1)} %down_ref.1, bf16[2000,4096]{1,0:T(8,128)(2,1)} %embed_ref.7, bf16[4096,896]{1,0:T(8,128)(2,1)} %gate_ref.5, ...), custom_call_target="tpu_custom_call" | custom-call | flops 7340032 | bytes 38540288 | tf_op jit(solution)/shard_map/pallas_call | solution.py:54
  16.6 1.6 %all-to-all-done = bf16[16,2,2000]{2,1,0:T(2,128)(2,1)S(1)} async-done(((bf16[16,2,2000]{2,1,0:T(2,128)(2,1)}), bf16[16,2,2000]{2,1,0:T(2,128)(2,1)S(1)}, u32[]{:S(2)}, u32[]{:S(2)}) %all-to-all-start) | async-done | bytes 128032 | tf_op jit(solution)/shard_map/all_to_all | solution.py:21
  18.3 0.1 reshape.21.slices_ref
  18.3 3.7 %shard_map.97 = (bf16[8,32,256]{2,1,0:T(8,128)(2,1)S(1)}, f32[32,1]{1,0:T(8,128)S(1)}, bf16[256,2048]{1,0:T(8,128)(2,1)S(1)}) custom-call(bf16[32,2000]{1,0:T(8,128)(2,1)S(1)} %reshape.21.slices_ref, bf16[256,2048]{1,0:T(8,128)(2,1)S(1)} %get-tuple-element.27.ready_ref, bf16[2000,4096]{1,0:T(8,128)(2,1)} %embed_ref.7, f32[1,4096]{1,0:T(1,128)S(1)} %get-tuple-element.28.head_ref), custom_call_target="tpu_custom_call" | custom-call | flops 262144000 | bytes 17576960 | tf_op jit(solution)/shard_map/pallas_call | solution.py:54
  22.0 0.1 collective-permute-start
  22.1 0.0 copy-start.2
  22.1 0.0 copy-start.1
  22.1 3.5 %shard_map.98 = (f32[8,32,256]{2,1,0:T(8,128)S(1)}, f32[32,1]{1,0:T(8,128)S(1)}) custom-call(bf16[32,2000]{1,0:T(8,128)(2,1)S(1)} %reshape.21.slices_ref, bf16[256,2048]{1,0:T(8,128)(2,1)S(1)} %get-tuple-element.29.ready_ref, bf16[2000,4096]{1,0:T(8,128)(2,1)} %embed_ref.7, f32[1,4096]{1,0:T(1,128)S(1)} %get-tuple-element.28.head_ref), custom_call_target="tpu_custom_call" | custom-call | flops 262144000 | bytes 17576960 | tf_op jit(solution)/shard_map/pallas_call | solution.py:54
  25.7 0.0 collective-permute-done
  25.7 11.7 %all_to_all.30 = bf16[8,32,256]{2,1,0:T(8,128)(2,1)S(1)} all-to-all(bf16[8,32,256]{2,1,0:T(8,128)(2,1)S(1)} %add_convert_fusion.1), channel_id=1, replica_groups={{0,2,4,6,8,10,12,14},{1,3,5,7,9,11,13,15},{16,18,20,22,24,26,28,30},{17..., dimensions={0} | all-to-all | bytes 262144 | tf_op jit(solution)/shard_map/all_to_all | solution.py:26
  37.4 9.9 %all_to_all.31.x_ref.mine_ref = bf16[8,32,256]{2,1,0:T(8,128)(2,1)S(1)} all-to-all(bf16[8,32,256]{2,1,0:T(8,128)(2,1)S(1)} %broadcast_in_dim.4), channel_id=1, replica_groups={{0,2,4,6,8,10,12,14},{1,3,5,7,9,11,13,15},{16,18,20,22,24,26,28,30},{17..., dimensions={0} | all-to-all | bytes 262144 | tf_op jit(solution)/shard_map/all_to_all | solution.py:26
  47.3 0.0 collective-permute-start.1
  47.3 0.0 copy-done.2
  47.3 3.7 %shard_map.99 = (f32[32,1792]{1,0:T(8,128)S(1)}, f32[32,1]{1,0:T(8,128)S(1)}, f32[32,1]{1,0:T(8,128)S(1)}, f32[1,4]{1,0:T(1,128)S(1)}, bf16[1536,1792]{1,0:T(8,128)(2,1)S(1)}, /*index=5*/bf16[512,1792]{1,0:T(8,128)(2,1)S(1)}) custom-call(bf16[8,32,256]{2,1,0:T(8,128)(2,1)S(1)} %all_to_all.31.x_ref.mine_ref, bf16[1,4096]{1,0:T(2,128)(2,1)S(1)} %reshape.22.gain_ref, ...), custom_call_target="tpu_custom_call" | custom-call | flops 234881024 | bytes 16654352 | tf_op jit(solution)/shard_map/pallas_call | solution.py:54
  51.1 0.0 collective-permute-done.1.x_ref.got_ref
  51.1 5.2 %shard_map.100 = (bf16[8,32,256]{2,1,0:T(8,128)(2,1)S(1)}, f32[32,1]{1,0:T(8,128)S(1)}, f32[32,1]{1,0:T(8,128)S(1)}, bf16[32,1792]{1,0:T(8,128)(2,1)S(1)}) custom-call(bf16[8,32,256]{2,1,0:T(8,128)(2,1)S(1)} %collective-permute-done.1.x_ref.got_ref, bf16[1,4096]{1,0:T(2,128)(2,1)S(1)} %reshape.22.gain_ref, bf16[4096,896]{1,0:T(8,128)(2,1)} %gate_ref.5, ...), custom_call_target="tpu_custom_call" | custom-call | flops 234881024 | bytes 16887552 | tf_op jit(solution)/shard_map/pallas_call | solution.py:54
  56.3 0.6 collective-permute-start.2
  56.9 2.2 %shard_map.101 = f32[8,32,256]{2,1,0:T(8,128)S(1)} custom-call(bf16[32,1792]{1,0:T(8,128)(2,1)S(1)} %get-tuple-element.38.d_both_ref, bf16[512,1792]{1,0:T(8,128)(2,1)S(1)} %get-tuple-element.32.ready_ref, bf16[1536,1792]{1,0:T(8,128)(2,1)S(1)} %get-tuple-element.39.both_ref), custom_call_target="tpu_custom_call" | custom-call | flops 234881024 | bytes 7454720 | tf_op jit(solution)/shard_map/pallas_call | solution.py:54
  59.1 0.0 collective-permute-done.2
  59.1 9.8 %all_to_all.32 = bf16[8,32,256]{2,1,0:T(8,128)(2,1)S(1)} all-to-all(bf16[8,32,256]{2,1,0:T(8,128)(2,1)S(1)} %add_convert_fusion), channel_id=1, replica_groups={{0,2,4,6,8,10,12,14},{1,3,5,7,9,11,13,15},{16,18,20,22,24,26,28,30},{17..., dimensions={0} | all-to-all | bytes 262144 | tf_op jit(solution)/shard_map/all_to_all | solution.py:26
  69.0 9.8 %all_to_all.33.d_mine_ref = bf16[8,32,256]{2,1,0:T(8,128)(2,1)S(1)} all-to-all(bf16[8,32,256]{2,1,0:T(8,128)(2,1)S(1)} %broadcast_in_dim.5), channel_id=1, replica_groups={{0,2,4,6,8,10,12,14},{1,3,5,7,9,11,13,15},{16,18,20,22,24,26,28,30},{17..., dimensions={0} | all-to-all | bytes 262144 | tf_op jit(solution)/shard_map/all_to_all | solution.py:26
  78.9 0.0 collective-permute-start.3
  78.9 1.6 %shard_map.102.ready_ref = bf16[256,4096]{1,0:T(8,128)(2,1)S(1)} custom-call(bf16[2000,4096]{1,0:T(8,128)(2,1)} %embed_ref.7, bf16[32,256]{1,0:T(8,128)(2,1)S(1)} %reduce_sum.25.after_ref), custom_call_target="tpu_custom_call" | custom-call | bytes 16400384 | tf_op jit(solution)/shard_map/pallas_call | solution.py:54
  80.4 0.0 collective-permute-done.3.d_got_ref
  80.4 7.1 %shard_map.103 = bf16[32,2012]{1,0:T(8,128)(2,1)S(1)} custom-call(bf16[8,32,256]{2,1,0:T(8,128)(2,1)S(1)} %all_to_all.31.x_ref.mine_ref, bf16[8,32,256]{2,1,0:T(8,128)(2,1)S(1)} %collective-permute-done.1.x_ref.got_ref, bf16[8,32,256]{2,1,0:T(8,128)(2,1)S(1)} %all_to_all.33.d_mine_ref, bf16[8,32,256]{2,1,0:T(8,128)(2,1)S(1)} %collective-permute-done.3.d_got_ref, ...), custom_call_target="tpu_custom_call" | custom-call | flops 524288000 | bytes 19030672 | tf_op jit(solution)/shard_map/pallas_call | solution.py:54
  87.6 0.1 reshape.24
  87.7 10.5 %all_to_all.34.back_ref = bf16[16,2,2012]{2,1,0:T(2,128)(2,1)S(1)} all-to-all(bf16[16,2,2012]{2,1,0:T(2,128)(2,1)S(1)} %reshape.24), channel_id=1, replica_groups=mesh['groups'=2,'dp'=16] {'dp'}, dimensions={0} | all-to-all | bytes 257536 | tf_op jit(solution)/shard_map/all_to_all | solution.py:21
  98.2 1.2 %shard_map.104 = (bf16[2,32000]{1,0:T(2,128)(2,1)}, f32[1,4]{1,0:T(1,128)}) custom-call(f32[2,32000]{1,0:T(2,128)S(1)} %get-tuple-element.25.probs_ref, bf16[16,2,2012]{2,1,0:T(2,128)(2,1)S(1)} %all_to_all.34.back_ref, f32[1,4]{1,0:T(1,128)S(1)} %get-tuple-element.45.counts_ref), custom_call_target="tpu_custom_call" | custom-call | bytes 384784 | tf_op jit(solution)/shard_map/pallas_call | solution.py:54
  (8 shorter events, 0.2 us)
Async XLA Ops:
  0.6 0.9 copy-start
  2.9 15.3 %all-to-all-start = ((bf16[16,2,2000]{2,1,0:T(2,128)(2,1)}), bf16[16,2,2000]{2,1,0:T(2,128)(2,1)S(1)}, u32[]{:S(2)}, u32[]{:S(2)}) async-start(bf16[16,2,2000]{2,1,0:T(2,128)(2,1)} %get-tuple-element.26.after_ref), calls=%async_computation | async-start | bytes 262144 | tf_op jit(solution)/shard_map/all_to_all | solution.py:21
  22.0 3.6 %collective-permute-start = (bf16[8,32,256]{2,1,0:T(8,128)(2,1)S(1)}, bf16[8,32,256]{2,1,0:T(8,128)(2,1)S(1)}, u32[]{:S(2)}, u32[]{:S(2)}) collective-permute-start(bf16[8,32,256]{2,1,0:T(8,128)(2,1)S(1)} %get-tuple-element.31), channel_id=1, source_target_pairs={{0,1},{1,0},{2,3},{3,2},{4,5},{5,4},{6,7},{7,6},{8,9},{9,8},{10,11... | collective-permute-start | bytes 393224 | tf_op jit(solution)/shard_map/ppermute | solution.py:17
  22.1 25.2 %copy-start.2 = (bf16[4096]{0:T(1024)(128)(2,1)S(1)}, bf16[4096]{0:T(1024)(128)(2,1)}, u32[]{:S(2)}) copy-start(bf16[4096]{0:T(1024)(128)(2,1)} %param.10) | copy-start | bytes 24580
  22.1 25.2 %copy-start.1 = (s32[4]{0:T(128)S(1)}, s32[4]{0:T(128)}, u32[]{:S(2)}) copy-start(s32[4]{0:T(128)} %param.15) | copy-start | bytes 52
  47.3 3.8 %collective-permute-start.1 = (bf16[8,32,256]{2,1,0:T(8,128)(2,1)S(1)}, bf16[8,32,256]{2,1,0:T(8,128)(2,1)S(1)}, u32[]{:S(2)}, u32[]{:S(2)}) collective-permute-start(bf16[8,32,256]{2,1,0:T(8,128)(2,1)S(1)} %all_to_all.31.x_ref.mine_ref), channel_id=1, source_target_pairs={{0,1},{1,0},{2,3},{3,2},{4,5},{5,4},{6,7},{7,6},{8,9},{9,8},{10,11... | collective-permute-start | bytes 393224 | tf_op jit(solution)/shard_map/ppermute | solution.py:17
  56.3 2.8 %collective-permute-start.2 = (bf16[8,32,256]{2,1,0:T(8,128)(2,1)S(1)}, bf16[8,32,256]{2,1,0:T(8,128)(2,1)S(1)}, u32[]{:S(2)}, u32[]{:S(2)}) collective-permute-start(bf16[8,32,256]{2,1,0:T(8,128)(2,1)S(1)} %get-tuple-element.40), channel_id=1, source_target_pairs={{0,1},{1,0},{2,3},{3,2},{4,5},{5,4},{6,7},{7,6},{8,9},{9,8},{10,11... | collective-permute-start | bytes 393224 | tf_op jit(solution)/shard_map/ppermute | solution.py:17
  78.9 1.6 %collective-permute-start.3 = (bf16[8,32,256]{2,1,0:T(8,128)(2,1)S(1)}, bf16[8,32,256]{2,1,0:T(8,128)(2,1)S(1)}, u32[]{:S(2)}, u32[]{:S(2)}) collective-permute-start(bf16[8,32,256]{2,1,0:T(8,128)(2,1)S(1)} %all_to_all.33.d_mine_ref), channel_id=1, source_target_pairs={{0,1},{1,0},{2,3},{3,2},{4,5},{5,4},{6,7},{7,6},{8,9},{9,8},{10,11... | collective-permute-start | bytes 393224 | tf_op jit(solution)/shard_map/ppermute | solution.py:17

commit v24 on v21

--- a/solution.py
+++ b/solution.py
@@ -356,7 +356,7 @@
     width = 2 * chips * own
     core = this_core()
     ready = ready_ref.shape[0]
-    tile, fine = 256, 64
+    tile, fine = 256, 128
     steps = (voc - ready) // tile
     last = ready + steps * tile
 
@@ -597,7 +597,7 @@
             kept=(12,), streamed=(13,), flops=2 * flops, room=2 * part * width,
             scratch=(
                 pltpu.VMEM((total, width), BF16), pltpu.VMEM((part - 256, width), BF16),
-                pltpu.SemaphoreType.DMA((-(-part // 64),)),
+                pltpu.SemaphoreType.DMA((-(-part // 128),)),
             ),
         )
     else:

time: 99.5 us -> 99.4 us (level)
  no operation moved by 1% of the time
where the time goes in v24:
time: 99.4 us; the launch traced here: 98.9 us
  blocking collectives  50.9 us (51%)
  Pallas kernels  33.8 us (34%)
  starting transfers between devices  9.66 us (10%)
  waiting for transfers between devices  2.5 us (3%)
  local copies, waits for them, and re-layouts  1.11 us (1%)
    all_to_all x4, blocking collectives, exchange_chips(): lax.all_to_all(blocks, 'dp', split_axis=0, concat_axis=0, axis_index_grou...  40.4 us
    pallas_call x10, Pallas kernels, call(): pl.pallas_call(kernel, out_shape=outs, in_specs=specs, out_specs=[VMEM_SP...  33.8 us
    all_to_all x1, blocking collectives, exchange(): return lax.all_to_all(blocks, 'dp', split_axis=0, concat_axis=0, tiled=True)  10.5 us
    all_to_all x1, starting transfers between devices, exchange(): return lax.all_to_all(blocks, 'dp', split_axis=0, concat_axis=0, tiled=True)  7.39 us
    all_to_all x1, waiting for transfers between devices, exchange(): return lax.all_to_all(blocks, 'dp', split_axis=0, concat_axis=0, tiled=True)  2.48 us
  transfers between devices with their start and end apart: 6, of which 1 were waited for; matrix products, arithmetic and copies ran while one was open for 0% of the time, Pallas kernels for 19%

profile of v24, /device:TPU:0, one launch (start us, length us, event | category | flops | bytes accessed | tf_op | source)
XLA Modules:
  0.0 98.9 jit_solution(3804684077285082536)
XLA Ops:
  0.6 0.9 copy-done
  1.5 1.4 %shard_map.95 = (bf16[16,2,2000]{2,1,0:T(2,128)(2,1)}, f32[2,32000]{1,0:T(2,128)S(1)}) custom-call(bf16[2,32000]{1,0:T(2,128)(2,1)S(1)} %copy-done), custom_call_target="tpu_custom_call" | custom-call | bytes 128000 | tf_op jit(solution)/shard_map/pallas_call | solution.py:54
  2.9 7.4 %all-to-all-start = ((bf16[16,2,2000]{2,1,0:T(2,128)(2,1)}), bf16[16,2,2000]{2,1,0:T(2,128)(2,1)S(1)}, u32[]{:S(2)}, u32[]{:S(2)}) async-start(bf16[16,2,2000]{2,1,0:T(2,128)(2,1)} %get-tuple-element.27.after_ref), calls=%async_computation | async-start | bytes 262144 | tf_op jit(solution)/shard_map/all_to_all | solution.py:21
  10.3 3.8 %shard_map.96 = (f32[1,512]{1,0:T(1,128)S(1)}, f32[1,4096]{1,0:T(1,128)S(1)}, bf16[256,2048]{1,0:T(8,128)(2,1)S(1)}) custom-call(bf16[4096]{0:T(1024)(128)(2,1)} %head_ref.1, bf16[896,4096]{1,0:T(8,128)(2,1)} %down_ref.1, bf16[2000,4096]{1,0:T(8,128)(2,1)} %embed_ref.7, bf16[16,2,2000]{2,1,0:T(2,128)(2,1)} %get-tuple-element.27.after_ref), custom_call_target="tpu_custom_call" | custom-call | flops 7340032 | bytes 23860224 | tf_op jit(solution)/shard_map/pallas_call | solution.py:54
  14.2 1.6 %collective-permute-start = (f32[1,512]{1,0:T(1,128)S(1)}, f32[1,512]{1,0:T(1,128)S(1)}, u32[]{:S(2)}, u32[]{:S(2)}) collective-permute-start(f32[1,512]{1,0:T(1,128)S(1)} %get-tuple-element.33.down_a), channel_id=1, source_target_pairs={{0,16},{16,0},{1,17},{17,1},{2,18},{18,2},{3,19},{19,3},{4,20},{20... | collective-permute-start | bytes 6152 | tf_op jit(solution)/shard_map/ppermute | solution.py:536
  15.8 2.5 %all-to-all-done = bf16[16,2,2000]{2,1,0:T(2,128)(2,1)S(1)} async-done(((bf16[16,2,2000]{2,1,0:T(2,128)(2,1)}), bf16[16,2,2000]{2,1,0:T(2,128)(2,1)S(1)}, u32[]{:S(2)}, u32[]{:S(2)}) %all-to-all-start) | async-done | bytes 128032 | tf_op jit(solution)/shard_map/all_to_all | solution.py:21
  18.3 0.1 reshape.21.slices_ref
  18.3 3.7 %shard_map.97 = (bf16[8,32,256]{2,1,0:T(8,128)(2,1)S(1)}, f32[32,1]{1,0:T(8,128)S(1)}, bf16[256,2048]{1,0:T(8,128)(2,1)S(1)}) custom-call(bf16[32,2000]{1,0:T(8,128)(2,1)S(1)} %reshape.21.slices_ref, bf16[2000,4096]{1,0:T(8,128)(2,1)} %embed_ref.7, f32[1,4096]{1,0:T(1,128)S(1)} %get-tuple-element.28.head_ref, bf16[256,2048]{1,0:T(8,128)(2,1)S(1)} %get-tuple-element.29.rest_0_), custom_call_target="tpu_custom_call" | custom-call | flops 262144000 | bytes 17576960 | tf_op jit(solution)/shard_map/pallas_call | solution.py:54
  22.0 0.0 collective-permute-done.down_b
  22.0 0.1 collective-permute-start.1
  22.1 0.0 copy-start.2
  22.1 0.0 copy-start.1
  22.1 3.5 %shard_map.98 = (f32[8,32,256]{2,1,0:T(8,128)S(1)}, f32[32,1]{1,0:T(8,128)S(1)}) custom-call(bf16[32,2000]{1,0:T(8,128)(2,1)S(1)} %reshape.21.slices_ref, bf16[2000,4096]{1,0:T(8,128)(2,1)} %embed_ref.7, f32[1,4096]{1,0:T(1,128)S(1)} %get-tuple-element.28.head_ref, bf16[256,2048]{1,0:T(8,128)(2,1)S(1)} %get-tuple-element.30.rest_0_), custom_call_target="tpu_custom_call" | custom-call | flops 262144000 | bytes 17576960 | tf_op jit(solution)/shard_map/pallas_call | solution.py:54
  25.7 0.0 collective-permute-done.1
  25.7 10.8 %all_to_all.30 = bf16[8,32,256]{2,1,0:T(8,128)(2,1)S(1)} all-to-all(bf16[8,32,256]{2,1,0:T(8,128)(2,1)S(1)} %add_convert_fusion.1), channel_id=1, replica_groups={{0,2,4,6,8,10,12,14},{1,3,5,7,9,11,13,15},{16,18,20,22,24,26,28,30},{17..., dimensions={0} | all-to-all | bytes 262144 | tf_op jit(solution)/shard_map/all_to_all | solution.py:26
  36.6 9.9 %all_to_all.31.x_ref.mine_ref = bf16[8,32,256]{2,1,0:T(8,128)(2,1)S(1)} all-to-all(bf16[8,32,256]{2,1,0:T(8,128)(2,1)S(1)} %broadcast_in_dim.4), channel_id=1, replica_groups={{0,2,4,6,8,10,12,14},{1,3,5,7,9,11,13,15},{16,18,20,22,24,26,28,30},{17..., dimensions={0} | all-to-all | bytes 262144 | tf_op jit(solution)/shard_map/all_to_all | solution.py:26
  46.5 0.0 collective-permute-start.2
  46.5 4.0 %shard_map.99 = (f32[32,1792]{1,0:T(8,128)S(1)}, f32[32,1]{1,0:T(8,128)S(1)}, f32[32,1]{1,0:T(8,128)S(1)}, f32[1,4]{1,0:T(1,128)S(1)}, bf16[2048,1792]{1,0:T(8,128)(2,1)S(1)}, /*index=5*/bf16[512,1792]{1,0:T(8,128)(2,1)S(1)}) custom-call(bf16[8,32,256]{2,1,0:T(8,128)(2,1)S(1)} %all_to_all.31.x_ref.mine_ref, bf16[1,4096]{1,0:T(2,128)(2,1)S(1)} %reshape.22.gain_ref, ...), custom_call_target="tpu_custom_call" | custom-call | flops 234881024 | bytes 14819344 | tf_op jit(solution)/shard_map/pallas_call | solution.py:54
  50.5 0.0 collective-permute-done.2.x_ref.got_ref
  50.5 5.2 %shard_map.100 = (bf16[8,32,256]{2,1,0:T(8,128)(2,1)S(1)}, f32[32,1]{1,0:T(8,128)S(1)}, f32[32,1]{1,0:T(8,128)S(1)}, bf16[32,1792]{1,0:T(8,128)(2,1)S(1)}) custom-call(bf16[8,32,256]{2,1,0:T(8,128)(2,1)S(1)} %collective-permute-done.2.x_ref.got_ref, bf16[1,4096]{1,0:T(2,128)(2,1)S(1)} %reshape.22.gain_ref, bf16[4096,896]{1,0:T(8,128)(2,1)} %gate_ref.3, ...), custom_call_target="tpu_custom_call" | custom-call | flops 234881024 | bytes 16888064 | tf_op jit(solution)/shard_map/pallas_call | solution.py:54
  55.7 0.6 collective-permute-start.3
  56.4 2.2 %shard_map.101 = f32[8,32,256]{2,1,0:T(8,128)S(1)} custom-call(bf16[32,1792]{1,0:T(8,128)(2,1)S(1)} %get-tuple-element.40.d_both_ref, bf16[2048,1792]{1,0:T(8,128)(2,1)S(1)} %get-tuple-element.41.both_ref), custom_call_target="tpu_custom_call" | custom-call | flops 234881024 | bytes 7454720 | tf_op jit(solution)/shard_map/pallas_call | solution.py:54
  58.6 0.0 collective-permute-done.3
  58.6 9.8 %all_to_all.32 = bf16[8,32,256]{2,1,0:T(8,128)(2,1)S(1)} all-to-all(bf16[8,32,256]{2,1,0:T(8,128)(2,1)S(1)} %add_convert_fusion), channel_id=1, replica_groups={{0,2,4,6,8,10,12,14},{1,3,5,7,9,11,13,15},{16,18,20,22,24,26,28,30},{17..., dimensions={0} | all-to-all | bytes 262144 | tf_op jit(solution)/shard_map/all_to_all | solution.py:26
  68.5 9.8 %all_to_all.33.d_mine_ref = bf16[8,32,256]{2,1,0:T(8,128)(2,1)S(1)} all-to-all(bf16[8,32,256]{2,1,0:T(8,128)(2,1)S(1)} %broadcast_in_dim.5), channel_id=1, replica_groups={{0,2,4,6,8,10,12,14},{1,3,5,7,9,11,13,15},{16,18,20,22,24,26,28,30},{17..., dimensions={0} | all-to-all | bytes 262144 | tf_op jit(solution)/shard_map/all_to_all | solution.py:26
  78.3 0.0 collective-permute-start.4
  78.3 1.6 %shard_map.102.ready_ref = bf16[256,4096]{1,0:T(8,128)(2,1)S(1)} custom-call(bf16[2000,4096]{1,0:T(8,128)(2,1)} %embed_ref.7, bf16[32,256]{1,0:T(8,128)(2,1)S(1)} %reduce_sum.25.after_ref), custom_call_target="tpu_custom_call" | custom-call | bytes 16400384 | tf_op jit(solution)/shard_map/pallas_call | solution.py:54
  79.9 0.0 collective-permute-done.4.d_got_ref
  79.9 7.1 %shard_map.103 = bf16[32,2012]{1,0:T(8,128)(2,1)S(1)} custom-call(bf16[8,32,256]{2,1,0:T(8,128)(2,1)S(1)} %all_to_all.31.x_ref.mine_ref, bf16[8,32,256]{2,1,0:T(8,128)(2,1)S(1)} %collective-permute-done.2.x_ref.got_ref, bf16[8,32,256]{2,1,0:T(8,128)(2,1)S(1)} %all_to_all.33.d_mine_ref, bf16[8,32,256]{2,1,0:T(8,128)(2,1)S(1)} %collective-permute-done.4.d_got_ref, ...), custom_call_target="tpu_custom_call" | custom-call | flops 524288000 | bytes 19030672 | tf_op jit(solution)/shard_map/pallas_call | solution.py:54
  87.1 0.1 reshape.24
  87.2 10.5 %all_to_all.34.back_ref = bf16[16,2,2012]{2,1,0:T(2,128)(2,1)S(1)} all-to-all(bf16[16,2,2012]{2,1,0:T(2,128)(2,1)S(1)} %reshape.24), channel_id=1, replica_groups=mesh['groups'=2,'dp'=16] {'dp'}, dimensions={0} | all-to-all | bytes 257536 | tf_op jit(solution)/shard_map/all_to_all | solution.py:21
  97.7 1.2 %shard_map.104 = (bf16[2,32000]{1,0:T(2,128)(2,1)}, f32[1,4]{1,0:T(1,128)}) custom-call(f32[2,32000]{1,0:T(2,128)S(1)} %get-tuple-element.26.probs_ref, bf16[16,2,2012]{2,1,0:T(2,128)(2,1)S(1)} %all_to_all.34.back_ref, f32[1,4]{1,0:T(1,128)S(1)} %get-tuple-element.47.counts_ref), custom_call_target="tpu_custom_call" | custom-call | bytes 384784 | tf_op jit(solution)/shard_map/pallas_call | solution.py:54
  (10 shorter events, 0.2 us)
Async XLA Ops:
  0.6 0.9 copy-start
  2.9 15.3 %all-to-all-start = ((bf16[16,2,2000]{2,1,0:T(2,128)(2,1)}), bf16[16,2,2000]{2,1,0:T(2,128)(2,1)S(1)}, u32[]{:S(2)}, u32[]{:S(2)}) async-start(bf16[16,2,2000]{2,1,0:T(2,128)(2,1)} %get-tuple-element.27.after_ref), calls=%async_computation | async-start | bytes 262144 | tf_op jit(solution)/shard_map/all_to_all | solution.py:21
  14.2 7.8 %collective-permute-start = (f32[1,512]{1,0:T(1,128)S(1)}, f32[1,512]{1,0:T(1,128)S(1)}, u32[]{:S(2)}, u32[]{:S(2)}) collective-permute-start(f32[1,512]{1,0:T(1,128)S(1)} %get-tuple-element.33.down_a), channel_id=1, source_target_pairs={{0,16},{16,0},{1,17},{17,1},{2,18},{18,2},{3,19},{19,3},{4,20},{20... | collective-permute-start | bytes 6152 | tf_op jit(solution)/shard_map/ppermute | solution.py:536
  22.0 3.6 %collective-permute-start.1 = (bf16[8,32,256]{2,1,0:T(8,128)(2,1)S(1)}, bf16[8,32,256]{2,1,0:T(8,128)(2,1)S(1)}, u32[]{:S(2)}, u32[]{:S(2)}) collective-permute-start(bf16[8,32,256]{2,1,0:T(8,128)(2,1)S(1)} %get-tuple-element.34), channel_id=1, source_target_pairs={{0,1},{1,0},{2,3},{3,2},{4,5},{5,4},{6,7},{7,6},{8,9},{9,8},{10,11... | collective-permute-start | bytes 393224 | tf_op jit(solution)/shard_map/ppermute | solution.py:17
  22.1 24.4 %copy-start.2 = (bf16[4096]{0:T(1024)(128)(2,1)S(1)}, bf16[4096]{0:T(1024)(128)(2,1)}, u32[]{:S(2)}) copy-start(bf16[4096]{0:T(1024)(128)(2,1)} %param.10) | copy-start | bytes 24580
  22.1 24.4 %copy-start.1 = (s32[4]{0:T(128)S(1)}, s32[4]{0:T(128)}, u32[]{:S(2)}) copy-start(s32[4]{0:T(128)} %param.15) | copy-start | bytes 52
  46.5 4.0 %collective-permute-start.2 = (bf16[8,32,256]{2,1,0:T(8,128)(2,1)S(1)}, bf16[8,32,256]{2,1,0:T(8,128)(2,1)S(1)}, u32[]{:S(2)}, u32[]{:S(2)}) collective-permute-start(bf16[8,32,256]{2,1,0:T(8,128)(2,1)S(1)} %all_to_all.31.x_ref.mine_ref), channel_id=1, source_target_pairs={{0,1},{1,0},{2,3},{3,2},{4,5},{5,4},{6,7},{7,6},{8,9},{9,8},{10,11... | collective-permute-start | bytes 393224 | tf_op jit(solution)/shard_map/ppermute | solution.py:17
  55.7 2.8 %collective-permute-start.3 = (bf16[8,32,256]{2,1,0:T(8,128)(2,1)S(1)}, bf16[8,32,256]{2,1,0:T(8,128)(2,1)S(1)}, u32[]{:S(2)}, u32[]{:S(2)}) collective-permute-start(bf16[8,32,256]{2,1,0:T(8,128)(2,1)S(1)} %get-tuple-element.42), channel_id=1, source_target_pairs={{0,1},{1,0},{2,3},{3,2},{4,5},{5,4},{6,7},{7,6},{8,9},{9,8},{10,11... | collective-permute-start | bytes 393224 | tf_op jit(solution)/shard_map/ppermute | solution.py:17
  78.3 1.6 %collective-permute-start.4 = (bf16[8,32,256]{2,1,0:T(8,128)(2,1)S(1)}, bf16[8,32,256]{2,1,0:T(8,128)(2,1)S(1)}, u32[]{:S(2)}, u32[]{:S(2)}) collective-permute-start(bf16[8,32,256]{2,1,0:T(8,128)(2,1)S(1)} %all_to_all.33.d_mine_ref), channel_id=1, source_target_pairs={{0,1},{1,0},{2,3},{3,2},{4,5},{5,4},{6,7},{7,6},{8,9},{9,8},{10,11... | collective-permute-start | bytes 393224 | tf_op jit(solution)/shard_map/ppermute | solution.py:17
